TPU v7x, 32 devices: a whole 2x2x4 slice. The times are simulated.
32 devices in a mesh: pairs: 2 (over x), cols: 16 (over z, y, core).
Axes of the slice: x: 2, y: 2, z: 4, core: 2. Of those that a mesh axis runs over, the one named last changes fastest.
Arguments:
- new_points: bfloat16 [4096, 512], P('pairs'), parts along dimension 0, may hold values from -8 to 8
- arch_points: bfloat16 [32768, 512], P(('pairs', 'cols')), parts along dimension 0, may hold values from -4 to 4
- new_mass: float32 [4096], P('pairs'), parts along dimension 0, may hold values from 0.3 to 3
- arch_mass: float32 [32768], P(('pairs', 'cols')), parts along dimension 0, may hold values from 0.3 to 3
Outputs:
- new_potential: float32 [4096], P('pairs'), parts along dimension 0
- arch_potential: float32 [32768], P(('pairs', 'cols')), parts along dimension 0
- new_grad: float32 [4096, 512], P(('pairs', 'cols')), parts along dimension 0
- arch_grad: float32 [32768, 512], P(('pairs', 'cols')), parts along dimension 0
There are 2 independent parts, one for each index of `pairs`. A program takes and returns all parts, laid end to end along the dimension named above; each array names one. Nothing has to cross between parts.
All inputs are finite; a program needn't handle non-finite values.
Results may differ from a plain program's by a relative error of at most 0.0028.
Values sent between devices are 32-bit elements; how exact they have to be, the bound alone decides.
No kernel may reach another device: no remote copies, remote signals or barrier semaphores. Data moves between devices by JAX's collectives and lax.ppermute only.
A program may use at most 64 MiB of HBM per device.

v0:
```python
import jax
import jax.numpy as jnp
from jax import lax
from jax.sharding import PartitionSpec as P

ITERS = 3


EPSILON = 0.05


def local(new_points, arch_points, new_mass, arch_mass):
    rows = new_points.shape[0]
    count = lax.axis_size("cols")
    total_cols = arch_points.shape[0] * count
    width = new_points.shape[1]
    new_float = new_points.astype(jnp.float32)
    arch_float = arch_points.astype(jnp.float32)
    sq_new = jnp.sum(new_float * new_float, 1)
    sq_arch = jnp.sum(arch_float * arch_float, 1)
    cross = lax.dot_general(
        new_points, arch_points, (((1,), (1,)), ((), ())), preferred_element_type=jnp.float32
    )
    cost = (sq_new[:, None] + sq_arch[None, :] - 2.0 * cross) / width
    log_new = jnp.log(new_mass / rows)
    log_arch = jnp.log(arch_mass / total_cols)
    arch_pot = jnp.zeros((arch_points.shape[0],), jnp.float32)
    arch_hist = [arch_pot]
    new_hist = []
    for step in range(ITERS):
        scores = log_arch[None, :] + (arch_pot[None, :] - cost) / EPSILON
        top = lax.pmax(jnp.max(scores, 1), "cols")
        total = lax.psum(jnp.sum(jnp.exp(scores - top[:, None]), 1), "cols")
        new_pot = -EPSILON * (top + jnp.log(total))
        weights = log_new[:, None] + (new_pot[:, None] - cost) / EPSILON
        col_top = jnp.max(weights, 0)
        arch_pot = -EPSILON * (col_top + jnp.log(jnp.sum(jnp.exp(weights - col_top[None, :]), 0)))
        new_hist.append(new_pot)
        arch_hist.append(arch_pot)
    arch_bar = arch_mass / total_cols
    cost_bar = jnp.zeros(cost.shape, jnp.float32)
    for step in reversed(range(ITERS)):
        new_pot = new_hist[step]
        q_tile = jnp.exp(
            log_new[:, None] + (new_pot[:, None] - cost + arch_hist[step + 1][None, :]) / EPSILON
        )
        w_tile = q_tile * arch_bar[None, :]
        cost_bar = cost_bar + w_tile
        new_bar = lax.psum(jnp.sum(w_tile, 1), "cols")
        if step == ITERS - 1:
            new_bar = new_bar + new_mass / rows
        p_tile = jnp.exp(
            log_arch[None, :] + (arch_hist[step][None, :] - cost + new_pot[:, None]) / EPSILON
        )
        v_tile = p_tile * new_bar[:, None]
        cost_bar = cost_bar + v_tile
        arch_bar = jnp.sum(v_tile, 0)
    bar_half = cost_bar.astype(jnp.bfloat16)
    row_weight = jnp.sum(cost_bar, 1)
    col_weight = jnp.sum(cost_bar, 0)
    back = lax.dot_general(
        bar_half, new_points, (((0,), (0,)), ((), ())), preferred_element_type=jnp.float32
    )
    arch_grad = total_cols * (col_weight[:, None] * arch_float - back)
    share = rows // count
    point_rows = new_points.astype(jnp.float32)
    whole = lax.psum(
        row_weight[:, None] * point_rows
        - jnp.dot(bar_half, arch_points, preferred_element_type=jnp.float32),
        "cols",
    )
    summed = lax.dynamic_slice_in_dim(whole, lax.axis_index("cols") * share, share, 0)
    new_grad = rows * summed
    return (new_hist[-1], arch_hist[-1], new_grad, arch_grad)


def solution(mesh):
    in_specs = (P("pairs", None), P(("pairs", "cols"), None), P("pairs"), P(("pairs", "cols")))
    out_specs = (
        P("pairs"),
        P(("pairs", "cols")),
        P(("pairs", "cols"), None),
        P(("pairs", "cols"), None),
    )
    return jax.shard_map(local, mesh=mesh, in_specs=in_specs, out_specs=out_specs, check_vma=False)
```

profile of v0, /device:TPU:0, one launch (start us, length us, event | category | flops | bytes accessed | tf_op | source)
XLA Modules:
  0.0 504.7 jit_solution(6599112384441278140)
XLA Ops:
  7.2 0.0 all-reduce.2.cloned.1.call-start
  7.2 0.7 broadcast_multiply_fusion
  7.9 2.1 fusion.11
  10.0 1.5 fusion.13
  11.5 8.1 %fusion = (f32[2048]{0:T(1024)S(1)}, f32[2048,1024]{0,1:T(8,128)}) fusion(f32[1024]{0:T(1024)S(1)} %get-tuple-element.8, bf16[2048,512]{1,0:T(8,128)(2,1)} %param.4, bf16[1024,512]{1,0:T(8,128)(2,1)} %param.5, f32[1024]{0:T(1024)S(1)} %fusion.13, f32[2048]{0:T(1024)S(1)} %fusion.11), kind=kOutput, calls=%fused_computation.19 | convolution fusion | flops 2164258816 | bytes 11558912 | tf_op jit(solution)/shard_map/dot_general | solution.py:21
  19.6 0.0 copy-start.3
  19.6 35.4 %pmax.21 = f32[2048]{0:T(1024)S(1)} all-reduce(f32[2048]{0:T(1024)S(1)} %get-tuple-element.9), channel_id=1, replica_groups=mesh['pairs'=2,'cols'=16] {'cols'}, use_global_device_ids=true, to_apply=%region_3.0 | all-reduce | flops 2048 | bytes 16384 | tf_op jit(solution)/shard_map/pmax | solution.py:32
  55.1 4.6 exponential_reduce_fusion.5
  59.7 30.0 %psum.49 = f32[2048]{0:T(1024)S(1)} all-reduce(f32[2048]{0:T(1024)S(1)} %exponential_reduce_fusion.5), channel_id=1, replica_groups=mesh['pairs'=2,'cols'=16] {'cols'}, use_global_device_ids=true, to_apply=%region_5.0 | all-reduce | flops 2048 | bytes 16384 | tf_op jit(solution)/shard_map/psum | solution.py:33
  89.7 0.0 copy-done.3
  89.7 0.0 slice-start
  89.7 4.7 fusion.1
  94.5 0.0 slice-start.1
  94.5 5.3 %exponential_reduce_fusion.4 = f32[1024]{0:T(1024)S(1)} fusion(f32[2048,1024]{0,1:T(8,128)} %get-tuple-element.10, f32[1024]{0:T(1024)S(1)} %fusion.1, f32[2048]{0:T(1024)S(1)} %add_multiply_fusion.2, f32[2048]{0:T(1024)S(1)} %multiply_log_fusion), kind=kLoop, calls=%fused_computation.14 | loop fusion | flops 10484736 | bytes 8413184 | tf_op jit(solution)/shard_map/reduce_sum | solution.py:37
  99.8 0.0 slice-done
  99.8 0.0 slice-done.1
  99.8 1.4 fusion.2
  101.3 30.0 %pmax.22 = f32[2048]{0:T(1024)S(1)} all-reduce(f32[2048]{0:T(1024)S(1)} %fusion.2), channel_id=1, replica_groups=mesh['pairs'=2,'cols'=16] {'cols'}, use_global_device_ids=true, to_apply=%region_9.0 | all-reduce | flops 2048 | bytes 16384 | tf_op jit(solution)/shard_map/pmax | solution.py:32
  131.3 4.5 exponential_reduce_fusion.3
  135.8 30.2 %psum.50 = f32[2048]{0:T(1024)S(1)} all-reduce(f32[2048]{0:T(1024)S(1)} %exponential_reduce_fusion.3), channel_id=1, replica_groups=mesh['pairs'=2,'cols'=16] {'cols'}, use_global_device_ids=true, to_apply=%region_11.0 | all-reduce | flops 2048 | bytes 16384 | tf_op jit(solution)/shard_map/psum | solution.py:33
  166.0 0.0 slice-start.2
  166.0 4.7 fusion.3
  170.7 0.0 slice-start.3
  170.7 5.3 %exponential_reduce_fusion.2 = f32[1024]{0:T(1024)S(1)} fusion(f32[2048,1024]{0,1:T(8,128)} %get-tuple-element.10, f32[1024]{0:T(1024)S(1)} %fusion.3, f32[2048]{0:T(1024)S(1)} %add_multiply_fusion.1, f32[2048]{0:T(1024)S(1)} %multiply_log_fusion), kind=kLoop, calls=%fused_computation.10 | loop fusion | flops 10484736 | bytes 8413184 | tf_op jit(solution)/shard_map/reduce_sum | solution.py:37
  176.1 0.0 slice-done.2
  176.1 0.0 slice-done.3
  176.1 1.4 fusion.4
  177.5 30.0 %pmax.23 = f32[2048]{0:T(1024)S(1)} all-reduce(f32[2048]{0:T(1024)S(1)} %fusion.4), channel_id=1, replica_groups=mesh['pairs'=2,'cols'=16] {'cols'}, use_global_device_ids=true, to_apply=%region_15.0 | all-reduce | flops 2048 | bytes 16384 | tf_op jit(solution)/shard_map/pmax | solution.py:32
  207.5 4.5 exponential_reduce_fusion.1
  212.1 30.0 %psum.51 = f32[2048]{0:T(1024)S(1)} all-reduce(f32[2048]{0:T(1024)S(1)} %exponential_reduce_fusion.1), channel_id=1, replica_groups=mesh['pairs'=2,'cols'=16] {'cols'}, use_global_device_ids=true, to_apply=%region_17.0 | all-reduce | flops 2048 | bytes 16384 | tf_op jit(solution)/shard_map/psum | solution.py:33
  242.1 0.0 copy-start.2
  242.1 0.0 slice-start.4
  242.1 4.7 fusion.5
  246.8 0.0 slice-start.5
  246.8 5.3 %exponential_reduce_fusion = f32[1024]{0:T(1024)S(1)} fusion(f32[2048,1024]{0,1:T(8,128)} %get-tuple-element.10, f32[1024]{0:T(1024)S(1)} %fusion.5, f32[2048]{0:T(1024)S(1)} %add_multiply_fusion, f32[2048]{0:T(1024)S(1)} %multiply_log_fusion), kind=kLoop, calls=%fused_computation.6 | loop fusion | flops 10484736 | bytes 8413184 | tf_op jit(solution)/shard_map/reduce_sum | solution.py:37
  252.1 0.0 copy-start.4
  252.1 0.0 slice-done.4
  252.1 0.0 slice-done.5
  252.1 2.8 fusion.6
  255.0 30.0 %psum.52 = f32[2048]{0:T(1024)S(1)} all-reduce(f32[2048]{0:T(1024)S(1)} %fusion.6), channel_id=1, replica_groups=mesh['pairs'=2,'cols'=16] {'cols'}, use_global_device_ids=true, to_apply=%region_21.0 | all-reduce | flops 2048 | bytes 16384 | tf_op jit(solution)/shard_map/psum | solution.py:49
  285.0 4.8 fusion.7
  289.8 4.8 fusion.8
  294.6 30.2 %psum.53 = f32[2048]{0:T(1024)S(1)} all-reduce(f32[2048]{0:T(1024)S(1)} %fusion.8), channel_id=1, replica_groups=mesh['pairs'=2,'cols'=16] {'cols'}, use_global_device_ids=true, to_apply=%region_24.0 | all-reduce | flops 2048 | bytes 16384 | tf_op jit(solution)/shard_map/psum | solution.py:49
  324.9 4.8 fusion.9
  329.7 4.8 fusion.10
  334.5 30.0 %psum.54 = f32[2048]{0:T(1024)S(1)} all-reduce(f32[2048]{0:T(1024)S(1)} %fusion.10), channel_id=1, replica_groups=mesh['pairs'=2,'cols'=16] {'cols'}, use_global_device_ids=true, to_apply=%region_27.0 | all-reduce | flops 2048 | bytes 16384 | tf_op jit(solution)/shard_map/psum | solution.py:49
  364.5 0.0 copy-done.2
  364.5 0.0 copy-done.4
  364.5 0.0 copy-start
  364.5 0.0 copy-start.1
  364.5 16.3 %fusion.22 = (f32[1024]{0:T(1024)S(1)}, f32[2048]{0:T(1024)S(1)}, bf16[2048,1024]{0,1:T(8,128)(2,1)S(1)}) fusion(f32[2048]{0:T(1024)S(1)} %psum.54, f32[2048,1024]{0,1:T(8,128)} %get-tuple-element.10, f32[1024]{0:T(1024)S(1)} %fusion.9, f32[2048]{0:T(1024)S(1)} %add_multiply_fusion.2, f32[2048]{0:T(1024)S(1)} %psum.53, f32[1024]{0:T(1024)S(1)} %add_multiply_fusion.5, ...), kind=kLoop, calls=%fused_computation.53 | loop fusion | flops 79688704 | bytes 12681216 | tf_op jit(solution)/shard_map/reduce_sum | solution.py:60
  380.8 0.0 copy-start.5
  380.8 2.0 copy-done.5
  382.8 0.0 copy-done
  382.8 0.0 copy-done.1
  382.8 4.5 fusion.12
  387.3 0.0 all-reduce.2.cloned.1.call-update
  387.3 5.9 %fusion.15 = f32[1024,512]{1,0:T(8,128)} fusion(bf16[1024,512]{1,0:T(8,128)(2,1)S(1)} %copy-done.1, bf16[2048,512]{1,0:T(8,128)(2,1)S(1)} %copy-done, bf16[2048,1024]{0,1:T(8,128)(2,1)} %copy-done.5, f32[1024]{0:T(1024)S(1)} %get-tuple-element.4), kind=kOutput, calls=%fused_computation.38 | convolution fusion | flops 2149580800 | bytes 9441280 | tf_op jit(solution)/shard_map/dot_general | solution.py:61
  393.2 103.0 %all-reduce.2.cloned.1.call-done = f32[2048,512]{1,0:T(8,128)} async-done(((f32[2048,512]{1,0:T(8,128)}), f32[2048,512]{1,0:T(8,128)}) %all-reduce.2.cloned.1.call-update) | async-done | bytes 4194320 | tf_op jit(solution)/shard_map/psum | solution.py:67
  496.2 1.7 dynamic-slice_multiply_fusion
  (11 shorter events, 0.1 us)
Async XLA Ops:
  7.2 489.0 %all-reduce.2.cloned.1.call-start = ((), (), s32[]{:S(2)}) async-start(), calls=%async_computation | async-start | bytes 8388608 | tf_op jit(solution)/shard_map/psum | solution.py:67
  19.6 70.1 %copy-start.3 = (f32[2048]{0:T(1024)S(1)}, f32[2048]{0:T(1024)}, u32[]{:S(2)}) copy-start(f32[2048]{0:T(1024)} %param.6) | copy-start | bytes 24580
  89.7 10.1 %slice-start = ((s8[8388608]{0:T(1024)(128)(4,1)}), s8[4194304]{0:T(1024)(128)(4,1)S(1)}, s32[]{:S(2)}) async-start(s8[8388608]{0:T(1024)(128)(4,1)} %bitcast.6), calls=%async_computation.1 | async-start | bytes 8388608
  94.5 5.3 %slice-start.1 = ((s8[8388608]{0:T(1024)(128)(4,1)}), s8[4194304]{0:T(1024)(128)(4,1)S(1)}, s32[]{:S(2)}) async-start(s8[8388608]{0:T(1024)(128)(4,1)} %bitcast.6), calls=%async_computation.2 | async-start | bytes 8388608
  166.0 10.0 %slice-start.2 = ((s8[8388608]{0:T(1024)(128)(4,1)}), s8[4194304]{0:T(1024)(128)(4,1)S(1)}, s32[]{:S(2)}) async-start(s8[8388608]{0:T(1024)(128)(4,1)} %bitcast.8), calls=%async_computation.3 | async-start | bytes 8388608
  170.7 5.3 %slice-start.3 = ((s8[8388608]{0:T(1024)(128)(4,1)}), s8[4194304]{0:T(1024)(128)(4,1)S(1)}, s32[]{:S(2)}) async-start(s8[8388608]{0:T(1024)(128)(4,1)} %bitcast.8), calls=%async_computation.4 | async-start | bytes 8388608
  242.1 122.4 %copy-start.2 = (f32[2048]{0:T(1024)}, f32[2048]{0:T(1024)S(1)}, u32[]{:S(2)}) copy-start(f32[2048]{0:T(1024)S(1)} %add_multiply_fusion) | copy-start | bytes 24580
  242.1 10.0 %slice-start.4 = ((s8[8388608]{0:T(1024)(128)(4,1)}), s8[4194304]{0:T(1024)(128)(4,1)S(1)}, s32[]{:S(2)}) async-start(s8[8388608]{0:T(1024)(128)(4,1)} %bitcast.10), calls=%async_computation.5 | async-start | bytes 8388608
  246.8 5.3 %slice-start.5 = ((s8[8388608]{0:T(1024)(128)(4,1)}), s8[4194304]{0:T(1024)(128)(4,1)S(1)}, s32[]{:S(2)}) async-start(s8[8388608]{0:T(1024)(128)(4,1)} %bitcast.10), calls=%async_computation.6 | async-start | bytes 8388608
  252.1 112.4 %copy-start.4 = (f32[1024]{0:T(1024)}, f32[1024]{0:T(1024)S(1)}, u32[]{:S(2)}) copy-start(f32[1024]{0:T(1024)S(1)} %add_multiply_fusion.3) | copy-start | bytes 12292
  364.5 18.3 %copy-start = (bf16[2048,512]{1,0:T(8,128)(2,1)S(1)}, bf16[2048,512]{1,0:T(8,128)(2,1)}, u32[]{:S(2)}) copy-start(bf16[2048,512]{1,0:T(8,128)(2,1)} %param.4) | copy-start | bytes 6291460
  364.5 18.3 %copy-start.1 = (bf16[1024,512]{1,0:T(8,128)(2,1)S(1)}, bf16[1024,512]{1,0:T(8,128)(2,1)}, u32[]{:S(2)}) copy-start(bf16[1024,512]{1,0:T(8,128)(2,1)} %param.5) | copy-start | bytes 3145732
  380.8 2.0 copy-start.5
Sparse Core Ops, SparseCore 0:
  387.5 108.6 all-reduce.1
where the time goes:
time: 505 us
  blocking collectives  276 us (55%)
  waiting for transfers between devices  103 us (20%)
  other arithmetic  90.9 us (18%)
  matrix products  18.5 us (4%)
  between operations  14.4 us (3%)
    psum x1, waiting for transfers between devices, local(): lax.psum(row_weight[:, None] * point_rows - jnp.dot(bar_half, arch_points...  103 us
    pmax x3, blocking collectives, local(): top = lax.pmax(jnp.max(scores, 1), 'cols')  95.4 us
    psum x3, blocking collectives, local(): new_bar = lax.psum(jnp.sum(w_tile, 1), 'cols')  90.2 us
    psum x3, blocking collectives, local(): total = lax.psum(jnp.sum(jnp.exp(scores - top[:, None]), 1), 'cols')  90.2 us
    reduce_sum x1, other arithmetic, local(): col_weight = jnp.sum(cost_bar, 0)  16.3 us
    reduce_sum x3, other arithmetic, local(): jnp.sum(jnp.exp(weights - col_top[None, :]), 0)  15.9 us
    reduce_max x3, other arithmetic, local(): col_top = jnp.max(weights, 0)  14.1 us
    reduce_sum x3, other arithmetic, local(): total = lax.psum(jnp.sum(jnp.exp(scores - top[:, None]), 1), 'cols')  13.7 us
  transfers between devices with their start and end apart: 1, of which 1 were waited for; matrix products, arithmetic and copies ran while one was open for 1% of the time, Pallas kernels for 0%

commit v1 on v0

v1 whole, which is shorter than its diff:
```python
import functools
import math
import jax
import jax.numpy as jnp
from jax import lax
from jax.experimental import pallas as pl
from jax.experimental.pallas import tpu as pltpu
from jax.sharding import PartitionSpec as P

EPSILON = 0.05
LOGK = math.log2(math.e) / EPSILON
LANES = 128
SUB = 8
VMEM = pltpu.VMEM
F32 = jnp.float32
BF16 = jnp.bfloat16


def params(mib=28):
    return pltpu.CompilerParams(vmem_limit_bytes=mib * 1024 * 1024)


def full(n):
    return [pl.BlockSpec(memory_space=VMEM)] * n


def column(row):
    return jnp.transpose(jnp.broadcast_to(row, (LANES, LANES)))


def lanes(x):
    return [x[:, l * LANES:(l + 1) * LANES] for l in range(x.shape[1] // LANES)]


def wide(x):
    return jnp.broadcast_to(x, (SUB, LANES))


def tree(op, xs):
    xs = list(xs)
    while len(xs) > 1:
        xs = [op(xs[i], xs[i + 1]) if i + 1 < len(xs) else xs[i] for i in range(0, len(xs), 2)]
    return xs[0]


def lane_sum(xs):
    return wide(jnp.sum(tree(jnp.add, xs), axis=1, keepdims=True))


def lane_max(xs):
    return wide(jnp.max(tree(jnp.maximum, xs), axis=1, keepdims=True))


def scores_kernel(total_cols, x_ref, y_ref, mass_ref, z_ref, b_ref, sq_ref, lse_ref, cb_ref):
    cols, width = y_ref.shape
    rows = x_ref.shape[0]
    for c in range(cols // LANES):
        s = pl.ds(c * LANES, LANES)
        b = column(mass_ref[:, s] * (1.0 / total_cols))
        b_ref[s, :] = b
        yf = y_ref[s, :].astype(F32)
        sq = jnp.sum(yf * yf, axis=1, keepdims=True) * (LOGK / width)
        sq = jnp.broadcast_to(sq, (LANES, LANES))
        sq_ref[s, :] = sq
        cb_ref[s, :] = jnp.log2(b) - sq
    step = 2 * LANES
    for r in range(rows // step):
        s = pl.ds(r * step, step)
        z_ref[:, s] = lax.dot_general(
            y_ref[...], x_ref[s, :], (((1,), (1,)), ((), ())), preferred_element_type=F32
        ) * (2.0 * LOGK / width)

        def top(g, m):
            q = pl.ds(pl.multiple_of(g * 64, 64), 64)
            cb = cb_ref[q, :]
            z = z_ref[q, s]
            for h in range(64 // SUB):
                hs = slice(h * SUB, (h + 1) * SUB)
                m = [jnp.maximum(a, v + cb[hs]) for a, v in zip(m, lanes(z[hs]))]
            return m

        first = [jnp.full((SUB, LANES), -jnp.inf, F32)] * (step // LANES)
        m = lax.fori_loop(0, cols // 64, top, first)
        m = [jnp.max(a, axis=0, keepdims=True) for a in m]
        mw = [wide(a) for a in m]

        def add(g, t):
            q = pl.ds(pl.multiple_of(g * 64, 64), 64)
            cb = cb_ref[q, :]
            z = z_ref[q, s]
            for h in range(64 // SUB):
                hs = slice(h * SUB, (h + 1) * SUB)
                t = [a + jnp.exp2(v + cb[hs] - n) for a, v, n in zip(t, lanes(z[hs]), mw)]
            return t

        t = lax.fori_loop(0, cols // 64, add, [jnp.zeros((SUB, LANES), F32)] * (step // LANES))
        for l, (n, v) in enumerate(zip(m, t)):
            lse_ref[:, pl.ds(r * step + l * LANES, LANES)] = n + jnp.log2(
                jnp.sum(v, axis=0, keepdims=True)
            )


def scores(new_points, arch_points, arch_mass, total_cols):
    rows, cols = new_points.shape[0], arch_points.shape[0]
    return pl.pallas_call(
        functools.partial(scores_kernel, total_cols),
        out_shape=(
            VMEM((cols, rows), F32),
            VMEM((cols, LANES), F32),
            VMEM((cols, LANES), F32),
            jax.ShapeDtypeStruct((1, rows), F32),
        ),
        in_specs=full(3),
        out_specs=tuple(full(4)),
        scratch_shapes=[pltpu.VMEM((cols, LANES), F32)],
        compiler_params=params(),
        name="scores",
    )(new_points, arch_points, arch_mass.reshape(1, cols))


def plan_kernel(z_ref, b_ref, sq_ref, w_ref, q_ref, beta_ref, vb_ref, part_ref):
    cols, rows = z_ref.shape
    w = [wide(a) for a in lanes(w_ref[...])]

    def body(g, acc):
        for h in range(2):
            s = pl.ds(pl.multiple_of(g * 2 * SUB, 2 * SUB) + h * SUB, SUB)
            e = [z + a for z, a in zip(lanes(z_ref[s, :]), w)]
            n = lane_max(e)
            e = [jnp.exp2(a - n) for a in e]
            t = lane_sum(e)
            beta = -(n + jnp.log2(t))
            r = 1.0 / t
            b = b_ref[s, :]
            beta_ref[s, :] = beta
            vb_ref[s, :] = b * jnp.exp2(-sq_ref[s, :] - beta)
            rb = []
            for l, a in enumerate(e):
                q = a * r
                q_ref[s, pl.ds(l * LANES, LANES)] = q
                rb.append(q)
            acc = [a + q * b for a, q in zip(acc, rb)]
        return acc

    acc = lax.fori_loop(0, cols // (2 * SUB), body, [jnp.zeros((SUB, LANES), F32)] * len(w))
    for l, a in enumerate(acc):
        part_ref[:, pl.ds(l * LANES, LANES)] = jnp.sum(a, axis=0, keepdims=True)


def plan(z, b, sq, w):
    cols, rows = z.shape
    return pl.pallas_call(
        plan_kernel,
        out_shape=(
            VMEM((cols, rows), F32),
            VMEM((cols, LANES), F32),
            VMEM((cols, LANES), F32),
            jax.ShapeDtypeStruct((1, rows), F32),
        ),
        in_specs=full(4),
        out_specs=tuple(full(4)),
        compiler_params=params(),
        name="plan",
    )(z, b, sq, w)


def sweep_kernel(kind, q_ref, b_ref, *refs):
    cols, rows = q_ref.shape
    v_ref = refs[0] if kind == "mid" else None
    w_ref, c_ref, part_ref = refs[-3:]
    w = [wide(a) for a in lanes(w_ref[...])]
    unroll = 4

    def body(g, acc):
        for h in range(unroll):
            s = pl.ds(pl.multiple_of(g * unroll * SUB, unroll * SUB) + h * SUB, SUB)
            q = lanes(q_ref[s, :])
            t = lane_sum([a * c for a, c in zip(q, w)])
            b = b_ref[s, :]
            if kind == "fwd":
                c = b / t
            elif kind == "mid":
                c = b * t * v_ref[s, :] * v_ref[s, :]
            else:
                c = b * t
            c_ref[s, :] = c
            acc = [a + d * c for a, d in zip(acc, q)]
        return acc

    acc = lax.fori_loop(0, cols // (unroll * SUB), body, [jnp.zeros((SUB, LANES), F32)] * len(w))
    for l, a in enumerate(acc):
        part_ref[:, pl.ds(l * LANES, LANES)] = jnp.sum(a, axis=0, keepdims=True)


def sweep(kind, q, b, w, *more):
    cols, rows = q.shape
    return pl.pallas_call(
        functools.partial(sweep_kernel, kind),
        out_shape=(VMEM((cols, LANES), F32), jax.ShapeDtypeStruct((1, rows), F32)),
        in_specs=full(3 + len(more)),
        out_specs=tuple(full(2)),
        compiler_params=params(),
        name="sweep_" + kind,
    )(q, b, *more, w)


def finish_kernel(total_cols, q_ref, x_ref, y_ref, b_ref, sq_ref, beta_ref, bv2_ref, bv3_ref,
                  mid_ref, gb1_ref, vb_ref, rows_ref, pot_ref, arch_ref, new_ref, half_ref, tr_ref):
    cols, rows = q_ref.shape
    width = y_ref.shape[1]
    step = 256
    for jb in range(cols // step):
        def body(g, carry):
            base = pl.multiple_of(g * 2 * SUB, 2 * SUB)
            parts = []
            for h in range(2):
                s = pl.ds(jb * step + base + h * SUB, SUB)
                b, bv2, bv3 = b_ref[s, :], bv2_ref[s, :], bv3_ref[s, :]
                mid, gb1, vb = mid_ref[s, :], gb1_ref[s, :], vb_ref[s, :]
                outs, dots = [], []
                for l in range(rows // LANES):
                    ls = pl.ds(l * LANES, LANES)
                    q = q_ref[s, ls]
                    r = [wide(rows_ref[pl.ds(i, 1), ls]) for i in range(5)]
                    c = r[0] * bv3 + r[1] * bv2 + r[2] * mid + r[3] * b + r[4] * vb + gb1
                    outs.append(q * c)
                    dots.append(q * r[4])
                gb0 = vb * lane_sum(dots)
                tr_ref[s, :] = b + 2.0 * (mid * b / bv2 + gb1) + gb0
                parts.append(outs)
            for l in range(rows // LANES):
                half_ref[pl.ds(base, 2 * SUB), pl.ds(l * LANES, LANES)] = jnp.concatenate(
                    [parts[0][l], parts[1][l]], axis=0).astype(BF16)
            return carry

        lax.fori_loop(0, step // (2 * SUB), body, 0)
        js = pl.ds(jb * step, step)
        y = y_ref[js, :]
        back = jnp.dot(half_ref[...], x_ref[...], preferred_element_type=F32)
        tr = tr_ref[js, :]
        for l in range(width // LANES):
            ls = slice(l * LANES, (l + 1) * LANES)
            arch_ref[js, ls] = total_cols * (tr * y[:, ls].astype(F32) - back[:, ls])
        prod = lax.dot_general(half_ref[...], y, (((0,), (0,)), ((), ())), preferred_element_type=F32)
        new_ref[...] = prod if jb == 0 else new_ref[...] + prod
    for c in range(cols // LANES):
        s = pl.ds(c * LANES, LANES)
        pot = (beta_ref[s, :] + sq_ref[s, :] + jnp.log2(bv3_ref[s, :] / b_ref[s, :])) * (1.0 / LOGK)
        pot_ref[:, s] = jnp.transpose(pot)[0:1, :]


def finish(total_cols, q, x, y, *rest):
    cols, rows = q.shape
    width = y.shape[1]
    return pl.pallas_call(
        functools.partial(finish_kernel, float(total_cols)),
        out_shape=(
            jax.ShapeDtypeStruct((1, cols), F32),
            jax.ShapeDtypeStruct((cols, width), F32),
            jax.ShapeDtypeStruct((rows, width), F32),
        ),
        in_specs=full(3 + len(rest)),
        out_specs=tuple(full(3)),
        scratch_shapes=[pltpu.VMEM((256, rows), BF16), pltpu.VMEM((cols, LANES), F32)],
        compiler_params=params(),
        name="finish",
    )(q, x, y, *rest)


def combine(x, count, join):
    def swap(v, k):
        return lax.ppermute(v, "cols", [(i, i ^ k) for i in range(count)])

    k = 1
    while k < count:
        if 4 * k <= count:
            x = join([x, swap(x, k), swap(x, 2 * k), swap(x, 3 * k)])
            k *= 4
        else:
            x = join([x, swap(x, k)])
            k *= 2
    return x


def add_join(xs):
    return tree(jnp.add, xs)


def lse_join(xs):
    m = tree(jnp.maximum, xs)
    return m + jnp.log2(tree(jnp.add, [jnp.exp2(x - m) for x in xs]))


def local(new_points, arch_points, new_mass, arch_mass):
    rows = new_points.shape[0]
    count = lax.axis_size("cols")
    if count & (count - 1):
        def reduce_add(x):
            return lax.psum(x, "cols")

        def reduce_lse(x):
            m = lax.pmax(x, "cols")
            return m + jnp.log2(lax.psum(jnp.exp2(x - m), "cols"))
    else:
        reduce_add = functools.partial(combine, count=count, join=add_join)
        reduce_lse = functools.partial(combine, count=count, join=lse_join)
    total_cols = arch_points.shape[0] * count
    width = new_points.shape[1]
    new_float = new_points.astype(F32)
    sq_new = jnp.sum(new_float * new_float, 1) * (LOGK / width)
    a = (new_mass / rows).reshape(1, rows)

    z, b, sq, lse = scores(new_points, arch_points, arch_mass, total_cols)
    alpha = -reduce_lse(lse)
    q, beta, vb, part = plan(z, b, sq, jnp.log2(a) + alpha)
    u2 = a / reduce_add(part)
    bv2, part = sweep("fwd", q, b, u2)
    u3 = a / reduce_add(part)
    bv3, part = sweep("fwd", q, b, u3)
    fbar3 = a + u3 * reduce_add(part)
    w3 = u3 * fbar3 / a
    mid, part = sweep("mid", q, b, w3, bv2 / b)
    fbar2 = u2 * reduce_add(part)
    w2 = u2 * fbar2 / a
    gb1, part = sweep("bwd", q, b, w2)
    fbar1 = reduce_add(part)
    w1 = fbar1 / a
    packed = jnp.concatenate([u3, w3, u2, w2, w1], axis=0)
    pot, arch_grad, product = finish(
        total_cols, q, new_points, arch_points, b, sq, beta, bv2, bv3, mid, gb1, vb, packed
    )
    share = rows // count
    start = lax.axis_index("cols") * share
    summed = lax.psum_scatter(product, "cols", scatter_dimension=0, tiled=True)
    row_weight = 2.0 * (fbar3 + fbar2 + fbar1) - a
    mine = lax.dynamic_slice_in_dim(row_weight.reshape(rows), start, share, 0)
    points = lax.dynamic_slice_in_dim(new_points, start, share, 0).astype(F32)
    new_grad = rows * (mine[:, None] * points - summed)
    new_pot = (alpha.reshape(rows) + jnp.log2(u3).reshape(rows) + sq_new) * (1.0 / LOGK)
    return (new_pot, pot.reshape(-1), new_grad, arch_grad)


def solution(mesh):
    in_specs = (P("pairs", None), P(("pairs", "cols"), None), P("pairs"), P(("pairs", "cols")))
    out_specs = (
        P("pairs"),
        P(("pairs", "cols")),
        P(("pairs", "cols"), None),
        P(("pairs", "cols"), None),
    )
    return jax.shard_map(local, mesh=mesh, in_specs=in_specs, out_specs=out_specs, check_vma=False)
```

time: 505 us -> 231 us (0.46)
  blocking collectives: 276 us -> 0 us
  other arithmetic: 90.9 us -> 4.01 us
  Pallas kernels: 0 us -> 50.6 us
  starting transfers between devices: 0.04 us -> 39.2 us
  local copies, waits for them, and re-layouts: 2.02 us -> 26.2 us
  matrix products: 18.5 us -> 0 us
  waiting for transfers between devices: 103 us -> 96.3 us
    psum x6 -> x0, blocking collectives: 180 us -> none  [the longest x3 90.2 us: local(): new_bar = lax.psum(jnp.sum(w_tile, 1), 'cols')]
    psum x1 -> x0, waiting for transfers between devices: 103 us -> none  [local(): lax.psum(row_weight[:, None] * point_rows - jnp.dot(bar_half, arch_points...]
    pmax x3 -> x0, blocking collectives: 95.4 us -> none  [local(): top = lax.pmax(jnp.max(scores, 1), 'cols')]
    reduce_sum x14 -> x1, other arithmetic: 71.5 us -> 0.48 us  [local(): sq_new = jnp.sum(new_float * new_float, 1) * (LOGK / width)]
    reduce_scatter x0 -> x1, waiting for transfers between devices: none -> 70.8 us  [local(): summed = lax.psum_scatter(product, 'cols', scatter_dimension=0, tiled=True)]
    pallas_call x0 -> x7, Pallas kernels: none -> 50.6 us  [the longest x4 15.2 us: sweep(): pl.pallas_call(functools.partial(sweep_kernel, kind), out_shape=(VMEM((co...]
    ppermute x0 -> x36, starting transfers between devices: none -> 39.2 us  [swap(): return lax.ppermute(v, 'cols', [(i, i ^ k) for i in range(count)])]
    ppermute x0 -> x36, waiting for transfers between devices: none -> 25.6 us  [swap(): return lax.ppermute(v, 'cols', [(i, i ^ k) for i in range(count)])]
  transfers between devices with their start and end apart: 1 -> 37, of which waited for: 1 -> 30; matrix products, arithmetic and copies ran while one was open for 1% -> 1% of each run, Pallas kernels for 0% -> 0%
where the time goes in v1:
time: 231 us
  waiting for transfers between devices  96.3 us (42%)
  Pallas kernels  50.6 us (22%)
  starting transfers between devices  39.2 us (17%)
  local copies, waits for them, and re-layouts  26.2 us (11%)
  between operations  14.3 us (6%)
  other arithmetic  4.01 us (2%)
    reduce_scatter x1, waiting for transfers between devices, local(): summed = lax.psum_scatter(product, 'cols', scatter_dimension=0, tiled=True)  70.8 us
    ppermute x36, starting transfers between devices, swap(): return lax.ppermute(v, 'cols', [(i, i ^ k) for i in range(count)])  39.2 us
    unnamed x44, local copies, waits for them, and re-layouts  26.2 us
    ppermute x36, waiting for transfers between devices, swap(): return lax.ppermute(v, 'cols', [(i, i ^ k) for i in range(count)])  25.6 us
    pallas_call x4, Pallas kernels, sweep(): pl.pallas_call(functools.partial(sweep_kernel, kind), out_shape=(VMEM((co...  15.2 us
    pallas_call x1, Pallas kernels, plan(): pl.pallas_call(plan_kernel, out_shape=(VMEM((cols, rows), F32), VMEM((col...  13.2 us
    pallas_call x1, Pallas kernels, finish(): pl.pallas_call(functools.partial(finish_kernel, float(total_cols)), out_s...  12.2 us
    pallas_call x1, Pallas kernels, scores(): pl.pallas_call(functools.partial(scores_kernel, total_cols), out_shape=(V...  9.93 us
  transfers between devices with their start and end apart: 37, of which 30 were waited for; matrix products, arithmetic and copies ran while one was open for 1% of the time, Pallas kernels for 0%

profile of v1, /device:TPU:0, one launch (start us, length us, event | category | flops | bytes accessed | tf_op | source)
XLA Modules:
  0.0 230.7 jit_solution(7727226423140644940)
XLA Ops:
  7.2 1.6 copy-done.2
  8.8 1.2 copy-done.7
  10.0 0.7 copy-done.21
  10.7 9.9 %scores.1 = (f32[1024,2048]{1,0:T(8,128)S(1)}, f32[1024,128]{1,0:T(8,128)S(1)}, f32[1024,128]{1,0:T(8,128)S(1)}, f32[1,2048]{1,0:T(1,128)S(1)}) custom-call(bf16[2048,512]{1,0:T(8,128)(2,1)S(1)} %copy-done.2, bf16[1024,512]{1,0:T(8,128)(2,1)S(1)} %copy-done.7, f32[1,1024]{1,0:T(1,128)S(1)} %bitcast.7), custom_call_target="tpu_custom_call" | custom-call | tf_op jit(solution)/shard_map/scores/pallas_call | solution.py:105
  20.7 3.3 %copy-done.4 = f32[1024,2048]{1,0:T(8,128)} copy-done((f32[1024,2048]{1,0:T(8,128)}, f32[1024,2048]{1,0:T(8,128)S(1)}, u32[]{:S(2)}) %copy-start.4) | copy-done | bytes 8388632
  24.0 2.4 %collective-permute-start.2 = (f32[1,2048]{1,0:T(1,128)S(1)}, f32[1,2048]{1,0:T(1,128)S(1)}, u32[]{:S(2)}, u32[]{:S(2)}) collective-permute-start(f32[1,2048]{1,0:T(1,128)S(1)} %get-tuple-element.23), channel_id=1, source_target_pairs={{0,3},{1,2},{2,1},{3,0},{4,7},{5,6},{6,5},{7,4},{8,11},{9,10},{10,... | collective-permute-start | bytes 24584 | tf_op jit(solution)/shard_map/ppermute | solution.py:272
  27.7 2.3 collective-permute-done.1
  30.1 3.7 %collective-permute-start.5 = (f32[1,2048]{1,0:T(1,128)S(1)}, f32[1,2048]{1,0:T(1,128)S(1)}, u32[]{:S(2)}, u32[]{:S(2)}) collective-permute-start(f32[1,2048]{1,0:T(1,128)S(1)} %multiply_add_fusion.2), channel_id=1, source_target_pairs={{0,12},{1,13},{2,14},{3,15},{4,8},{5,9},{6,10},{7,11},{8,4},{9,5},... | collective-permute-start | bytes 24584 | tf_op jit(solution)/shard_map/ppermute | solution.py:272
  33.8 0.8 collective-permute-start.3
  34.6 0.7 broadcast_multiply_fusion
  35.7 2.6 %collective-permute-done.4 = f32[1,2048]{1,0:T(1,128)S(1)} collective-permute-done((f32[1,2048]{1,0:T(1,128)S(1)}, f32[1,2048]{1,0:T(1,128)S(1)}, u32[]{:S(2)}, u32[]{:S(2)}) %collective-permute-start.4) | collective-permute-done | bytes 8224 | tf_op jit(solution)/shard_map/ppermute | solution.py:272
  38.4 3.4 %copy-done.5 = f32[1024,2048]{1,0:T(8,128)S(1)} copy-done((f32[1024,2048]{1,0:T(8,128)S(1)}, f32[1024,2048]{1,0:T(8,128)}, u32[]{:S(2)}) %copy-start.5) | copy-done | bytes 8388632
  41.8 13.2 %plan.1 = (f32[1024,2048]{1,0:T(8,128)S(1)}, f32[1024,128]{1,0:T(8,128)S(1)}, f32[1024,128]{1,0:T(8,128)S(1)}, f32[1,2048]{1,0:T(1,128)S(1)}) custom-call(f32[1024,2048]{1,0:T(8,128)S(1)} %copy-done.5, f32[1024,128]{1,0:T(8,128)S(1)} %get-tuple-element.25.b_ref, f32[1024,128]{1,0:T(8,128)S(1)} %get-tuple-element.26.sq_ref, f32[1,2048]{1,0:T(1,128)S(1)} %get-tuple-element.50.w_ref), custom_call_target="tpu_custom_call" | custom-call | tf_op jit(solution)/shard_map/plan/pallas_call | solution.py:152
  55.0 0.8 copy-done.13
  56.4 1.2 collective-permute-start.6
  57.7 1.2 collective-permute-done.8
  59.5 1.5 collective-permute-start.11
  61.7 2.3 collective-permute-start.9
  64.0 1.1 collective-permute-done.11
  65.7 3.9 %sweep_fwd.2 = (f32[1024,128]{1,0:T(8,128)S(1)}, f32[1,2048]{1,0:T(1,128)S(1)}) custom-call(f32[1024,2048]{1,0:T(8,128)S(1)} %get-tuple-element.27.q_ref, f32[1024,128]{1,0:T(8,128)S(1)} %get-tuple-element.25.b_ref, f32[1,2048]{1,0:T(1,128)S(1)} %add_divide_fusion.1.refs_0_), custom_call_target="tpu_custom_call" | custom-call | tf_op jit(solution)/shard_map/sweep_fwd/pallas_call | solution.py:197
  70.4 1.2 collective-permute-start.12
  71.6 1.2 collective-permute-done.14
  73.5 2.6 %collective-permute-start.17 = (f32[1,2048]{1,0:T(1,128)S(1)}, f32[1,2048]{1,0:T(1,128)S(1)}, u32[]{:S(2)}, u32[]{:S(2)}) collective-permute-start(f32[1,2048]{1,0:T(1,128)S(1)} %add_add_fusion.4), channel_id=1, source_target_pairs={{0,12},{1,13},{2,14},{3,15},{4,8},{5,9},{6,10},{7,11},{8,4},{9,5},... | collective-permute-start | bytes 24584 | tf_op jit(solution)/shard_map/ppermute | solution.py:272
  76.0 0.9 collective-permute-start.16
  76.9 1.0 collective-permute-start.15
  77.9 1.1 collective-permute-done.17
  79.0 1.6 collective-permute-done.16
  80.7 3.9 %sweep_fwd.3 = (f32[1024,128]{1,0:T(8,128)S(1)}, f32[1,2048]{1,0:T(1,128)S(1)}) custom-call(f32[1024,2048]{1,0:T(8,128)S(1)} %get-tuple-element.27.q_ref, f32[1024,128]{1,0:T(8,128)S(1)} %get-tuple-element.25.b_ref, f32[1,2048]{1,0:T(1,128)S(1)} %get-tuple-element.49.refs_0_), custom_call_target="tpu_custom_call" | custom-call | tf_op jit(solution)/shard_map/sweep_fwd/pallas_call | solution.py:197
  84.6 0.8 copy-done.15
  86.0 1.2 collective-permute-start.18
  87.3 1.2 collective-permute-done.20
  89.1 1.4 collective-permute-start.23
  90.6 1.0 collective-permute-start.22
  91.5 2.0 collective-permute-start.21
  93.6 1.0 collective-permute-done.23
  95.2 3.8 %sweep_mid.1 = (f32[1024,128]{1,0:T(8,128)S(1)}, f32[1,2048]{1,0:T(1,128)S(1)}) custom-call(f32[1024,2048]{1,0:T(8,128)S(1)} %get-tuple-element.27.q_ref, f32[1024,128]{1,0:T(8,128)S(1)} %get-tuple-element.25.b_ref, f32[1024,128]{1,0:T(8,128)S(1)} %div.28.refs_0_, f32[1,2048]{1,0:T(1,128)S(1)} %get-tuple-element.46.refs_1_), custom_call_target="tpu_custom_call" | custom-call | tf_op jit(solution)/shard_map/sweep_mid/pallas_call | solution.py:197
  99.0 0.8 copy-done.17
  100.5 1.2 collective-permute-start.24
  101.7 1.2 collective-permute-done.26
  103.5 2.6 %collective-permute-start.29 = (f32[1,2048]{1,0:T(1,128)S(1)}, f32[1,2048]{1,0:T(1,128)S(1)}, u32[]{:S(2)}, u32[]{:S(2)}) collective-permute-start(f32[1,2048]{1,0:T(1,128)S(1)} %add_add_fusion.2), channel_id=1, source_target_pairs={{0,12},{1,13},{2,14},{3,15},{4,8},{5,9},{6,10},{7,11},{8,4},{9,5},... | collective-permute-start | bytes 24584 | tf_op jit(solution)/shard_map/ppermute | solution.py:272
  106.1 1.0 collective-permute-start.28
  107.1 0.9 collective-permute-start.27
  108.0 1.1 collective-permute-done.29
  109.1 1.6 collective-permute-done.28
  110.8 3.6 %sweep_bwd.1 = (f32[1024,128]{1,0:T(8,128)S(1)}, f32[1,2048]{1,0:T(1,128)S(1)}) custom-call(f32[1024,2048]{1,0:T(8,128)S(1)} %get-tuple-element.27.q_ref, f32[1024,128]{1,0:T(8,128)S(1)} %get-tuple-element.25.b_ref, f32[1,2048]{1,0:T(1,128)S(1)} %get-tuple-element.44.refs_0_), custom_call_target="tpu_custom_call" | custom-call | tf_op jit(solution)/shard_map/sweep_bwd/pallas_call | solution.py:197
  114.5 0.8 copy-done.19
  115.9 1.2 collective-permute-start.30
  117.1 1.2 collective-permute-done.32
  118.9 1.4 collective-permute-start.35
  120.4 1.0 collective-permute-start.34
  121.4 2.0 collective-permute-start.33
  123.4 1.1 collective-permute-done.35
  125.1 3.4 %copy-done.1 = f32[1024,2048]{1,0:T(8,128)S(1)} copy-done((f32[1024,2048]{1,0:T(8,128)S(1)}, f32[1024,2048]{1,0:T(8,128)}, u32[]{:S(2)}) %copy-start.1) | copy-done | bytes 8388632
  128.5 1.2 copy-done.8
  129.7 1.0 copy-done.10
  130.8 1.0 copy-done.12
  131.8 1.0 copy-done.14
  132.9 1.0 copy-done.16
  133.9 1.0 copy-done.18
  135.0 1.0 copy-done.20
  136.0 12.2 %finish.1 = (f32[1,1024]{1,0:T(1,128)}, f32[1024,512]{1,0:T(8,128)}, f32[2048,512]{1,0:T(8,128)S(1)}) custom-call(f32[1024,2048]{1,0:T(8,128)S(1)} %copy-done.1, bf16[2048,512]{1,0:T(8,128)(2,1)S(1)} %copy-done.3, bf16[1024,512]{1,0:T(8,128)(2,1)S(1)} %copy-done.8, f32[1024,128]{1,0:T(8,128)S(1)} %get-tuple-element.25.b_ref, f32[1024,128]{1,0:T(8,128)S(1)} %copy-done.10, ...), custom_call_target="tpu_custom_call" | custom-call | tf_op jit(solution)/shard_map/finish/pallas_call | solution.py:255
  148.2 2.0 copy-done.6
  151.3 70.8 %reduce-scatter.2.cloned.1.call-done = f32[128,512]{1,0:T(8,128)} async-done(((f32[2048,512]{1,0:T(8,128)}), f32[128,512]{1,0:T(8,128)}) %reduce-scatter.2.cloned.1.call-update) | async-done | bytes 262160 | tf_op jit(solution)/shard_map/reduce_scatter | solution.py:334
  222.1 1.8 subtract_multiply_fusion
  (81 shorter events, 12.4 us)
Async XLA Ops:
  7.2 214.9 %reduce-scatter.2.cloned.1.call-start = ((), (), s32[]{:S(2)}) async-start(), calls=%async_computation.1 | async-start | bytes 4456448 | tf_op jit(solution)/shard_map/reduce_scatter | solution.py:334
  7.2 1.6 copy-start.2
  8.8 1.2 copy-start.7
  10.0 0.7 copy-start.21
  20.7 3.3 %copy-start.4 = (f32[1024,2048]{1,0:T(8,128)}, f32[1024,2048]{1,0:T(8,128)S(1)}, u32[]{:S(2)}) copy-start(f32[1024,2048]{1,0:T(8,128)S(1)} %get-tuple-element.24.z_ref) | copy-start | bytes 25165828
  24.0 31.1 %copy-start.9 = (f32[1024,128]{1,0:T(8,128)}, f32[1024,128]{1,0:T(8,128)S(1)}, u32[]{:S(2)}) copy-start(f32[1024,128]{1,0:T(8,128)S(1)} %get-tuple-element.26.sq_ref) | copy-start | bytes 1572868
  24.0 3.8 %collective-permute-start.2 = (f32[1,2048]{1,0:T(1,128)S(1)}, f32[1,2048]{1,0:T(1,128)S(1)}, u32[]{:S(2)}, u32[]{:S(2)}) collective-permute-start(f32[1,2048]{1,0:T(1,128)S(1)} %get-tuple-element.23), channel_id=1, source_target_pairs={{0,3},{1,2},{2,1},{3,0},{4,7},{5,6},{6,5},{7,4},{8,11},{9,10},{10,... | collective-permute-start | bytes 24584 | tf_op jit(solution)/shard_map/ppermute | solution.py:272
  26.4 3.7 %collective-permute-start.1 = (f32[1,2048]{1,0:T(1,128)S(1)}, f32[1,2048]{1,0:T(1,128)S(1)}, u32[]{:S(2)}, u32[]{:S(2)}) collective-permute-start(f32[1,2048]{1,0:T(1,128)S(1)} %get-tuple-element.23), channel_id=1, source_target_pairs={{0,2},{1,3},{2,0},{3,1},{4,6},{5,7},{6,4},{7,5},{8,10},{9,11},{10,... | collective-permute-start | bytes 24584 | tf_op jit(solution)/shard_map/ppermute | solution.py:272
  27.0 3.1 %collective-permute-start = (f32[1,2048]{1,0:T(1,128)S(1)}, f32[1,2048]{1,0:T(1,128)S(1)}, u32[]{:S(2)}, u32[]{:S(2)}) collective-permute-start(f32[1,2048]{1,0:T(1,128)S(1)} %get-tuple-element.23), channel_id=1, source_target_pairs={{0,1},{1,0},{2,3},{3,2},{4,5},{5,4},{6,7},{7,6},{8,9},{9,8},{10,11... | collective-permute-start | bytes 24584 | tf_op jit(solution)/shard_map/ppermute | solution.py:272
  30.1 5.6 %collective-permute-start.5 = (f32[1,2048]{1,0:T(1,128)S(1)}, f32[1,2048]{1,0:T(1,128)S(1)}, u32[]{:S(2)}, u32[]{:S(2)}) collective-permute-start(f32[1,2048]{1,0:T(1,128)S(1)} %multiply_add_fusion.2), channel_id=1, source_target_pairs={{0,12},{1,13},{2,14},{3,15},{4,8},{5,9},{6,10},{7,11},{8,4},{9,5},... | collective-permute-start | bytes 24584 | tf_op jit(solution)/shard_map/ppermute | solution.py:272
  33.8 4.5 %collective-permute-start.4 = (f32[1,2048]{1,0:T(1,128)S(1)}, f32[1,2048]{1,0:T(1,128)S(1)}, u32[]{:S(2)}, u32[]{:S(2)}) collective-permute-start(f32[1,2048]{1,0:T(1,128)S(1)} %multiply_add_fusion.2), channel_id=1, source_target_pairs={{0,8},{1,9},{2,10},{3,11},{4,12},{5,13},{6,14},{7,15},{8,0},{9,1},... | collective-permute-start | bytes 24584 | tf_op jit(solution)/shard_map/ppermute | solution.py:272
  33.8 4.5 %collective-permute-start.3 = (f32[1,2048]{1,0:T(1,128)S(1)}, f32[1,2048]{1,0:T(1,128)S(1)}, u32[]{:S(2)}, u32[]{:S(2)}) collective-permute-start(f32[1,2048]{1,0:T(1,128)S(1)} %multiply_add_fusion.2), channel_id=1, source_target_pairs={{0,4},{1,5},{2,6},{3,7},{4,0},{5,1},{6,2},{7,3},{8,12},{9,13},{10,... | collective-permute-start | bytes 24584 | tf_op jit(solution)/shard_map/ppermute | solution.py:272
  38.4 3.4 %copy-start.5 = (f32[1024,2048]{1,0:T(8,128)S(1)}, f32[1024,2048]{1,0:T(8,128)}, u32[]{:S(2)}) copy-start(f32[1024,2048]{1,0:T(8,128)} %copy-done.4) | copy-start | bytes 25165828
  55.0 0.8 copy-start.13
  55.8 13.8 %copy-start.11 = (f32[1024,128]{1,0:T(8,128)}, f32[1024,128]{1,0:T(8,128)S(1)}, u32[]{:S(2)}) copy-start(f32[1024,128]{1,0:T(8,128)S(1)} %get-tuple-element.30.beta_ref) | copy-start | bytes 1572868
  55.8 55.0 %copy-start = (f32[1024,2048]{1,0:T(8,128)}, f32[1024,2048]{1,0:T(8,128)S(1)}, u32[]{:S(2)}) copy-start(f32[1024,2048]{1,0:T(8,128)S(1)} %get-tuple-element.27.q_ref) | copy-start | bytes 25165828
  55.8 3.1 %collective-permute-start.8 = (f32[1,2048]{1,0:T(1,128)S(1)}, f32[1,2048]{1,0:T(1,128)S(1)}, u32[]{:S(2)}, u32[]{:S(2)}) collective-permute-start(f32[1,2048]{1,0:T(1,128)S(1)} %get-tuple-element.28), channel_id=1, source_target_pairs={{0,3},{1,2},{2,1},{3,0},{4,7},{5,6},{6,5},{7,4},{8,11},{9,10},{10,... | collective-permute-start | bytes 24584 | tf_op jit(solution)/shard_map/ppermute | solution.py:272
  55.8 3.7 %collective-permute-start.7 = (f32[1,2048]{1,0:T(1,128)S(1)}, f32[1,2048]{1,0:T(1,128)S(1)}, u32[]{:S(2)}, u32[]{:S(2)}) collective-permute-start(f32[1,2048]{1,0:T(1,128)S(1)} %get-tuple-element.28), channel_id=1, source_target_pairs={{0,2},{1,3},{2,0},{3,1},{4,6},{5,7},{6,4},{7,5},{8,10},{9,11},{10,... | collective-permute-start | bytes 24584 | tf_op jit(solution)/shard_map/ppermute | solution.py:272
  56.4 3.1 %collective-permute-start.6 = (f32[1,2048]{1,0:T(1,128)S(1)}, f32[1,2048]{1,0:T(1,128)S(1)}, u32[]{:S(2)}, u32[]{:S(2)}) collective-permute-start(f32[1,2048]{1,0:T(1,128)S(1)} %get-tuple-element.28), channel_id=1, source_target_pairs={{0,1},{1,0},{2,3},{3,2},{4,5},{5,4},{6,7},{7,6},{8,9},{9,8},{10,11... | collective-permute-start | bytes 24584 | tf_op jit(solution)/shard_map/ppermute | solution.py:272
  59.5 5.6 %collective-permute-start.11 = (f32[1,2048]{1,0:T(1,128)S(1)}, f32[1,2048]{1,0:T(1,128)S(1)}, u32[]{:S(2)}, u32[]{:S(2)}) collective-permute-start(f32[1,2048]{1,0:T(1,128)S(1)} %add_add_fusion.5), channel_id=1, source_target_pairs={{0,12},{1,13},{2,14},{3,15},{4,8},{5,9},{6,10},{7,11},{8,4},{9,5},... | collective-permute-start | bytes 24584 | tf_op jit(solution)/shard_map/ppermute | solution.py:272
  61.1 4.6 %collective-permute-start.10 = (f32[1,2048]{1,0:T(1,128)S(1)}, f32[1,2048]{1,0:T(1,128)S(1)}, u32[]{:S(2)}, u32[]{:S(2)}) collective-permute-start(f32[1,2048]{1,0:T(1,128)S(1)} %add_add_fusion.5), channel_id=1, source_target_pairs={{0,8},{1,9},{2,10},{3,11},{4,12},{5,13},{6,14},{7,15},{8,0},{9,1},... | collective-permute-start | bytes 24584 | tf_op jit(solution)/shard_map/ppermute | solution.py:272
  61.7 4.0 %collective-permute-start.9 = (f32[1,2048]{1,0:T(1,128)S(1)}, f32[1,2048]{1,0:T(1,128)S(1)}, u32[]{:S(2)}, u32[]{:S(2)}) collective-permute-start(f32[1,2048]{1,0:T(1,128)S(1)} %add_add_fusion.5), channel_id=1, source_target_pairs={{0,4},{1,5},{2,6},{3,7},{4,0},{5,1},{6,2},{7,3},{8,12},{9,13},{10,... | collective-permute-start | bytes 24584 | tf_op jit(solution)/shard_map/ppermute | solution.py:272
  69.6 3.1 %collective-permute-start.14 = (f32[1,2048]{1,0:T(1,128)S(1)}, f32[1,2048]{1,0:T(1,128)S(1)}, u32[]{:S(2)}, u32[]{:S(2)}) collective-permute-start(f32[1,2048]{1,0:T(1,128)S(1)} %get-tuple-element.29), channel_id=1, source_target_pairs={{0,3},{1,2},{2,1},{3,0},{4,7},{5,6},{6,5},{7,4},{8,11},{9,10},{10,... | collective-permute-start | bytes 24584 | tf_op jit(solution)/shard_map/ppermute | solution.py:272
  69.7 3.7 %collective-permute-start.13 = (f32[1,2048]{1,0:T(1,128)S(1)}, f32[1,2048]{1,0:T(1,128)S(1)}, u32[]{:S(2)}, u32[]{:S(2)}) collective-permute-start(f32[1,2048]{1,0:T(1,128)S(1)} %get-tuple-element.29), channel_id=1, source_target_pairs={{0,2},{1,3},{2,0},{3,1},{4,6},{5,7},{6,4},{7,5},{8,10},{9,11},{10,... | collective-permute-start | bytes 24584 | tf_op jit(solution)/shard_map/ppermute | solution.py:272
  70.4 3.0 %collective-permute-start.12 = (f32[1,2048]{1,0:T(1,128)S(1)}, f32[1,2048]{1,0:T(1,128)S(1)}, u32[]{:S(2)}, u32[]{:S(2)}) collective-permute-start(f32[1,2048]{1,0:T(1,128)S(1)} %get-tuple-element.29), channel_id=1, source_target_pairs={{0,1},{1,0},{2,3},{3,2},{4,5},{5,4},{6,7},{7,6},{8,9},{9,8},{10,11... | collective-permute-start | bytes 24584 | tf_op jit(solution)/shard_map/ppermute | solution.py:272
  73.5 5.5 %collective-permute-start.17 = (f32[1,2048]{1,0:T(1,128)S(1)}, f32[1,2048]{1,0:T(1,128)S(1)}, u32[]{:S(2)}, u32[]{:S(2)}) collective-permute-start(f32[1,2048]{1,0:T(1,128)S(1)} %add_add_fusion.4), channel_id=1, source_target_pairs={{0,12},{1,13},{2,14},{3,15},{4,8},{5,9},{6,10},{7,11},{8,4},{9,5},... | collective-permute-start | bytes 24584 | tf_op jit(solution)/shard_map/ppermute | solution.py:272
  76.0 4.6 %collective-permute-start.16 = (f32[1,2048]{1,0:T(1,128)S(1)}, f32[1,2048]{1,0:T(1,128)S(1)}, u32[]{:S(2)}, u32[]{:S(2)}) collective-permute-start(f32[1,2048]{1,0:T(1,128)S(1)} %add_add_fusion.4), channel_id=1, source_target_pairs={{0,8},{1,9},{2,10},{3,11},{4,12},{5,13},{6,14},{7,15},{8,0},{9,1},... | collective-permute-start | bytes 24584 | tf_op jit(solution)/shard_map/ppermute | solution.py:272
  76.9 3.7 %collective-permute-start.15 = (f32[1,2048]{1,0:T(1,128)S(1)}, f32[1,2048]{1,0:T(1,128)S(1)}, u32[]{:S(2)}, u32[]{:S(2)}) collective-permute-start(f32[1,2048]{1,0:T(1,128)S(1)} %add_add_fusion.4), channel_id=1, source_target_pairs={{0,4},{1,5},{2,6},{3,7},{4,0},{5,1},{6,2},{7,3},{8,12},{9,13},{10,... | collective-permute-start | bytes 24584 | tf_op jit(solution)/shard_map/ppermute | solution.py:272
  84.6 0.8 copy-start.15
  85.4 3.1 %collective-permute-start.20 = (f32[1,2048]{1,0:T(1,128)S(1)}, f32[1,2048]{1,0:T(1,128)S(1)}, u32[]{:S(2)}, u32[]{:S(2)}) collective-permute-start(f32[1,2048]{1,0:T(1,128)S(1)} %get-tuple-element.33), channel_id=1, source_target_pairs={{0,3},{1,2},{2,1},{3,0},{4,7},{5,6},{6,5},{7,4},{8,11},{9,10},{10,... | collective-permute-start | bytes 24584 | tf_op jit(solution)/shard_map/ppermute | solution.py:272
  85.4 3.7 %collective-permute-start.19 = (f32[1,2048]{1,0:T(1,128)S(1)}, f32[1,2048]{1,0:T(1,128)S(1)}, u32[]{:S(2)}, u32[]{:S(2)}) collective-permute-start(f32[1,2048]{1,0:T(1,128)S(1)} %get-tuple-element.33), channel_id=1, source_target_pairs={{0,2},{1,3},{2,0},{3,1},{4,6},{5,7},{6,4},{7,5},{8,10},{9,11},{10,... | collective-permute-start | bytes 24584 | tf_op jit(solution)/shard_map/ppermute | solution.py:272
  86.0 3.0 %collective-permute-start.18 = (f32[1,2048]{1,0:T(1,128)S(1)}, f32[1,2048]{1,0:T(1,128)S(1)}, u32[]{:S(2)}, u32[]{:S(2)}) collective-permute-start(f32[1,2048]{1,0:T(1,128)S(1)} %get-tuple-element.33), channel_id=1, source_target_pairs={{0,1},{1,0},{2,3},{3,2},{4,5},{5,4},{6,7},{7,6},{8,9},{9,8},{10,11... | collective-permute-start | bytes 24584 | tf_op jit(solution)/shard_map/ppermute | solution.py:272
  89.1 5.6 %collective-permute-start.23 = (f32[1,2048]{1,0:T(1,128)S(1)}, f32[1,2048]{1,0:T(1,128)S(1)}, u32[]{:S(2)}, u32[]{:S(2)}) collective-permute-start(f32[1,2048]{1,0:T(1,128)S(1)} %add_add_fusion.3), channel_id=1, source_target_pairs={{0,12},{1,13},{2,14},{3,15},{4,8},{5,9},{6,10},{7,11},{8,4},{9,5},... | collective-permute-start | bytes 24584 | tf_op jit(solution)/shard_map/ppermute | solution.py:272
  90.6 4.5 %collective-permute-start.22 = (f32[1,2048]{1,0:T(1,128)S(1)}, f32[1,2048]{1,0:T(1,128)S(1)}, u32[]{:S(2)}, u32[]{:S(2)}) collective-permute-start(f32[1,2048]{1,0:T(1,128)S(1)} %add_add_fusion.3), channel_id=1, source_target_pairs={{0,8},{1,9},{2,10},{3,11},{4,12},{5,13},{6,14},{7,15},{8,0},{9,1},... | collective-permute-start | bytes 24584 | tf_op jit(solution)/shard_map/ppermute | solution.py:272
  91.5 3.7 %collective-permute-start.21 = (f32[1,2048]{1,0:T(1,128)S(1)}, f32[1,2048]{1,0:T(1,128)S(1)}, u32[]{:S(2)}, u32[]{:S(2)}) collective-permute-start(f32[1,2048]{1,0:T(1,128)S(1)} %add_add_fusion.3), channel_id=1, source_target_pairs={{0,4},{1,5},{2,6},{3,7},{4,0},{5,1},{6,2},{7,3},{8,12},{9,13},{10,... | collective-permute-start | bytes 24584 | tf_op jit(solution)/shard_map/ppermute | solution.py:272
  99.0 0.8 copy-start.17
  99.8 3.1 %collective-permute-start.26 = (f32[1,2048]{1,0:T(1,128)S(1)}, f32[1,2048]{1,0:T(1,128)S(1)}, u32[]{:S(2)}, u32[]{:S(2)}) collective-permute-start(f32[1,2048]{1,0:T(1,128)S(1)} %get-tuple-element.35), channel_id=1, source_target_pairs={{0,3},{1,2},{2,1},{3,0},{4,7},{5,6},{6,5},{7,4},{8,11},{9,10},{10,... | collective-permute-start | bytes 24584 | tf_op jit(solution)/shard_map/ppermute | solution.py:272
  99.8 3.7 %collective-permute-start.25 = (f32[1,2048]{1,0:T(1,128)S(1)}, f32[1,2048]{1,0:T(1,128)S(1)}, u32[]{:S(2)}, u32[]{:S(2)}) collective-permute-start(f32[1,2048]{1,0:T(1,128)S(1)} %get-tuple-element.35), channel_id=1, source_target_pairs={{0,2},{1,3},{2,0},{3,1},{4,6},{5,7},{6,4},{7,5},{8,10},{9,11},{10,... | collective-permute-start | bytes 24584 | tf_op jit(solution)/shard_map/ppermute | solution.py:272
  100.5 3.0 %collective-permute-start.24 = (f32[1,2048]{1,0:T(1,128)S(1)}, f32[1,2048]{1,0:T(1,128)S(1)}, u32[]{:S(2)}, u32[]{:S(2)}) collective-permute-start(f32[1,2048]{1,0:T(1,128)S(1)} %get-tuple-element.35), channel_id=1, source_target_pairs={{0,1},{1,0},{2,3},{3,2},{4,5},{5,4},{6,7},{7,6},{8,9},{9,8},{10,11... | collective-permute-start | bytes 24584 | tf_op jit(solution)/shard_map/ppermute | solution.py:272
  103.5 5.5 %collective-permute-start.29 = (f32[1,2048]{1,0:T(1,128)S(1)}, f32[1,2048]{1,0:T(1,128)S(1)}, u32[]{:S(2)}, u32[]{:S(2)}) collective-permute-start(f32[1,2048]{1,0:T(1,128)S(1)} %add_add_fusion.2), channel_id=1, source_target_pairs={{0,12},{1,13},{2,14},{3,15},{4,8},{5,9},{6,10},{7,11},{8,4},{9,5},... | collective-permute-start | bytes 24584 | tf_op jit(solution)/shard_map/ppermute | solution.py:272
  106.1 4.5 %collective-permute-start.28 = (f32[1,2048]{1,0:T(1,128)S(1)}, f32[1,2048]{1,0:T(1,128)S(1)}, u32[]{:S(2)}, u32[]{:S(2)}) collective-permute-start(f32[1,2048]{1,0:T(1,128)S(1)} %add_add_fusion.2), channel_id=1, source_target_pairs={{0,8},{1,9},{2,10},{3,11},{4,12},{5,13},{6,14},{7,15},{8,0},{9,1},... | collective-permute-start | bytes 24584 | tf_op jit(solution)/shard_map/ppermute | solution.py:272
  107.1 3.7 %collective-permute-start.27 = (f32[1,2048]{1,0:T(1,128)S(1)}, f32[1,2048]{1,0:T(1,128)S(1)}, u32[]{:S(2)}, u32[]{:S(2)}) collective-permute-start(f32[1,2048]{1,0:T(1,128)S(1)} %add_add_fusion.2), channel_id=1, source_target_pairs={{0,4},{1,5},{2,6},{3,7},{4,0},{5,1},{6,2},{7,3},{8,12},{9,13},{10,... | collective-permute-start | bytes 24584 | tf_op jit(solution)/shard_map/ppermute | solution.py:272
  110.8 14.3 %copy-start.3 = (bf16[2048,512]{1,0:T(8,128)(2,1)S(1)}, bf16[2048,512]{1,0:T(8,128)(2,1)}, u32[]{:S(2)}) copy-start(bf16[2048,512]{1,0:T(8,128)(2,1)} %x_ref.3) | copy-start | bytes 6291460
  114.4 0.8 copy-start.19
  115.2 3.1 %collective-permute-start.32 = (f32[1,2048]{1,0:T(1,128)S(1)}, f32[1,2048]{1,0:T(1,128)S(1)}, u32[]{:S(2)}, u32[]{:S(2)}) collective-permute-start(f32[1,2048]{1,0:T(1,128)S(1)} %get-tuple-element.38), channel_id=1, source_target_pairs={{0,3},{1,2},{2,1},{3,0},{4,7},{5,6},{6,5},{7,4},{8,11},{9,10},{10,... | collective-permute-start | bytes 24584 | tf_op jit(solution)/shard_map/ppermute | solution.py:272
  115.2 3.7 %collective-permute-start.31 = (f32[1,2048]{1,0:T(1,128)S(1)}, f32[1,2048]{1,0:T(1,128)S(1)}, u32[]{:S(2)}, u32[]{:S(2)}) collective-permute-start(f32[1,2048]{1,0:T(1,128)S(1)} %get-tuple-element.38), channel_id=1, source_target_pairs={{0,2},{1,3},{2,0},{3,1},{4,6},{5,7},{6,4},{7,5},{8,10},{9,11},{10,... | collective-permute-start | bytes 24584 | tf_op jit(solution)/shard_map/ppermute | solution.py:272
  115.9 3.0 %collective-permute-start.30 = (f32[1,2048]{1,0:T(1,128)S(1)}, f32[1,2048]{1,0:T(1,128)S(1)}, u32[]{:S(2)}, u32[]{:S(2)}) collective-permute-start(f32[1,2048]{1,0:T(1,128)S(1)} %get-tuple-element.38), channel_id=1, source_target_pairs={{0,1},{1,0},{2,3},{3,2},{4,5},{5,4},{6,7},{7,6},{8,9},{9,8},{10,11... | collective-permute-start | bytes 24584 | tf_op jit(solution)/shard_map/ppermute | solution.py:272
  118.9 5.6 %collective-permute-start.35 = (f32[1,2048]{1,0:T(1,128)S(1)}, f32[1,2048]{1,0:T(1,128)S(1)}, u32[]{:S(2)}, u32[]{:S(2)}) collective-permute-start(f32[1,2048]{1,0:T(1,128)S(1)} %add_add_fusion.1), channel_id=1, source_target_pairs={{0,12},{1,13},{2,14},{3,15},{4,8},{5,9},{6,10},{7,11},{8,4},{9,5},... | collective-permute-start | bytes 24584 | tf_op jit(solution)/shard_map/ppermute | solution.py:272
  120.4 4.5 %collective-permute-start.34 = (f32[1,2048]{1,0:T(1,128)S(1)}, f32[1,2048]{1,0:T(1,128)S(1)}, u32[]{:S(2)}, u32[]{:S(2)}) collective-permute-start(f32[1,2048]{1,0:T(1,128)S(1)} %add_add_fusion.1), channel_id=1, source_target_pairs={{0,8},{1,9},{2,10},{3,11},{4,12},{5,13},{6,14},{7,15},{8,0},{9,1},... | collective-permute-start | bytes 24584 | tf_op jit(solution)/shard_map/ppermute | solution.py:272
  121.4 3.7 %collective-permute-start.33 = (f32[1,2048]{1,0:T(1,128)S(1)}, f32[1,2048]{1,0:T(1,128)S(1)}, u32[]{:S(2)}, u32[]{:S(2)}) collective-permute-start(f32[1,2048]{1,0:T(1,128)S(1)} %add_add_fusion.1), channel_id=1, source_target_pairs={{0,4},{1,5},{2,6},{3,7},{4,0},{5,1},{6,2},{7,3},{8,12},{9,13},{10,... | collective-permute-start | bytes 24584 | tf_op jit(solution)/shard_map/ppermute | solution.py:272
  125.1 3.4 %copy-start.1 = (f32[1024,2048]{1,0:T(8,128)S(1)}, f32[1024,2048]{1,0:T(8,128)}, u32[]{:S(2)}) copy-start(f32[1024,2048]{1,0:T(8,128)} %copy-done) | copy-start | bytes 25165828
  128.5 1.2 copy-start.8
  129.7 1.0 copy-start.10
  130.8 1.0 copy-start.12
  131.8 1.0 copy-start.14
  132.9 1.0 copy-start.16
  133.9 1.0 copy-start.18
  135.0 1.0 copy-start.20
  148.2 2.0 copy-start.6
Sparse Core Ops, SparseCore 0:
  150.3 71.6 reduce-scatter.1

commit v2 on v1

v2 whole, which is shorter than its diff:
```python
import functools
import math
import jax
import jax.numpy as jnp
from jax import lax
from jax.experimental import pallas as pl
from jax.experimental.pallas import tpu as pltpu
from jax.sharding import PartitionSpec as P

EPSILON = 0.05
LOGK = math.log2(math.e) / EPSILON
LANES = 128
SUB = 8
VMEM = pltpu.VMEM
F32 = jnp.float32
BF16 = jnp.bfloat16


def params(mib=28):
    return pltpu.CompilerParams(vmem_limit_bytes=mib * 1024 * 1024)


def full(n):
    return [pl.BlockSpec(memory_space=VMEM)] * n


def column(row):
    return jnp.transpose(jnp.broadcast_to(row, (LANES, LANES)))


def lanes(x):
    return [x[:, l * LANES:(l + 1) * LANES] for l in range(x.shape[1] // LANES)]


def wide(x):
    return jnp.broadcast_to(x, (SUB, LANES))


def tree(op, xs):
    xs = list(xs)
    while len(xs) > 1:
        xs = [op(xs[i], xs[i + 1]) if i + 1 < len(xs) else xs[i] for i in range(0, len(xs), 2)]
    return xs[0]


def lane_sum(xs):
    return wide(jnp.sum(tree(jnp.add, xs), axis=1, keepdims=True))


def lane_max(xs):
    return wide(jnp.max(tree(jnp.maximum, xs), axis=1, keepdims=True))


def rows_of(i, n):
    return pl.ds(pl.multiple_of(i * n, n), n)


def scores_kernel(total_cols, x_ref, y_ref, mass_ref, z_ref, b_ref, sq_ref, lse_ref, cb_ref):
    cols, width = y_ref.shape
    rows = x_ref.shape[0]
    for c in range(cols // LANES):
        s = pl.ds(c * LANES, LANES)
        b = column(mass_ref[:, s] * (1.0 / total_cols))
        b_ref[s, :] = b
        yf = y_ref[s, :].astype(F32)
        sq = jnp.sum(yf * yf, axis=1, keepdims=True) * (LOGK / width)
        sq = jnp.broadcast_to(sq, (LANES, LANES))
        sq_ref[s, :] = sq
        cb_ref[s, :] = jnp.log2(b) - sq
    step = 2 * LANES
    many = 4

    def reduce_block(r):
        for l in range(step // LANES):
            ls = pl.ds(r * step + l * LANES, LANES)
            m = [None] * many
            for g in range(cols // SUB):
                s = pl.ds(g * SUB, SUB)
                v = z_ref[s, ls] + cb_ref[s, :]
                m[g % many] = v if m[g % many] is None else jnp.maximum(m[g % many], v)
            m = jnp.max(tree(jnp.maximum, m), axis=0, keepdims=True)
            mw = wide(m)
            t = [None] * many
            for g in range(cols // SUB):
                s = pl.ds(g * SUB, SUB)
                v = jnp.exp2(z_ref[s, ls] + cb_ref[s, :] - mw)
                t[g % many] = v if t[g % many] is None else t[g % many] + v
            lse_ref[:, ls] = m + jnp.log2(jnp.sum(tree(jnp.add, t), axis=0, keepdims=True))

    for r in range(rows // step):
        s = pl.ds(r * step, step)
        z_ref[:, s] = lax.dot_general(
            y_ref[...], x_ref[s, :], (((1,), (1,)), ((), ())), preferred_element_type=F32
        ) * (2.0 * LOGK / width)
        if r > 0:
            reduce_block(r - 1)
    reduce_block(rows // step - 1)


def scores(new_points, arch_points, arch_mass, total_cols):
    rows, cols = new_points.shape[0], arch_points.shape[0]
    return pl.pallas_call(
        functools.partial(scores_kernel, total_cols),
        out_shape=(
            VMEM((cols, rows), F32),
            VMEM((cols, LANES), F32),
            VMEM((cols, LANES), F32),
            jax.ShapeDtypeStruct((1, rows), F32),
        ),
        in_specs=full(3),
        out_specs=tuple(full(4)),
        scratch_shapes=[pltpu.VMEM((cols, LANES), F32)],
        compiler_params=params(),
        name="scores",
    )(new_points, arch_points, arch_mass.reshape(1, cols))


CHUNK = 128


def groups(i):
    return [pl.ds(pl.multiple_of(i * CHUNK, CHUNK) + h * SUB, SUB) for h in range(CHUNK // SUB)]


def column_dots(e_ref, w, tmp_ref):
    def body(i, carry):
        for s in groups(i):
            tmp_ref[s, :] = tree(jnp.add, [a * c for a, c in zip(lanes(e_ref[s, :]), w)])
        return carry

    lax.fori_loop(0, e_ref.shape[0] // CHUNK, body, 0)


def row_sums(e_ref, c_ref, part_ref):
    def body(i, acc):
        for s in groups(i):
            c = c_ref[s, :]
            acc = [a + d * c for a, d in zip(acc, lanes(e_ref[s, :]))]
        return acc

    cols, rows = e_ref.shape
    acc = lax.fori_loop(0, cols // CHUNK, body, [jnp.zeros((SUB, LANES), F32)] * (rows // LANES))
    for l, a in enumerate(acc):
        part_ref[:, pl.ds(l * LANES, LANES)] = jnp.sum(a, axis=0, keepdims=True)


def spread(x, op):
    return jnp.broadcast_to(op(x, axis=1, keepdims=True), x.shape)


def plan_kernel(z_ref, b_ref, sq_ref, w_ref, e_ref, n_ref, r_ref, br_ref, vbr_ref, part_ref, tmp_ref):
    cols, rows = z_ref.shape
    w = [wide(a) for a in lanes(w_ref[...])]

    def top(i, carry):
        for s in groups(i):
            tmp_ref[s, :] = tree(jnp.maximum, [a + c for a, c in zip(lanes(z_ref[s, :]), w)])
        return carry

    lax.fori_loop(0, cols // CHUNK, top, 0)

    def spread_top(i, carry):
        s = rows_of(i, CHUNK)
        n_ref[s, :] = spread(tmp_ref[s, :], jnp.max)
        return carry

    lax.fori_loop(0, cols // CHUNK, spread_top, 0)

    def powers(i, carry):
        for s in groups(i):
            n = n_ref[s, :]
            e = [jnp.exp2(a + c - n) for a, c in zip(lanes(z_ref[s, :]), w)]
            for l, a in enumerate(e):
                e_ref[s, pl.ds(l * LANES, LANES)] = a
            tmp_ref[s, :] = tree(jnp.add, e)
        return carry

    lax.fori_loop(0, cols // CHUNK, powers, 0)

    def scale(i, carry):
        s = rows_of(i, CHUNK)
        t = spread(tmp_ref[s, :], jnp.sum)
        r = 1.0 / t
        br = b_ref[s, :] * r
        r_ref[s, :] = r
        br_ref[s, :] = br
        vbr_ref[s, :] = br * jnp.exp2(n_ref[s, :] + jnp.log2(t) - sq_ref[s, :])
        return carry

    lax.fori_loop(0, cols // CHUNK, scale, 0)
    row_sums(e_ref, br_ref, part_ref)


def plan(z, b, sq, w):
    cols, rows = z.shape
    return pl.pallas_call(
        plan_kernel,
        out_shape=(VMEM((cols, rows), F32),) + (VMEM((cols, LANES), F32),) * 4
        + (jax.ShapeDtypeStruct((1, rows), F32),),
        in_specs=full(4),
        out_specs=tuple(full(6)),
        scratch_shapes=[pltpu.VMEM((cols, LANES), F32)],
        input_output_aliases={0: 0},
        compiler_params=params(8),
        name="plan",
    )(z, b, sq, w)


def sweep_kernel(kind, e_ref, b_ref, *refs):
    cols, rows = e_ref.shape
    more = refs[:-4]
    w_ref, c_ref, part_ref, tmp_ref = refs[-4:]
    column_dots(e_ref, [wide(a) for a in lanes(w_ref[...])], tmp_ref)

    def weigh(i, carry):
        s = rows_of(i, CHUNK)
        t = spread(tmp_ref[s, :], jnp.sum)
        b = b_ref[s, :]
        if kind == "fwd":
            c = b / t
        elif kind == "mid":
            v = more[0][s, :]
            c = v * v * t / b
        else:
            c = b * t * more[0][s, :]
        c_ref[s, :] = c
        return carry

    lax.fori_loop(0, cols // CHUNK, weigh, 0)
    row_sums(e_ref, c_ref, part_ref)


def sweep(kind, e, b, *more):
    cols, rows = e.shape
    return pl.pallas_call(
        functools.partial(sweep_kernel, kind),
        out_shape=(VMEM((cols, LANES), F32), jax.ShapeDtypeStruct((1, rows), F32)),
        in_specs=full(2 + len(more)),
        out_specs=tuple(full(2)),
        scratch_shapes=[pltpu.VMEM((cols, LANES), F32)],
        compiler_params=params(8),
        name="sweep_" + kind,
    )(e, b, *more)


def mix_kernel(share, pieces, me_ref, e_ref, y_ref, *refs):
    c_refs, r_refs = refs[:6], refs[6:11]
    half_ref, keep_ref = refs[11:13]
    send_refs, prod_ref = refs[13:-1], refs[-1]
    cols, rows = e_ref.shape
    pair = 2 * share
    me = me_ref[0]
    core = me % 2
    for p in range(rows // pair):
        lo = pl.multiple_of(((me // 2) ^ p) * pair, pair)
        spots = [pl.ds(pl.multiple_of(lo + l * LANES, LANES), LANES) for l in range(pair // LANES)]
        r = [[wide(ref[:, ls]) for ref in r_refs] for ls in spots]
        for g in range(cols // (2 * SUB)):
            outs = [[] for _ in spots]
            for h in range(2):
                s = pl.ds(g * 2 * SUB + h * SUB, SUB)
                c = [ref[s, :] for ref in c_refs]
                for o, rl, ls in zip(outs, r, spots):
                    terms = [a * b for a, b in zip(c, rl)] + [c[5]]
                    o.append(e_ref[s, ls] * tree(jnp.add, terms))
            for o, ls in zip(outs, spots):
                half_ref[pl.ds(g * 2 * SUB, 2 * SUB), ls] = jnp.concatenate(o, axis=0).astype(BF16)
        prod_ref[p % 2] = lax.dot_general(
            half_ref[:, pl.ds(lo, pair)], y_ref[...], (((0,), (0,)), ((), ())),
            preferred_element_type=F32,
        )
        keep_ref[p] = prod_ref[p % 2, pl.ds(pl.multiple_of(core * share, share), share), :]
        at = (1 - core) * share
        for ref, n in zip(send_refs, pieces):
            ref[p] = prod_ref[p % 2, pl.ds(pl.multiple_of(at, 8), n), :]
            at = at + n


def mix(share, pieces, me, e, y, columns, weights):
    cols, rows = e.shape
    width = y.shape[1]
    pairs = rows // (2 * share)
    out = [VMEM((cols, rows), BF16), jax.ShapeDtypeStruct((pairs, share, width), F32)]
    out += [jax.ShapeDtypeStruct((pairs, n, width), F32) for n in pieces]
    got = pl.pallas_call(
        functools.partial(mix_kernel, share, pieces),
        out_shape=tuple(out),
        in_specs=[pl.BlockSpec(memory_space=pltpu.SMEM)] + full(13),
        out_specs=tuple(full(len(out))),
        scratch_shapes=[pltpu.VMEM((2, 2 * share, width), F32)],
        compiler_params=params(16),
        name="mix",
    )(me.reshape(1), e, y, *columns, *weights)
    return got[0], got[1], got[2:]


def back_kernel(total_cols, half_ref, x_ref, y_ref, e_ref, b_ref, r_ref, n_ref, sq_ref, bv2_ref,
                bv3_ref, mid_ref, gb1_ref, vbr_ref, w_ref, pot_ref, arch_ref, tmp_ref):
    cols, rows = e_ref.shape
    width = y_ref.shape[1]
    column_dots(e_ref, [wide(a) for a in lanes(w_ref[...])], tmp_ref)
    step = 256
    for j in range(cols // step):
        s = pl.ds(j * step, step)
        b = b_ref[s, :]
        gb0 = vbr_ref[s, :] * spread(tmp_ref[s, :], jnp.sum)
        gb2 = mid_ref[s, :] * b / bv2_ref[s, :]
        tr = b + 2.0 * (gb2 + gb1_ref[s, :] / r_ref[s, :]) + gb0
        back = jnp.dot(half_ref[s, :], x_ref[...], preferred_element_type=F32)
        for l in range(width // LANES):
            ls = slice(l * LANES, (l + 1) * LANES)
            arch_ref[s, ls] = total_cols * (tr * y_ref[s, ls].astype(F32) - back[:, ls])
    for c in range(cols // LANES):
        s = pl.ds(c * LANES, LANES)
        pot = (sq_ref[s, :] - n_ref[s, :] + jnp.log2(bv3_ref[s, :] / b_ref[s, :])) * (1.0 / LOGK)
        pot_ref[:, s] = jnp.transpose(pot)[0:1, :]


def back(total_cols, half, x, y, *rest):
    cols, rows = half.shape
    width = y.shape[1]
    return pl.pallas_call(
        functools.partial(back_kernel, float(total_cols)),
        out_shape=(
            jax.ShapeDtypeStruct((1, cols), F32),
            jax.ShapeDtypeStruct((cols, width), F32),
        ),
        in_specs=full(3 + len(rest)),
        out_specs=tuple(full(2)),
        scratch_shapes=[pltpu.VMEM((cols, LANES), F32)],
        compiler_params=params(16),
        cost_estimate=pl.CostEstimate(
            flops=2 * cols * rows * width, bytes_accessed=16 * 1024 * 1024, transcendentals=0
        ),
        name="back",
    )(half, x, y, *rest)


def swap(v, k, count):
    return lax.ppermute(v, "cols", [(i, i ^ k) for i in range(count)])


def scatter_sum(keep, sends, pieces, count):
    bits = [1 << i for i in range(1, count.bit_length() - 1)]
    done, at = [], 0
    for i, (send, n) in enumerate(zip(sends, pieces)):
        got = swap(send, 1, count)
        v = {p: keep[p, at:at + n] + got[p] for p in range(count // 2)}
        at += n
        order = bits if i < (len(pieces) + 1) // 2 else bits[1:] + bits[:1]
        for k in order:
            away = [p for p in sorted(v) if p & (k // 2)]
            got = swap(jnp.concatenate([v[p] for p in away], axis=0), k, count)
            v = {p ^ (k // 2): v[p ^ (k // 2)] + got[j * n:(j + 1) * n] for j, p in enumerate(away)}
        done.append(v[0])
    return jnp.concatenate(done, axis=0)


def combine(x, count, join):
    k = 1
    while k < count:
        if 4 * k <= count:
            x = join([x] + [swap(x, j * k, count) for j in (1, 2, 3)])
            k *= 4
        else:
            x = join([x, swap(x, k, count)])
            k *= 2
    return x


def add_join(xs):
    return tree(jnp.add, xs)


def lse_join(xs):
    m = tree(jnp.maximum, xs)
    return m + jnp.log2(tree(jnp.add, [jnp.exp2(x - m) for x in xs]))


def local(new_points, arch_points, new_mass, arch_mass):
    rows, width = new_points.shape
    count = lax.axis_size("cols")
    assert count & (count - 1) == 0
    reduce_add = functools.partial(combine, count=count, join=add_join)
    reduce_lse = functools.partial(combine, count=count, join=lse_join)
    total_cols = arch_points.shape[0] * count
    share = rows // count
    me = lax.axis_index("cols")
    new_float = new_points.astype(F32)
    sq_new = jnp.sum(new_float * new_float, 1) * (LOGK / width)
    a = (new_mass / rows).reshape(1, rows)

    z, b, sq, lse = scores(new_points, arch_points, arch_mass, total_cols)
    alpha = -reduce_lse(lse)
    e, n, r, br, vbr, part = plan(z, b, sq, jnp.log2(a) + alpha)
    u2 = a / reduce_add(part)
    bv2, part = sweep("fwd", e, b, u2)
    u3 = a / reduce_add(part)
    bv3, part = sweep("fwd", e, b, u3)
    fbar3 = a + u3 * reduce_add(part)
    w3 = u3 * fbar3 / a
    mid, part = sweep("mid", e, b, bv2, w3)
    fbar2 = u2 * reduce_add(part)
    w2 = u2 * fbar2 / a
    gb1, part = sweep("bwd", e, br, r, w2)
    fbar1 = reduce_add(part)
    w1 = fbar1 / a
    pieces = [share * f // 16 for f in (6, 6, 4)]
    half, keep, sends = mix(
        share, pieces, me, e, arch_points, (bv3, bv2, mid, br, vbr, gb1), (u3, w3, u2, w2, w1)
    )
    pot, arch_grad = back(
        total_cols, half, new_points, arch_points, e, b, r, n, sq, bv2, bv3, mid, gb1, vbr, w1
    )
    summed = scatter_sum(keep, sends, pieces, count)
    row_weight = 2.0 * (fbar3 + fbar2 + fbar1) - a
    mine = lax.dynamic_slice_in_dim(row_weight.reshape(rows), me * share, share, 0)
    points = lax.dynamic_slice_in_dim(new_points, me * share, share, 0).astype(F32)
    new_grad = rows * (mine[:, None] * points - summed)
    new_pot = (alpha.reshape(rows) + jnp.log2(u3).reshape(rows) + sq_new) * (1.0 / LOGK)
    return (new_pot, pot.reshape(-1), new_grad, arch_grad)


def solution(mesh):
    in_specs = (P("pairs", None), P(("pairs", "cols"), None), P("pairs"), P(("pairs", "cols")))
    out_specs = (
        P("pairs"),
        P(("pairs", "cols")),
        P(("pairs", "cols"), None),
        P(("pairs", "cols"), None),
    )
    return jax.shard_map(local, mesh=mesh, in_specs=in_specs, out_specs=out_specs, check_vma=False)
```

time: 231 us -> 179 us (0.77)
  waiting for transfers between devices: 96.3 us -> 59.4 us
  Pallas kernels: 50.6 us -> 28.8 us
  between operations: 14.3 us -> 1.05 us
  starting transfers between devices: 39.2 us -> 49.2 us
  local copies, waits for them, and re-layouts: 26.2 us -> 31.9 us
  other arithmetic: 4.01 us -> 7.91 us
    reduce_scatter x1 -> x0, waiting for transfers between devices: 70.8 us -> none  [local(): summed = lax.psum_scatter(product, 'cols', scatter_dimension=0, tiled=True)]
    ppermute x36 -> x48, waiting for transfers between devices: 25.6 us -> 59.4 us  [swap(): return lax.ppermute(v, 'cols', [(i, i ^ k) for i in range(count)])]
    ppermute x36 -> x48, starting transfers between devices: 39.2 us -> 49.2 us  [swap(): return lax.ppermute(v, 'cols', [(i, i ^ k) for i in range(count)])]
    pallas_call x2 -> x3, Pallas kernels: 25.4 us -> 17.1 us  [the longest x1 6.94 us: mix(): pl.pallas_call(functools.partial(mix_kernel, share, pieces), out_shape=tu...]
    pallas_call x4, Pallas kernels: 15.2 us -> 7.97 us  [sweep(): pl.pallas_call(functools.partial(sweep_kernel, kind), out_shape=(VMEM((co...]
    pallas_call x1, Pallas kernels: 9.93 us -> 3.78 us  [scores(): pl.pallas_call(functools.partial(scores_kernel, total_cols), out_shape=(V...]
    unnamed x44 -> x70, local copies, waits for them, and re-layouts: 26.2 us -> 31.9 us
    add x1 -> x10, other arithmetic: 0.08 us -> 5.57 us  [the longest x7 4.1 us: scatter_sum(): v[p ^ k // 2] + got[j * n:(j + 1) * n]]
  transfers between devices with their start and end apart: 37 -> 48, of which waited for: 30 -> 29; matrix products, arithmetic and copies ran while one was open for 1% -> 3% of each run, Pallas kernels for 0% -> 3%
where the time goes in v2:
time: 179 us; the launch traced here: 178 us
  waiting for transfers between devices  59.4 us (33%)
  starting transfers between devices  49.2 us (27%)
  local copies, waits for them, and re-layouts  31.9 us (18%)
  Pallas kernels  28.8 us (16%)
  other arithmetic  7.91 us (4%)
    ppermute x48, waiting for transfers between devices, swap(): return lax.ppermute(v, 'cols', [(i, i ^ k) for i in range(count)])  59.4 us
    ppermute x48, starting transfers between devices, swap(): return lax.ppermute(v, 'cols', [(i, i ^ k) for i in range(count)])  49.2 us
    unnamed x70, local copies, waits for them, and re-layouts  31.9 us
    pallas_call x4, Pallas kernels, sweep(): pl.pallas_call(functools.partial(sweep_kernel, kind), out_shape=(VMEM((co...  7.97 us
    pallas_call x1, Pallas kernels, mix(): pl.pallas_call(functools.partial(mix_kernel, share, pieces), out_shape=tu...  6.94 us
    pallas_call x1, Pallas kernels, plan(): pl.pallas_call(plan_kernel, out_shape=(VMEM((cols, rows), F32),) + (VMEM(...  5.59 us
    pallas_call x1, Pallas kernels, back(): pl.pallas_call(functools.partial(back_kernel, float(total_cols)), out_sha...  4.55 us
    add x7, other arithmetic, scatter_sum(): v[p ^ k // 2] + got[j * n:(j + 1) * n]  4.1 us
  transfers between devices with their start and end apart: 48, of which 29 were waited for; matrix products, arithmetic and copies ran while one was open for 3% of the time, Pallas kernels for 3%

profile of v2, /device:TPU:0, one launch (start us, length us, event | category | flops | bytes accessed | tf_op | source)
XLA Modules:
  0.0 178.3 jit_solution(412701644398092500)
XLA Ops:
  0.6 1.6 copy-done.3
  2.2 1.2 copy-done.5
  4.1 3.8 %scores.1 = (f32[1024,2048]{1,0:T(8,128)S(1)}, f32[1024,128]{1,0:T(8,128)S(1)}, f32[1024,128]{1,0:T(8,128)S(1)}, f32[1,2048]{1,0:T(1,128)S(1)}) custom-call(bf16[2048,512]{1,0:T(8,128)(2,1)S(1)} %copy-done.3, bf16[1024,512]{1,0:T(8,128)(2,1)S(1)} %copy-done.5, f32[1,1024]{1,0:T(1,128)S(1)} %bitcast.80), custom_call_target="tpu_custom_call" | custom-call | tf_op jit(solution)/shard_map/scores/pallas_call | solution.py:102
  8.5 2.6 %collective-permute-start.1 = (f32[1,2048]{1,0:T(1,128)S(1)}, f32[1,2048]{1,0:T(1,128)S(1)}, u32[]{:S(2)}, u32[]{:S(2)}) collective-permute-start(f32[1,2048]{1,0:T(1,128)S(1)} %get-tuple-element.29), channel_id=1, source_target_pairs={{0,2},{1,3},{2,0},{3,1},{4,6},{5,7},{6,4},{7,5},{8,10},{9,11},{10,... | collective-permute-start | bytes 24584 | tf_op jit(solution)/shard_map/ppermute | solution.py:340
  11.1 1.6 collective-permute-done.1
  12.7 1.4 collective-permute-done.2
  14.2 1.6 collective-permute-start.3
  15.8 2.6 %collective-permute-start.4 = (f32[1,2048]{1,0:T(1,128)S(1)}, f32[1,2048]{1,0:T(1,128)S(1)}, u32[]{:S(2)}, u32[]{:S(2)}) collective-permute-start(f32[1,2048]{1,0:T(1,128)S(1)} %multiply_add_fusion.2), channel_id=1, source_target_pairs={{0,8},{1,9},{2,10},{3,11},{4,12},{5,13},{6,14},{7,15},{8,0},{9,1},... | collective-permute-start | bytes 24584 | tf_op jit(solution)/shard_map/ppermute | solution.py:340
  18.7 1.7 collective-permute-done.4
  20.4 3.5 %collective-permute-done.5 = f32[1,2048]{1,0:T(1,128)S(1)} collective-permute-done((f32[1,2048]{1,0:T(1,128)S(1)}, f32[1,2048]{1,0:T(1,128)S(1)}, u32[]{:S(2)}, u32[]{:S(2)}) %collective-permute-start.5) | collective-permute-done | bytes 8224 | tf_op jit(solution)/shard_map/ppermute | solution.py:340
  24.0 5.6 %plan.1 = (f32[1024,2048]{1,0:T(8,128)S(1)}, f32[1024,128]{1,0:T(8,128)S(1)}, f32[1024,128]{1,0:T(8,128)S(1)}, f32[1024,128]{1,0:T(8,128)S(1)}, f32[1024,128]{1,0:T(8,128)S(1)}, /*index=5*/f32[1,2048]{1,0:T(1,128)S(1)}) custom-call(f32[1024,2048]{1,0:T(8,128)S(1)} %get-tuple-element.30.z_ref, ...), custom_call_target="tpu_custom_call", output_to_operand_aliasing={{0}: (0, {})} | custom-call | tf_op jit(solution)/shard_map/plan/pallas_call | solution.py:196
  31.1 1.2 collective-permute-start.8
  32.3 1.9 %collective-permute-done.7 = f32[1,2048]{1,0:T(1,128)S(1)} collective-permute-done((f32[1,2048]{1,0:T(1,128)S(1)}, f32[1,2048]{1,0:T(1,128)S(1)}, u32[]{:S(2)}, u32[]{:S(2)}) %collective-permute-start.7) | collective-permute-done | bytes 8224 | tf_op jit(solution)/shard_map/ppermute | solution.py:340
  35.4 2.5 %collective-permute-start.9 = (f32[1,2048]{1,0:T(1,128)S(1)}, f32[1,2048]{1,0:T(1,128)S(1)}, u32[]{:S(2)}, u32[]{:S(2)}) collective-permute-start(f32[1,2048]{1,0:T(1,128)S(1)} %add_add_fusion.5), channel_id=1, source_target_pairs={{0,4},{1,5},{2,6},{3,7},{4,0},{5,1},{6,2},{7,3},{8,12},{9,13},{10,... | collective-permute-start | bytes 24584 | tf_op jit(solution)/shard_map/ppermute | solution.py:340
  37.8 1.1 collective-permute-done.10
  39.9 2.0 %sweep_fwd.2 = (f32[1024,128]{1,0:T(8,128)S(1)}, f32[1,2048]{1,0:T(1,128)S(1)}) custom-call(f32[1024,2048]{1,0:T(8,128)S(1)} %get-tuple-element.33.e_ref, f32[1024,128]{1,0:T(8,128)S(1)} %get-tuple-element.31.b_ref, f32[1,2048]{1,0:T(1,128)S(1)} %add_divide_fusion.1.refs_0_.refs_8_), custom_call_target="tpu_custom_call" | custom-call | tf_op jit(solution)/shard_map/sweep_fwd/pallas_call | solution.py:235
  42.0 1.4 collective-permute-start.13
  43.9 1.9 %collective-permute-done.13 = f32[1,2048]{1,0:T(1,128)S(1)} collective-permute-done((f32[1,2048]{1,0:T(1,128)S(1)}, f32[1,2048]{1,0:T(1,128)S(1)}, u32[]{:S(2)}, u32[]{:S(2)}) %collective-permute-start.13) | collective-permute-done | bytes 8224 | tf_op jit(solution)/shard_map/ppermute | solution.py:340
  46.5 1.7 collective-permute-start.15
  49.2 1.8 %collective-permute-start.17 = (f32[1,2048]{1,0:T(1,128)S(1)}, f32[1,2048]{1,0:T(1,128)S(1)}, u32[]{:S(2)}, u32[]{:S(2)}) collective-permute-start(f32[1,2048]{1,0:T(1,128)S(1)} %add_add_fusion.4), channel_id=1, source_target_pairs={{0,12},{1,13},{2,14},{3,15},{4,8},{5,9},{6,10},{7,11},{8,4},{9,5},... | collective-permute-start | bytes 24584 | tf_op jit(solution)/shard_map/ppermute | solution.py:340
  51.0 1.8 collective-permute-done.16
  52.8 1.9 %collective-permute-done.17 = f32[1,2048]{1,0:T(1,128)S(1)} collective-permute-done((f32[1,2048]{1,0:T(1,128)S(1)}, f32[1,2048]{1,0:T(1,128)S(1)}, u32[]{:S(2)}, u32[]{:S(2)}) %collective-permute-start.17) | collective-permute-done | bytes 8224 | tf_op jit(solution)/shard_map/ppermute | solution.py:340
  54.7 2.0 %sweep_fwd.3 = (f32[1024,128]{1,0:T(8,128)S(1)}, f32[1,2048]{1,0:T(1,128)S(1)}) custom-call(f32[1024,2048]{1,0:T(8,128)S(1)} %get-tuple-element.33.e_ref, f32[1024,128]{1,0:T(8,128)S(1)} %get-tuple-element.31.b_ref, f32[1,2048]{1,0:T(1,128)S(1)} %get-tuple-element.61.refs_0_.refs_6_), custom_call_target="tpu_custom_call" | custom-call | tf_op jit(solution)/shard_map/sweep_fwd/pallas_call | solution.py:235
  58.2 1.2 collective-permute-start.20
  59.4 1.8 %collective-permute-done.19 = f32[1,2048]{1,0:T(1,128)S(1)} collective-permute-done((f32[1,2048]{1,0:T(1,128)S(1)}, f32[1,2048]{1,0:T(1,128)S(1)}, u32[]{:S(2)}, u32[]{:S(2)}) %collective-permute-start.19) | collective-permute-done | bytes 8224 | tf_op jit(solution)/shard_map/ppermute | solution.py:340
  61.3 2.4 %collective-permute-start.22 = (f32[1,2048]{1,0:T(1,128)S(1)}, f32[1,2048]{1,0:T(1,128)S(1)}, u32[]{:S(2)}, u32[]{:S(2)}) collective-permute-start(f32[1,2048]{1,0:T(1,128)S(1)} %add_add_fusion.3), channel_id=1, source_target_pairs={{0,8},{1,9},{2,10},{3,11},{4,12},{5,13},{6,14},{7,15},{8,0},{9,1},... | collective-permute-start | bytes 24584 | tf_op jit(solution)/shard_map/ppermute | solution.py:340
  63.7 2.0 %collective-permute-start.23 = (f32[1,2048]{1,0:T(1,128)S(1)}, f32[1,2048]{1,0:T(1,128)S(1)}, u32[]{:S(2)}, u32[]{:S(2)}) collective-permute-start(f32[1,2048]{1,0:T(1,128)S(1)} %add_add_fusion.3), channel_id=1, source_target_pairs={{0,12},{1,13},{2,14},{3,15},{4,8},{5,9},{6,10},{7,11},{8,4},{9,5},... | collective-permute-start | bytes 24584 | tf_op jit(solution)/shard_map/ppermute | solution.py:340
  66.0 3.2 %collective-permute-done.23 = f32[1,2048]{1,0:T(1,128)S(1)} collective-permute-done((f32[1,2048]{1,0:T(1,128)S(1)}, f32[1,2048]{1,0:T(1,128)S(1)}, u32[]{:S(2)}, u32[]{:S(2)}) %collective-permute-start.23) | collective-permute-done | bytes 8224 | tf_op jit(solution)/shard_map/ppermute | solution.py:340
  69.2 2.0 %sweep_mid.1 = (f32[1024,128]{1,0:T(8,128)S(1)}, f32[1,2048]{1,0:T(1,128)S(1)}) custom-call(f32[1024,2048]{1,0:T(8,128)S(1)} %get-tuple-element.33.e_ref, f32[1024,128]{1,0:T(8,128)S(1)} %get-tuple-element.31.b_ref, f32[1024,128]{1,0:T(8,128)S(1)} %get-tuple-element.37.refs_0_.refs_1_.bv2_ref, f32[1,2048]{1,0:T(1,128)S(1)} %get-tuple-element.58.refs_1_.refs_7_), custom_call_target="tpu_custom_call" | custom-call | tf_op jit(solution)/shard_map/sweep_mid/pallas_call | solution.py:235
  72.0 1.4 collective-permute-start.25
  73.8 1.8 %collective-permute-done.25 = f32[1,2048]{1,0:T(1,128)S(1)} collective-permute-done((f32[1,2048]{1,0:T(1,128)S(1)}, f32[1,2048]{1,0:T(1,128)S(1)}, u32[]{:S(2)}, u32[]{:S(2)}) %collective-permute-start.25) | collective-permute-done | bytes 8224 | tf_op jit(solution)/shard_map/ppermute | solution.py:340
  76.5 2.6 %collective-permute-start.28 = (f32[1,2048]{1,0:T(1,128)S(1)}, f32[1,2048]{1,0:T(1,128)S(1)}, u32[]{:S(2)}, u32[]{:S(2)}) collective-permute-start(f32[1,2048]{1,0:T(1,128)S(1)} %add_add_fusion.2), channel_id=1, source_target_pairs={{0,8},{1,9},{2,10},{3,11},{4,12},{5,13},{6,14},{7,15},{8,0},{9,1},... | collective-permute-start | bytes 24584 | tf_op jit(solution)/shard_map/ppermute | solution.py:340
  79.1 1.8 %collective-permute-start.29 = (f32[1,2048]{1,0:T(1,128)S(1)}, f32[1,2048]{1,0:T(1,128)S(1)}, u32[]{:S(2)}, u32[]{:S(2)}) collective-permute-start(f32[1,2048]{1,0:T(1,128)S(1)} %add_add_fusion.2), channel_id=1, source_target_pairs={{0,12},{1,13},{2,14},{3,15},{4,8},{5,9},{6,10},{7,11},{8,4},{9,5},... | collective-permute-start | bytes 24584 | tf_op jit(solution)/shard_map/ppermute | solution.py:340
  81.1 3.4 %collective-permute-done.29 = f32[1,2048]{1,0:T(1,128)S(1)} collective-permute-done((f32[1,2048]{1,0:T(1,128)S(1)}, f32[1,2048]{1,0:T(1,128)S(1)}, u32[]{:S(2)}, u32[]{:S(2)}) %collective-permute-start.29) | collective-permute-done | bytes 8224 | tf_op jit(solution)/shard_map/ppermute | solution.py:340
  84.6 2.0 %sweep_bwd.1 = (f32[1024,128]{1,0:T(8,128)S(1)}, f32[1,2048]{1,0:T(1,128)S(1)}) custom-call(f32[1024,2048]{1,0:T(8,128)S(1)} %get-tuple-element.33.e_ref, f32[1024,128]{1,0:T(8,128)S(1)} %get-tuple-element.40.b_ref.refs_3_, f32[1024,128]{1,0:T(8,128)S(1)} %get-tuple-element.42.refs_0_.r_ref, f32[1,2048]{1,0:T(1,128)S(1)} %get-tuple-element.56.refs_1_.refs_9_), custom_call_target="tpu_custom_call" | custom-call | tf_op jit(solution)/shard_map/sweep_bwd/pallas_call | solution.py:235
  88.0 1.2 collective-permute-start.32
  89.2 1.8 %collective-permute-done.31 = f32[1,2048]{1,0:T(1,128)S(1)} collective-permute-done((f32[1,2048]{1,0:T(1,128)S(1)}, f32[1,2048]{1,0:T(1,128)S(1)}, u32[]{:S(2)}, u32[]{:S(2)}) %collective-permute-start.31) | collective-permute-done | bytes 8224 | tf_op jit(solution)/shard_map/ppermute | solution.py:340
  91.2 2.4 %collective-permute-start.34 = (f32[1,2048]{1,0:T(1,128)S(1)}, f32[1,2048]{1,0:T(1,128)S(1)}, u32[]{:S(2)}, u32[]{:S(2)}) collective-permute-start(f32[1,2048]{1,0:T(1,128)S(1)} %add_add_fusion.1), channel_id=1, source_target_pairs={{0,8},{1,9},{2,10},{3,11},{4,12},{5,13},{6,14},{7,15},{8,0},{9,1},... | collective-permute-start | bytes 24584 | tf_op jit(solution)/shard_map/ppermute | solution.py:340
  93.6 2.0 %collective-permute-start.35 = (f32[1,2048]{1,0:T(1,128)S(1)}, f32[1,2048]{1,0:T(1,128)S(1)}, u32[]{:S(2)}, u32[]{:S(2)}) collective-permute-start(f32[1,2048]{1,0:T(1,128)S(1)} %add_add_fusion.1), channel_id=1, source_target_pairs={{0,12},{1,13},{2,14},{3,15},{4,8},{5,9},{6,10},{7,11},{8,4},{9,5},... | collective-permute-start | bytes 24584 | tf_op jit(solution)/shard_map/ppermute | solution.py:340
  95.8 3.2 %collective-permute-done.35 = f32[1,2048]{1,0:T(1,128)S(1)} collective-permute-done((f32[1,2048]{1,0:T(1,128)S(1)}, f32[1,2048]{1,0:T(1,128)S(1)}, u32[]{:S(2)}, u32[]{:S(2)}) %collective-permute-start.35) | collective-permute-done | bytes 8224 | tf_op jit(solution)/shard_map/ppermute | solution.py:340
  99.1 3.4 %copy-done.1 = f32[1024,2048]{1,0:T(8,128)S(1)} copy-done((f32[1024,2048]{1,0:T(8,128)S(1)}, f32[1024,2048]{1,0:T(8,128)}, u32[]{:S(2)}) %copy-start.1) | copy-done | bytes 8388632
  102.4 1.2 copy-done.6
  103.7 1.0 copy-done.11
  104.7 1.0 copy-done.14
  106.8 1.0 copy-done.20
  108.9 6.9 %mix.1 = (bf16[1024,2048]{1,0:T(8,128)(2,1)S(1)}, f32[8,128,512]{2,1,0:T(8,128)S(1)}, f32[8,48,512]{2,1,0:T(8,128)}, f32[8,48,512]{2,1,0:T(8,128)}, f32[8,32,512]{2,1,0:T(8,128)S(1)}) custom-call(s32[1]{0:T(128)} %bitcast.4.me_ref, f32[1024,2048]{1,0:T(8,128)S(1)} %copy-done.1, bf16[1024,512]{1,0:T(8,128)(2,1)S(1)} %copy-done.6, f32[1024,128]{1,0:T(8,128)S(1)} %copy-done.14, ...), custom_call_target="tpu_custom_call" | custom-call | tf_op jit(solution)/shard_map/mix/pallas_call | solution.py:285
  115.8 2.1 %copy-done.8 = bf16[1024,2048]{1,0:T(8,128)(2,1)} copy-done((bf16[1024,2048]{1,0:T(8,128)(2,1)}, bf16[1024,2048]{1,0:T(8,128)(2,1)S(1)}, u32[]{:S(2)}) %copy-start.8) | copy-done | bytes 4194328
  117.9 1.3 copy-done.22
  122.1 3.4 %copy-done.2 = f32[1024,2048]{1,0:T(8,128)S(1)} copy-done((f32[1024,2048]{1,0:T(8,128)S(1)}, f32[1024,2048]{1,0:T(8,128)}, u32[]{:S(2)}) %copy-start.2) | copy-done | bytes 8388632
  125.5 2.2 %copy-done.9 = bf16[1024,2048]{1,0:T(8,128)(2,1)S(1)} copy-done((bf16[1024,2048]{1,0:T(8,128)(2,1)S(1)}, bf16[1024,2048]{1,0:T(8,128)(2,1)}, u32[]{:S(2)}) %copy-start.9) | copy-done | bytes 4194328
  132.9 4.6 %back.1 = (f32[1,1024]{1,0:T(1,128)}, f32[1024,512]{1,0:T(8,128)}) custom-call(bf16[1024,2048]{1,0:T(8,128)(2,1)S(1)} %copy-done.9, bf16[2048,512]{1,0:T(8,128)(2,1)S(1)} %copy-done.4, bf16[1024,512]{1,0:T(8,128)(2,1)S(1)} %copy-done.7, f32[1024,2048]{1,0:T(8,128)S(1)} %copy-done.2, f32[1024,128]{1,0:T(8,128)S(1)} %get-tuple-element.31.b_ref, ...), custom_call_target="tpu_custom_call" | custom-call | flops 2147483648 | bytes 16777216 | tf_op jit(solution)/shard_map/back/pallas_call | solution.py:322
  137.4 1.4 fusion.17
  138.8 1.4 collective-permute-start.37
  141.2 9.7 %collective-permute-done.37 = f32[192,512]{1,0:T(8,128)S(1)} collective-permute-done((f32[192,512]{1,0:T(8,128)S(1)}, f32[192,512]{1,0:T(8,128)S(1)}, u32[]{:S(2)}, u32[]{:S(2)}) %collective-permute-start.37) | collective-permute-done | bytes 393248 | tf_op jit(solution)/shard_map/ppermute | solution.py:340
  152.0 2.6 %collective-permute-start.46 = (f32[64,512]{1,0:T(8,128)S(1)}, f32[64,512]{1,0:T(8,128)S(1)}, u32[]{:S(2)}, u32[]{:S(2)}) collective-permute-start(f32[64,512]{1,0:T(8,128)S(1)} %pad_maximum_fusion.5), channel_id=1, source_target_pairs={{0,8},{1,9},{2,10},{3,11},{4,12},{5,13},{6,14},{7,15},{8,0},{9,1},... | collective-permute-start | bytes 393224 | tf_op jit(solution)/shard_map/ppermute | solution.py:340
  154.7 3.8 %collective-permute-done.41 = f32[192,512]{1,0:T(8,128)S(1)} collective-permute-done((f32[192,512]{1,0:T(8,128)S(1)}, f32[192,512]{1,0:T(8,128)S(1)}, u32[]{:S(2)}, u32[]{:S(2)}) %collective-permute-start.41) | collective-permute-done | bytes 393248 | tf_op jit(solution)/shard_map/ppermute | solution.py:340
  158.4 1.5 collective-permute-done.38
  160.0 1.1 slice_add_fusion.6
  161.2 2.6 %collective-permute-start.39 = (f32[48,512]{1,0:T(8,128)S(1)}, f32[48,512]{1,0:T(8,128)S(1)}, u32[]{:S(2)}, u32[]{:S(2)}) collective-permute-start(f32[48,512]{1,0:T(8,128)S(1)} %get-tuple-element.84), channel_id=1, source_target_pairs={{0,8},{1,9},{2,10},{3,11},{4,12},{5,13},{6,14},{7,15},{8,0},{9,1},... | collective-permute-start | bytes 294920 | tf_op jit(solution)/shard_map/ppermute | solution.py:340
  163.8 1.4 collective-permute-start.47
  165.2 2.2 %collective-permute-done.39 = f32[48,512]{1,0:T(8,128)S(1)} collective-permute-done((f32[48,512]{1,0:T(8,128)S(1)}, f32[48,512]{1,0:T(8,128)S(1)}, u32[]{:S(2)}, u32[]{:S(2)}) %collective-permute-start.39) | collective-permute-done | bytes 98336 | tf_op jit(solution)/shard_map/ppermute | solution.py:340
  167.4 1.5 collective-permute-done.42
  170.0 1.3 collective-permute-start.43
  171.3 5.3 %collective-permute-done.43 = f32[48,512]{1,0:T(8,128)S(1)} collective-permute-done((f32[48,512]{1,0:T(8,128)S(1)}, f32[48,512]{1,0:T(8,128)S(1)}, u32[]{:S(2)}, u32[]{:S(2)}) %collective-permute-start.43) | collective-permute-done | bytes 98336 | tf_op jit(solution)/shard_map/ppermute | solution.py:340
  (142 shorter events, 29.0 us)
Async XLA Ops:
  0.6 1.6 copy-start.3
  4.1 14.5 %copy-start.34 = (f32[2048]{0:T(1024)S(1)}, f32[2048]{0:T(1024)}, u32[]{:S(2)}) copy-start(f32[2048]{0:T(1024)} %param.6) | copy-start | bytes 24580
  7.9 21.6 %copy-start.24 = (f32[1024,128]{1,0:T(8,128)}, f32[1024,128]{1,0:T(8,128)S(1)}, u32[]{:S(2)}) copy-start(f32[1024,128]{1,0:T(8,128)S(1)} %get-tuple-element.32.sq_ref) | copy-start | bytes 1572868
  7.9 3.2 %collective-permute-start = (f32[1,2048]{1,0:T(1,128)S(1)}, f32[1,2048]{1,0:T(1,128)S(1)}, u32[]{:S(2)}, u32[]{:S(2)}) collective-permute-start(f32[1,2048]{1,0:T(1,128)S(1)} %get-tuple-element.29), channel_id=1, source_target_pairs={{0,1},{1,0},{2,3},{3,2},{4,5},{5,4},{6,7},{7,6},{8,9},{9,8},{10,11... | collective-permute-start | bytes 24584 | tf_op jit(solution)/shard_map/ppermute | solution.py:340
  8.5 4.2 %collective-permute-start.1 = (f32[1,2048]{1,0:T(1,128)S(1)}, f32[1,2048]{1,0:T(1,128)S(1)}, u32[]{:S(2)}, u32[]{:S(2)}) collective-permute-start(f32[1,2048]{1,0:T(1,128)S(1)} %get-tuple-element.29), channel_id=1, source_target_pairs={{0,2},{1,3},{2,0},{3,1},{4,6},{5,7},{6,4},{7,5},{8,10},{9,11},{10,... | collective-permute-start | bytes 24584 | tf_op jit(solution)/shard_map/ppermute | solution.py:340
  11.0 3.1 %collective-permute-start.2 = (f32[1,2048]{1,0:T(1,128)S(1)}, f32[1,2048]{1,0:T(1,128)S(1)}, u32[]{:S(2)}, u32[]{:S(2)}) collective-permute-start(f32[1,2048]{1,0:T(1,128)S(1)} %get-tuple-element.29), channel_id=1, source_target_pairs={{0,3},{1,2},{2,1},{3,0},{4,7},{5,6},{6,5},{7,4},{8,11},{9,10},{10,... | collective-permute-start | bytes 24584 | tf_op jit(solution)/shard_map/ppermute | solution.py:340
  14.2 4.5 %collective-permute-start.3 = (f32[1,2048]{1,0:T(1,128)S(1)}, f32[1,2048]{1,0:T(1,128)S(1)}, u32[]{:S(2)}, u32[]{:S(2)}) collective-permute-start(f32[1,2048]{1,0:T(1,128)S(1)} %multiply_add_fusion.2), channel_id=1, source_target_pairs={{0,4},{1,5},{2,6},{3,7},{4,0},{5,1},{6,2},{7,3},{8,12},{9,13},{10,... | collective-permute-start | bytes 24584 | tf_op jit(solution)/shard_map/ppermute | solution.py:340
  15.8 4.5 %collective-permute-start.4 = (f32[1,2048]{1,0:T(1,128)S(1)}, f32[1,2048]{1,0:T(1,128)S(1)}, u32[]{:S(2)}, u32[]{:S(2)}) collective-permute-start(f32[1,2048]{1,0:T(1,128)S(1)} %multiply_add_fusion.2), channel_id=1, source_target_pairs={{0,8},{1,9},{2,10},{3,11},{4,12},{5,13},{6,14},{7,15},{8,0},{9,1},... | collective-permute-start | bytes 24584 | tf_op jit(solution)/shard_map/ppermute | solution.py:340
  18.4 5.4 %collective-permute-start.5 = (f32[1,2048]{1,0:T(1,128)S(1)}, f32[1,2048]{1,0:T(1,128)S(1)}, u32[]{:S(2)}, u32[]{:S(2)}) collective-permute-start(f32[1,2048]{1,0:T(1,128)S(1)} %multiply_add_fusion.2), channel_id=1, source_target_pairs={{0,12},{1,13},{2,14},{3,15},{4,8},{5,9},{6,10},{7,11},{8,4},{9,5},... | collective-permute-start | bytes 24584 | tf_op jit(solution)/shard_map/ppermute | solution.py:340
  30.4 11.6 %copy-start.10 = (f32[1024,128]{1,0:T(8,128)}, f32[1024,128]{1,0:T(8,128)S(1)}, u32[]{:S(2)}) copy-start(f32[1024,128]{1,0:T(8,128)S(1)} %get-tuple-element.41.refs_4_.vbr_ref) | copy-start | bytes 1572868
  30.4 54.2 %copy-start = (f32[1024,2048]{1,0:T(8,128)}, f32[1024,2048]{1,0:T(8,128)S(1)}, u32[]{:S(2)}) copy-start(f32[1024,2048]{1,0:T(8,128)S(1)} %get-tuple-element.33.e_ref) | copy-start | bytes 25165828
  30.4 54.2 %copy-start.26 = (f32[1024,128]{1,0:T(8,128)}, f32[1024,128]{1,0:T(8,128)S(1)}, u32[]{:S(2)}) copy-start(f32[1024,128]{1,0:T(8,128)S(1)} %get-tuple-element.42.refs_0_.r_ref) | copy-start | bytes 1572868
  30.4 54.2 %copy-start.28 = (f32[1024,128]{1,0:T(8,128)}, f32[1024,128]{1,0:T(8,128)S(1)}, u32[]{:S(2)}) copy-start(f32[1024,128]{1,0:T(8,128)S(1)} %get-tuple-element.40.b_ref.refs_3_) | copy-start | bytes 1572868
  30.4 1.9 %collective-permute-start.6 = (f32[1,2048]{1,0:T(1,128)S(1)}, f32[1,2048]{1,0:T(1,128)S(1)}, u32[]{:S(2)}, u32[]{:S(2)}) collective-permute-start(f32[1,2048]{1,0:T(1,128)S(1)} %get-tuple-element.34), channel_id=1, source_target_pairs={{0,1},{1,0},{2,3},{3,2},{4,5},{5,4},{6,7},{7,6},{8,9},{9,8},{10,11... | collective-permute-start | bytes 24584 | tf_op jit(solution)/shard_map/ppermute | solution.py:340
  30.5 3.8 %collective-permute-start.7 = (f32[1,2048]{1,0:T(1,128)S(1)}, f32[1,2048]{1,0:T(1,128)S(1)}, u32[]{:S(2)}, u32[]{:S(2)}) collective-permute-start(f32[1,2048]{1,0:T(1,128)S(1)} %get-tuple-element.34), channel_id=1, source_target_pairs={{0,2},{1,3},{2,0},{3,1},{4,6},{5,7},{6,4},{7,5},{8,10},{9,11},{10,... | collective-permute-start | bytes 24584 | tf_op jit(solution)/shard_map/ppermute | solution.py:340
  31.1 3.1 %collective-permute-start.8 = (f32[1,2048]{1,0:T(1,128)S(1)}, f32[1,2048]{1,0:T(1,128)S(1)}, u32[]{:S(2)}, u32[]{:S(2)}) collective-permute-start(f32[1,2048]{1,0:T(1,128)S(1)} %get-tuple-element.34), channel_id=1, source_target_pairs={{0,3},{1,2},{2,1},{3,0},{4,7},{5,6},{6,5},{7,4},{8,11},{9,10},{10,... | collective-permute-start | bytes 24584 | tf_op jit(solution)/shard_map/ppermute | solution.py:340
  34.3 4.6 %collective-permute-start.10 = (f32[1,2048]{1,0:T(1,128)S(1)}, f32[1,2048]{1,0:T(1,128)S(1)}, u32[]{:S(2)}, u32[]{:S(2)}) collective-permute-start(f32[1,2048]{1,0:T(1,128)S(1)} %add_add_fusion.5), channel_id=1, source_target_pairs={{0,8},{1,9},{2,10},{3,11},{4,12},{5,13},{6,14},{7,15},{8,0},{9,1},... | collective-permute-start | bytes 24584 | tf_op jit(solution)/shard_map/ppermute | solution.py:340
  34.4 5.5 %collective-permute-start.11 = (f32[1,2048]{1,0:T(1,128)S(1)}, f32[1,2048]{1,0:T(1,128)S(1)}, u32[]{:S(2)}, u32[]{:S(2)}) collective-permute-start(f32[1,2048]{1,0:T(1,128)S(1)} %add_add_fusion.5), channel_id=1, source_target_pairs={{0,12},{1,13},{2,14},{3,15},{4,8},{5,9},{6,10},{7,11},{8,4},{9,5},... | collective-permute-start | bytes 24584 | tf_op jit(solution)/shard_map/ppermute | solution.py:340
  35.4 4.5 %collective-permute-start.9 = (f32[1,2048]{1,0:T(1,128)S(1)}, f32[1,2048]{1,0:T(1,128)S(1)}, u32[]{:S(2)}, u32[]{:S(2)}) collective-permute-start(f32[1,2048]{1,0:T(1,128)S(1)} %add_add_fusion.5), channel_id=1, source_target_pairs={{0,4},{1,5},{2,6},{3,7},{4,0},{5,1},{6,2},{7,3},{8,12},{9,13},{10,... | collective-permute-start | bytes 24584 | tf_op jit(solution)/shard_map/ppermute | solution.py:340
  41.9 1.9 %collective-permute-start.12 = (f32[1,2048]{1,0:T(1,128)S(1)}, f32[1,2048]{1,0:T(1,128)S(1)}, u32[]{:S(2)}, u32[]{:S(2)}) collective-permute-start(f32[1,2048]{1,0:T(1,128)S(1)} %get-tuple-element.35), channel_id=1, source_target_pairs={{0,1},{1,0},{2,3},{3,2},{4,5},{5,4},{6,7},{7,6},{8,9},{9,8},{10,11... | collective-permute-start | bytes 24584 | tf_op jit(solution)/shard_map/ppermute | solution.py:340
  42.0 3.7 %collective-permute-start.13 = (f32[1,2048]{1,0:T(1,128)S(1)}, f32[1,2048]{1,0:T(1,128)S(1)}, u32[]{:S(2)}, u32[]{:S(2)}) collective-permute-start(f32[1,2048]{1,0:T(1,128)S(1)} %get-tuple-element.35), channel_id=1, source_target_pairs={{0,2},{1,3},{2,0},{3,1},{4,6},{5,7},{6,4},{7,5},{8,10},{9,11},{10,... | collective-permute-start | bytes 24584 | tf_op jit(solution)/shard_map/ppermute | solution.py:340
  43.4 3.1 %collective-permute-start.14 = (f32[1,2048]{1,0:T(1,128)S(1)}, f32[1,2048]{1,0:T(1,128)S(1)}, u32[]{:S(2)}, u32[]{:S(2)}) collective-permute-start(f32[1,2048]{1,0:T(1,128)S(1)} %get-tuple-element.35), channel_id=1, source_target_pairs={{0,3},{1,2},{2,1},{3,0},{4,7},{5,6},{6,5},{7,4},{8,11},{9,10},{10,... | collective-permute-start | bytes 24584 | tf_op jit(solution)/shard_map/ppermute | solution.py:340
  46.5 4.5 %collective-permute-start.15 = (f32[1,2048]{1,0:T(1,128)S(1)}, f32[1,2048]{1,0:T(1,128)S(1)}, u32[]{:S(2)}, u32[]{:S(2)}) collective-permute-start(f32[1,2048]{1,0:T(1,128)S(1)} %add_add_fusion.4), channel_id=1, source_target_pairs={{0,4},{1,5},{2,6},{3,7},{4,0},{5,1},{6,2},{7,3},{8,12},{9,13},{10,... | collective-permute-start | bytes 24584 | tf_op jit(solution)/shard_map/ppermute | solution.py:340
  48.2 4.5 %collective-permute-start.16 = (f32[1,2048]{1,0:T(1,128)S(1)}, f32[1,2048]{1,0:T(1,128)S(1)}, u32[]{:S(2)}, u32[]{:S(2)}) collective-permute-start(f32[1,2048]{1,0:T(1,128)S(1)} %add_add_fusion.4), channel_id=1, source_target_pairs={{0,8},{1,9},{2,10},{3,11},{4,12},{5,13},{6,14},{7,15},{8,0},{9,1},... | collective-permute-start | bytes 24584 | tf_op jit(solution)/shard_map/ppermute | solution.py:340
  49.2 5.4 %collective-permute-start.17 = (f32[1,2048]{1,0:T(1,128)S(1)}, f32[1,2048]{1,0:T(1,128)S(1)}, u32[]{:S(2)}, u32[]{:S(2)}) collective-permute-start(f32[1,2048]{1,0:T(1,128)S(1)} %add_add_fusion.4), channel_id=1, source_target_pairs={{0,12},{1,13},{2,14},{3,15},{4,8},{5,9},{6,10},{7,11},{8,4},{9,5},... | collective-permute-start | bytes 24584 | tf_op jit(solution)/shard_map/ppermute | solution.py:340
  57.5 1.9 %collective-permute-start.18 = (f32[1,2048]{1,0:T(1,128)S(1)}, f32[1,2048]{1,0:T(1,128)S(1)}, u32[]{:S(2)}, u32[]{:S(2)}) collective-permute-start(f32[1,2048]{1,0:T(1,128)S(1)} %get-tuple-element.38), channel_id=1, source_target_pairs={{0,1},{1,0},{2,3},{3,2},{4,5},{5,4},{6,7},{7,6},{8,9},{9,8},{10,11... | collective-permute-start | bytes 24584 | tf_op jit(solution)/shard_map/ppermute | solution.py:340
  57.5 3.7 %collective-permute-start.19 = (f32[1,2048]{1,0:T(1,128)S(1)}, f32[1,2048]{1,0:T(1,128)S(1)}, u32[]{:S(2)}, u32[]{:S(2)}) collective-permute-start(f32[1,2048]{1,0:T(1,128)S(1)} %get-tuple-element.38), channel_id=1, source_target_pairs={{0,2},{1,3},{2,0},{3,1},{4,6},{5,7},{6,4},{7,5},{8,10},{9,11},{10,... | collective-permute-start | bytes 24584 | tf_op jit(solution)/shard_map/ppermute | solution.py:340
  58.2 3.1 %collective-permute-start.20 = (f32[1,2048]{1,0:T(1,128)S(1)}, f32[1,2048]{1,0:T(1,128)S(1)}, u32[]{:S(2)}, u32[]{:S(2)}) collective-permute-start(f32[1,2048]{1,0:T(1,128)S(1)} %get-tuple-element.38), channel_id=1, source_target_pairs={{0,3},{1,2},{2,1},{3,0},{4,7},{5,6},{6,5},{7,4},{8,11},{9,10},{10,... | collective-permute-start | bytes 24584 | tf_op jit(solution)/shard_map/ppermute | solution.py:340
  61.3 4.5 %collective-permute-start.21 = (f32[1,2048]{1,0:T(1,128)S(1)}, f32[1,2048]{1,0:T(1,128)S(1)}, u32[]{:S(2)}, u32[]{:S(2)}) collective-permute-start(f32[1,2048]{1,0:T(1,128)S(1)} %add_add_fusion.3), channel_id=1, source_target_pairs={{0,4},{1,5},{2,6},{3,7},{4,0},{5,1},{6,2},{7,3},{8,12},{9,13},{10,... | collective-permute-start | bytes 24584 | tf_op jit(solution)/shard_map/ppermute | solution.py:340
  61.3 4.6 %collective-permute-start.22 = (f32[1,2048]{1,0:T(1,128)S(1)}, f32[1,2048]{1,0:T(1,128)S(1)}, u32[]{:S(2)}, u32[]{:S(2)}) collective-permute-start(f32[1,2048]{1,0:T(1,128)S(1)} %add_add_fusion.3), channel_id=1, source_target_pairs={{0,8},{1,9},{2,10},{3,11},{4,12},{5,13},{6,14},{7,15},{8,0},{9,1},... | collective-permute-start | bytes 24584 | tf_op jit(solution)/shard_map/ppermute | solution.py:340
  63.7 5.4 %collective-permute-start.23 = (f32[1,2048]{1,0:T(1,128)S(1)}, f32[1,2048]{1,0:T(1,128)S(1)}, u32[]{:S(2)}, u32[]{:S(2)}) collective-permute-start(f32[1,2048]{1,0:T(1,128)S(1)} %add_add_fusion.3), channel_id=1, source_target_pairs={{0,12},{1,13},{2,14},{3,15},{4,8},{5,9},{6,10},{7,11},{8,4},{9,5},... | collective-permute-start | bytes 24584 | tf_op jit(solution)/shard_map/ppermute | solution.py:340
  72.0 1.9 %collective-permute-start.24 = (f32[1,2048]{1,0:T(1,128)S(1)}, f32[1,2048]{1,0:T(1,128)S(1)}, u32[]{:S(2)}, u32[]{:S(2)}) collective-permute-start(f32[1,2048]{1,0:T(1,128)S(1)} %get-tuple-element.43), channel_id=1, source_target_pairs={{0,1},{1,0},{2,3},{3,2},{4,5},{5,4},{6,7},{7,6},{8,9},{9,8},{10,11... | collective-permute-start | bytes 24584 | tf_op jit(solution)/shard_map/ppermute | solution.py:340
  72.0 3.7 %collective-permute-start.25 = (f32[1,2048]{1,0:T(1,128)S(1)}, f32[1,2048]{1,0:T(1,128)S(1)}, u32[]{:S(2)}, u32[]{:S(2)}) collective-permute-start(f32[1,2048]{1,0:T(1,128)S(1)} %get-tuple-element.43), channel_id=1, source_target_pairs={{0,2},{1,3},{2,0},{3,1},{4,6},{5,7},{6,4},{7,5},{8,10},{9,11},{10,... | collective-permute-start | bytes 24584 | tf_op jit(solution)/shard_map/ppermute | solution.py:340
  73.3 3.1 %collective-permute-start.26 = (f32[1,2048]{1,0:T(1,128)S(1)}, f32[1,2048]{1,0:T(1,128)S(1)}, u32[]{:S(2)}, u32[]{:S(2)}) collective-permute-start(f32[1,2048]{1,0:T(1,128)S(1)} %get-tuple-element.43), channel_id=1, source_target_pairs={{0,3},{1,2},{2,1},{3,0},{4,7},{5,6},{6,5},{7,4},{8,11},{9,10},{10,... | collective-permute-start | bytes 24584 | tf_op jit(solution)/shard_map/ppermute | solution.py:340
  76.4 4.5 %collective-permute-start.27 = (f32[1,2048]{1,0:T(1,128)S(1)}, f32[1,2048]{1,0:T(1,128)S(1)}, u32[]{:S(2)}, u32[]{:S(2)}) collective-permute-start(f32[1,2048]{1,0:T(1,128)S(1)} %add_add_fusion.2), channel_id=1, source_target_pairs={{0,4},{1,5},{2,6},{3,7},{4,0},{5,1},{6,2},{7,3},{8,12},{9,13},{10,... | collective-permute-start | bytes 24584 | tf_op jit(solution)/shard_map/ppermute | solution.py:340
  76.5 4.6 %collective-permute-start.28 = (f32[1,2048]{1,0:T(1,128)S(1)}, f32[1,2048]{1,0:T(1,128)S(1)}, u32[]{:S(2)}, u32[]{:S(2)}) collective-permute-start(f32[1,2048]{1,0:T(1,128)S(1)} %add_add_fusion.2), channel_id=1, source_target_pairs={{0,8},{1,9},{2,10},{3,11},{4,12},{5,13},{6,14},{7,15},{8,0},{9,1},... | collective-permute-start | bytes 24584 | tf_op jit(solution)/shard_map/ppermute | solution.py:340
  79.1 5.4 %collective-permute-start.29 = (f32[1,2048]{1,0:T(1,128)S(1)}, f32[1,2048]{1,0:T(1,128)S(1)}, u32[]{:S(2)}, u32[]{:S(2)}) collective-permute-start(f32[1,2048]{1,0:T(1,128)S(1)} %add_add_fusion.2), channel_id=1, source_target_pairs={{0,12},{1,13},{2,14},{3,15},{4,8},{5,9},{6,10},{7,11},{8,4},{9,5},... | collective-permute-start | bytes 24584 | tf_op jit(solution)/shard_map/ppermute | solution.py:340
  87.4 1.9 %collective-permute-start.30 = (f32[1,2048]{1,0:T(1,128)S(1)}, f32[1,2048]{1,0:T(1,128)S(1)}, u32[]{:S(2)}, u32[]{:S(2)}) collective-permute-start(f32[1,2048]{1,0:T(1,128)S(1)} %get-tuple-element.45), channel_id=1, source_target_pairs={{0,1},{1,0},{2,3},{3,2},{4,5},{5,4},{6,7},{7,6},{8,9},{9,8},{10,11... | collective-permute-start | bytes 24584 | tf_op jit(solution)/shard_map/ppermute | solution.py:340
  87.4 3.7 %collective-permute-start.31 = (f32[1,2048]{1,0:T(1,128)S(1)}, f32[1,2048]{1,0:T(1,128)S(1)}, u32[]{:S(2)}, u32[]{:S(2)}) collective-permute-start(f32[1,2048]{1,0:T(1,128)S(1)} %get-tuple-element.45), channel_id=1, source_target_pairs={{0,2},{1,3},{2,0},{3,1},{4,6},{5,7},{6,4},{7,5},{8,10},{9,11},{10,... | collective-permute-start | bytes 24584 | tf_op jit(solution)/shard_map/ppermute | solution.py:340
  88.0 3.1 %collective-permute-start.32 = (f32[1,2048]{1,0:T(1,128)S(1)}, f32[1,2048]{1,0:T(1,128)S(1)}, u32[]{:S(2)}, u32[]{:S(2)}) collective-permute-start(f32[1,2048]{1,0:T(1,128)S(1)} %get-tuple-element.45), channel_id=1, source_target_pairs={{0,3},{1,2},{2,1},{3,0},{4,7},{5,6},{6,5},{7,4},{8,11},{9,10},{10,... | collective-permute-start | bytes 24584 | tf_op jit(solution)/shard_map/ppermute | solution.py:340
  91.1 4.5 %collective-permute-start.33 = (f32[1,2048]{1,0:T(1,128)S(1)}, f32[1,2048]{1,0:T(1,128)S(1)}, u32[]{:S(2)}, u32[]{:S(2)}) collective-permute-start(f32[1,2048]{1,0:T(1,128)S(1)} %add_add_fusion.1), channel_id=1, source_target_pairs={{0,4},{1,5},{2,6},{3,7},{4,0},{5,1},{6,2},{7,3},{8,12},{9,13},{10,... | collective-permute-start | bytes 24584 | tf_op jit(solution)/shard_map/ppermute | solution.py:340
  91.2 4.6 %collective-permute-start.34 = (f32[1,2048]{1,0:T(1,128)S(1)}, f32[1,2048]{1,0:T(1,128)S(1)}, u32[]{:S(2)}, u32[]{:S(2)}) collective-permute-start(f32[1,2048]{1,0:T(1,128)S(1)} %add_add_fusion.1), channel_id=1, source_target_pairs={{0,8},{1,9},{2,10},{3,11},{4,12},{5,13},{6,14},{7,15},{8,0},{9,1},... | collective-permute-start | bytes 24584 | tf_op jit(solution)/shard_map/ppermute | solution.py:340
  93.6 5.4 %collective-permute-start.35 = (f32[1,2048]{1,0:T(1,128)S(1)}, f32[1,2048]{1,0:T(1,128)S(1)}, u32[]{:S(2)}, u32[]{:S(2)}) collective-permute-start(f32[1,2048]{1,0:T(1,128)S(1)} %add_add_fusion.1), channel_id=1, source_target_pairs={{0,12},{1,13},{2,14},{3,15},{4,8},{5,9},{6,10},{7,11},{8,4},{9,5},... | collective-permute-start | bytes 24584 | tf_op jit(solution)/shard_map/ppermute | solution.py:340
  99.0 3.4 %copy-start.1 = (f32[1024,2048]{1,0:T(8,128)S(1)}, f32[1024,2048]{1,0:T(8,128)}, u32[]{:S(2)}) copy-start(f32[1024,2048]{1,0:T(8,128)} %copy-done) | copy-start | bytes 25165828
  108.9 11.7 %copy-start.4 = (bf16[2048,512]{1,0:T(8,128)(2,1)S(1)}, bf16[2048,512]{1,0:T(8,128)(2,1)}, u32[]{:S(2)}) copy-start(bf16[2048,512]{1,0:T(8,128)(2,1)} %x_ref.3) | copy-start | bytes 6291460
  115.8 2.1 %copy-start.8 = (bf16[1024,2048]{1,0:T(8,128)(2,1)}, bf16[1024,2048]{1,0:T(8,128)(2,1)S(1)}, u32[]{:S(2)}) copy-start(bf16[1024,2048]{1,0:T(8,128)(2,1)S(1)} %get-tuple-element.46.half_ref) | copy-start | bytes 12582916
  117.9 1.3 copy-start.22
  120.0 17.4 %collective-permute-start.36 = (f32[8,48,512]{2,1,0:T(8,128)}, f32[8,48,512]{2,1,0:T(8,128)}, u32[]{:S(2)}, u32[]{:S(2)}) collective-permute-start(f32[8,48,512]{2,1,0:T(8,128)} %get-tuple-element.50), channel_id=1, source_target_pairs={{0,1},{1,0},{2,3},{3,2},{4,5},{5,4},{6,7},{7,6},{8,9},{9,8},{10,11... | collective-permute-start | bytes 2359304 | tf_op jit(solution)/shard_map/ppermute | solution.py:340
  120.0 17.4 %collective-permute-start.40 = (f32[8,48,512]{2,1,0:T(8,128)}, f32[8,48,512]{2,1,0:T(8,128)}, u32[]{:S(2)}, u32[]{:S(2)}) collective-permute-start(f32[8,48,512]{2,1,0:T(8,128)} %get-tuple-element.51), channel_id=1, source_target_pairs={{0,1},{1,0},{2,3},{3,2},{4,5},{5,4},{6,7},{7,6},{8,9},{9,8},{10,11... | collective-permute-start | bytes 2359304 | tf_op jit(solution)/shard_map/ppermute | solution.py:340
  120.6 1.4 copy-start.12
  120.6 1.5 copy-start.15
  121.7 18.6 %collective-permute-start.44 = (f32[8,32,512]{2,1,0:T(8,128)}, f32[8,32,512]{2,1,0:T(8,128)S(1)}, u32[]{:S(2)}, u32[]{:S(2)}) collective-permute-start(f32[8,32,512]{2,1,0:T(8,128)} %copy-done.33), channel_id=1, source_target_pairs={{0,1},{1,0},{2,3},{3,2},{4,5},{5,4},{6,7},{7,6},{8,9},{9,8},{10,11... | collective-permute-start | bytes 1572872 | tf_op jit(solution)/shard_map/ppermute | solution.py:340
  122.1 3.4 %copy-start.2 = (f32[1024,2048]{1,0:T(8,128)S(1)}, f32[1024,2048]{1,0:T(8,128)}, u32[]{:S(2)}) copy-start(f32[1024,2048]{1,0:T(8,128)} %copy-done) | copy-start | bytes 25165828
  125.5 2.2 %copy-start.9 = (bf16[1024,2048]{1,0:T(8,128)(2,1)S(1)}, bf16[1024,2048]{1,0:T(8,128)(2,1)}, u32[]{:S(2)}) copy-start(bf16[1024,2048]{1,0:T(8,128)(2,1)} %copy-done.8) | copy-start | bytes 12582916
  132.9 4.6 %copy-start.23 = (f32[8,128,512]{2,1,0:T(8,128)S(1)}, f32[8,128,512]{2,1,0:T(8,128)}, u32[]{:S(2)}) copy-start(f32[8,128,512]{2,1,0:T(8,128)} %copy-done.22) | copy-start | bytes 6291460
  138.8 12.0 %collective-permute-start.37 = (f32[192,512]{1,0:T(8,128)S(1)}, f32[192,512]{1,0:T(8,128)S(1)}, u32[]{:S(2)}, u32[]{:S(2)}) collective-permute-start(f32[192,512]{1,0:T(8,128)S(1)} %pad_maximum_fusion), channel_id=1, source_target_pairs={{0,2},{1,3},{2,0},{3,1},{4,6},{5,7},{6,4},{7,5},{8,10},{9,11},{10,... | collective-permute-start | bytes 1179656 | tf_op jit(solution)/shard_map/ppermute | solution.py:340
  140.3 11.6 %collective-permute-start.45 = (f32[128,512]{1,0:T(8,128)S(1)}, f32[128,512]{1,0:T(8,128)S(1)}, u32[]{:S(2)}, u32[]{:S(2)}) collective-permute-start(f32[128,512]{1,0:T(8,128)S(1)} %pad_maximum_fusion.2), channel_id=1, source_target_pairs={{0,4},{1,5},{2,6},{3,7},{4,0},{5,1},{6,2},{7,3},{8,12},{9,13},{10,... | collective-permute-start | bytes 786440 | tf_op jit(solution)/shard_map/ppermute | solution.py:340
  140.5 18.0 %collective-permute-start.41 = (f32[192,512]{1,0:T(8,128)S(1)}, f32[192,512]{1,0:T(8,128)S(1)}, u32[]{:S(2)}, u32[]{:S(2)}) collective-permute-start(f32[192,512]{1,0:T(8,128)S(1)} %pad_maximum_fusion.1), channel_id=1, source_target_pairs={{0,2},{1,3},{2,0},{3,1},{4,6},{5,7},{6,4},{7,5},{8,10},{9,11},{10,... | collective-permute-start | bytes 1179656 | tf_op jit(solution)/shard_map/ppermute | solution.py:340
  151.9 8.1 %collective-permute-start.38 = (f32[96,512]{1,0:T(8,128)S(1)}, f32[96,512]{1,0:T(8,128)S(1)}, u32[]{:S(2)}, u32[]{:S(2)}) collective-permute-start(f32[96,512]{1,0:T(8,128)S(1)} %pad_maximum_fusion.3), channel_id=1, source_target_pairs={{0,4},{1,5},{2,6},{3,7},{4,0},{5,1},{6,2},{7,3},{8,12},{9,13},{10,... | collective-permute-start | bytes 589832 | tf_op jit(solution)/shard_map/ppermute | solution.py:340
  152.0 11.7 %collective-permute-start.46 = (f32[64,512]{1,0:T(8,128)S(1)}, f32[64,512]{1,0:T(8,128)S(1)}, u32[]{:S(2)}, u32[]{:S(2)}) collective-permute-start(f32[64,512]{1,0:T(8,128)S(1)} %pad_maximum_fusion.5), channel_id=1, source_target_pairs={{0,8},{1,9},{2,10},{3,11},{4,12},{5,13},{6,14},{7,15},{8,0},{9,1},... | collective-permute-start | bytes 393224 | tf_op jit(solution)/shard_map/ppermute | solution.py:340
  161.1 7.9 %collective-permute-start.42 = (f32[96,512]{1,0:T(8,128)S(1)}, f32[96,512]{1,0:T(8,128)S(1)}, u32[]{:S(2)}, u32[]{:S(2)}) collective-permute-start(f32[96,512]{1,0:T(8,128)S(1)} %pad_maximum_fusion.4), channel_id=1, source_target_pairs={{0,4},{1,5},{2,6},{3,7},{4,0},{5,1},{6,2},{7,3},{8,12},{9,13},{10,... | collective-permute-start | bytes 589832 | tf_op jit(solution)/shard_map/ppermute | solution.py:340
  161.2 6.2 %collective-permute-start.39 = (f32[48,512]{1,0:T(8,128)S(1)}, f32[48,512]{1,0:T(8,128)S(1)}, u32[]{:S(2)}, u32[]{:S(2)}) collective-permute-start(f32[48,512]{1,0:T(8,128)S(1)} %get-tuple-element.84), channel_id=1, source_target_pairs={{0,8},{1,9},{2,10},{3,11},{4,12},{5,13},{6,14},{7,15},{8,0},{9,1},... | collective-permute-start | bytes 294920 | tf_op jit(solution)/shard_map/ppermute | solution.py:340
  163.8 7.5 %collective-permute-start.47 = (f32[32,512]{1,0:T(8,128)S(1)}, f32[32,512]{1,0:T(8,128)S(1)}, u32[]{:S(2)}, u32[]{:S(2)}) collective-permute-start(f32[32,512]{1,0:T(8,128)S(1)} %slice_add_fusion.28), channel_id=1, source_target_pairs={{0,2},{1,3},{2,0},{3,1},{4,6},{5,7},{6,4},{7,5},{8,10},{9,11},{10,... | collective-permute-start | bytes 196616 | tf_op jit(solution)/shard_map/ppermute | solution.py:340
  170.0 6.6 %collective-permute-start.43 = (f32[48,512]{1,0:T(8,128)S(1)}, f32[48,512]{1,0:T(8,128)S(1)}, u32[]{:S(2)}, u32[]{:S(2)}) collective-permute-start(f32[48,512]{1,0:T(8,128)S(1)} %get-tuple-element.83), channel_id=1, source_target_pairs={{0,8},{1,9},{2,10},{3,11},{4,12},{5,13},{6,14},{7,15},{8,0},{9,1},... | collective-permute-start | bytes 294920 | tf_op jit(solution)/shard_map/ppermute | solution.py:340
  (19 other events, 18.8 us)

commit v3 on v2

--- a/solution.py
+++ b/solution.py
@@ -55,9 +55,12 @@
     return pl.ds(pl.multiple_of(i * n, n), n)
 
 
-def scores_kernel(total_cols, x_ref, y_ref, mass_ref, z_ref, b_ref, sq_ref, lse_ref, cb_ref):
+def scores_kernel(total_cols, share, x_ref, y_ref, mass_ref, z_ref, b_ref, sq_ref, lse_ref, mine_ref,
+                  cb_ref):
     cols, width = y_ref.shape
     rows = x_ref.shape[0]
+    first = pl.multiple_of(lax.axis_index("cols") * share, share)
+    mine_ref[...] = x_ref[pl.ds(first, share), :].astype(F32)
     for c in range(cols // LANES):
         s = pl.ds(c * LANES, LANES)
         b = column(mass_ref[:, s] * (1.0 / total_cols))
@@ -97,18 +100,19 @@
     reduce_block(rows // step - 1)
 
 
-def scores(new_points, arch_points, arch_mass, total_cols):
+def scores(new_points, arch_points, arch_mass, total_cols, share):
     rows, cols = new_points.shape[0], arch_points.shape[0]
     return pl.pallas_call(
-        functools.partial(scores_kernel, total_cols),
+        functools.partial(scores_kernel, total_cols, share),
         out_shape=(
             VMEM((cols, rows), F32),
             VMEM((cols, LANES), F32),
             VMEM((cols, LANES), F32),
             jax.ShapeDtypeStruct((1, rows), F32),
+            VMEM((share, new_points.shape[1]), F32),
         ),
         in_specs=full(3),
-        out_specs=tuple(full(4)),
+        out_specs=tuple(full(5)),
         scratch_shapes=[pltpu.VMEM((cols, LANES), F32)],
         compiler_params=params(),
         name="scores",
@@ -243,13 +247,13 @@
     )(e, b, *more)
 
 
-def mix_kernel(share, pieces, me_ref, e_ref, y_ref, *refs):
+def mix_kernel(share, pieces, e_ref, y_ref, *refs):
     c_refs, r_refs = refs[:6], refs[6:11]
     half_ref, keep_ref = refs[11:13]
     send_refs, prod_ref = refs[13:-1], refs[-1]
     cols, rows = e_ref.shape
     pair = 2 * share
-    me = me_ref[0]
+    me = lax.axis_index("cols")
     core = me % 2
     for p in range(rows // pair):
         lo = pl.multiple_of(((me // 2) ^ p) * pair, pair)
@@ -276,7 +280,7 @@
             at = at + n
 
 
-def mix(share, pieces, me, e, y, columns, weights):
+def mix(share, pieces, e, y, columns, weights):
     cols, rows = e.shape
     width = y.shape[1]
     pairs = rows // (2 * share)
@@ -285,17 +289,19 @@
     got = pl.pallas_call(
         functools.partial(mix_kernel, share, pieces),
         out_shape=tuple(out),
-        in_specs=[pl.BlockSpec(memory_space=pltpu.SMEM)] + full(13),
+        in_specs=full(13),
         out_specs=tuple(full(len(out))),
         scratch_shapes=[pltpu.VMEM((2, 2 * share, width), F32)],
         compiler_params=params(16),
         name="mix",
-    )(me.reshape(1), e, y, *columns, *weights)
+    )(e, y, *columns, *weights)
     return got[0], got[1], got[2:]
 
 
 def back_kernel(total_cols, half_ref, x_ref, y_ref, e_ref, b_ref, r_ref, n_ref, sq_ref, bv2_ref,
-                bv3_ref, mid_ref, gb1_ref, vbr_ref, w_ref, pot_ref, arch_ref, tmp_ref):
+                bv3_ref, mid_ref, gb1_ref, vbr_ref, w_ref, alpha_ref, u3_ref, after_ref, pot_ref, arch_ref,
+                new_ref, tmp_ref):
+    del after_ref
     cols, rows = e_ref.shape
     width = y_ref.shape[1]
     column_dots(e_ref, [wide(a) for a in lanes(w_ref[...])], tmp_ref)
@@ -314,6 +320,18 @@
         s = pl.ds(c * LANES, LANES)
         pot = (sq_ref[s, :] - n_ref[s, :] + jnp.log2(bv3_ref[s, :] / b_ref[s, :])) * (1.0 / LOGK)
         pot_ref[:, s] = jnp.transpose(pot)[0:1, :]
+    ones = jnp.ones((SUB, width), BF16)
+    for i in range(rows // step):
+        s = pl.ds(i * step, step)
+        xf = x_ref[s, :].astype(F32)
+        square = xf * xf
+        high = square.astype(BF16)
+        low = (square - high.astype(F32)).astype(BF16)
+        sq = sum(
+            lax.dot_general(ones, v, (((1,), (1,)), ((), ())), preferred_element_type=F32)
+            for v in (high, low)
+        )[0:1, :] * (LOGK / width)
+        new_ref[:, s] = (alpha_ref[:, s] + jnp.log2(u3_ref[:, s]) + sq) * (1.0 / LOGK)
 
 
 def back(total_cols, half, x, y, *rest):
@@ -324,9 +342,10 @@
         out_shape=(
             jax.ShapeDtypeStruct((1, cols), F32),
             jax.ShapeDtypeStruct((cols, width), F32),
+            jax.ShapeDtypeStruct((1, rows), F32),
         ),
-        in_specs=full(3 + len(rest)),
-        out_specs=tuple(full(2)),
+        in_specs=full(2 + len(rest)) + [pl.BlockSpec(memory_space=pl.ANY)],
+        out_specs=tuple(full(3)),
         scratch_shapes=[pltpu.VMEM((cols, LANES), F32)],
         compiler_params=params(16),
         cost_estimate=pl.CostEstimate(
@@ -340,20 +359,58 @@
     return lax.ppermute(v, "cols", [(i, i ^ k) for i in range(count)])
 
 
-def scatter_sum(keep, sends, pieces, count):
+def scatter_sum(keep, sends, pieces, count, meanwhile):
     bits = [1 << i for i in range(1, count.bit_length() - 1)]
-    done, at = [], 0
-    for i, (send, n) in enumerate(zip(sends, pieces)):
+    held, at = [], 0
+    for send, n in zip(sends, pieces):
         got = swap(send, 1, count)
-        v = {p: keep[p, at:at + n] + got[p] for p in range(count // 2)}
+        held.append({p: (keep[p, at:at + n], got[p]) for p in range(count // 2)})
         at += n
+    other = meanwhile(got)
+    done = []
+    for i, (v, n) in enumerate(zip(held, pieces)):
         order = bits if i < (len(pieces) + 1) // 2 else bits[1:] + bits[:1]
         for k in order:
+            v = {p: a + b for p, (a, b) in v.items()}
             away = [p for p in sorted(v) if p & (k // 2)]
             got = swap(jnp.concatenate([v[p] for p in away], axis=0), k, count)
-            v = {p ^ (k // 2): v[p ^ (k // 2)] + got[j * n:(j + 1) * n] for j, p in enumerate(away)}
-        done.append(v[0])
-    return jnp.concatenate(done, axis=0)
+            v = {p ^ (k // 2): (v[p ^ (k // 2)], got[j * n:(j + 1) * n]) for j, p in enumerate(away)}
+        done += v[0]
+    return done, other
+
+
+def gradient_kernel(pieces, scale, *refs):
+    weight_ref, mine_ref = refs[:2]
+    terms, (out_ref, col_ref) = refs[2:-2], refs[-2:]
+    share, width = mine_ref.shape
+    pair = 2 * share
+    me = lax.axis_index("cols")
+    lo = pl.multiple_of((me // 2) * pair, pair)
+    for l in range(pair // LANES):
+        at = pl.multiple_of(lo + l * LANES, LANES)
+        col_ref[pl.ds(l * LANES, LANES), :] = column(weight_ref[:, pl.ds(at, LANES)])
+    at = 0
+    for i, n in enumerate(pieces):
+        col = col_ref[pl.ds(pl.multiple_of((me % 2) * share + at, 8), n), :]
+        for l in range(width // LANES):
+            ls = pl.ds(l * LANES, LANES)
+            out_ref[pl.ds(at, n), ls] = scale * (
+                col * mine_ref[pl.ds(at, n), ls] - (terms[2 * i][:, ls] + terms[2 * i + 1][:, ls])
+            )
+        at += n
+
+
+def gradient(pieces, scale, weight, mine, terms):
+    share, width = mine.shape
+    return pl.pallas_call(
+        functools.partial(gradient_kernel, pieces, float(scale)),
+        out_shape=jax.ShapeDtypeStruct((share, width), F32),
+        in_specs=full(2 + len(terms)),
+        out_specs=full(1)[0],
+        scratch_shapes=[pltpu.VMEM((2 * share, LANES), F32)],
+        compiler_params=params(8),
+        name="gradient",
+    )(weight, mine, *terms)
 
 
 def combine(x, count, join):
@@ -378,19 +435,16 @@
 
 
 def local(new_points, arch_points, new_mass, arch_mass):
-    rows, width = new_points.shape
+    rows = new_points.shape[0]
     count = lax.axis_size("cols")
     assert count & (count - 1) == 0
     reduce_add = functools.partial(combine, count=count, join=add_join)
     reduce_lse = functools.partial(combine, count=count, join=lse_join)
     total_cols = arch_points.shape[0] * count
     share = rows // count
-    me = lax.axis_index("cols")
-    new_float = new_points.astype(F32)
-    sq_new = jnp.sum(new_float * new_float, 1) * (LOGK / width)
     a = (new_mass / rows).reshape(1, rows)
 
-    z, b, sq, lse = scores(new_points, arch_points, arch_mass, total_cols)
+    z, b, sq, lse, mine = scores(new_points, arch_points, arch_mass, total_cols, share)
     alpha = -reduce_lse(lse)
     e, n, r, br, vbr, part = plan(z, b, sq, jnp.log2(a) + alpha)
     u2 = a / reduce_add(part)
@@ -407,18 +461,18 @@
     w1 = fbar1 / a
     pieces = [share * f // 16 for f in (6, 6, 4)]
     half, keep, sends = mix(
-        share, pieces, me, e, arch_points, (bv3, bv2, mid, br, vbr, gb1), (u3, w3, u2, w2, w1)
+        share, pieces, e, arch_points, (bv3, bv2, mid, br, vbr, gb1), (u3, w3, u2, w2, w1)
     )
-    pot, arch_grad = back(
-        total_cols, half, new_points, arch_points, e, b, r, n, sq, bv2, bv3, mid, gb1, vbr, w1
+    terms, (pot, arch_grad, new_pot) = scatter_sum(
+        keep, sends, pieces, count,
+        lambda after: back(
+            total_cols, half, new_points, arch_points, e, b, r, n, sq, bv2, bv3, mid, gb1, vbr, w1,
+            alpha, u3, after
+        ),
     )
-    summed = scatter_sum(keep, sends, pieces, count)
     row_weight = 2.0 * (fbar3 + fbar2 + fbar1) - a
-    mine = lax.dynamic_slice_in_dim(row_weight.reshape(rows), me * share, share, 0)
-    points = lax.dynamic_slice_in_dim(new_points, me * share, share, 0).astype(F32)
-    new_grad = rows * (mine[:, None] * points - summed)
-    new_pot = (alpha.reshape(rows) + jnp.log2(u3).reshape(rows) + sq_new) * (1.0 / LOGK)
-    return (new_pot, pot.reshape(-1), new_grad, arch_grad)
+    new_grad = gradient(pieces, rows, row_weight, mine, terms)
+    return (new_pot.reshape(-1), pot.reshape(-1), new_grad, arch_grad)
 
 
 def solution(mesh):

time: 179 us -> 148 us (0.83)
  local copies, waits for them, and re-layouts: 31.9 us -> 3.51 us
  other arithmetic: 7.91 us -> 1.01 us
  waiting for transfers between devices: 59.4 us -> 64 us
    unnamed x70 -> x12, local copies, waits for them, and re-layouts: 31.9 us -> 3.51 us
    add x10 -> x6, other arithmetic: 5.53 us -> 0.49 us  [scatter_sum(): v = {p: a + b for p, (a, b) in v.items()}]
    ppermute x48, waiting for transfers between devices: 59.4 us -> 64 us  [swap(): return lax.ppermute(v, 'cols', [(i, i ^ k) for i in range(count)])]
    pallas_call x1 -> x2, Pallas kernels: 3.78 us -> 4.66 us  [the longest x1 3.79 us: scores(): pl.pallas_call(functools.partial(scores_kernel, total_cols, share), out_s...]
  transfers between devices with their start and end apart: 48 -> 48, of which waited for: 29 -> 33; matrix products, arithmetic and copies ran while one was open for 3% -> 0% of each run, Pallas kernels for 3% -> 4%
where the time goes in v3:
time: 148 us
  waiting for transfers between devices  64 us (43%)
  starting transfers between devices  48.9 us (33%)
  Pallas kernels  29.7 us (20%)
  local copies, waits for them, and re-layouts  3.51 us (2%)
    ppermute x48, waiting for transfers between devices, swap(): return lax.ppermute(v, 'cols', [(i, i ^ k) for i in range(count)])  64 us
    ppermute x48, starting transfers between devices, swap(): return lax.ppermute(v, 'cols', [(i, i ^ k) for i in range(count)])  48.9 us
    pallas_call x4, Pallas kernels, sweep(): pl.pallas_call(functools.partial(sweep_kernel, kind), out_shape=(VMEM((co...  7.95 us
    pallas_call x1, Pallas kernels, mix(): pl.pallas_call(functools.partial(mix_kernel, share, pieces), out_shape=tu...  5.98 us
    pallas_call x1, Pallas kernels, plan(): pl.pallas_call(plan_kernel, out_shape=(VMEM((cols, rows), F32),) + (VMEM(...  5.57 us
    pallas_call x1, Pallas kernels, back(): pl.pallas_call(functools.partial(back_kernel, float(total_cols)), out_sha...  5.56 us
    pallas_call x1, Pallas kernels, scores(): pl.pallas_call(functools.partial(scores_kernel, total_cols, share), out_s...  3.79 us
    unnamed x12, local copies, waits for them, and re-layouts  3.51 us
  transfers between devices with their start and end apart: 48, of which 33 were waited for; matrix products, arithmetic and copies ran while one was open for 0% of the time, Pallas kernels for 4%

profile of v3, /device:TPU:0, one launch (start us, length us, event | category | flops | bytes accessed | tf_op | source)
XLA Modules:
  0.0 148.1 jit_solution(7535766032612958134)
XLA Ops:
  0.6 1.2 copy-done
  1.9 1.6 %copy-done.2 = bf16[2048,512]{1,0:T(8,128)(2,1)S(1)} copy-done((bf16[2048,512]{1,0:T(8,128)(2,1)S(1)}, bf16[2048,512]{1,0:T(8,128)(2,1)}, u32[]{:S(2)}) %copy-start.2) | copy-done | bytes 2097176
  4.1 3.8 %scores.1 = (f32[1024,2048]{1,0:T(8,128)S(1)}, f32[1024,128]{1,0:T(8,128)S(1)}, f32[1024,128]{1,0:T(8,128)S(1)}, f32[1,2048]{1,0:T(1,128)S(1)}, f32[128,512]{1,0:T(8,128)S(1)}) custom-call(bf16[2048,512]{1,0:T(8,128)(2,1)S(1)} %copy-done.2, bf16[1024,512]{1,0:T(8,128)(2,1)S(1)} %copy-done, f32[1,1024]{1,0:T(1,128)S(1)} %bitcast.77), custom_call_target="tpu_custom_call" | custom-call | tf_op jit(solution)/shard_map/scores/pallas_call | solution.py:105
  8.5 2.6 %collective-permute-start.1 = (f32[1,2048]{1,0:T(1,128)S(1)}, f32[1,2048]{1,0:T(1,128)S(1)}, u32[]{:S(2)}, u32[]{:S(2)}) collective-permute-start(f32[1,2048]{1,0:T(1,128)S(1)} %get-tuple-element.34), channel_id=1, source_target_pairs={{0,2},{1,3},{2,0},{3,1},{4,6},{5,7},{6,4},{7,5},{8,10},{9,11},{10,... | collective-permute-start | bytes 24584 | tf_op jit(solution)/shard_map/ppermute | solution.py:359
  11.1 1.6 %collective-permute-done.1 = f32[1,2048]{1,0:T(1,128)S(1)} collective-permute-done((f32[1,2048]{1,0:T(1,128)S(1)}, f32[1,2048]{1,0:T(1,128)S(1)}, u32[]{:S(2)}, u32[]{:S(2)}) %collective-permute-start.1) | collective-permute-done | bytes 8224 | tf_op jit(solution)/shard_map/ppermute | solution.py:359
  12.7 1.4 collective-permute-done.2
  14.2 1.6 %collective-permute-start.3 = (f32[1,2048]{1,0:T(1,128)S(1)}, f32[1,2048]{1,0:T(1,128)S(1)}, u32[]{:S(2)}, u32[]{:S(2)}) collective-permute-start(f32[1,2048]{1,0:T(1,128)S(1)} %multiply_add_fusion.1), channel_id=1, source_target_pairs={{0,4},{1,5},{2,6},{3,7},{4,0},{5,1},{6,2},{7,3},{8,12},{9,13},{10,... | collective-permute-start | bytes 24584 | tf_op jit(solution)/shard_map/ppermute | solution.py:359
  15.8 2.6 %collective-permute-start.4 = (f32[1,2048]{1,0:T(1,128)S(1)}, f32[1,2048]{1,0:T(1,128)S(1)}, u32[]{:S(2)}, u32[]{:S(2)}) collective-permute-start(f32[1,2048]{1,0:T(1,128)S(1)} %multiply_add_fusion.1), channel_id=1, source_target_pairs={{0,8},{1,9},{2,10},{3,11},{4,12},{5,13},{6,14},{7,15},{8,0},{9,1},... | collective-permute-start | bytes 24584 | tf_op jit(solution)/shard_map/ppermute | solution.py:359
  18.7 1.7 %collective-permute-done.4 = f32[1,2048]{1,0:T(1,128)S(1)} collective-permute-done((f32[1,2048]{1,0:T(1,128)S(1)}, f32[1,2048]{1,0:T(1,128)S(1)}, u32[]{:S(2)}, u32[]{:S(2)}) %collective-permute-start.4) | collective-permute-done | bytes 8224 | tf_op jit(solution)/shard_map/ppermute | solution.py:359
  20.4 3.5 %collective-permute-done.5 = f32[1,2048]{1,0:T(1,128)S(1)} collective-permute-done((f32[1,2048]{1,0:T(1,128)S(1)}, f32[1,2048]{1,0:T(1,128)S(1)}, u32[]{:S(2)}, u32[]{:S(2)}) %collective-permute-start.5) | collective-permute-done | bytes 8224 | tf_op jit(solution)/shard_map/ppermute | solution.py:359
  24.0 5.6 %plan.1 = (f32[1024,2048]{1,0:T(8,128)S(1)}, f32[1024,128]{1,0:T(8,128)S(1)}, f32[1024,128]{1,0:T(8,128)S(1)}, f32[1024,128]{1,0:T(8,128)S(1)}, f32[1024,128]{1,0:T(8,128)S(1)}, /*index=5*/f32[1,2048]{1,0:T(1,128)S(1)}) custom-call(f32[1024,2048]{1,0:T(8,128)S(1)} %get-tuple-element.31.z_ref, ...), custom_call_target="tpu_custom_call", output_to_operand_aliasing={{0}: (0, {})} | custom-call | tf_op jit(solution)/shard_map/plan/pallas_call | solution.py:200
  30.3 1.2 collective-permute-start.8
  31.5 1.9 %collective-permute-done.7 = f32[1,2048]{1,0:T(1,128)S(1)} collective-permute-done((f32[1,2048]{1,0:T(1,128)S(1)}, f32[1,2048]{1,0:T(1,128)S(1)}, u32[]{:S(2)}, u32[]{:S(2)}) %collective-permute-start.7) | collective-permute-done | bytes 8224 | tf_op jit(solution)/shard_map/ppermute | solution.py:359
  33.5 1.0 collective-permute-start.11
  34.5 2.5 %collective-permute-start.9 = (f32[1,2048]{1,0:T(1,128)S(1)}, f32[1,2048]{1,0:T(1,128)S(1)}, u32[]{:S(2)}, u32[]{:S(2)}) collective-permute-start(f32[1,2048]{1,0:T(1,128)S(1)} %add_add_fusion.5), channel_id=1, source_target_pairs={{0,4},{1,5},{2,6},{3,7},{4,0},{5,1},{6,2},{7,3},{8,12},{9,13},{10,... | collective-permute-start | bytes 24584 | tf_op jit(solution)/shard_map/ppermute | solution.py:359
  37.0 1.1 collective-permute-done.10
  38.1 1.0 collective-permute-done.11
  39.1 2.0 %sweep_fwd.2 = (f32[1024,128]{1,0:T(8,128)S(1)}, f32[1,2048]{1,0:T(1,128)S(1)}) custom-call(f32[1024,2048]{1,0:T(8,128)S(1)} %get-tuple-element.35.e_ref, f32[1024,128]{1,0:T(8,128)S(1)} %get-tuple-element.32.b_ref, f32[1,2048]{1,0:T(1,128)S(1)} %add_divide_fusion.1.refs_0_.refs_8_), custom_call_target="tpu_custom_call" | custom-call | tf_op jit(solution)/shard_map/sweep_fwd/pallas_call | solution.py:239
  41.2 1.4 collective-permute-start.13
  43.0 1.9 %collective-permute-done.13 = f32[1,2048]{1,0:T(1,128)S(1)} collective-permute-done((f32[1,2048]{1,0:T(1,128)S(1)}, f32[1,2048]{1,0:T(1,128)S(1)}, u32[]{:S(2)}, u32[]{:S(2)}) %collective-permute-start.13) | collective-permute-done | bytes 8224 | tf_op jit(solution)/shard_map/ppermute | solution.py:359
  44.9 0.8 collective-permute-done.14
  45.7 1.7 %collective-permute-start.15 = (f32[1,2048]{1,0:T(1,128)S(1)}, f32[1,2048]{1,0:T(1,128)S(1)}, u32[]{:S(2)}, u32[]{:S(2)}) collective-permute-start(f32[1,2048]{1,0:T(1,128)S(1)} %add_add_fusion.4), channel_id=1, source_target_pairs={{0,4},{1,5},{2,6},{3,7},{4,0},{5,1},{6,2},{7,3},{8,12},{9,13},{10,... | collective-permute-start | bytes 24584 | tf_op jit(solution)/shard_map/ppermute | solution.py:359
  47.4 1.0 collective-permute-start.16
  48.3 1.8 %collective-permute-start.17 = (f32[1,2048]{1,0:T(1,128)S(1)}, f32[1,2048]{1,0:T(1,128)S(1)}, u32[]{:S(2)}, u32[]{:S(2)}) collective-permute-start(f32[1,2048]{1,0:T(1,128)S(1)} %add_add_fusion.4), channel_id=1, source_target_pairs={{0,12},{1,13},{2,14},{3,15},{4,8},{5,9},{6,10},{7,11},{8,4},{9,5},... | collective-permute-start | bytes 24584 | tf_op jit(solution)/shard_map/ppermute | solution.py:359
  50.1 1.8 %collective-permute-done.16 = f32[1,2048]{1,0:T(1,128)S(1)} collective-permute-done((f32[1,2048]{1,0:T(1,128)S(1)}, f32[1,2048]{1,0:T(1,128)S(1)}, u32[]{:S(2)}, u32[]{:S(2)}) %collective-permute-start.16) | collective-permute-done | bytes 8224 | tf_op jit(solution)/shard_map/ppermute | solution.py:359
  51.9 1.9 %collective-permute-done.17 = f32[1,2048]{1,0:T(1,128)S(1)} collective-permute-done((f32[1,2048]{1,0:T(1,128)S(1)}, f32[1,2048]{1,0:T(1,128)S(1)}, u32[]{:S(2)}, u32[]{:S(2)}) %collective-permute-start.17) | collective-permute-done | bytes 8224 | tf_op jit(solution)/shard_map/ppermute | solution.py:359
  53.8 2.0 %sweep_fwd.3 = (f32[1024,128]{1,0:T(8,128)S(1)}, f32[1,2048]{1,0:T(1,128)S(1)}) custom-call(f32[1024,2048]{1,0:T(8,128)S(1)} %get-tuple-element.35.e_ref, f32[1024,128]{1,0:T(8,128)S(1)} %get-tuple-element.32.b_ref, f32[1,2048]{1,0:T(1,128)S(1)} %add_divide_fusion.refs_0_.refs_6_.u3_ref), custom_call_target="tpu_custom_call" | custom-call | tf_op jit(solution)/shard_map/sweep_fwd/pallas_call | solution.py:239
  55.9 0.7 collective-permute-start.19
  56.6 1.1 collective-permute-start.20
  57.8 1.9 %collective-permute-done.19 = f32[1,2048]{1,0:T(1,128)S(1)} collective-permute-done((f32[1,2048]{1,0:T(1,128)S(1)}, f32[1,2048]{1,0:T(1,128)S(1)}, u32[]{:S(2)}, u32[]{:S(2)}) %collective-permute-start.19) | collective-permute-done | bytes 8224 | tf_op jit(solution)/shard_map/ppermute | solution.py:359
  59.8 2.4 %collective-permute-start.22 = (f32[1,2048]{1,0:T(1,128)S(1)}, f32[1,2048]{1,0:T(1,128)S(1)}, u32[]{:S(2)}, u32[]{:S(2)}) collective-permute-start(f32[1,2048]{1,0:T(1,128)S(1)} %add_add_fusion.3), channel_id=1, source_target_pairs={{0,8},{1,9},{2,10},{3,11},{4,12},{5,13},{6,14},{7,15},{8,0},{9,1},... | collective-permute-start | bytes 24584 | tf_op jit(solution)/shard_map/ppermute | solution.py:359
  62.2 2.0 %collective-permute-start.23 = (f32[1,2048]{1,0:T(1,128)S(1)}, f32[1,2048]{1,0:T(1,128)S(1)}, u32[]{:S(2)}, u32[]{:S(2)}) collective-permute-start(f32[1,2048]{1,0:T(1,128)S(1)} %add_add_fusion.3), channel_id=1, source_target_pairs={{0,12},{1,13},{2,14},{3,15},{4,8},{5,9},{6,10},{7,11},{8,4},{9,5},... | collective-permute-start | bytes 24584 | tf_op jit(solution)/shard_map/ppermute | solution.py:359
  64.4 3.2 %collective-permute-done.23 = f32[1,2048]{1,0:T(1,128)S(1)} collective-permute-done((f32[1,2048]{1,0:T(1,128)S(1)}, f32[1,2048]{1,0:T(1,128)S(1)}, u32[]{:S(2)}, u32[]{:S(2)}) %collective-permute-start.23) | collective-permute-done | bytes 8224 | tf_op jit(solution)/shard_map/ppermute | solution.py:359
  67.6 2.0 %sweep_mid.1 = (f32[1024,128]{1,0:T(8,128)S(1)}, f32[1,2048]{1,0:T(1,128)S(1)}) custom-call(f32[1024,2048]{1,0:T(8,128)S(1)} %get-tuple-element.35.e_ref, f32[1024,128]{1,0:T(8,128)S(1)} %get-tuple-element.32.b_ref, f32[1024,128]{1,0:T(8,128)S(1)} %get-tuple-element.39.refs_0_.refs_1_.bv2_ref, f32[1,2048]{1,0:T(1,128)S(1)} %get-tuple-element.62.refs_1_.refs_7_), custom_call_target="tpu_custom_call" | custom-call | tf_op jit(solution)/shard_map/sweep_mid/pallas_call | solution.py:239
  69.7 1.4 collective-permute-start.25
  71.6 1.9 %collective-permute-done.25 = f32[1,2048]{1,0:T(1,128)S(1)} collective-permute-done((f32[1,2048]{1,0:T(1,128)S(1)}, f32[1,2048]{1,0:T(1,128)S(1)}, u32[]{:S(2)}, u32[]{:S(2)}) %collective-permute-start.25) | collective-permute-done | bytes 8224 | tf_op jit(solution)/shard_map/ppermute | solution.py:359
  73.4 0.8 collective-permute-done.26
  74.3 2.6 %collective-permute-start.28 = (f32[1,2048]{1,0:T(1,128)S(1)}, f32[1,2048]{1,0:T(1,128)S(1)}, u32[]{:S(2)}, u32[]{:S(2)}) collective-permute-start(f32[1,2048]{1,0:T(1,128)S(1)} %add_add_fusion.2), channel_id=1, source_target_pairs={{0,8},{1,9},{2,10},{3,11},{4,12},{5,13},{6,14},{7,15},{8,0},{9,1},... | collective-permute-start | bytes 24584 | tf_op jit(solution)/shard_map/ppermute | solution.py:359
  76.9 1.8 %collective-permute-start.29 = (f32[1,2048]{1,0:T(1,128)S(1)}, f32[1,2048]{1,0:T(1,128)S(1)}, u32[]{:S(2)}, u32[]{:S(2)}) collective-permute-start(f32[1,2048]{1,0:T(1,128)S(1)} %add_add_fusion.2), channel_id=1, source_target_pairs={{0,12},{1,13},{2,14},{3,15},{4,8},{5,9},{6,10},{7,11},{8,4},{9,5},... | collective-permute-start | bytes 24584 | tf_op jit(solution)/shard_map/ppermute | solution.py:359
  79.0 3.4 %collective-permute-done.29 = f32[1,2048]{1,0:T(1,128)S(1)} collective-permute-done((f32[1,2048]{1,0:T(1,128)S(1)}, f32[1,2048]{1,0:T(1,128)S(1)}, u32[]{:S(2)}, u32[]{:S(2)}) %collective-permute-start.29) | collective-permute-done | bytes 8224 | tf_op jit(solution)/shard_map/ppermute | solution.py:359
  82.4 2.0 %sweep_bwd.1 = (f32[1024,128]{1,0:T(8,128)S(1)}, f32[1,2048]{1,0:T(1,128)S(1)}) custom-call(f32[1024,2048]{1,0:T(8,128)S(1)} %get-tuple-element.35.e_ref, f32[1024,128]{1,0:T(8,128)S(1)} %get-tuple-element.42.b_ref.refs_3_, f32[1024,128]{1,0:T(8,128)S(1)} %get-tuple-element.44.refs_0_.r_ref, f32[1,2048]{1,0:T(1,128)S(1)} %get-tuple-element.60.refs_1_.refs_9_), custom_call_target="tpu_custom_call" | custom-call | tf_op jit(solution)/shard_map/sweep_bwd/pallas_call | solution.py:239
  85.1 1.1 collective-permute-start.32
  86.3 1.9 %collective-permute-done.31 = f32[1,2048]{1,0:T(1,128)S(1)} collective-permute-done((f32[1,2048]{1,0:T(1,128)S(1)}, f32[1,2048]{1,0:T(1,128)S(1)}, u32[]{:S(2)}, u32[]{:S(2)}) %collective-permute-start.31) | collective-permute-done | bytes 8224 | tf_op jit(solution)/shard_map/ppermute | solution.py:359
  88.3 2.4 %collective-permute-start.34 = (f32[1,2048]{1,0:T(1,128)S(1)}, f32[1,2048]{1,0:T(1,128)S(1)}, u32[]{:S(2)}, u32[]{:S(2)}) collective-permute-start(f32[1,2048]{1,0:T(1,128)S(1)} %add_add_fusion.1), channel_id=1, source_target_pairs={{0,8},{1,9},{2,10},{3,11},{4,12},{5,13},{6,14},{7,15},{8,0},{9,1},... | collective-permute-start | bytes 24584 | tf_op jit(solution)/shard_map/ppermute | solution.py:359
  90.7 2.0 %collective-permute-start.35 = (f32[1,2048]{1,0:T(1,128)S(1)}, f32[1,2048]{1,0:T(1,128)S(1)}, u32[]{:S(2)}, u32[]{:S(2)}) collective-permute-start(f32[1,2048]{1,0:T(1,128)S(1)} %add_add_fusion.1), channel_id=1, source_target_pairs={{0,12},{1,13},{2,14},{3,15},{4,8},{5,9},{6,10},{7,11},{8,4},{9,5},... | collective-permute-start | bytes 24584 | tf_op jit(solution)/shard_map/ppermute | solution.py:359
  92.9 3.2 %collective-permute-done.35 = f32[1,2048]{1,0:T(1,128)S(1)} collective-permute-done((f32[1,2048]{1,0:T(1,128)S(1)}, f32[1,2048]{1,0:T(1,128)S(1)}, u32[]{:S(2)}, u32[]{:S(2)}) %collective-permute-start.35) | collective-permute-done | bytes 8224 | tf_op jit(solution)/shard_map/ppermute | solution.py:359
  96.2 6.0 %mix.1 = (bf16[1024,2048]{1,0:T(8,128)(2,1)S(1)}, f32[8,128,512]{2,1,0:T(8,128)S(1)}, f32[8,48,512]{2,1,0:T(8,128)S(1)}, f32[8,48,512]{2,1,0:T(8,128)S(1)}, f32[8,32,512]{2,1,0:T(8,128)S(1)}) custom-call(f32[1024,2048]{1,0:T(8,128)S(1)} %get-tuple-element.35.e_ref, bf16[1024,512]{1,0:T(8,128)(2,1)S(1)} %copy-done.1, ...), custom_call_target="tpu_custom_call" | custom-call | tf_op jit(solution)/shard_map/mix/pallas_call | solution.py:289
  102.8 1.3 collective-permute-done.36.after_ref
  104.3 1.0 collective-permute-done.37
  105.3 1.1 collective-permute-done.41
  106.6 1.4 collective-permute-start.38
  108.8 3.9 %collective-permute-done.45 = f32[128,512]{1,0:T(8,128)S(1)} collective-permute-done((f32[128,512]{1,0:T(8,128)S(1)}, f32[128,512]{1,0:T(8,128)S(1)}, u32[]{:S(2)}, u32[]{:S(2)}) %collective-permute-start.45) | collective-permute-done | bytes 262176 | tf_op jit(solution)/shard_map/ppermute | solution.py:359
  112.7 0.9 collective-permute-start.46
  113.5 5.1 %collective-permute-done.38 = f32[192,512]{1,0:T(8,128)S(1)} collective-permute-done((f32[192,512]{1,0:T(8,128)S(1)}, f32[192,512]{1,0:T(8,128)S(1)}, u32[]{:S(2)}, u32[]{:S(2)}) %collective-permute-start.38) | collective-permute-done | bytes 393248 | tf_op jit(solution)/shard_map/ppermute | solution.py:359
  118.6 7.6 %collective-permute-done.42 = f32[192,512]{1,0:T(8,128)S(1)} collective-permute-done((f32[192,512]{1,0:T(8,128)S(1)}, f32[192,512]{1,0:T(8,128)S(1)}, u32[]{:S(2)}, u32[]{:S(2)}) %collective-permute-start.42) | collective-permute-done | bytes 393248 | tf_op jit(solution)/shard_map/ppermute | solution.py:359
  126.5 2.1 %collective-permute-start.43 = (f32[96,512]{1,0:T(8,128)S(1)}, f32[96,512]{1,0:T(8,128)S(1)}, u32[]{:S(2)}, u32[]{:S(2)}) collective-permute-start(f32[96,512]{1,0:T(8,128)S(1)} %pad_maximum_fusion.4), channel_id=1, source_target_pairs={{0,4},{1,5},{2,6},{3,7},{4,0},{5,1},{6,2},{7,3},{8,12},{9,13},{10,... | collective-permute-start | bytes 589832 | tf_op jit(solution)/shard_map/ppermute | solution.py:359
  128.6 1.4 collective-permute-start.47
  130.0 4.2 %collective-permute-done.39 = f32[96,512]{1,0:T(8,128)S(1)} collective-permute-done((f32[96,512]{1,0:T(8,128)S(1)}, f32[96,512]{1,0:T(8,128)S(1)}, u32[]{:S(2)}, u32[]{:S(2)}) %collective-permute-start.39) | collective-permute-done | bytes 196640 | tf_op jit(solution)/shard_map/ppermute | solution.py:359
  134.3 2.5 %collective-permute-done.43 = f32[96,512]{1,0:T(8,128)S(1)} collective-permute-done((f32[96,512]{1,0:T(8,128)S(1)}, f32[96,512]{1,0:T(8,128)S(1)}, u32[]{:S(2)}, u32[]{:S(2)}) %collective-permute-start.43) | collective-permute-done | bytes 196640 | tf_op jit(solution)/shard_map/ppermute | solution.py:359
  136.9 0.9 collective-permute-start.40
  137.8 2.1 %collective-permute-start.44 = (f32[48,512]{1,0:T(8,128)S(1)}, f32[48,512]{1,0:T(8,128)S(1)}, u32[]{:S(2)}, u32[]{:S(2)}) collective-permute-start(f32[48,512]{1,0:T(8,128)S(1)} %get-tuple-element.66), channel_id=1, source_target_pairs={{0,8},{1,9},{2,10},{3,11},{4,12},{5,13},{6,14},{7,15},{8,0},{9,1},... | collective-permute-start | bytes 294920 | tf_op jit(solution)/shard_map/ppermute | solution.py:359
  139.9 5.6 %back.1 = (f32[1,1024]{1,0:T(1,128)}, f32[1024,512]{1,0:T(8,128)}, f32[1,2048]{1,0:T(1,128)}) custom-call(bf16[1024,2048]{1,0:T(8,128)(2,1)S(1)} %get-tuple-element.48.half_ref, bf16[2048,512]{1,0:T(8,128)(2,1)S(1)} %copy-done.3, bf16[1024,512]{1,0:T(8,128)(2,1)S(1)} %copy-done.1, f32[1024,2048]{1,0:T(8,128)S(1)} %get-tuple-element.35.e_ref, ...), custom_call_target="tpu_custom_call" | custom-call | flops 2147483648 | bytes 16777216 | tf_op jit(solution)/shard_map/back/pallas_call | solution.py:340
  146.0 1.3 collective-permute-done.44.refs_5_
  147.3 0.9 gradient.1
  (79 shorter events, 8.4 us)
Async XLA Ops:
  0.6 1.2 copy-start
  1.9 1.6 %copy-start.2 = (bf16[2048,512]{1,0:T(8,128)(2,1)S(1)}, bf16[2048,512]{1,0:T(8,128)(2,1)}, u32[]{:S(2)}) copy-start(bf16[2048,512]{1,0:T(8,128)(2,1)} %x_ref.3) | copy-start | bytes 6291460
  3.5 0.7 copy-start.4
  4.1 14.5 %copy-start.5 = (f32[2048]{0:T(1024)S(1)}, f32[2048]{0:T(1024)}, u32[]{:S(2)}) copy-start(f32[2048]{0:T(1024)} %param.6) | copy-start | bytes 24580
  7.9 3.2 %collective-permute-start = (f32[1,2048]{1,0:T(1,128)S(1)}, f32[1,2048]{1,0:T(1,128)S(1)}, u32[]{:S(2)}, u32[]{:S(2)}) collective-permute-start(f32[1,2048]{1,0:T(1,128)S(1)} %get-tuple-element.34), channel_id=1, source_target_pairs={{0,1},{1,0},{2,3},{3,2},{4,5},{5,4},{6,7},{7,6},{8,9},{9,8},{10,11... | collective-permute-start | bytes 24584 | tf_op jit(solution)/shard_map/ppermute | solution.py:359
  8.5 4.2 %collective-permute-start.1 = (f32[1,2048]{1,0:T(1,128)S(1)}, f32[1,2048]{1,0:T(1,128)S(1)}, u32[]{:S(2)}, u32[]{:S(2)}) collective-permute-start(f32[1,2048]{1,0:T(1,128)S(1)} %get-tuple-element.34), channel_id=1, source_target_pairs={{0,2},{1,3},{2,0},{3,1},{4,6},{5,7},{6,4},{7,5},{8,10},{9,11},{10,... | collective-permute-start | bytes 24584 | tf_op jit(solution)/shard_map/ppermute | solution.py:359
  11.0 3.1 %collective-permute-start.2 = (f32[1,2048]{1,0:T(1,128)S(1)}, f32[1,2048]{1,0:T(1,128)S(1)}, u32[]{:S(2)}, u32[]{:S(2)}) collective-permute-start(f32[1,2048]{1,0:T(1,128)S(1)} %get-tuple-element.34), channel_id=1, source_target_pairs={{0,3},{1,2},{2,1},{3,0},{4,7},{5,6},{6,5},{7,4},{8,11},{9,10},{10,... | collective-permute-start | bytes 24584 | tf_op jit(solution)/shard_map/ppermute | solution.py:359
  14.2 4.5 %collective-permute-start.3 = (f32[1,2048]{1,0:T(1,128)S(1)}, f32[1,2048]{1,0:T(1,128)S(1)}, u32[]{:S(2)}, u32[]{:S(2)}) collective-permute-start(f32[1,2048]{1,0:T(1,128)S(1)} %multiply_add_fusion.1), channel_id=1, source_target_pairs={{0,4},{1,5},{2,6},{3,7},{4,0},{5,1},{6,2},{7,3},{8,12},{9,13},{10,... | collective-permute-start | bytes 24584 | tf_op jit(solution)/shard_map/ppermute | solution.py:359
  15.8 4.5 %collective-permute-start.4 = (f32[1,2048]{1,0:T(1,128)S(1)}, f32[1,2048]{1,0:T(1,128)S(1)}, u32[]{:S(2)}, u32[]{:S(2)}) collective-permute-start(f32[1,2048]{1,0:T(1,128)S(1)} %multiply_add_fusion.1), channel_id=1, source_target_pairs={{0,8},{1,9},{2,10},{3,11},{4,12},{5,13},{6,14},{7,15},{8,0},{9,1},... | collective-permute-start | bytes 24584 | tf_op jit(solution)/shard_map/ppermute | solution.py:359
  18.4 5.4 %collective-permute-start.5 = (f32[1,2048]{1,0:T(1,128)S(1)}, f32[1,2048]{1,0:T(1,128)S(1)}, u32[]{:S(2)}, u32[]{:S(2)}) collective-permute-start(f32[1,2048]{1,0:T(1,128)S(1)} %multiply_add_fusion.1), channel_id=1, source_target_pairs={{0,12},{1,13},{2,14},{3,15},{4,8},{5,9},{6,10},{7,11},{8,4},{9,5},... | collective-permute-start | bytes 24584 | tf_op jit(solution)/shard_map/ppermute | solution.py:359
  29.5 1.9 %collective-permute-start.6 = (f32[1,2048]{1,0:T(1,128)S(1)}, f32[1,2048]{1,0:T(1,128)S(1)}, u32[]{:S(2)}, u32[]{:S(2)}) collective-permute-start(f32[1,2048]{1,0:T(1,128)S(1)} %get-tuple-element.36), channel_id=1, source_target_pairs={{0,1},{1,0},{2,3},{3,2},{4,5},{5,4},{6,7},{7,6},{8,9},{9,8},{10,11... | collective-permute-start | bytes 24584 | tf_op jit(solution)/shard_map/ppermute | solution.py:359
  29.6 3.8 %collective-permute-start.7 = (f32[1,2048]{1,0:T(1,128)S(1)}, f32[1,2048]{1,0:T(1,128)S(1)}, u32[]{:S(2)}, u32[]{:S(2)}) collective-permute-start(f32[1,2048]{1,0:T(1,128)S(1)} %get-tuple-element.36), channel_id=1, source_target_pairs={{0,2},{1,3},{2,0},{3,1},{4,6},{5,7},{6,4},{7,5},{8,10},{9,11},{10,... | collective-permute-start | bytes 24584 | tf_op jit(solution)/shard_map/ppermute | solution.py:359
  30.3 3.1 %collective-permute-start.8 = (f32[1,2048]{1,0:T(1,128)S(1)}, f32[1,2048]{1,0:T(1,128)S(1)}, u32[]{:S(2)}, u32[]{:S(2)}) collective-permute-start(f32[1,2048]{1,0:T(1,128)S(1)} %get-tuple-element.36), channel_id=1, source_target_pairs={{0,3},{1,2},{2,1},{3,0},{4,7},{5,6},{6,5},{7,4},{8,11},{9,10},{10,... | collective-permute-start | bytes 24584 | tf_op jit(solution)/shard_map/ppermute | solution.py:359
  33.4 4.6 %collective-permute-start.10 = (f32[1,2048]{1,0:T(1,128)S(1)}, f32[1,2048]{1,0:T(1,128)S(1)}, u32[]{:S(2)}, u32[]{:S(2)}) collective-permute-start(f32[1,2048]{1,0:T(1,128)S(1)} %add_add_fusion.5), channel_id=1, source_target_pairs={{0,8},{1,9},{2,10},{3,11},{4,12},{5,13},{6,14},{7,15},{8,0},{9,1},... | collective-permute-start | bytes 24584 | tf_op jit(solution)/shard_map/ppermute | solution.py:359
  33.5 5.5 %collective-permute-start.11 = (f32[1,2048]{1,0:T(1,128)S(1)}, f32[1,2048]{1,0:T(1,128)S(1)}, u32[]{:S(2)}, u32[]{:S(2)}) collective-permute-start(f32[1,2048]{1,0:T(1,128)S(1)} %add_add_fusion.5), channel_id=1, source_target_pairs={{0,12},{1,13},{2,14},{3,15},{4,8},{5,9},{6,10},{7,11},{8,4},{9,5},... | collective-permute-start | bytes 24584 | tf_op jit(solution)/shard_map/ppermute | solution.py:359
  34.5 4.5 %collective-permute-start.9 = (f32[1,2048]{1,0:T(1,128)S(1)}, f32[1,2048]{1,0:T(1,128)S(1)}, u32[]{:S(2)}, u32[]{:S(2)}) collective-permute-start(f32[1,2048]{1,0:T(1,128)S(1)} %add_add_fusion.5), channel_id=1, source_target_pairs={{0,4},{1,5},{2,6},{3,7},{4,0},{5,1},{6,2},{7,3},{8,12},{9,13},{10,... | collective-permute-start | bytes 24584 | tf_op jit(solution)/shard_map/ppermute | solution.py:359
  41.1 1.9 %collective-permute-start.12 = (f32[1,2048]{1,0:T(1,128)S(1)}, f32[1,2048]{1,0:T(1,128)S(1)}, u32[]{:S(2)}, u32[]{:S(2)}) collective-permute-start(f32[1,2048]{1,0:T(1,128)S(1)} %get-tuple-element.37), channel_id=1, source_target_pairs={{0,1},{1,0},{2,3},{3,2},{4,5},{5,4},{6,7},{7,6},{8,9},{9,8},{10,11... | collective-permute-start | bytes 24584 | tf_op jit(solution)/shard_map/ppermute | solution.py:359
  41.2 3.7 %collective-permute-start.13 = (f32[1,2048]{1,0:T(1,128)S(1)}, f32[1,2048]{1,0:T(1,128)S(1)}, u32[]{:S(2)}, u32[]{:S(2)}) collective-permute-start(f32[1,2048]{1,0:T(1,128)S(1)} %get-tuple-element.37), channel_id=1, source_target_pairs={{0,2},{1,3},{2,0},{3,1},{4,6},{5,7},{6,4},{7,5},{8,10},{9,11},{10,... | collective-permute-start | bytes 24584 | tf_op jit(solution)/shard_map/ppermute | solution.py:359
  42.6 3.1 %collective-permute-start.14 = (f32[1,2048]{1,0:T(1,128)S(1)}, f32[1,2048]{1,0:T(1,128)S(1)}, u32[]{:S(2)}, u32[]{:S(2)}) collective-permute-start(f32[1,2048]{1,0:T(1,128)S(1)} %get-tuple-element.37), channel_id=1, source_target_pairs={{0,3},{1,2},{2,1},{3,0},{4,7},{5,6},{6,5},{7,4},{8,11},{9,10},{10,... | collective-permute-start | bytes 24584 | tf_op jit(solution)/shard_map/ppermute | solution.py:359
  45.7 4.5 %collective-permute-start.15 = (f32[1,2048]{1,0:T(1,128)S(1)}, f32[1,2048]{1,0:T(1,128)S(1)}, u32[]{:S(2)}, u32[]{:S(2)}) collective-permute-start(f32[1,2048]{1,0:T(1,128)S(1)} %add_add_fusion.4), channel_id=1, source_target_pairs={{0,4},{1,5},{2,6},{3,7},{4,0},{5,1},{6,2},{7,3},{8,12},{9,13},{10,... | collective-permute-start | bytes 24584 | tf_op jit(solution)/shard_map/ppermute | solution.py:359
  47.4 4.5 %collective-permute-start.16 = (f32[1,2048]{1,0:T(1,128)S(1)}, f32[1,2048]{1,0:T(1,128)S(1)}, u32[]{:S(2)}, u32[]{:S(2)}) collective-permute-start(f32[1,2048]{1,0:T(1,128)S(1)} %add_add_fusion.4), channel_id=1, source_target_pairs={{0,8},{1,9},{2,10},{3,11},{4,12},{5,13},{6,14},{7,15},{8,0},{9,1},... | collective-permute-start | bytes 24584 | tf_op jit(solution)/shard_map/ppermute | solution.py:359
  48.3 5.4 %collective-permute-start.17 = (f32[1,2048]{1,0:T(1,128)S(1)}, f32[1,2048]{1,0:T(1,128)S(1)}, u32[]{:S(2)}, u32[]{:S(2)}) collective-permute-start(f32[1,2048]{1,0:T(1,128)S(1)} %add_add_fusion.4), channel_id=1, source_target_pairs={{0,12},{1,13},{2,14},{3,15},{4,8},{5,9},{6,10},{7,11},{8,4},{9,5},... | collective-permute-start | bytes 24584 | tf_op jit(solution)/shard_map/ppermute | solution.py:359
  55.8 1.9 %collective-permute-start.18 = (f32[1,2048]{1,0:T(1,128)S(1)}, f32[1,2048]{1,0:T(1,128)S(1)}, u32[]{:S(2)}, u32[]{:S(2)}) collective-permute-start(f32[1,2048]{1,0:T(1,128)S(1)} %get-tuple-element.40), channel_id=1, source_target_pairs={{0,1},{1,0},{2,3},{3,2},{4,5},{5,4},{6,7},{7,6},{8,9},{9,8},{10,11... | collective-permute-start | bytes 24584 | tf_op jit(solution)/shard_map/ppermute | solution.py:359
  55.9 3.7 %collective-permute-start.19 = (f32[1,2048]{1,0:T(1,128)S(1)}, f32[1,2048]{1,0:T(1,128)S(1)}, u32[]{:S(2)}, u32[]{:S(2)}) collective-permute-start(f32[1,2048]{1,0:T(1,128)S(1)} %get-tuple-element.40), channel_id=1, source_target_pairs={{0,2},{1,3},{2,0},{3,1},{4,6},{5,7},{6,4},{7,5},{8,10},{9,11},{10,... | collective-permute-start | bytes 24584 | tf_op jit(solution)/shard_map/ppermute | solution.py:359
  56.6 3.1 %collective-permute-start.20 = (f32[1,2048]{1,0:T(1,128)S(1)}, f32[1,2048]{1,0:T(1,128)S(1)}, u32[]{:S(2)}, u32[]{:S(2)}) collective-permute-start(f32[1,2048]{1,0:T(1,128)S(1)} %get-tuple-element.40), channel_id=1, source_target_pairs={{0,3},{1,2},{2,1},{3,0},{4,7},{5,6},{6,5},{7,4},{8,11},{9,10},{10,... | collective-permute-start | bytes 24584 | tf_op jit(solution)/shard_map/ppermute | solution.py:359
  59.7 4.5 %collective-permute-start.21 = (f32[1,2048]{1,0:T(1,128)S(1)}, f32[1,2048]{1,0:T(1,128)S(1)}, u32[]{:S(2)}, u32[]{:S(2)}) collective-permute-start(f32[1,2048]{1,0:T(1,128)S(1)} %add_add_fusion.3), channel_id=1, source_target_pairs={{0,4},{1,5},{2,6},{3,7},{4,0},{5,1},{6,2},{7,3},{8,12},{9,13},{10,... | collective-permute-start | bytes 24584 | tf_op jit(solution)/shard_map/ppermute | solution.py:359
  59.8 4.6 %collective-permute-start.22 = (f32[1,2048]{1,0:T(1,128)S(1)}, f32[1,2048]{1,0:T(1,128)S(1)}, u32[]{:S(2)}, u32[]{:S(2)}) collective-permute-start(f32[1,2048]{1,0:T(1,128)S(1)} %add_add_fusion.3), channel_id=1, source_target_pairs={{0,8},{1,9},{2,10},{3,11},{4,12},{5,13},{6,14},{7,15},{8,0},{9,1},... | collective-permute-start | bytes 24584 | tf_op jit(solution)/shard_map/ppermute | solution.py:359
  62.2 5.4 %collective-permute-start.23 = (f32[1,2048]{1,0:T(1,128)S(1)}, f32[1,2048]{1,0:T(1,128)S(1)}, u32[]{:S(2)}, u32[]{:S(2)}) collective-permute-start(f32[1,2048]{1,0:T(1,128)S(1)} %add_add_fusion.3), channel_id=1, source_target_pairs={{0,12},{1,13},{2,14},{3,15},{4,8},{5,9},{6,10},{7,11},{8,4},{9,5},... | collective-permute-start | bytes 24584 | tf_op jit(solution)/shard_map/ppermute | solution.py:359
  69.6 1.9 %collective-permute-start.24 = (f32[1,2048]{1,0:T(1,128)S(1)}, f32[1,2048]{1,0:T(1,128)S(1)}, u32[]{:S(2)}, u32[]{:S(2)}) collective-permute-start(f32[1,2048]{1,0:T(1,128)S(1)} %get-tuple-element.45), channel_id=1, source_target_pairs={{0,1},{1,0},{2,3},{3,2},{4,5},{5,4},{6,7},{7,6},{8,9},{9,8},{10,11... | collective-permute-start | bytes 24584 | tf_op jit(solution)/shard_map/ppermute | solution.py:359
  69.7 3.7 %collective-permute-start.25 = (f32[1,2048]{1,0:T(1,128)S(1)}, f32[1,2048]{1,0:T(1,128)S(1)}, u32[]{:S(2)}, u32[]{:S(2)}) collective-permute-start(f32[1,2048]{1,0:T(1,128)S(1)} %get-tuple-element.45), channel_id=1, source_target_pairs={{0,2},{1,3},{2,0},{3,1},{4,6},{5,7},{6,4},{7,5},{8,10},{9,11},{10,... | collective-permute-start | bytes 24584 | tf_op jit(solution)/shard_map/ppermute | solution.py:359
  71.1 3.1 %collective-permute-start.26 = (f32[1,2048]{1,0:T(1,128)S(1)}, f32[1,2048]{1,0:T(1,128)S(1)}, u32[]{:S(2)}, u32[]{:S(2)}) collective-permute-start(f32[1,2048]{1,0:T(1,128)S(1)} %get-tuple-element.45), channel_id=1, source_target_pairs={{0,3},{1,2},{2,1},{3,0},{4,7},{5,6},{6,5},{7,4},{8,11},{9,10},{10,... | collective-permute-start | bytes 24584 | tf_op jit(solution)/shard_map/ppermute | solution.py:359
  74.2 4.5 %collective-permute-start.27 = (f32[1,2048]{1,0:T(1,128)S(1)}, f32[1,2048]{1,0:T(1,128)S(1)}, u32[]{:S(2)}, u32[]{:S(2)}) collective-permute-start(f32[1,2048]{1,0:T(1,128)S(1)} %add_add_fusion.2), channel_id=1, source_target_pairs={{0,4},{1,5},{2,6},{3,7},{4,0},{5,1},{6,2},{7,3},{8,12},{9,13},{10,... | collective-permute-start | bytes 24584 | tf_op jit(solution)/shard_map/ppermute | solution.py:359
  74.3 4.7 %collective-permute-start.28 = (f32[1,2048]{1,0:T(1,128)S(1)}, f32[1,2048]{1,0:T(1,128)S(1)}, u32[]{:S(2)}, u32[]{:S(2)}) collective-permute-start(f32[1,2048]{1,0:T(1,128)S(1)} %add_add_fusion.2), channel_id=1, source_target_pairs={{0,8},{1,9},{2,10},{3,11},{4,12},{5,13},{6,14},{7,15},{8,0},{9,1},... | collective-permute-start | bytes 24584 | tf_op jit(solution)/shard_map/ppermute | solution.py:359
  76.9 5.4 %collective-permute-start.29 = (f32[1,2048]{1,0:T(1,128)S(1)}, f32[1,2048]{1,0:T(1,128)S(1)}, u32[]{:S(2)}, u32[]{:S(2)}) collective-permute-start(f32[1,2048]{1,0:T(1,128)S(1)} %add_add_fusion.2), channel_id=1, source_target_pairs={{0,12},{1,13},{2,14},{3,15},{4,8},{5,9},{6,10},{7,11},{8,4},{9,5},... | collective-permute-start | bytes 24584 | tf_op jit(solution)/shard_map/ppermute | solution.py:359
  82.4 13.8 %copy-start.1 = (bf16[1024,512]{1,0:T(8,128)(2,1)S(1)}, bf16[1024,512]{1,0:T(8,128)(2,1)}, u32[]{:S(2)}) copy-start(bf16[1024,512]{1,0:T(8,128)(2,1)} %y_ref.5) | copy-start | bytes 3145732
  84.3 1.9 %collective-permute-start.30 = (f32[1,2048]{1,0:T(1,128)S(1)}, f32[1,2048]{1,0:T(1,128)S(1)}, u32[]{:S(2)}, u32[]{:S(2)}) collective-permute-start(f32[1,2048]{1,0:T(1,128)S(1)} %get-tuple-element.47), channel_id=1, source_target_pairs={{0,1},{1,0},{2,3},{3,2},{4,5},{5,4},{6,7},{7,6},{8,9},{9,8},{10,11... | collective-permute-start | bytes 24584 | tf_op jit(solution)/shard_map/ppermute | solution.py:359
  84.4 3.7 %collective-permute-start.31 = (f32[1,2048]{1,0:T(1,128)S(1)}, f32[1,2048]{1,0:T(1,128)S(1)}, u32[]{:S(2)}, u32[]{:S(2)}) collective-permute-start(f32[1,2048]{1,0:T(1,128)S(1)} %get-tuple-element.47), channel_id=1, source_target_pairs={{0,2},{1,3},{2,0},{3,1},{4,6},{5,7},{6,4},{7,5},{8,10},{9,11},{10,... | collective-permute-start | bytes 24584 | tf_op jit(solution)/shard_map/ppermute | solution.py:359
  85.1 3.1 %collective-permute-start.32 = (f32[1,2048]{1,0:T(1,128)S(1)}, f32[1,2048]{1,0:T(1,128)S(1)}, u32[]{:S(2)}, u32[]{:S(2)}) collective-permute-start(f32[1,2048]{1,0:T(1,128)S(1)} %get-tuple-element.47), channel_id=1, source_target_pairs={{0,3},{1,2},{2,1},{3,0},{4,7},{5,6},{6,5},{7,4},{8,11},{9,10},{10,... | collective-permute-start | bytes 24584 | tf_op jit(solution)/shard_map/ppermute | solution.py:359
  88.2 4.5 %collective-permute-start.33 = (f32[1,2048]{1,0:T(1,128)S(1)}, f32[1,2048]{1,0:T(1,128)S(1)}, u32[]{:S(2)}, u32[]{:S(2)}) collective-permute-start(f32[1,2048]{1,0:T(1,128)S(1)} %add_add_fusion.1), channel_id=1, source_target_pairs={{0,4},{1,5},{2,6},{3,7},{4,0},{5,1},{6,2},{7,3},{8,12},{9,13},{10,... | collective-permute-start | bytes 24584 | tf_op jit(solution)/shard_map/ppermute | solution.py:359
  88.3 4.6 %collective-permute-start.34 = (f32[1,2048]{1,0:T(1,128)S(1)}, f32[1,2048]{1,0:T(1,128)S(1)}, u32[]{:S(2)}, u32[]{:S(2)}) collective-permute-start(f32[1,2048]{1,0:T(1,128)S(1)} %add_add_fusion.1), channel_id=1, source_target_pairs={{0,8},{1,9},{2,10},{3,11},{4,12},{5,13},{6,14},{7,15},{8,0},{9,1},... | collective-permute-start | bytes 24584 | tf_op jit(solution)/shard_map/ppermute | solution.py:359
  90.7 5.4 %collective-permute-start.35 = (f32[1,2048]{1,0:T(1,128)S(1)}, f32[1,2048]{1,0:T(1,128)S(1)}, u32[]{:S(2)}, u32[]{:S(2)}) collective-permute-start(f32[1,2048]{1,0:T(1,128)S(1)} %add_add_fusion.1), channel_id=1, source_target_pairs={{0,12},{1,13},{2,14},{3,15},{4,8},{5,9},{6,10},{7,11},{8,4},{9,5},... | collective-permute-start | bytes 24584 | tf_op jit(solution)/shard_map/ppermute | solution.py:359
  102.2 2.0 %collective-permute-start.36 = (f32[8,32,512]{2,1,0:T(8,128)S(1)}, f32[8,32,512]{2,1,0:T(8,128)S(1)}, u32[]{:S(2)}, u32[]{:S(2)}) collective-permute-start(f32[8,32,512]{2,1,0:T(8,128)S(1)} %get-tuple-element.50), channel_id=1, source_target_pairs={{0,1},{1,0},{2,3},{3,2},{4,5},{5,4},{6,7},{7,6},{8,9},{9,8},{10,11... | collective-permute-start | bytes 1572872 | tf_op jit(solution)/shard_map/ppermute | solution.py:359
  102.3 3.0 %collective-permute-start.37 = (f32[8,48,512]{2,1,0:T(8,128)S(1)}, f32[8,48,512]{2,1,0:T(8,128)S(1)}, u32[]{:S(2)}, u32[]{:S(2)}) collective-permute-start(f32[8,48,512]{2,1,0:T(8,128)S(1)} %get-tuple-element.55), channel_id=1, source_target_pairs={{0,1},{1,0},{2,3},{3,2},{4,5},{5,4},{6,7},{7,6},{8,9},{9,8},{10,11... | collective-permute-start | bytes 2359304 | tf_op jit(solution)/shard_map/ppermute | solution.py:359
  102.8 3.6 %collective-permute-start.41 = (f32[8,48,512]{2,1,0:T(8,128)S(1)}, f32[8,48,512]{2,1,0:T(8,128)S(1)}, u32[]{:S(2)}, u32[]{:S(2)}) collective-permute-start(f32[8,48,512]{2,1,0:T(8,128)S(1)} %get-tuple-element.56), channel_id=1, source_target_pairs={{0,1},{1,0},{2,3},{3,2},{4,5},{5,4},{6,7},{7,6},{8,9},{9,8},{10,11... | collective-permute-start | bytes 2359304 | tf_op jit(solution)/shard_map/ppermute | solution.py:359
  104.2 8.4 %collective-permute-start.45 = (f32[128,512]{1,0:T(8,128)S(1)}, f32[128,512]{1,0:T(8,128)S(1)}, u32[]{:S(2)}, u32[]{:S(2)}) collective-permute-start(f32[128,512]{1,0:T(8,128)S(1)} %pad_maximum_fusion.2), channel_id=1, source_target_pairs={{0,4},{1,5},{2,6},{3,7},{4,0},{5,1},{6,2},{7,3},{8,12},{9,13},{10,... | collective-permute-start | bytes 786440 | tf_op jit(solution)/shard_map/ppermute | solution.py:359
  106.6 12.0 %collective-permute-start.38 = (f32[192,512]{1,0:T(8,128)S(1)}, f32[192,512]{1,0:T(8,128)S(1)}, u32[]{:S(2)}, u32[]{:S(2)}) collective-permute-start(f32[192,512]{1,0:T(8,128)S(1)} %pad_maximum_fusion), channel_id=1, source_target_pairs={{0,2},{1,3},{2,0},{3,1},{4,6},{5,7},{6,4},{7,5},{8,10},{9,11},{10,... | collective-permute-start | bytes 1179656 | tf_op jit(solution)/shard_map/ppermute | solution.py:359
  108.0 18.2 %collective-permute-start.42 = (f32[192,512]{1,0:T(8,128)S(1)}, f32[192,512]{1,0:T(8,128)S(1)}, u32[]{:S(2)}, u32[]{:S(2)}) collective-permute-start(f32[192,512]{1,0:T(8,128)S(1)} %pad_maximum_fusion.1), channel_id=1, source_target_pairs={{0,2},{1,3},{2,0},{3,1},{4,6},{5,7},{6,4},{7,5},{8,10},{9,11},{10,... | collective-permute-start | bytes 1179656 | tf_op jit(solution)/shard_map/ppermute | solution.py:359
  112.7 15.9 %collective-permute-start.46 = (f32[64,512]{1,0:T(8,128)S(1)}, f32[64,512]{1,0:T(8,128)S(1)}, u32[]{:S(2)}, u32[]{:S(2)}) collective-permute-start(f32[64,512]{1,0:T(8,128)S(1)} %pad_maximum_fusion.5), channel_id=1, source_target_pairs={{0,8},{1,9},{2,10},{3,11},{4,12},{5,13},{6,14},{7,15},{8,0},{9,1},... | collective-permute-start | bytes 393224 | tf_op jit(solution)/shard_map/ppermute | solution.py:359
  126.3 13.6 %copy-start.3 = (bf16[2048,512]{1,0:T(8,128)(2,1)S(1)}, bf16[2048,512]{1,0:T(8,128)(2,1)}, u32[]{:S(2)}) copy-start(bf16[2048,512]{1,0:T(8,128)(2,1)} %x_ref.3) | copy-start | bytes 6291460
  126.4 7.9 %collective-permute-start.39 = (f32[96,512]{1,0:T(8,128)S(1)}, f32[96,512]{1,0:T(8,128)S(1)}, u32[]{:S(2)}, u32[]{:S(2)}) collective-permute-start(f32[96,512]{1,0:T(8,128)S(1)} %pad_maximum_fusion.3), channel_id=1, source_target_pairs={{0,4},{1,5},{2,6},{3,7},{4,0},{5,1},{6,2},{7,3},{8,12},{9,13},{10,... | collective-permute-start | bytes 589832 | tf_op jit(solution)/shard_map/ppermute | solution.py:359
  126.5 10.3 %collective-permute-start.43 = (f32[96,512]{1,0:T(8,128)S(1)}, f32[96,512]{1,0:T(8,128)S(1)}, u32[]{:S(2)}, u32[]{:S(2)}) collective-permute-start(f32[96,512]{1,0:T(8,128)S(1)} %pad_maximum_fusion.4), channel_id=1, source_target_pairs={{0,4},{1,5},{2,6},{3,7},{4,0},{5,1},{6,2},{7,3},{8,12},{9,13},{10,... | collective-permute-start | bytes 589832 | tf_op jit(solution)/shard_map/ppermute | solution.py:359
  128.6 16.9 %collective-permute-start.47 = (f32[32,512]{1,0:T(8,128)S(1)}, f32[32,512]{1,0:T(8,128)S(1)}, u32[]{:S(2)}, u32[]{:S(2)}) collective-permute-start(f32[32,512]{1,0:T(8,128)S(1)} %get-tuple-element.74), channel_id=1, source_target_pairs={{0,2},{1,3},{2,0},{3,1},{4,6},{5,7},{6,4},{7,5},{8,10},{9,11},{10,... | collective-permute-start | bytes 196616 | tf_op jit(solution)/shard_map/ppermute | solution.py:359
  136.9 9.1 %collective-permute-start.40 = (f32[48,512]{1,0:T(8,128)S(1)}, f32[48,512]{1,0:T(8,128)S(1)}, u32[]{:S(2)}, u32[]{:S(2)}) collective-permute-start(f32[48,512]{1,0:T(8,128)S(1)} %get-tuple-element.91), channel_id=1, source_target_pairs={{0,8},{1,9},{2,10},{3,11},{4,12},{5,13},{6,14},{7,15},{8,0},{9,1},... | collective-permute-start | bytes 294920 | tf_op jit(solution)/shard_map/ppermute | solution.py:359
  137.8 9.5 %collective-permute-start.44 = (f32[48,512]{1,0:T(8,128)S(1)}, f32[48,512]{1,0:T(8,128)S(1)}, u32[]{:S(2)}, u32[]{:S(2)}) collective-permute-start(f32[48,512]{1,0:T(8,128)S(1)} %get-tuple-element.66), channel_id=1, source_target_pairs={{0,8},{1,9},{2,10},{3,11},{4,12},{5,13},{6,14},{7,15},{8,0},{9,1},... | collective-permute-start | bytes 294920 | tf_op jit(solution)/shard_map/ppermute | solution.py:359

commit v4 on v3

--- a/solution.py
+++ b/solution.py
@@ -249,8 +249,8 @@
 
 def mix_kernel(share, pieces, e_ref, y_ref, *refs):
     c_refs, r_refs = refs[:6], refs[6:11]
-    half_ref, keep_ref = refs[11:13]
-    send_refs, prod_ref = refs[13:-1], refs[-1]
+    half_ref, prod_ref = refs[11], refs[-1]
+    keep_refs, send_refs = refs[12:-1:2], refs[13:-1:2]
     cols, rows = e_ref.shape
     pair = 2 * share
     me = lax.axis_index("cols")
@@ -273,20 +273,24 @@
             half_ref[:, pl.ds(lo, pair)], y_ref[...], (((0,), (0,)), ((), ())),
             preferred_element_type=F32,
         )
-        keep_ref[p] = prod_ref[p % 2, pl.ds(pl.multiple_of(core * share, share), share), :]
-        at = (1 - core) * share
-        for ref, n in zip(send_refs, pieces):
-            ref[p] = prod_ref[p % 2, pl.ds(pl.multiple_of(at, 8), n), :]
-            at = at + n
+        for refs, side in ((keep_refs, core), (send_refs, 1 - core)):
+            at = side * share
+            for ref, (n, bits) in zip(refs, pieces):
+                ref[spot(p, bits)] = prod_ref[p % 2, pl.ds(pl.multiple_of(at, SUB), n), :]
+                at = at + n
+
+
+def spot(p, bits):
+    return sum(bool(2 * p & k) << i for i, k in enumerate(reversed(bits)))
 
 
 def mix(share, pieces, e, y, columns, weights):
     cols, rows = e.shape
     width = y.shape[1]
-    pairs = rows // (2 * share)
-    out = [VMEM((cols, rows), BF16), jax.ShapeDtypeStruct((pairs, share, width), F32)]
-    out += [jax.ShapeDtypeStruct((pairs, n, width), F32) for n in pieces]
-    got = pl.pallas_call(
+    out = [VMEM((cols, rows), BF16)]
+    for n, _ in pieces:
+        out += [jax.ShapeDtypeStruct((rows // (2 * share), n, width), F32)] * 2
+    half, *got = pl.pallas_call(
         functools.partial(mix_kernel, share, pieces),
         out_shape=tuple(out),
         in_specs=full(13),
@@ -295,7 +299,7 @@
         compiler_params=params(16),
         name="mix",
     )(e, y, *columns, *weights)
-    return got[0], got[1], got[2:]
+    return half, got[0::2], got[1::2]
 
 
 def back_kernel(total_cols, half_ref, x_ref, y_ref, e_ref, b_ref, r_ref, n_ref, sq_ref, bv2_ref,
@@ -359,24 +363,46 @@
     return lax.ppermute(v, "cols", [(i, i ^ k) for i in range(count)])
 
 
-def scatter_sum(keep, sends, pieces, count, meanwhile):
-    bits = [1 << i for i in range(1, count.bit_length() - 1)]
-    held, at = [], 0
-    for send, n in zip(sends, pieces):
-        got = swap(send, 1, count)
-        held.append({p: (keep[p, at:at + n], got[p]) for p in range(count // 2)})
-        at += n
-    other = meanwhile(got)
-    done = []
-    for i, (v, n) in enumerate(zip(held, pieces)):
-        order = bits if i < (len(pieces) + 1) // 2 else bits[1:] + bits[:1]
-        for k in order:
-            v = {p: a + b for p, (a, b) in v.items()}
-            away = [p for p in sorted(v) if p & (k // 2)]
-            got = swap(jnp.concatenate([v[p] for p in away], axis=0), k, count)
-            v = {p ^ (k // 2): (v[p ^ (k // 2)], got[j * n:(j + 1) * n]) for j, p in enumerate(away)}
-        done += v[0]
-    return done, other
+def fold_kernel(keep_ref, got_ref, after_ref, stay_ref, away_ref):
+    del after_ref
+    half = keep_ref.shape[0] // 2
+    for i in range(half):
+        stay_ref[i] = keep_ref[i] + got_ref[i]
+        away_ref[i] = keep_ref[half + i] + got_ref[half + i]
+
+
+def fold(keep, got, after):
+    blocks, n, width = keep.shape
+    return pl.pallas_call(
+        fold_kernel,
+        out_shape=(jax.ShapeDtypeStruct((blocks // 2, n, width), F32),) * 2,
+        in_specs=full(2) + [pl.BlockSpec(memory_space=pl.ANY)],
+        out_specs=tuple(full(2)),
+        compiler_params=params(8),
+        name="fold",
+    )(keep, got, after)
+
+
+def scatter_sum(keeps, sends, pieces, count, after, meanwhile):
+    keeps = list(keeps)
+    gots = [swap(send, 1, count) for send in sends]
+
+    def advance(i, step, after):
+        keeps[i], away = fold(keeps[i], gots[i], after)
+        gots[i] = swap(away, pieces[i][1][step], count)
+        return away
+
+    steps = count.bit_length() - 2
+    other = None
+    for t in range(steps + 1):
+        turn = [(0, t), (1, t), (2, t)] if t == 0 else [(2, t), (0, t)] + [(1, t - 1)] * (t > 1)
+        for i, step in turn:
+            if step < steps:
+                after = advance(i, step, after)
+        if t == 0:
+            other = meanwhile(after)
+            after = other[0]
+    return [x[0] for pair in zip(keeps, gots) for x in pair], other
 
 
 def gradient_kernel(pieces, scale, *refs):
@@ -390,7 +416,7 @@
         at = pl.multiple_of(lo + l * LANES, LANES)
         col_ref[pl.ds(l * LANES, LANES), :] = column(weight_ref[:, pl.ds(at, LANES)])
     at = 0
-    for i, n in enumerate(pieces):
+    for i, (n, _) in enumerate(pieces):
         col = col_ref[pl.ds(pl.multiple_of((me % 2) * share + at, 8), n), :]
         for l in range(width // LANES):
             ls = pl.ds(l * LANES, LANES)
@@ -432,6 +458,14 @@
 def lse_join(xs):
     m = tree(jnp.maximum, xs)
     return m + jnp.log2(tree(jnp.add, [jnp.exp2(x - m) for x in xs]))
+
+
+def routes(share, count):
+    bits = [1 << i for i in range(1, count.bit_length() - 1)]
+    units = share // SUB
+    first = units * 6 // 16
+    last = units - 2 * first
+    return [(first * SUB, bits), (first * SUB, bits), (last * SUB, bits[1:] + bits[:1])]
 
 
 def local(new_points, arch_points, new_mass, arch_mass):
@@ -459,12 +493,12 @@
     gb1, part = sweep("bwd", e, br, r, w2)
     fbar1 = reduce_add(part)
     w1 = fbar1 / a
-    pieces = [share * f // 16 for f in (6, 6, 4)]
-    half, keep, sends = mix(
+    pieces = routes(share, count)
+    half, keeps, sends = mix(
         share, pieces, e, arch_points, (bv3, bv2, mid, br, vbr, gb1), (u3, w3, u2, w2, w1)
     )
     terms, (pot, arch_grad, new_pot) = scatter_sum(
-        keep, sends, pieces, count,
+        keeps, sends, pieces, count, part,
         lambda after: back(
             total_cols, half, new_points, arch_points, e, b, r, n, sq, bv2, bv3, mid, gb1, vbr, w1,
             alpha, u3, after

time: 148 us -> 133 us (0.90)
  waiting for transfers between devices: 64 us -> 46.3 us
    ppermute x48, waiting for transfers between devices: 64 us -> 46.3 us  [swap(): return lax.ppermute(v, 'cols', [(i, i ^ k) for i in range(count)])]
  transfers between devices with their start and end apart: 48 -> 48, of which waited for: 33 -> 39; matrix products, arithmetic and copies ran while one was open for 0% -> 1% of each run, Pallas kernels for 4% -> 4%
where the time goes in v4:
time: 133 us
  starting transfers between devices  50.1 us (38%)
  waiting for transfers between devices  46.3 us (35%)
  Pallas kernels  30.2 us (23%)
  local copies, waits for them, and re-layouts  4.2 us (3%)
    ppermute x48, starting transfers between devices, swap(): return lax.ppermute(v, 'cols', [(i, i ^ k) for i in range(count)])  50.1 us
    ppermute x48, waiting for transfers between devices, swap(): return lax.ppermute(v, 'cols', [(i, i ^ k) for i in range(count)])  46.3 us
    pallas_call x4, Pallas kernels, sweep(): pl.pallas_call(functools.partial(sweep_kernel, kind), out_shape=(VMEM((co...  7.95 us
    pallas_call x1, Pallas kernels, mix(): pl.pallas_call(functools.partial(mix_kernel, share, pieces), out_shape=tu...  5.98 us
    pallas_call x1, Pallas kernels, plan(): pl.pallas_call(plan_kernel, out_shape=(VMEM((cols, rows), F32),) + (VMEM(...  5.58 us
    pallas_call x1, Pallas kernels, back(): pl.pallas_call(functools.partial(back_kernel, float(total_cols)), out_sha...  5.56 us
    unnamed x12, local copies, waits for them, and re-layouts  4.2 us
    pallas_call x1, Pallas kernels, scores(): pl.pallas_call(functools.partial(scores_kernel, total_cols, share), out_s...  3.79 us
  transfers between devices with their start and end apart: 48, of which 39 were waited for; matrix products, arithmetic and copies ran while one was open for 1% of the time, Pallas kernels for 4%

profile of v4, /device:TPU:0, one launch (start us, length us, event | category | flops | bytes accessed | tf_op | source)
XLA Modules:
  0.0 132.7 jit_solution(18314008902283843171)
XLA Ops:
  0.6 1.2 copy-done
  1.9 1.6 %copy-done.2 = bf16[2048,512]{1,0:T(8,128)(2,1)S(1)} copy-done((bf16[2048,512]{1,0:T(8,128)(2,1)S(1)}, bf16[2048,512]{1,0:T(8,128)(2,1)}, u32[]{:S(2)}) %copy-start.2) | copy-done | bytes 2097176
  4.1 3.8 %scores.1 = (f32[1024,2048]{1,0:T(8,128)S(1)}, f32[1024,128]{1,0:T(8,128)S(1)}, f32[1024,128]{1,0:T(8,128)S(1)}, f32[1,2048]{1,0:T(1,128)S(1)}, f32[128,512]{1,0:T(8,128)S(1)}) custom-call(bf16[2048,512]{1,0:T(8,128)(2,1)S(1)} %copy-done.2, bf16[1024,512]{1,0:T(8,128)(2,1)S(1)} %copy-done, f32[1,1024]{1,0:T(1,128)S(1)} %bitcast.17), custom_call_target="tpu_custom_call" | custom-call | tf_op jit(solution)/shard_map/scores/pallas_call | solution.py:105
  7.9 2.5 %collective-permute-start.2 = (f32[1,2048]{1,0:T(1,128)S(1)}, f32[1,2048]{1,0:T(1,128)S(1)}, u32[]{:S(2)}, u32[]{:S(2)}) collective-permute-start(f32[1,2048]{1,0:T(1,128)S(1)} %get-tuple-element.54), channel_id=1, source_target_pairs={{0,3},{1,2},{2,1},{3,0},{4,7},{5,6},{6,5},{7,4},{8,11},{9,10},{10,... | collective-permute-start | bytes 24584 | tf_op jit(solution)/shard_map/ppermute | solution.py:363
  11.8 2.3 %collective-permute-done.1 = f32[1,2048]{1,0:T(1,128)S(1)} collective-permute-done((f32[1,2048]{1,0:T(1,128)S(1)}, f32[1,2048]{1,0:T(1,128)S(1)}, u32[]{:S(2)}, u32[]{:S(2)}) %collective-permute-start.1) | collective-permute-done | bytes 8224 | tf_op jit(solution)/shard_map/ppermute | solution.py:363
  14.1 3.7 %collective-permute-start.5 = (f32[1,2048]{1,0:T(1,128)S(1)}, f32[1,2048]{1,0:T(1,128)S(1)}, u32[]{:S(2)}, u32[]{:S(2)}) collective-permute-start(f32[1,2048]{1,0:T(1,128)S(1)} %multiply_add_fusion.1), channel_id=1, source_target_pairs={{0,12},{1,13},{2,14},{3,15},{4,8},{5,9},{6,10},{7,11},{8,4},{9,5},... | collective-permute-start | bytes 24584 | tf_op jit(solution)/shard_map/ppermute | solution.py:363
  17.8 0.8 collective-permute-start.3
  18.6 0.7 broadcast_multiply_fusion
  19.8 2.6 %collective-permute-done.4 = f32[1,2048]{1,0:T(1,128)S(1)} collective-permute-done((f32[1,2048]{1,0:T(1,128)S(1)}, f32[1,2048]{1,0:T(1,128)S(1)}, u32[]{:S(2)}, u32[]{:S(2)}) %collective-permute-start.4) | collective-permute-done | bytes 8224 | tf_op jit(solution)/shard_map/ppermute | solution.py:363
  22.4 5.6 %plan.1 = (f32[1024,2048]{1,0:T(8,128)S(1)}, f32[1024,128]{1,0:T(8,128)S(1)}, f32[1024,128]{1,0:T(8,128)S(1)}, f32[1024,128]{1,0:T(8,128)S(1)}, f32[1024,128]{1,0:T(8,128)S(1)}, /*index=5*/f32[1,2048]{1,0:T(1,128)S(1)}) custom-call(f32[1024,2048]{1,0:T(8,128)S(1)} %get-tuple-element.51.z_ref, ...), custom_call_target="tpu_custom_call", output_to_operand_aliasing={{0}: (0, {})} | custom-call | tf_op jit(solution)/shard_map/plan/pallas_call | solution.py:200
  28.1 0.7 collective-permute-start.7
  28.8 1.1 collective-permute-start.6
  29.9 1.2 collective-permute-done.8
  31.8 1.5 %collective-permute-start.11 = (f32[1,2048]{1,0:T(1,128)S(1)}, f32[1,2048]{1,0:T(1,128)S(1)}, u32[]{:S(2)}, u32[]{:S(2)}) collective-permute-start(f32[1,2048]{1,0:T(1,128)S(1)} %add_add_fusion.5), channel_id=1, source_target_pairs={{0,12},{1,13},{2,14},{3,15},{4,8},{5,9},{6,10},{7,11},{8,4},{9,5},... | collective-permute-start | bytes 24584 | tf_op jit(solution)/shard_map/ppermute | solution.py:363
  34.0 2.3 %collective-permute-start.9 = (f32[1,2048]{1,0:T(1,128)S(1)}, f32[1,2048]{1,0:T(1,128)S(1)}, u32[]{:S(2)}, u32[]{:S(2)}) collective-permute-start(f32[1,2048]{1,0:T(1,128)S(1)} %add_add_fusion.5), channel_id=1, source_target_pairs={{0,4},{1,5},{2,6},{3,7},{4,0},{5,1},{6,2},{7,3},{8,12},{9,13},{10,... | collective-permute-start | bytes 24584 | tf_op jit(solution)/shard_map/ppermute | solution.py:363
  36.3 1.1 collective-permute-done.11
  38.0 2.0 %sweep_fwd.2 = (f32[1024,128]{1,0:T(8,128)S(1)}, f32[1,2048]{1,0:T(1,128)S(1)}) custom-call(f32[1024,2048]{1,0:T(8,128)S(1)} %get-tuple-element.55.e_ref, f32[1024,128]{1,0:T(8,128)S(1)} %get-tuple-element.52.b_ref, f32[1,2048]{1,0:T(1,128)S(1)} %add_divide_fusion.1.refs_0_.refs_8_), custom_call_target="tpu_custom_call" | custom-call | tf_op jit(solution)/shard_map/sweep_fwd/pallas_call | solution.py:239
  40.1 0.7 collective-permute-start.13
  40.8 1.1 collective-permute-start.12
  42.0 1.2 collective-permute-done.14
  43.9 2.6 %collective-permute-start.17 = (f32[1,2048]{1,0:T(1,128)S(1)}, f32[1,2048]{1,0:T(1,128)S(1)}, u32[]{:S(2)}, u32[]{:S(2)}) collective-permute-start(f32[1,2048]{1,0:T(1,128)S(1)} %add_add_fusion.4), channel_id=1, source_target_pairs={{0,12},{1,13},{2,14},{3,15},{4,8},{5,9},{6,10},{7,11},{8,4},{9,5},... | collective-permute-start | bytes 24584 | tf_op jit(solution)/shard_map/ppermute | solution.py:363
  46.4 0.9 collective-permute-start.16
  47.3 1.0 collective-permute-start.15
  48.3 1.1 collective-permute-done.17
  49.4 1.6 %collective-permute-done.16 = f32[1,2048]{1,0:T(1,128)S(1)} collective-permute-done((f32[1,2048]{1,0:T(1,128)S(1)}, f32[1,2048]{1,0:T(1,128)S(1)}, u32[]{:S(2)}, u32[]{:S(2)}) %collective-permute-start.16) | collective-permute-done | bytes 8224 | tf_op jit(solution)/shard_map/ppermute | solution.py:363
  51.1 2.0 %sweep_fwd.3 = (f32[1024,128]{1,0:T(8,128)S(1)}, f32[1,2048]{1,0:T(1,128)S(1)}) custom-call(f32[1024,2048]{1,0:T(8,128)S(1)} %get-tuple-element.55.e_ref, f32[1024,128]{1,0:T(8,128)S(1)} %get-tuple-element.52.b_ref, f32[1,2048]{1,0:T(1,128)S(1)} %add_divide_fusion.refs_0_.refs_6_.u3_ref), custom_call_target="tpu_custom_call" | custom-call | tf_op jit(solution)/shard_map/sweep_fwd/pallas_call | solution.py:239
  53.2 0.7 collective-permute-start.19
  53.9 1.1 collective-permute-start.18
  55.0 1.2 collective-permute-done.20
  56.9 1.4 %collective-permute-start.23 = (f32[1,2048]{1,0:T(1,128)S(1)}, f32[1,2048]{1,0:T(1,128)S(1)}, u32[]{:S(2)}, u32[]{:S(2)}) collective-permute-start(f32[1,2048]{1,0:T(1,128)S(1)} %add_add_fusion.3), channel_id=1, source_target_pairs={{0,12},{1,13},{2,14},{3,15},{4,8},{5,9},{6,10},{7,11},{8,4},{9,5},... | collective-permute-start | bytes 24584 | tf_op jit(solution)/shard_map/ppermute | solution.py:363
  58.4 1.0 collective-permute-start.22
  59.4 2.0 %collective-permute-start.21 = (f32[1,2048]{1,0:T(1,128)S(1)}, f32[1,2048]{1,0:T(1,128)S(1)}, u32[]{:S(2)}, u32[]{:S(2)}) collective-permute-start(f32[1,2048]{1,0:T(1,128)S(1)} %add_add_fusion.3), channel_id=1, source_target_pairs={{0,4},{1,5},{2,6},{3,7},{4,0},{5,1},{6,2},{7,3},{8,12},{9,13},{10,... | collective-permute-start | bytes 24584 | tf_op jit(solution)/shard_map/ppermute | solution.py:363
  61.4 1.1 collective-permute-done.23
  63.0 2.0 %sweep_mid.1 = (f32[1024,128]{1,0:T(8,128)S(1)}, f32[1,2048]{1,0:T(1,128)S(1)}) custom-call(f32[1024,2048]{1,0:T(8,128)S(1)} %get-tuple-element.55.e_ref, f32[1024,128]{1,0:T(8,128)S(1)} %get-tuple-element.52.b_ref, f32[1024,128]{1,0:T(8,128)S(1)} %get-tuple-element.59.refs_0_.refs_1_.bv2_ref, f32[1,2048]{1,0:T(1,128)S(1)} %get-tuple-element.102.refs_1_.refs_7_), custom_call_target="tpu_custom_call" | custom-call | tf_op jit(solution)/shard_map/sweep_mid/pallas_call | solution.py:239
  65.1 0.7 collective-permute-start.25
  65.8 1.1 collective-permute-start.24
  66.9 1.2 collective-permute-done.26
  68.8 2.6 %collective-permute-start.29 = (f32[1,2048]{1,0:T(1,128)S(1)}, f32[1,2048]{1,0:T(1,128)S(1)}, u32[]{:S(2)}, u32[]{:S(2)}) collective-permute-start(f32[1,2048]{1,0:T(1,128)S(1)} %add_add_fusion.2), channel_id=1, source_target_pairs={{0,12},{1,13},{2,14},{3,15},{4,8},{5,9},{6,10},{7,11},{8,4},{9,5},... | collective-permute-start | bytes 24584 | tf_op jit(solution)/shard_map/ppermute | solution.py:363
  71.4 1.0 collective-permute-start.28
  72.4 0.9 collective-permute-start.27
  73.3 1.1 collective-permute-done.29
  74.4 1.6 %collective-permute-done.28 = f32[1,2048]{1,0:T(1,128)S(1)} collective-permute-done((f32[1,2048]{1,0:T(1,128)S(1)}, f32[1,2048]{1,0:T(1,128)S(1)}, u32[]{:S(2)}, u32[]{:S(2)}) %collective-permute-start.28) | collective-permute-done | bytes 8224 | tf_op jit(solution)/shard_map/ppermute | solution.py:363
  76.1 2.0 %sweep_bwd.1 = (f32[1024,128]{1,0:T(8,128)S(1)}, f32[1,2048]{1,0:T(1,128)S(1)}) custom-call(f32[1024,2048]{1,0:T(8,128)S(1)} %get-tuple-element.55.e_ref, f32[1024,128]{1,0:T(8,128)S(1)} %get-tuple-element.62.b_ref.refs_3_, f32[1024,128]{1,0:T(8,128)S(1)} %get-tuple-element.64.refs_0_.r_ref, f32[1,2048]{1,0:T(1,128)S(1)} %get-tuple-element.100.refs_1_.refs_9_), custom_call_target="tpu_custom_call" | custom-call | tf_op jit(solution)/shard_map/sweep_bwd/pallas_call | solution.py:239
  78.1 0.7 collective-permute-start.31
  78.8 1.1 collective-permute-start.30
  80.0 1.2 collective-permute-done.32
  81.9 1.4 %collective-permute-start.35 = (f32[1,2048]{1,0:T(1,128)S(1)}, f32[1,2048]{1,0:T(1,128)S(1)}, u32[]{:S(2)}, u32[]{:S(2)}) collective-permute-start(f32[1,2048]{1,0:T(1,128)S(1)} %add_add_fusion.1), channel_id=1, source_target_pairs={{0,12},{1,13},{2,14},{3,15},{4,8},{5,9},{6,10},{7,11},{8,4},{9,5},... | collective-permute-start | bytes 24584 | tf_op jit(solution)/shard_map/ppermute | solution.py:363
  83.3 1.0 collective-permute-start.34
  84.3 2.0 %collective-permute-start.33 = (f32[1,2048]{1,0:T(1,128)S(1)}, f32[1,2048]{1,0:T(1,128)S(1)}, u32[]{:S(2)}, u32[]{:S(2)}) collective-permute-start(f32[1,2048]{1,0:T(1,128)S(1)} %add_add_fusion.1), channel_id=1, source_target_pairs={{0,4},{1,5},{2,6},{3,7},{4,0},{5,1},{6,2},{7,3},{8,12},{9,13},{10,... | collective-permute-start | bytes 24584 | tf_op jit(solution)/shard_map/ppermute | solution.py:363
  86.3 1.1 collective-permute-done.35
  88.0 6.0 %mix.1 = (bf16[1024,2048]{1,0:T(8,128)(2,1)S(1)}, f32[8,48,512]{2,1,0:T(8,128)S(1)}, f32[8,48,512]{2,1,0:T(8,128)S(1)}, f32[8,48,512]{2,1,0:T(8,128)S(1)}, f32[8...) custom-call(f32[1024,2048]{1,0:T(8,128)S(1)} %get-tuple-element.55.e_ref, ...), custom_call_target="tpu_custom_call" | custom-call | tf_op jit(solution)/shard_map/mix/pallas_call | solution.py:293
  94.7 1.7 %collective-permute-done.38.got_ref = f32[8,48,512]{2,1,0:T(8,128)S(1)} collective-permute-done((f32[8,48,512]{2,1,0:T(8,128)S(1)}, f32[8,48,512]{2,1,0:T(8,128)S(1)}, u32[]{:S(2)}, u32[]{:S(2)}) %collective-permute-start.38) | collective-permute-done | bytes 786464 | tf_op jit(solution)/shard_map/ppermute | solution.py:363
  98.3 2.1 %collective-permute-start.40 = (f32[4,32,512]{2,1,0:T(8,128)S(1)}, f32[4,32,512]{2,1,0:T(8,128)S(1)}, u32[]{:S(2)}, u32[]{:S(2)}) collective-permute-start(f32[4,32,512]{2,1,0:T(8,128)S(1)} %get-tuple-element.78.after_ref), channel_id=1, source_target_pairs={{0,4},{1,5},{2,6},{3,7},{4,0},{5,1},{6,2},{7,3},{8,12},{9,13},{10,... | collective-permute-start | bytes 786440 | tf_op jit(solution)/shard_map/ppermute | solution.py:363
  101.0 5.6 %back.1 = (f32[1,1024]{1,0:T(1,128)}, f32[1024,512]{1,0:T(8,128)}, f32[1,2048]{1,0:T(1,128)}) custom-call(bf16[1024,2048]{1,0:T(8,128)(2,1)S(1)} %get-tuple-element.68.half_ref, bf16[2048,512]{1,0:T(8,128)(2,1)S(1)} %copy-done.3, bf16[1024,512]{1,0:T(8,128)(2,1)S(1)} %copy-done.1, f32[1024,2048]{1,0:T(8,128)S(1)} %get-tuple-element.55.e_ref, ...), custom_call_target="tpu_custom_call" | custom-call | flops 2147483648 | bytes 16777216 | tf_op jit(solution)/shard_map/back/pallas_call | solution.py:344
  107.7 0.8 collective-permute-done.39.got_ref
  108.6 2.1 %collective-permute-start.41 = (f32[2,48,512]{2,1,0:T(8,128)S(1)}, f32[2,48,512]{2,1,0:T(8,128)S(1)}, u32[]{:S(2)}, u32[]{:S(2)}) collective-permute-start(f32[2,48,512]{2,1,0:T(8,128)S(1)} %get-tuple-element.86.after_ref), channel_id=1, source_target_pairs={{0,4},{1,5},{2,6},{3,7},{4,0},{5,1},{6,2},{7,3},{8,12},{9,13},{10,... | collective-permute-start | bytes 589832 | tf_op jit(solution)/shard_map/ppermute | solution.py:363
  110.7 1.0 collective-permute-start.42
  111.7 5.2 %collective-permute-done.42.got_ref = f32[2,32,512]{2,1,0:T(8,128)S(1)} collective-permute-done((f32[2,32,512]{2,1,0:T(8,128)S(1)}, f32[2,32,512]{2,1,0:T(8,128)S(1)}, u32[]{:S(2)}, u32[]{:S(2)}) %collective-permute-start.42) | collective-permute-done | bytes 131104 | tf_op jit(solution)/shard_map/ppermute | solution.py:363
  117.2 1.7 %collective-permute-start.45 = (f32[2,48,512]{2,1,0:T(8,128)S(1)}, f32[2,48,512]{2,1,0:T(8,128)S(1)}, u32[]{:S(2)}, u32[]{:S(2)}) collective-permute-start(f32[2,48,512]{2,1,0:T(8,128)S(1)} %get-tuple-element.93.after_ref), channel_id=1, source_target_pairs={{0,4},{1,5},{2,6},{3,7},{4,0},{5,1},{6,2},{7,3},{8,12},{9,13},{10,... | collective-permute-start | bytes 589832 | tf_op jit(solution)/shard_map/ppermute | solution.py:363
  118.9 1.0 collective-permute-start.43
  119.9 5.7 %collective-permute-done.45.got_ref = f32[2,48,512]{2,1,0:T(8,128)S(1)} collective-permute-done((f32[2,48,512]{2,1,0:T(8,128)S(1)}, f32[2,48,512]{2,1,0:T(8,128)S(1)}, u32[]{:S(2)}, u32[]{:S(2)}) %collective-permute-start.45) | collective-permute-done | bytes 196640 | tf_op jit(solution)/shard_map/ppermute | solution.py:363
  126.4 3.7 %collective-permute-done.47 = f32[1,32,512]{2,1,0:T(8,128)S(1)} collective-permute-done((f32[1,32,512]{2,1,0:T(8,128)S(1)}, f32[1,32,512]{2,1,0:T(8,128)S(1)}, u32[]{:S(2)}, u32[]{:S(2)}) %collective-permute-start.47) | collective-permute-done | bytes 65568 | tf_op jit(solution)/shard_map/ppermute | solution.py:363
  130.1 1.8 %collective-permute-done.46 = f32[1,48,512]{2,1,0:T(8,128)S(1)} collective-permute-done((f32[1,48,512]{2,1,0:T(8,128)S(1)}, f32[1,48,512]{2,1,0:T(8,128)S(1)}, u32[]{:S(2)}, u32[]{:S(2)}) %collective-permute-start.46) | collective-permute-done | bytes 98336 | tf_op jit(solution)/shard_map/ppermute | solution.py:363
  131.9 0.9 gradient.1
  (76 shorter events, 14.6 us)
Async XLA Ops:
  0.6 1.2 copy-start
  1.9 1.6 %copy-start.2 = (bf16[2048,512]{1,0:T(8,128)(2,1)S(1)}, bf16[2048,512]{1,0:T(8,128)(2,1)}, u32[]{:S(2)}) copy-start(bf16[2048,512]{1,0:T(8,128)(2,1)} %x_ref.3) | copy-start | bytes 6291460
  3.5 0.7 copy-start.4
  7.9 3.8 %collective-permute-start.2 = (f32[1,2048]{1,0:T(1,128)S(1)}, f32[1,2048]{1,0:T(1,128)S(1)}, u32[]{:S(2)}, u32[]{:S(2)}) collective-permute-start(f32[1,2048]{1,0:T(1,128)S(1)} %get-tuple-element.54), channel_id=1, source_target_pairs={{0,3},{1,2},{2,1},{3,0},{4,7},{5,6},{6,5},{7,4},{8,11},{9,10},{10,... | collective-permute-start | bytes 24584 | tf_op jit(solution)/shard_map/ppermute | solution.py:363
  10.4 3.7 %collective-permute-start.1 = (f32[1,2048]{1,0:T(1,128)S(1)}, f32[1,2048]{1,0:T(1,128)S(1)}, u32[]{:S(2)}, u32[]{:S(2)}) collective-permute-start(f32[1,2048]{1,0:T(1,128)S(1)} %get-tuple-element.54), channel_id=1, source_target_pairs={{0,2},{1,3},{2,0},{3,1},{4,6},{5,7},{6,4},{7,5},{8,10},{9,11},{10,... | collective-permute-start | bytes 24584 | tf_op jit(solution)/shard_map/ppermute | solution.py:363
  11.0 3.0 %collective-permute-start = (f32[1,2048]{1,0:T(1,128)S(1)}, f32[1,2048]{1,0:T(1,128)S(1)}, u32[]{:S(2)}, u32[]{:S(2)}) collective-permute-start(f32[1,2048]{1,0:T(1,128)S(1)} %get-tuple-element.54), channel_id=1, source_target_pairs={{0,1},{1,0},{2,3},{3,2},{4,5},{5,4},{6,7},{7,6},{8,9},{9,8},{10,11... | collective-permute-start | bytes 24584 | tf_op jit(solution)/shard_map/ppermute | solution.py:363
  14.1 5.6 %collective-permute-start.5 = (f32[1,2048]{1,0:T(1,128)S(1)}, f32[1,2048]{1,0:T(1,128)S(1)}, u32[]{:S(2)}, u32[]{:S(2)}) collective-permute-start(f32[1,2048]{1,0:T(1,128)S(1)} %multiply_add_fusion.1), channel_id=1, source_target_pairs={{0,12},{1,13},{2,14},{3,15},{4,8},{5,9},{6,10},{7,11},{8,4},{9,5},... | collective-permute-start | bytes 24584 | tf_op jit(solution)/shard_map/ppermute | solution.py:363
  17.8 4.5 %collective-permute-start.4 = (f32[1,2048]{1,0:T(1,128)S(1)}, f32[1,2048]{1,0:T(1,128)S(1)}, u32[]{:S(2)}, u32[]{:S(2)}) collective-permute-start(f32[1,2048]{1,0:T(1,128)S(1)} %multiply_add_fusion.1), channel_id=1, source_target_pairs={{0,8},{1,9},{2,10},{3,11},{4,12},{5,13},{6,14},{7,15},{8,0},{9,1},... | collective-permute-start | bytes 24584 | tf_op jit(solution)/shard_map/ppermute | solution.py:363
  17.8 4.5 %collective-permute-start.3 = (f32[1,2048]{1,0:T(1,128)S(1)}, f32[1,2048]{1,0:T(1,128)S(1)}, u32[]{:S(2)}, u32[]{:S(2)}) collective-permute-start(f32[1,2048]{1,0:T(1,128)S(1)} %multiply_add_fusion.1), channel_id=1, source_target_pairs={{0,4},{1,5},{2,6},{3,7},{4,0},{5,1},{6,2},{7,3},{8,12},{9,13},{10,... | collective-permute-start | bytes 24584 | tf_op jit(solution)/shard_map/ppermute | solution.py:363
  28.0 3.1 %collective-permute-start.8 = (f32[1,2048]{1,0:T(1,128)S(1)}, f32[1,2048]{1,0:T(1,128)S(1)}, u32[]{:S(2)}, u32[]{:S(2)}) collective-permute-start(f32[1,2048]{1,0:T(1,128)S(1)} %get-tuple-element.56), channel_id=1, source_target_pairs={{0,3},{1,2},{2,1},{3,0},{4,7},{5,6},{6,5},{7,4},{8,11},{9,10},{10,... | collective-permute-start | bytes 24584 | tf_op jit(solution)/shard_map/ppermute | solution.py:363
  28.1 3.7 %collective-permute-start.7 = (f32[1,2048]{1,0:T(1,128)S(1)}, f32[1,2048]{1,0:T(1,128)S(1)}, u32[]{:S(2)}, u32[]{:S(2)}) collective-permute-start(f32[1,2048]{1,0:T(1,128)S(1)} %get-tuple-element.56), channel_id=1, source_target_pairs={{0,2},{1,3},{2,0},{3,1},{4,6},{5,7},{6,4},{7,5},{8,10},{9,11},{10,... | collective-permute-start | bytes 24584 | tf_op jit(solution)/shard_map/ppermute | solution.py:363
  28.8 3.0 %collective-permute-start.6 = (f32[1,2048]{1,0:T(1,128)S(1)}, f32[1,2048]{1,0:T(1,128)S(1)}, u32[]{:S(2)}, u32[]{:S(2)}) collective-permute-start(f32[1,2048]{1,0:T(1,128)S(1)} %get-tuple-element.56), channel_id=1, source_target_pairs={{0,1},{1,0},{2,3},{3,2},{4,5},{5,4},{6,7},{7,6},{8,9},{9,8},{10,11... | collective-permute-start | bytes 24584 | tf_op jit(solution)/shard_map/ppermute | solution.py:363
  31.8 5.6 %collective-permute-start.11 = (f32[1,2048]{1,0:T(1,128)S(1)}, f32[1,2048]{1,0:T(1,128)S(1)}, u32[]{:S(2)}, u32[]{:S(2)}) collective-permute-start(f32[1,2048]{1,0:T(1,128)S(1)} %add_add_fusion.5), channel_id=1, source_target_pairs={{0,12},{1,13},{2,14},{3,15},{4,8},{5,9},{6,10},{7,11},{8,4},{9,5},... | collective-permute-start | bytes 24584 | tf_op jit(solution)/shard_map/ppermute | solution.py:363
  33.4 4.6 %collective-permute-start.10 = (f32[1,2048]{1,0:T(1,128)S(1)}, f32[1,2048]{1,0:T(1,128)S(1)}, u32[]{:S(2)}, u32[]{:S(2)}) collective-permute-start(f32[1,2048]{1,0:T(1,128)S(1)} %add_add_fusion.5), channel_id=1, source_target_pairs={{0,8},{1,9},{2,10},{3,11},{4,12},{5,13},{6,14},{7,15},{8,0},{9,1},... | collective-permute-start | bytes 24584 | tf_op jit(solution)/shard_map/ppermute | solution.py:363
  34.0 4.0 %collective-permute-start.9 = (f32[1,2048]{1,0:T(1,128)S(1)}, f32[1,2048]{1,0:T(1,128)S(1)}, u32[]{:S(2)}, u32[]{:S(2)}) collective-permute-start(f32[1,2048]{1,0:T(1,128)S(1)} %add_add_fusion.5), channel_id=1, source_target_pairs={{0,4},{1,5},{2,6},{3,7},{4,0},{5,1},{6,2},{7,3},{8,12},{9,13},{10,... | collective-permute-start | bytes 24584 | tf_op jit(solution)/shard_map/ppermute | solution.py:363
  40.0 3.1 %collective-permute-start.14 = (f32[1,2048]{1,0:T(1,128)S(1)}, f32[1,2048]{1,0:T(1,128)S(1)}, u32[]{:S(2)}, u32[]{:S(2)}) collective-permute-start(f32[1,2048]{1,0:T(1,128)S(1)} %get-tuple-element.57), channel_id=1, source_target_pairs={{0,3},{1,2},{2,1},{3,0},{4,7},{5,6},{6,5},{7,4},{8,11},{9,10},{10,... | collective-permute-start | bytes 24584 | tf_op jit(solution)/shard_map/ppermute | solution.py:363
  40.1 3.7 %collective-permute-start.13 = (f32[1,2048]{1,0:T(1,128)S(1)}, f32[1,2048]{1,0:T(1,128)S(1)}, u32[]{:S(2)}, u32[]{:S(2)}) collective-permute-start(f32[1,2048]{1,0:T(1,128)S(1)} %get-tuple-element.57), channel_id=1, source_target_pairs={{0,2},{1,3},{2,0},{3,1},{4,6},{5,7},{6,4},{7,5},{8,10},{9,11},{10,... | collective-permute-start | bytes 24584 | tf_op jit(solution)/shard_map/ppermute | solution.py:363
  40.8 3.0 %collective-permute-start.12 = (f32[1,2048]{1,0:T(1,128)S(1)}, f32[1,2048]{1,0:T(1,128)S(1)}, u32[]{:S(2)}, u32[]{:S(2)}) collective-permute-start(f32[1,2048]{1,0:T(1,128)S(1)} %get-tuple-element.57), channel_id=1, source_target_pairs={{0,1},{1,0},{2,3},{3,2},{4,5},{5,4},{6,7},{7,6},{8,9},{9,8},{10,11... | collective-permute-start | bytes 24584 | tf_op jit(solution)/shard_map/ppermute | solution.py:363
  43.9 5.5 %collective-permute-start.17 = (f32[1,2048]{1,0:T(1,128)S(1)}, f32[1,2048]{1,0:T(1,128)S(1)}, u32[]{:S(2)}, u32[]{:S(2)}) collective-permute-start(f32[1,2048]{1,0:T(1,128)S(1)} %add_add_fusion.4), channel_id=1, source_target_pairs={{0,12},{1,13},{2,14},{3,15},{4,8},{5,9},{6,10},{7,11},{8,4},{9,5},... | collective-permute-start | bytes 24584 | tf_op jit(solution)/shard_map/ppermute | solution.py:363
  46.4 4.6 %collective-permute-start.16 = (f32[1,2048]{1,0:T(1,128)S(1)}, f32[1,2048]{1,0:T(1,128)S(1)}, u32[]{:S(2)}, u32[]{:S(2)}) collective-permute-start(f32[1,2048]{1,0:T(1,128)S(1)} %add_add_fusion.4), channel_id=1, source_target_pairs={{0,8},{1,9},{2,10},{3,11},{4,12},{5,13},{6,14},{7,15},{8,0},{9,1},... | collective-permute-start | bytes 24584 | tf_op jit(solution)/shard_map/ppermute | solution.py:363
  47.3 3.7 %collective-permute-start.15 = (f32[1,2048]{1,0:T(1,128)S(1)}, f32[1,2048]{1,0:T(1,128)S(1)}, u32[]{:S(2)}, u32[]{:S(2)}) collective-permute-start(f32[1,2048]{1,0:T(1,128)S(1)} %add_add_fusion.4), channel_id=1, source_target_pairs={{0,4},{1,5},{2,6},{3,7},{4,0},{5,1},{6,2},{7,3},{8,12},{9,13},{10,... | collective-permute-start | bytes 24584 | tf_op jit(solution)/shard_map/ppermute | solution.py:363
  53.1 3.1 %collective-permute-start.20 = (f32[1,2048]{1,0:T(1,128)S(1)}, f32[1,2048]{1,0:T(1,128)S(1)}, u32[]{:S(2)}, u32[]{:S(2)}) collective-permute-start(f32[1,2048]{1,0:T(1,128)S(1)} %get-tuple-element.60), channel_id=1, source_target_pairs={{0,3},{1,2},{2,1},{3,0},{4,7},{5,6},{6,5},{7,4},{8,11},{9,10},{10,... | collective-permute-start | bytes 24584 | tf_op jit(solution)/shard_map/ppermute | solution.py:363
  53.2 3.7 %collective-permute-start.19 = (f32[1,2048]{1,0:T(1,128)S(1)}, f32[1,2048]{1,0:T(1,128)S(1)}, u32[]{:S(2)}, u32[]{:S(2)}) collective-permute-start(f32[1,2048]{1,0:T(1,128)S(1)} %get-tuple-element.60), channel_id=1, source_target_pairs={{0,2},{1,3},{2,0},{3,1},{4,6},{5,7},{6,4},{7,5},{8,10},{9,11},{10,... | collective-permute-start | bytes 24584 | tf_op jit(solution)/shard_map/ppermute | solution.py:363
  53.9 3.0 %collective-permute-start.18 = (f32[1,2048]{1,0:T(1,128)S(1)}, f32[1,2048]{1,0:T(1,128)S(1)}, u32[]{:S(2)}, u32[]{:S(2)}) collective-permute-start(f32[1,2048]{1,0:T(1,128)S(1)} %get-tuple-element.60), channel_id=1, source_target_pairs={{0,1},{1,0},{2,3},{3,2},{4,5},{5,4},{6,7},{7,6},{8,9},{9,8},{10,11... | collective-permute-start | bytes 24584 | tf_op jit(solution)/shard_map/ppermute | solution.py:363
  56.9 5.5 %collective-permute-start.23 = (f32[1,2048]{1,0:T(1,128)S(1)}, f32[1,2048]{1,0:T(1,128)S(1)}, u32[]{:S(2)}, u32[]{:S(2)}) collective-permute-start(f32[1,2048]{1,0:T(1,128)S(1)} %add_add_fusion.3), channel_id=1, source_target_pairs={{0,12},{1,13},{2,14},{3,15},{4,8},{5,9},{6,10},{7,11},{8,4},{9,5},... | collective-permute-start | bytes 24584 | tf_op jit(solution)/shard_map/ppermute | solution.py:363
  58.4 4.5 %collective-permute-start.22 = (f32[1,2048]{1,0:T(1,128)S(1)}, f32[1,2048]{1,0:T(1,128)S(1)}, u32[]{:S(2)}, u32[]{:S(2)}) collective-permute-start(f32[1,2048]{1,0:T(1,128)S(1)} %add_add_fusion.3), channel_id=1, source_target_pairs={{0,8},{1,9},{2,10},{3,11},{4,12},{5,13},{6,14},{7,15},{8,0},{9,1},... | collective-permute-start | bytes 24584 | tf_op jit(solution)/shard_map/ppermute | solution.py:363
  59.4 3.7 %collective-permute-start.21 = (f32[1,2048]{1,0:T(1,128)S(1)}, f32[1,2048]{1,0:T(1,128)S(1)}, u32[]{:S(2)}, u32[]{:S(2)}) collective-permute-start(f32[1,2048]{1,0:T(1,128)S(1)} %add_add_fusion.3), channel_id=1, source_target_pairs={{0,4},{1,5},{2,6},{3,7},{4,0},{5,1},{6,2},{7,3},{8,12},{9,13},{10,... | collective-permute-start | bytes 24584 | tf_op jit(solution)/shard_map/ppermute | solution.py:363
  65.0 3.1 %collective-permute-start.26 = (f32[1,2048]{1,0:T(1,128)S(1)}, f32[1,2048]{1,0:T(1,128)S(1)}, u32[]{:S(2)}, u32[]{:S(2)}) collective-permute-start(f32[1,2048]{1,0:T(1,128)S(1)} %get-tuple-element.65), channel_id=1, source_target_pairs={{0,3},{1,2},{2,1},{3,0},{4,7},{5,6},{6,5},{7,4},{8,11},{9,10},{10,... | collective-permute-start | bytes 24584 | tf_op jit(solution)/shard_map/ppermute | solution.py:363
  65.1 3.7 %collective-permute-start.25 = (f32[1,2048]{1,0:T(1,128)S(1)}, f32[1,2048]{1,0:T(1,128)S(1)}, u32[]{:S(2)}, u32[]{:S(2)}) collective-permute-start(f32[1,2048]{1,0:T(1,128)S(1)} %get-tuple-element.65), channel_id=1, source_target_pairs={{0,2},{1,3},{2,0},{3,1},{4,6},{5,7},{6,4},{7,5},{8,10},{9,11},{10,... | collective-permute-start | bytes 24584 | tf_op jit(solution)/shard_map/ppermute | solution.py:363
  65.8 3.0 %collective-permute-start.24 = (f32[1,2048]{1,0:T(1,128)S(1)}, f32[1,2048]{1,0:T(1,128)S(1)}, u32[]{:S(2)}, u32[]{:S(2)}) collective-permute-start(f32[1,2048]{1,0:T(1,128)S(1)} %get-tuple-element.65), channel_id=1, source_target_pairs={{0,1},{1,0},{2,3},{3,2},{4,5},{5,4},{6,7},{7,6},{8,9},{9,8},{10,11... | collective-permute-start | bytes 24584 | tf_op jit(solution)/shard_map/ppermute | solution.py:363
  68.8 5.5 %collective-permute-start.29 = (f32[1,2048]{1,0:T(1,128)S(1)}, f32[1,2048]{1,0:T(1,128)S(1)}, u32[]{:S(2)}, u32[]{:S(2)}) collective-permute-start(f32[1,2048]{1,0:T(1,128)S(1)} %add_add_fusion.2), channel_id=1, source_target_pairs={{0,12},{1,13},{2,14},{3,15},{4,8},{5,9},{6,10},{7,11},{8,4},{9,5},... | collective-permute-start | bytes 24584 | tf_op jit(solution)/shard_map/ppermute | solution.py:363
  71.4 4.5 %collective-permute-start.28 = (f32[1,2048]{1,0:T(1,128)S(1)}, f32[1,2048]{1,0:T(1,128)S(1)}, u32[]{:S(2)}, u32[]{:S(2)}) collective-permute-start(f32[1,2048]{1,0:T(1,128)S(1)} %add_add_fusion.2), channel_id=1, source_target_pairs={{0,8},{1,9},{2,10},{3,11},{4,12},{5,13},{6,14},{7,15},{8,0},{9,1},... | collective-permute-start | bytes 24584 | tf_op jit(solution)/shard_map/ppermute | solution.py:363
  72.4 3.7 %collective-permute-start.27 = (f32[1,2048]{1,0:T(1,128)S(1)}, f32[1,2048]{1,0:T(1,128)S(1)}, u32[]{:S(2)}, u32[]{:S(2)}) collective-permute-start(f32[1,2048]{1,0:T(1,128)S(1)} %add_add_fusion.2), channel_id=1, source_target_pairs={{0,4},{1,5},{2,6},{3,7},{4,0},{5,1},{6,2},{7,3},{8,12},{9,13},{10,... | collective-permute-start | bytes 24584 | tf_op jit(solution)/shard_map/ppermute | solution.py:363
  76.1 11.9 %copy-start.1 = (bf16[1024,512]{1,0:T(8,128)(2,1)S(1)}, bf16[1024,512]{1,0:T(8,128)(2,1)}, u32[]{:S(2)}) copy-start(bf16[1024,512]{1,0:T(8,128)(2,1)} %y_ref.5) | copy-start | bytes 3145732
  78.1 3.1 %collective-permute-start.32 = (f32[1,2048]{1,0:T(1,128)S(1)}, f32[1,2048]{1,0:T(1,128)S(1)}, u32[]{:S(2)}, u32[]{:S(2)}) collective-permute-start(f32[1,2048]{1,0:T(1,128)S(1)} %get-tuple-element.67.after_ref), channel_id=1, source_target_pairs={{0,3},{1,2},{2,1},{3,0},{4,7},{5,6},{6,5},{7,4},{8,11},{9,10},{10,... | collective-permute-start | bytes 24584 | tf_op jit(solution)/shard_map/ppermute | solution.py:363
  78.1 3.7 %collective-permute-start.31 = (f32[1,2048]{1,0:T(1,128)S(1)}, f32[1,2048]{1,0:T(1,128)S(1)}, u32[]{:S(2)}, u32[]{:S(2)}) collective-permute-start(f32[1,2048]{1,0:T(1,128)S(1)} %get-tuple-element.67.after_ref), channel_id=1, source_target_pairs={{0,2},{1,3},{2,0},{3,1},{4,6},{5,7},{6,4},{7,5},{8,10},{9,11},{10,... | collective-permute-start | bytes 24584 | tf_op jit(solution)/shard_map/ppermute | solution.py:363
  78.8 3.0 %collective-permute-start.30 = (f32[1,2048]{1,0:T(1,128)S(1)}, f32[1,2048]{1,0:T(1,128)S(1)}, u32[]{:S(2)}, u32[]{:S(2)}) collective-permute-start(f32[1,2048]{1,0:T(1,128)S(1)} %get-tuple-element.67.after_ref), channel_id=1, source_target_pairs={{0,1},{1,0},{2,3},{3,2},{4,5},{5,4},{6,7},{7,6},{8,9},{9,8},{10,11... | collective-permute-start | bytes 24584 | tf_op jit(solution)/shard_map/ppermute | solution.py:363
  81.9 5.5 %collective-permute-start.35 = (f32[1,2048]{1,0:T(1,128)S(1)}, f32[1,2048]{1,0:T(1,128)S(1)}, u32[]{:S(2)}, u32[]{:S(2)}) collective-permute-start(f32[1,2048]{1,0:T(1,128)S(1)} %add_add_fusion.1), channel_id=1, source_target_pairs={{0,12},{1,13},{2,14},{3,15},{4,8},{5,9},{6,10},{7,11},{8,4},{9,5},... | collective-permute-start | bytes 24584 | tf_op jit(solution)/shard_map/ppermute | solution.py:363
  83.3 4.5 %collective-permute-start.34 = (f32[1,2048]{1,0:T(1,128)S(1)}, f32[1,2048]{1,0:T(1,128)S(1)}, u32[]{:S(2)}, u32[]{:S(2)}) collective-permute-start(f32[1,2048]{1,0:T(1,128)S(1)} %add_add_fusion.1), channel_id=1, source_target_pairs={{0,8},{1,9},{2,10},{3,11},{4,12},{5,13},{6,14},{7,15},{8,0},{9,1},... | collective-permute-start | bytes 24584 | tf_op jit(solution)/shard_map/ppermute | solution.py:363
  84.3 3.7 %collective-permute-start.33 = (f32[1,2048]{1,0:T(1,128)S(1)}, f32[1,2048]{1,0:T(1,128)S(1)}, u32[]{:S(2)}, u32[]{:S(2)}) collective-permute-start(f32[1,2048]{1,0:T(1,128)S(1)} %add_add_fusion.1), channel_id=1, source_target_pairs={{0,4},{1,5},{2,6},{3,7},{4,0},{5,1},{6,2},{7,3},{8,12},{9,13},{10,... | collective-permute-start | bytes 24584 | tf_op jit(solution)/shard_map/ppermute | solution.py:363
  94.0 7.0 %copy-start.3 = (bf16[2048,512]{1,0:T(8,128)(2,1)S(1)}, bf16[2048,512]{1,0:T(8,128)(2,1)}, u32[]{:S(2)}) copy-start(bf16[2048,512]{1,0:T(8,128)(2,1)} %x_ref.3) | copy-start | bytes 6291460
  94.0 2.4 %collective-permute-start.38 = (f32[8,48,512]{2,1,0:T(8,128)S(1)}, f32[8,48,512]{2,1,0:T(8,128)S(1)}, u32[]{:S(2)}, u32[]{:S(2)}) collective-permute-start(f32[8,48,512]{2,1,0:T(8,128)S(1)} %get-tuple-element.75), channel_id=1, source_target_pairs={{0,1},{1,0},{2,3},{3,2},{4,5},{5,4},{6,7},{7,6},{8,9},{9,8},{10,11... | collective-permute-start | bytes 2359304 | tf_op jit(solution)/shard_map/ppermute | solution.py:363
  94.1 3.4 %collective-permute-start.37 = (f32[8,48,512]{2,1,0:T(8,128)S(1)}, f32[8,48,512]{2,1,0:T(8,128)S(1)}, u32[]{:S(2)}, u32[]{:S(2)}) collective-permute-start(f32[8,48,512]{2,1,0:T(8,128)S(1)} %get-tuple-element.73), channel_id=1, source_target_pairs={{0,1},{1,0},{2,3},{3,2},{4,5},{5,4},{6,7},{7,6},{8,9},{9,8},{10,11... | collective-permute-start | bytes 2359304 | tf_op jit(solution)/shard_map/ppermute | solution.py:363
  94.6 3.6 %collective-permute-start.36 = (f32[8,32,512]{2,1,0:T(8,128)S(1)}, f32[8,32,512]{2,1,0:T(8,128)S(1)}, u32[]{:S(2)}, u32[]{:S(2)}) collective-permute-start(f32[8,32,512]{2,1,0:T(8,128)S(1)} %get-tuple-element.71), channel_id=1, source_target_pairs={{0,1},{1,0},{2,3},{3,2},{4,5},{5,4},{6,7},{7,6},{8,9},{9,8},{10,11... | collective-permute-start | bytes 1572872 | tf_op jit(solution)/shard_map/ppermute | solution.py:363
  96.5 12.0 %collective-permute-start.39 = (f32[4,48,512]{2,1,0:T(8,128)S(1)}, f32[4,48,512]{2,1,0:T(8,128)S(1)}, u32[]{:S(2)}, u32[]{:S(2)}) collective-permute-start(f32[4,48,512]{2,1,0:T(8,128)S(1)} %get-tuple-element.76.after_ref), channel_id=1, source_target_pairs={{0,2},{1,3},{2,0},{3,1},{4,6},{5,7},{6,4},{7,5},{8,10},{9,11},{10,... | collective-permute-start | bytes 1179656 | tf_op jit(solution)/shard_map/ppermute | solution.py:363
  98.3 8.7 %collective-permute-start.40 = (f32[4,32,512]{2,1,0:T(8,128)S(1)}, f32[4,32,512]{2,1,0:T(8,128)S(1)}, u32[]{:S(2)}, u32[]{:S(2)}) collective-permute-start(f32[4,32,512]{2,1,0:T(8,128)S(1)} %get-tuple-element.78.after_ref), channel_id=1, source_target_pairs={{0,4},{1,5},{2,6},{3,7},{4,0},{5,1},{6,2},{7,3},{8,12},{9,13},{10,... | collective-permute-start | bytes 786440 | tf_op jit(solution)/shard_map/ppermute | solution.py:363
  100.4 16.7 %collective-permute-start.44 = (f32[4,48,512]{2,1,0:T(8,128)S(1)}, f32[4,48,512]{2,1,0:T(8,128)S(1)}, u32[]{:S(2)}, u32[]{:S(2)}) collective-permute-start(f32[4,48,512]{2,1,0:T(8,128)S(1)} %get-tuple-element.77.after_ref), channel_id=1, source_target_pairs={{0,2},{1,3},{2,0},{3,1},{4,6},{5,7},{6,4},{7,5},{8,10},{9,11},{10,... | collective-permute-start | bytes 1179656 | tf_op jit(solution)/shard_map/ppermute | solution.py:363
  107.0 0.7 copy-start.5
  108.6 8.6 %collective-permute-start.41 = (f32[2,48,512]{2,1,0:T(8,128)S(1)}, f32[2,48,512]{2,1,0:T(8,128)S(1)}, u32[]{:S(2)}, u32[]{:S(2)}) collective-permute-start(f32[2,48,512]{2,1,0:T(8,128)S(1)} %get-tuple-element.86.after_ref), channel_id=1, source_target_pairs={{0,4},{1,5},{2,6},{3,7},{4,0},{5,1},{6,2},{7,3},{8,12},{9,13},{10,... | collective-permute-start | bytes 589832 | tf_op jit(solution)/shard_map/ppermute | solution.py:363
  110.7 6.2 %collective-permute-start.42 = (f32[2,32,512]{2,1,0:T(8,128)S(1)}, f32[2,32,512]{2,1,0:T(8,128)S(1)}, u32[]{:S(2)}, u32[]{:S(2)}) collective-permute-start(f32[2,32,512]{2,1,0:T(8,128)S(1)} %get-tuple-element.84.after_ref), channel_id=1, source_target_pairs={{0,8},{1,9},{2,10},{3,11},{4,12},{5,13},{6,14},{7,15},{8,0},{9,1},... | collective-permute-start | bytes 393224 | tf_op jit(solution)/shard_map/ppermute | solution.py:363
  117.2 8.5 %collective-permute-start.45 = (f32[2,48,512]{2,1,0:T(8,128)S(1)}, f32[2,48,512]{2,1,0:T(8,128)S(1)}, u32[]{:S(2)}, u32[]{:S(2)}) collective-permute-start(f32[2,48,512]{2,1,0:T(8,128)S(1)} %get-tuple-element.93.after_ref), channel_id=1, source_target_pairs={{0,4},{1,5},{2,6},{3,7},{4,0},{5,1},{6,2},{7,3},{8,12},{9,13},{10,... | collective-permute-start | bytes 589832 | tf_op jit(solution)/shard_map/ppermute | solution.py:363
  118.9 11.2 %collective-permute-start.43 = (f32[1,48,512]{2,1,0:T(8,128)S(1)}, f32[1,48,512]{2,1,0:T(8,128)S(1)}, u32[]{:S(2)}, u32[]{:S(2)}) collective-permute-start(f32[1,48,512]{2,1,0:T(8,128)S(1)} %get-tuple-element.90.after_ref), channel_id=1, source_target_pairs={{0,8},{1,9},{2,10},{3,11},{4,12},{5,13},{6,14},{7,15},{8,0},{9,1},... | collective-permute-start | bytes 294920 | tf_op jit(solution)/shard_map/ppermute | solution.py:363
  125.7 6.2 %collective-permute-start.46 = (f32[1,48,512]{2,1,0:T(8,128)S(1)}, f32[1,48,512]{2,1,0:T(8,128)S(1)}, u32[]{:S(2)}, u32[]{:S(2)}) collective-permute-start(f32[1,48,512]{2,1,0:T(8,128)S(1)} %get-tuple-element.95), channel_id=1, source_target_pairs={{0,8},{1,9},{2,10},{3,11},{4,12},{5,13},{6,14},{7,15},{8,0},{9,1},... | collective-permute-start | bytes 294920 | tf_op jit(solution)/shard_map/ppermute | solution.py:363
  125.8 4.3 %collective-permute-start.47 = (f32[1,32,512]{2,1,0:T(8,128)S(1)}, f32[1,32,512]{2,1,0:T(8,128)S(1)}, u32[]{:S(2)}, u32[]{:S(2)}) collective-permute-start(f32[1,32,512]{2,1,0:T(8,128)S(1)} %get-tuple-element.88.after_ref), channel_id=1, source_target_pairs={{0,2},{1,3},{2,0},{3,1},{4,6},{5,7},{6,4},{7,5},{8,10},{9,11},{10,... | collective-permute-start | bytes 196616 | tf_op jit(solution)/shard_map/ppermute | solution.py:363

commit v5 on v4

--- a/solution.py
+++ b/solution.py
@@ -55,12 +55,19 @@
     return pl.ds(pl.multiple_of(i * n, n), n)
 
 
-def scores_kernel(total_cols, share, x_ref, y_ref, mass_ref, z_ref, b_ref, sq_ref, lse_ref, mine_ref,
-                  cb_ref):
+def scores_kernel(total_cols, share, x_hbm, y_hbm, mass_hbm, z_ref, b_ref, sq_ref, lse_ref, mine_ref,
+                  cb_ref, x_ref, y_ref, mass_ref, sems):
     cols, width = y_ref.shape
     rows = x_ref.shape[0]
-    first = pl.multiple_of(lax.axis_index("cols") * share, share)
-    mine_ref[...] = x_ref[pl.ds(first, share), :].astype(F32)
+    step = 2 * LANES
+    copies = [
+        pltpu.make_async_copy(hbm, ref, sems.at[i])
+        for i, (hbm, ref) in enumerate(((x_hbm, x_ref), (y_hbm, y_ref), (mass_hbm, mass_ref)))
+    ]
+    for copy in copies:
+        copy.start()
+    for copy in copies:
+        copy.wait()
     for c in range(cols // LANES):
         s = pl.ds(c * LANES, LANES)
         b = column(mass_ref[:, s] * (1.0 / total_cols))
@@ -70,7 +77,6 @@
         sq = jnp.broadcast_to(sq, (LANES, LANES))
         sq_ref[s, :] = sq
         cb_ref[s, :] = jnp.log2(b) - sq
-    step = 2 * LANES
     many = 4
 
     def reduce_block(r):
@@ -98,6 +104,8 @@
         if r > 0:
             reduce_block(r - 1)
     reduce_block(rows // step - 1)
+    first = pl.multiple_of(lax.axis_index("cols") * share, share)
+    mine_ref[...] = x_ref[pl.ds(first, share), :].astype(F32)
 
 
 def scores(new_points, arch_points, arch_mass, total_cols, share):
@@ -111,15 +119,21 @@
             jax.ShapeDtypeStruct((1, rows), F32),
             VMEM((share, new_points.shape[1]), F32),
         ),
-        in_specs=full(3),
+        in_specs=[pl.BlockSpec(memory_space=pltpu.HBM)] * 3,
         out_specs=tuple(full(5)),
-        scratch_shapes=[pltpu.VMEM((cols, LANES), F32)],
-        compiler_params=params(),
+        scratch_shapes=[
+            pltpu.VMEM((cols, LANES), F32),
+            pltpu.VMEM(new_points.shape, BF16),
+            pltpu.VMEM(arch_points.shape, BF16),
+            pltpu.VMEM((1, cols), F32),
+            pltpu.SemaphoreType.DMA((3,)),
+        ],
+        compiler_params=params(50),
         name="scores",
     )(new_points, arch_points, arch_mass.reshape(1, cols))
 
 
-CHUNK = 128
+CHUNK = 512
 
 
 def groups(i):
@@ -249,28 +263,37 @@
 
 def mix_kernel(share, pieces, e_ref, y_ref, *refs):
     c_refs, r_refs = refs[:6], refs[6:11]
-    half_ref, prod_ref = refs[11], refs[-1]
-    keep_refs, send_refs = refs[12:-1:2], refs[13:-1:2]
+    half_ref, (prod_ref, left_ref, right_ref) = refs[11], refs[-3:]
+    keep_refs, send_refs = refs[12:-3:2], refs[13:-3:2]
     cols, rows = e_ref.shape
     pair = 2 * share
     me = lax.axis_index("cols")
     core = me % 2
+    entry = lax.broadcasted_iota(jnp.int32, (SUB, LANES), 1)
+    for g in range(cols // (2 * SUB)):
+        outs = []
+        for h in range(2):
+            s = pl.ds(g * 2 * SUB + h * SUB, SUB)
+            outs.append(split_parts([ref[s, :] for ref in c_refs], entry, LEFT))
+        left_ref[pl.ds(g * 2 * SUB, 2 * SUB), :] = jnp.concatenate(outs, axis=0).astype(BF16)
+    for l in range(rows // LANES):
+        ls = pl.ds(l * LANES, LANES)
+        r = [wide(ref[:, ls]) for ref in r_refs] + [jnp.ones((SUB, LANES), F32)]
+        for g in range(LANES // (2 * SUB)):
+            outs = []
+            for h in range(2):
+                at = lax.broadcasted_iota(jnp.int32, (SUB, LANES), 0) + (2 * g + h) * SUB
+                outs.append(split_parts(r, at, RIGHT) if (2 * g + h) * SUB < 36 else jnp.zeros((SUB, LANES), F32))
+            right_ref[pl.ds(g * 2 * SUB, 2 * SUB), ls] = jnp.concatenate(outs, axis=0).astype(BF16)
     for p in range(rows // pair):
         lo = pl.multiple_of(((me // 2) ^ p) * pair, pair)
-        spots = [pl.ds(pl.multiple_of(lo + l * LANES, LANES), LANES) for l in range(pair // LANES)]
-        r = [[wide(ref[:, ls]) for ref in r_refs] for ls in spots]
-        for g in range(cols // (2 * SUB)):
-            outs = [[] for _ in spots]
-            for h in range(2):
-                s = pl.ds(g * 2 * SUB + h * SUB, SUB)
-                c = [ref[s, :] for ref in c_refs]
-                for o, rl, ls in zip(outs, r, spots):
-                    terms = [a * b for a, b in zip(c, rl)] + [c[5]]
-                    o.append(e_ref[s, ls] * tree(jnp.add, terms))
-            for o, ls in zip(outs, spots):
-                half_ref[pl.ds(g * 2 * SUB, 2 * SUB), ls] = jnp.concatenate(o, axis=0).astype(BF16)
+        block = pl.ds(lo, pair)
+        for g in range(cols // MIX):
+            s = pl.ds(g * MIX, MIX)
+            scale = jnp.dot(left_ref[s, :], right_ref[:, block], preferred_element_type=F32)
+            half_ref[s, block] = (e_ref[s, block] * scale).astype(BF16)
         prod_ref[p % 2] = lax.dot_general(
-            half_ref[:, pl.ds(lo, pair)], y_ref[...], (((0,), (0,)), ((), ())),
+            half_ref[:, block], y_ref[...], (((0,), (0,)), ((), ())),
             preferred_element_type=F32,
         )
         for refs, side in ((keep_refs, core), (send_refs, 1 - core)):
@@ -278,6 +301,22 @@
             for ref, (n, bits) in zip(refs, pieces):
                 ref[spot(p, bits)] = prod_ref[p % 2, pl.ds(pl.multiple_of(at, SUB), n), :]
                 at = at + n
+
+
+LEFT = (0, 0, 1, 0, 1, 2)
+RIGHT = (0, 1, 0, 2, 1, 0)
+MIX = 256
+
+
+def split_parts(values, entry, which):
+    x = jnp.zeros_like(values[0])
+    for t, v in enumerate(values):
+        x = jnp.where((entry >= 6 * t) & (entry < 6 * t + 6), v, x)
+    first = x.astype(BF16).astype(F32)
+    rest = x - first
+    second = rest.astype(BF16).astype(F32)
+    part = sum(jnp.where(entry % 6 == q, w, 0) for q, w in enumerate(which))
+    return jnp.where(part == 0, first, jnp.where(part == 1, second, rest - second))
 
 
 def spot(p, bits):
@@ -295,7 +334,11 @@
         out_shape=tuple(out),
         in_specs=full(13),
         out_specs=tuple(full(len(out))),
-        scratch_shapes=[pltpu.VMEM((2, 2 * share, width), F32)],
+        scratch_shapes=[
+            pltpu.VMEM((2, 2 * share, width), F32),
+            pltpu.VMEM((cols, LANES), BF16),
+            pltpu.VMEM((LANES, rows), BF16),
+        ],
         compiler_params=params(16),
         name="mix",
     )(e, y, *columns, *weights)

time: 133 us -> 128 us (0.962)
  local copies, waits for them, and re-layouts: 4.2 us -> 0.7 us
  Pallas kernels: 30.2 us -> 27.4 us
    unnamed x12 -> x6, local copies, waits for them, and re-layouts: 4.2 us -> 0.7 us
    pallas_call x4, Pallas kernels: 7.95 us -> 5.8 us  [sweep(): pl.pallas_call(functools.partial(sweep_kernel, kind), out_shape=(VMEM((co...]
    pallas_call x1, Pallas kernels: 3.79 us -> 5.83 us  [scores(): pl.pallas_call(functools.partial(scores_kernel, total_cols, share), out_s...]
where the time goes in v5:
time: 128 us
  starting transfers between devices  50.2 us (39%)
  waiting for transfers between devices  46.7 us (36%)
  Pallas kernels  27.4 us (21%)
  other arithmetic  1.8 us (1%)
    ppermute x48, starting transfers between devices, swap(): return lax.ppermute(v, 'cols', [(i, i ^ k) for i in range(count)])  50.2 us
    ppermute x48, waiting for transfers between devices, swap(): return lax.ppermute(v, 'cols', [(i, i ^ k) for i in range(count)])  46.7 us
    pallas_call x1, Pallas kernels, scores(): pl.pallas_call(functools.partial(scores_kernel, total_cols, share), out_s...  5.83 us
    pallas_call x4, Pallas kernels, sweep(): pl.pallas_call(functools.partial(sweep_kernel, kind), out_shape=(VMEM((co...  5.8 us
    pallas_call x1, Pallas kernels, back(): pl.pallas_call(functools.partial(back_kernel, float(total_cols)), out_sha...  5.19 us
    pallas_call x1, Pallas kernels, mix(): pl.pallas_call(functools.partial(mix_kernel, share, pieces), out_shape=tu...  5.01 us
    pallas_call x1, Pallas kernels, plan(): pl.pallas_call(plan_kernel, out_shape=(VMEM((cols, rows), F32),) + (VMEM(...  4.33 us
  transfers between devices with their start and end apart: 48, of which 39 were waited for; matrix products, arithmetic and copies ran while one was open for 1% of the time, Pallas kernels for 4%

profile of v5, /device:TPU:0, one launch (start us, length us, event | category | flops | bytes accessed | tf_op | source)
XLA Modules:
  0.0 127.8 jit_solution(16941065603104731174)
XLA Ops:
  0.6 5.8 %scores.1 = (f32[1024,2048]{1,0:T(8,128)S(1)}, f32[1024,128]{1,0:T(8,128)S(1)}, f32[1024,128]{1,0:T(8,128)S(1)}, f32[1,2048]{1,0:T(1,128)}, f32[128,512]{1,0:T(8,128)S(1)}) custom-call(bf16[2048,512]{1,0:T(8,128)(2,1)} %x_ref.1, bf16[1024,512]{1,0:T(8,128)(2,1)} %y_ref.3, f32[1,1024]{1,0:T(1,128)} %bitcast.25), custom_call_target="tpu_custom_call" | custom-call | tf_op jit(solution)/shard_map/scores/pallas_call | solution.py:113
  6.5 2.5 %collective-permute-start.2 = (f32[1,2048]{1,0:T(1,128)}, f32[1,2048]{1,0:T(1,128)S(1)}, u32[]{:S(2)}, u32[]{:S(2)}) collective-permute-start(f32[1,2048]{1,0:T(1,128)} %get-tuple-element.54), channel_id=1, source_target_pairs={{0,3},{1,2},{2,1},{3,0},{4,7},{5,6},{6,5},{7,4},{8,11},{9,10},{10,... | collective-permute-start | bytes 24584 | tf_op jit(solution)/shard_map/ppermute | solution.py:406
  9.6 0.9 collective-permute-done.2
  10.5 2.3 %collective-permute-done.1 = f32[1,2048]{1,0:T(1,128)S(1)} collective-permute-done((f32[1,2048]{1,0:T(1,128)}, f32[1,2048]{1,0:T(1,128)S(1)}, u32[]{:S(2)}, u32[]{:S(2)}) %collective-permute-start.1) | collective-permute-done | bytes 8224 | tf_op jit(solution)/shard_map/ppermute | solution.py:406
  12.8 0.8 multiply_add_fusion.1
  13.6 3.7 %collective-permute-start.5 = (f32[1,2048]{1,0:T(1,128)S(1)}, f32[1,2048]{1,0:T(1,128)S(1)}, u32[]{:S(2)}, u32[]{:S(2)}) collective-permute-start(f32[1,2048]{1,0:T(1,128)S(1)} %multiply_add_fusion.1), channel_id=1, source_target_pairs={{0,12},{1,13},{2,14},{3,15},{4,8},{5,9},{6,10},{7,11},{8,4},{9,5},... | collective-permute-start | bytes 24584 | tf_op jit(solution)/shard_map/ppermute | solution.py:406
  17.3 0.8 collective-permute-start.3
  18.0 0.7 broadcast_multiply_fusion
  19.2 2.6 %collective-permute-done.4 = f32[1,2048]{1,0:T(1,128)S(1)} collective-permute-done((f32[1,2048]{1,0:T(1,128)S(1)}, f32[1,2048]{1,0:T(1,128)S(1)}, u32[]{:S(2)}, u32[]{:S(2)}) %collective-permute-start.4) | collective-permute-done | bytes 8224 | tf_op jit(solution)/shard_map/ppermute | solution.py:406
  21.9 4.3 %plan.1 = (f32[1024,2048]{1,0:T(8,128)S(1)}, f32[1024,128]{1,0:T(8,128)S(1)}, f32[1024,128]{1,0:T(8,128)S(1)}, f32[1024,128]{1,0:T(8,128)S(1)}, f32[1024,128]{1,0:T(8,128)S(1)}, /*index=5*/f32[1,2048]{1,0:T(1,128)S(1)}) custom-call(f32[1024,2048]{1,0:T(8,128)S(1)} %get-tuple-element.51.z_ref, ...), custom_call_target="tpu_custom_call", output_to_operand_aliasing={{0}: (0, {})} | custom-call | tf_op jit(solution)/shard_map/plan/pallas_call | solution.py:214
  27.0 1.1 collective-permute-start.6
  28.1 1.2 collective-permute-done.8
  30.0 1.5 %collective-permute-start.11 = (f32[1,2048]{1,0:T(1,128)S(1)}, f32[1,2048]{1,0:T(1,128)S(1)}, u32[]{:S(2)}, u32[]{:S(2)}) collective-permute-start(f32[1,2048]{1,0:T(1,128)S(1)} %add_add_fusion.5), channel_id=1, source_target_pairs={{0,12},{1,13},{2,14},{3,15},{4,8},{5,9},{6,10},{7,11},{8,4},{9,5},... | collective-permute-start | bytes 24584 | tf_op jit(solution)/shard_map/ppermute | solution.py:406
  32.2 2.3 %collective-permute-start.9 = (f32[1,2048]{1,0:T(1,128)S(1)}, f32[1,2048]{1,0:T(1,128)S(1)}, u32[]{:S(2)}, u32[]{:S(2)}) collective-permute-start(f32[1,2048]{1,0:T(1,128)S(1)} %add_add_fusion.5), channel_id=1, source_target_pairs={{0,4},{1,5},{2,6},{3,7},{4,0},{5,1},{6,2},{7,3},{8,12},{9,13},{10,... | collective-permute-start | bytes 24584 | tf_op jit(solution)/shard_map/ppermute | solution.py:406
  34.5 1.1 collective-permute-done.11
  36.2 1.4 %sweep_fwd.2 = (f32[1024,128]{1,0:T(8,128)S(1)}, f32[1,2048]{1,0:T(1,128)S(1)}) custom-call(f32[1024,2048]{1,0:T(8,128)S(1)} %get-tuple-element.55.e_ref, f32[1024,128]{1,0:T(8,128)S(1)} %get-tuple-element.52.b_ref, f32[1,2048]{1,0:T(1,128)S(1)} %add_divide_fusion.1.refs_0_.refs_8_), custom_call_target="tpu_custom_call" | custom-call | tf_op jit(solution)/shard_map/sweep_fwd/pallas_call | solution.py:253
  38.4 1.1 collective-permute-start.12
  39.6 1.2 collective-permute-done.14
  41.5 2.6 %collective-permute-start.17 = (f32[1,2048]{1,0:T(1,128)S(1)}, f32[1,2048]{1,0:T(1,128)S(1)}, u32[]{:S(2)}, u32[]{:S(2)}) collective-permute-start(f32[1,2048]{1,0:T(1,128)S(1)} %add_add_fusion.4), channel_id=1, source_target_pairs={{0,12},{1,13},{2,14},{3,15},{4,8},{5,9},{6,10},{7,11},{8,4},{9,5},... | collective-permute-start | bytes 24584 | tf_op jit(solution)/shard_map/ppermute | solution.py:406
  44.0 0.9 collective-permute-start.16
  44.9 1.0 collective-permute-start.15
  45.9 1.1 collective-permute-done.17
  47.0 1.6 %collective-permute-done.16 = f32[1,2048]{1,0:T(1,128)S(1)} collective-permute-done((f32[1,2048]{1,0:T(1,128)S(1)}, f32[1,2048]{1,0:T(1,128)S(1)}, u32[]{:S(2)}, u32[]{:S(2)}) %collective-permute-start.16) | collective-permute-done | bytes 8224 | tf_op jit(solution)/shard_map/ppermute | solution.py:406
  48.7 1.4 %sweep_fwd.3 = (f32[1024,128]{1,0:T(8,128)S(1)}, f32[1,2048]{1,0:T(1,128)S(1)}) custom-call(f32[1024,2048]{1,0:T(8,128)S(1)} %get-tuple-element.55.e_ref, f32[1024,128]{1,0:T(8,128)S(1)} %get-tuple-element.52.b_ref, f32[1,2048]{1,0:T(1,128)S(1)} %add_divide_fusion.refs_0_.refs_6_.u3_ref), custom_call_target="tpu_custom_call" | custom-call | tf_op jit(solution)/shard_map/sweep_fwd/pallas_call | solution.py:253
  50.2 0.7 collective-permute-start.19
  50.9 1.1 collective-permute-start.18
  52.0 1.2 collective-permute-done.20
  53.9 1.4 %collective-permute-start.23 = (f32[1,2048]{1,0:T(1,128)S(1)}, f32[1,2048]{1,0:T(1,128)S(1)}, u32[]{:S(2)}, u32[]{:S(2)}) collective-permute-start(f32[1,2048]{1,0:T(1,128)S(1)} %add_add_fusion.3), channel_id=1, source_target_pairs={{0,12},{1,13},{2,14},{3,15},{4,8},{5,9},{6,10},{7,11},{8,4},{9,5},... | collective-permute-start | bytes 24584 | tf_op jit(solution)/shard_map/ppermute | solution.py:406
  55.4 1.0 collective-permute-start.22
  56.4 2.0 %collective-permute-start.21 = (f32[1,2048]{1,0:T(1,128)S(1)}, f32[1,2048]{1,0:T(1,128)S(1)}, u32[]{:S(2)}, u32[]{:S(2)}) collective-permute-start(f32[1,2048]{1,0:T(1,128)S(1)} %add_add_fusion.3), channel_id=1, source_target_pairs={{0,4},{1,5},{2,6},{3,7},{4,0},{5,1},{6,2},{7,3},{8,12},{9,13},{10,... | collective-permute-start | bytes 24584 | tf_op jit(solution)/shard_map/ppermute | solution.py:406
  58.4 1.1 collective-permute-done.23
  60.0 1.4 %sweep_mid.1 = (f32[1024,128]{1,0:T(8,128)S(1)}, f32[1,2048]{1,0:T(1,128)S(1)}) custom-call(f32[1024,2048]{1,0:T(8,128)S(1)} %get-tuple-element.55.e_ref, f32[1024,128]{1,0:T(8,128)S(1)} %get-tuple-element.52.b_ref, f32[1024,128]{1,0:T(8,128)S(1)} %get-tuple-element.59.refs_0_.refs_1_.bv2_ref, f32[1,2048]{1,0:T(1,128)S(1)} %get-tuple-element.102.refs_1_.refs_7_), custom_call_target="tpu_custom_call" | custom-call | tf_op jit(solution)/shard_map/sweep_mid/pallas_call | solution.py:253
  61.5 0.7 collective-permute-start.25
  62.2 1.1 collective-permute-start.24
  63.4 1.2 collective-permute-done.26
  65.3 2.6 %collective-permute-start.29 = (f32[1,2048]{1,0:T(1,128)S(1)}, f32[1,2048]{1,0:T(1,128)S(1)}, u32[]{:S(2)}, u32[]{:S(2)}) collective-permute-start(f32[1,2048]{1,0:T(1,128)S(1)} %add_add_fusion.2), channel_id=1, source_target_pairs={{0,12},{1,13},{2,14},{3,15},{4,8},{5,9},{6,10},{7,11},{8,4},{9,5},... | collective-permute-start | bytes 24584 | tf_op jit(solution)/shard_map/ppermute | solution.py:406
  67.8 1.0 collective-permute-start.28
  68.8 0.9 collective-permute-start.27
  69.7 1.1 collective-permute-done.29
  70.8 1.6 %collective-permute-done.28 = f32[1,2048]{1,0:T(1,128)S(1)} collective-permute-done((f32[1,2048]{1,0:T(1,128)S(1)}, f32[1,2048]{1,0:T(1,128)S(1)}, u32[]{:S(2)}, u32[]{:S(2)}) %collective-permute-start.28) | collective-permute-done | bytes 8224 | tf_op jit(solution)/shard_map/ppermute | solution.py:406
  72.5 1.6 %sweep_bwd.1 = (f32[1024,128]{1,0:T(8,128)S(1)}, f32[1,2048]{1,0:T(1,128)S(1)}) custom-call(f32[1024,2048]{1,0:T(8,128)S(1)} %get-tuple-element.55.e_ref, f32[1024,128]{1,0:T(8,128)S(1)} %get-tuple-element.62.b_ref.refs_3_, f32[1024,128]{1,0:T(8,128)S(1)} %get-tuple-element.64.refs_0_.r_ref, f32[1,2048]{1,0:T(1,128)S(1)} %get-tuple-element.100.refs_1_.refs_9_), custom_call_target="tpu_custom_call" | custom-call | tf_op jit(solution)/shard_map/sweep_bwd/pallas_call | solution.py:253
  74.9 1.1 collective-permute-start.30
  76.0 1.2 collective-permute-done.32
  77.9 1.4 %collective-permute-start.35 = (f32[1,2048]{1,0:T(1,128)S(1)}, f32[1,2048]{1,0:T(1,128)S(1)}, u32[]{:S(2)}, u32[]{:S(2)}) collective-permute-start(f32[1,2048]{1,0:T(1,128)S(1)} %add_add_fusion.1), channel_id=1, source_target_pairs={{0,12},{1,13},{2,14},{3,15},{4,8},{5,9},{6,10},{7,11},{8,4},{9,5},... | collective-permute-start | bytes 24584 | tf_op jit(solution)/shard_map/ppermute | solution.py:406
  79.4 1.0 collective-permute-start.34
  80.4 2.0 %collective-permute-start.33 = (f32[1,2048]{1,0:T(1,128)S(1)}, f32[1,2048]{1,0:T(1,128)S(1)}, u32[]{:S(2)}, u32[]{:S(2)}) collective-permute-start(f32[1,2048]{1,0:T(1,128)S(1)} %add_add_fusion.1), channel_id=1, source_target_pairs={{0,4},{1,5},{2,6},{3,7},{4,0},{5,1},{6,2},{7,3},{8,12},{9,13},{10,... | collective-permute-start | bytes 24584 | tf_op jit(solution)/shard_map/ppermute | solution.py:406
  82.4 1.1 collective-permute-done.35
  84.1 5.0 %mix.1 = (bf16[1024,2048]{1,0:T(8,128)(2,1)S(1)}, f32[8,48,512]{2,1,0:T(8,128)S(1)}, f32[8,48,512]{2,1,0:T(8,128)S(1)}, f32[8,48,512]{2,1,0:T(8,128)S(1)}, f32[8...) custom-call(f32[1024,2048]{1,0:T(8,128)S(1)} %get-tuple-element.55.e_ref, ...), custom_call_target="tpu_custom_call" | custom-call | tf_op jit(solution)/shard_map/mix/pallas_call | solution.py:332
  89.8 1.7 %collective-permute-done.38.got_ref = f32[8,48,512]{2,1,0:T(8,128)S(1)} collective-permute-done((f32[8,48,512]{2,1,0:T(8,128)S(1)}, f32[8,48,512]{2,1,0:T(8,128)S(1)}, u32[]{:S(2)}, u32[]{:S(2)}) %collective-permute-start.38) | collective-permute-done | bytes 786464 | tf_op jit(solution)/shard_map/ppermute | solution.py:406
  91.6 0.7 collective-permute-start.39
  93.4 2.1 %collective-permute-start.40 = (f32[4,32,512]{2,1,0:T(8,128)S(1)}, f32[4,32,512]{2,1,0:T(8,128)S(1)}, u32[]{:S(2)}, u32[]{:S(2)}) collective-permute-start(f32[4,32,512]{2,1,0:T(8,128)S(1)} %get-tuple-element.78.after_ref), channel_id=1, source_target_pairs={{0,4},{1,5},{2,6},{3,7},{4,0},{5,1},{6,2},{7,3},{8,12},{9,13},{10,... | collective-permute-start | bytes 786440 | tf_op jit(solution)/shard_map/ppermute | solution.py:406
  96.2 5.2 %back.1 = (f32[1,1024]{1,0:T(1,128)}, f32[1024,512]{1,0:T(8,128)}, f32[1,2048]{1,0:T(1,128)}) custom-call(bf16[1024,2048]{1,0:T(8,128)(2,1)S(1)} %get-tuple-element.68.half_ref, bf16[2048,512]{1,0:T(8,128)(2,1)S(1)} %copy-done.1, bf16[1024,512]{1,0:T(8,128)(2,1)S(1)} %copy-done, f32[1024,2048]{1,0:T(8,128)S(1)} %get-tuple-element.55.e_ref, ...), custom_call_target="tpu_custom_call" | custom-call | flops 2147483648 | bytes 16777216 | tf_op jit(solution)/shard_map/back/pallas_call | solution.py:387
  101.3 0.8 collective-permute-done.40.got_ref
  102.8 0.8 collective-permute-done.39.got_ref
  103.6 2.1 %collective-permute-start.41 = (f32[2,48,512]{2,1,0:T(8,128)S(1)}, f32[2,48,512]{2,1,0:T(8,128)S(1)}, u32[]{:S(2)}, u32[]{:S(2)}) collective-permute-start(f32[2,48,512]{2,1,0:T(8,128)S(1)} %get-tuple-element.86.after_ref), channel_id=1, source_target_pairs={{0,4},{1,5},{2,6},{3,7},{4,0},{5,1},{6,2},{7,3},{8,12},{9,13},{10,... | collective-permute-start | bytes 589832 | tf_op jit(solution)/shard_map/ppermute | solution.py:406
  105.7 1.0 collective-permute-start.42
  106.8 5.1 %collective-permute-done.42.got_ref = f32[2,32,512]{2,1,0:T(8,128)S(1)} collective-permute-done((f32[2,32,512]{2,1,0:T(8,128)S(1)}, f32[2,32,512]{2,1,0:T(8,128)S(1)}, u32[]{:S(2)}, u32[]{:S(2)}) %collective-permute-start.42) | collective-permute-done | bytes 131104 | tf_op jit(solution)/shard_map/ppermute | solution.py:406
  112.3 1.7 %collective-permute-start.45 = (f32[2,48,512]{2,1,0:T(8,128)S(1)}, f32[2,48,512]{2,1,0:T(8,128)S(1)}, u32[]{:S(2)}, u32[]{:S(2)}) collective-permute-start(f32[2,48,512]{2,1,0:T(8,128)S(1)} %get-tuple-element.93.after_ref), channel_id=1, source_target_pairs={{0,4},{1,5},{2,6},{3,7},{4,0},{5,1},{6,2},{7,3},{8,12},{9,13},{10,... | collective-permute-start | bytes 589832 | tf_op jit(solution)/shard_map/ppermute | solution.py:406
  114.0 1.0 collective-permute-start.43
  115.1 5.7 %collective-permute-done.45.got_ref = f32[2,48,512]{2,1,0:T(8,128)S(1)} collective-permute-done((f32[2,48,512]{2,1,0:T(8,128)S(1)}, f32[2,48,512]{2,1,0:T(8,128)S(1)}, u32[]{:S(2)}, u32[]{:S(2)}) %collective-permute-start.45) | collective-permute-done | bytes 196640 | tf_op jit(solution)/shard_map/ppermute | solution.py:406
  120.8 0.7 collective-permute-start.47
  121.5 3.6 %collective-permute-done.47 = f32[1,32,512]{2,1,0:T(8,128)S(1)} collective-permute-done((f32[1,32,512]{2,1,0:T(8,128)S(1)}, f32[1,32,512]{2,1,0:T(8,128)S(1)}, u32[]{:S(2)}, u32[]{:S(2)}) %collective-permute-start.47) | collective-permute-done | bytes 65568 | tf_op jit(solution)/shard_map/ppermute | solution.py:406
  125.2 1.7 %collective-permute-done.46 = f32[1,48,512]{2,1,0:T(8,128)S(1)} collective-permute-done((f32[1,48,512]{2,1,0:T(8,128)S(1)}, f32[1,48,512]{2,1,0:T(8,128)S(1)}, u32[]{:S(2)}, u32[]{:S(2)}) %collective-permute-start.46) | collective-permute-done | bytes 98336 | tf_op jit(solution)/shard_map/ppermute | solution.py:406
  126.9 0.9 gradient.1
  (70 shorter events, 13.4 us)
Async XLA Ops:
  6.5 4.0 %collective-permute-start.2 = (f32[1,2048]{1,0:T(1,128)}, f32[1,2048]{1,0:T(1,128)S(1)}, u32[]{:S(2)}, u32[]{:S(2)}) collective-permute-start(f32[1,2048]{1,0:T(1,128)} %get-tuple-element.54), channel_id=1, source_target_pairs={{0,3},{1,2},{2,1},{3,0},{4,7},{5,6},{6,5},{7,4},{8,11},{9,10},{10,... | collective-permute-start | bytes 24584 | tf_op jit(solution)/shard_map/ppermute | solution.py:406
  8.9 3.9 %collective-permute-start.1 = (f32[1,2048]{1,0:T(1,128)}, f32[1,2048]{1,0:T(1,128)S(1)}, u32[]{:S(2)}, u32[]{:S(2)}) collective-permute-start(f32[1,2048]{1,0:T(1,128)} %get-tuple-element.54), channel_id=1, source_target_pairs={{0,2},{1,3},{2,0},{3,1},{4,6},{5,7},{6,4},{7,5},{8,10},{9,11},{10,... | collective-permute-start | bytes 24584 | tf_op jit(solution)/shard_map/ppermute | solution.py:406
  9.6 3.2 %collective-permute-start = (f32[1,2048]{1,0:T(1,128)}, f32[1,2048]{1,0:T(1,128)S(1)}, u32[]{:S(2)}, u32[]{:S(2)}) collective-permute-start(f32[1,2048]{1,0:T(1,128)} %get-tuple-element.54), channel_id=1, source_target_pairs={{0,1},{1,0},{2,3},{3,2},{4,5},{5,4},{6,7},{7,6},{8,9},{9,8},{10,11... | collective-permute-start | bytes 24584 | tf_op jit(solution)/shard_map/ppermute | solution.py:406
  13.6 5.6 %collective-permute-start.5 = (f32[1,2048]{1,0:T(1,128)S(1)}, f32[1,2048]{1,0:T(1,128)S(1)}, u32[]{:S(2)}, u32[]{:S(2)}) collective-permute-start(f32[1,2048]{1,0:T(1,128)S(1)} %multiply_add_fusion.1), channel_id=1, source_target_pairs={{0,12},{1,13},{2,14},{3,15},{4,8},{5,9},{6,10},{7,11},{8,4},{9,5},... | collective-permute-start | bytes 24584 | tf_op jit(solution)/shard_map/ppermute | solution.py:406
  17.3 4.5 %collective-permute-start.4 = (f32[1,2048]{1,0:T(1,128)S(1)}, f32[1,2048]{1,0:T(1,128)S(1)}, u32[]{:S(2)}, u32[]{:S(2)}) collective-permute-start(f32[1,2048]{1,0:T(1,128)S(1)} %multiply_add_fusion.1), channel_id=1, source_target_pairs={{0,8},{1,9},{2,10},{3,11},{4,12},{5,13},{6,14},{7,15},{8,0},{9,1},... | collective-permute-start | bytes 24584 | tf_op jit(solution)/shard_map/ppermute | solution.py:406
  17.3 4.5 %collective-permute-start.3 = (f32[1,2048]{1,0:T(1,128)S(1)}, f32[1,2048]{1,0:T(1,128)S(1)}, u32[]{:S(2)}, u32[]{:S(2)}) collective-permute-start(f32[1,2048]{1,0:T(1,128)S(1)} %multiply_add_fusion.1), channel_id=1, source_target_pairs={{0,4},{1,5},{2,6},{3,7},{4,0},{5,1},{6,2},{7,3},{8,12},{9,13},{10,... | collective-permute-start | bytes 24584 | tf_op jit(solution)/shard_map/ppermute | solution.py:406
  26.2 3.1 %collective-permute-start.8 = (f32[1,2048]{1,0:T(1,128)S(1)}, f32[1,2048]{1,0:T(1,128)S(1)}, u32[]{:S(2)}, u32[]{:S(2)}) collective-permute-start(f32[1,2048]{1,0:T(1,128)S(1)} %get-tuple-element.56), channel_id=1, source_target_pairs={{0,3},{1,2},{2,1},{3,0},{4,7},{5,6},{6,5},{7,4},{8,11},{9,10},{10,... | collective-permute-start | bytes 24584 | tf_op jit(solution)/shard_map/ppermute | solution.py:406
  26.3 3.7 %collective-permute-start.7 = (f32[1,2048]{1,0:T(1,128)S(1)}, f32[1,2048]{1,0:T(1,128)S(1)}, u32[]{:S(2)}, u32[]{:S(2)}) collective-permute-start(f32[1,2048]{1,0:T(1,128)S(1)} %get-tuple-element.56), channel_id=1, source_target_pairs={{0,2},{1,3},{2,0},{3,1},{4,6},{5,7},{6,4},{7,5},{8,10},{9,11},{10,... | collective-permute-start | bytes 24584 | tf_op jit(solution)/shard_map/ppermute | solution.py:406
  27.0 3.0 %collective-permute-start.6 = (f32[1,2048]{1,0:T(1,128)S(1)}, f32[1,2048]{1,0:T(1,128)S(1)}, u32[]{:S(2)}, u32[]{:S(2)}) collective-permute-start(f32[1,2048]{1,0:T(1,128)S(1)} %get-tuple-element.56), channel_id=1, source_target_pairs={{0,1},{1,0},{2,3},{3,2},{4,5},{5,4},{6,7},{7,6},{8,9},{9,8},{10,11... | collective-permute-start | bytes 24584 | tf_op jit(solution)/shard_map/ppermute | solution.py:406
  30.0 5.6 %collective-permute-start.11 = (f32[1,2048]{1,0:T(1,128)S(1)}, f32[1,2048]{1,0:T(1,128)S(1)}, u32[]{:S(2)}, u32[]{:S(2)}) collective-permute-start(f32[1,2048]{1,0:T(1,128)S(1)} %add_add_fusion.5), channel_id=1, source_target_pairs={{0,12},{1,13},{2,14},{3,15},{4,8},{5,9},{6,10},{7,11},{8,4},{9,5},... | collective-permute-start | bytes 24584 | tf_op jit(solution)/shard_map/ppermute | solution.py:406
  31.6 4.6 %collective-permute-start.10 = (f32[1,2048]{1,0:T(1,128)S(1)}, f32[1,2048]{1,0:T(1,128)S(1)}, u32[]{:S(2)}, u32[]{:S(2)}) collective-permute-start(f32[1,2048]{1,0:T(1,128)S(1)} %add_add_fusion.5), channel_id=1, source_target_pairs={{0,8},{1,9},{2,10},{3,11},{4,12},{5,13},{6,14},{7,15},{8,0},{9,1},... | collective-permute-start | bytes 24584 | tf_op jit(solution)/shard_map/ppermute | solution.py:406
  32.2 4.0 %collective-permute-start.9 = (f32[1,2048]{1,0:T(1,128)S(1)}, f32[1,2048]{1,0:T(1,128)S(1)}, u32[]{:S(2)}, u32[]{:S(2)}) collective-permute-start(f32[1,2048]{1,0:T(1,128)S(1)} %add_add_fusion.5), channel_id=1, source_target_pairs={{0,4},{1,5},{2,6},{3,7},{4,0},{5,1},{6,2},{7,3},{8,12},{9,13},{10,... | collective-permute-start | bytes 24584 | tf_op jit(solution)/shard_map/ppermute | solution.py:406
  37.6 3.1 %collective-permute-start.14 = (f32[1,2048]{1,0:T(1,128)S(1)}, f32[1,2048]{1,0:T(1,128)S(1)}, u32[]{:S(2)}, u32[]{:S(2)}) collective-permute-start(f32[1,2048]{1,0:T(1,128)S(1)} %get-tuple-element.57), channel_id=1, source_target_pairs={{0,3},{1,2},{2,1},{3,0},{4,7},{5,6},{6,5},{7,4},{8,11},{9,10},{10,... | collective-permute-start | bytes 24584 | tf_op jit(solution)/shard_map/ppermute | solution.py:406
  37.7 3.7 %collective-permute-start.13 = (f32[1,2048]{1,0:T(1,128)S(1)}, f32[1,2048]{1,0:T(1,128)S(1)}, u32[]{:S(2)}, u32[]{:S(2)}) collective-permute-start(f32[1,2048]{1,0:T(1,128)S(1)} %get-tuple-element.57), channel_id=1, source_target_pairs={{0,2},{1,3},{2,0},{3,1},{4,6},{5,7},{6,4},{7,5},{8,10},{9,11},{10,... | collective-permute-start | bytes 24584 | tf_op jit(solution)/shard_map/ppermute | solution.py:406
  38.4 3.0 %collective-permute-start.12 = (f32[1,2048]{1,0:T(1,128)S(1)}, f32[1,2048]{1,0:T(1,128)S(1)}, u32[]{:S(2)}, u32[]{:S(2)}) collective-permute-start(f32[1,2048]{1,0:T(1,128)S(1)} %get-tuple-element.57), channel_id=1, source_target_pairs={{0,1},{1,0},{2,3},{3,2},{4,5},{5,4},{6,7},{7,6},{8,9},{9,8},{10,11... | collective-permute-start | bytes 24584 | tf_op jit(solution)/shard_map/ppermute | solution.py:406
  41.5 5.5 %collective-permute-start.17 = (f32[1,2048]{1,0:T(1,128)S(1)}, f32[1,2048]{1,0:T(1,128)S(1)}, u32[]{:S(2)}, u32[]{:S(2)}) collective-permute-start(f32[1,2048]{1,0:T(1,128)S(1)} %add_add_fusion.4), channel_id=1, source_target_pairs={{0,12},{1,13},{2,14},{3,15},{4,8},{5,9},{6,10},{7,11},{8,4},{9,5},... | collective-permute-start | bytes 24584 | tf_op jit(solution)/shard_map/ppermute | solution.py:406
  44.0 4.6 %collective-permute-start.16 = (f32[1,2048]{1,0:T(1,128)S(1)}, f32[1,2048]{1,0:T(1,128)S(1)}, u32[]{:S(2)}, u32[]{:S(2)}) collective-permute-start(f32[1,2048]{1,0:T(1,128)S(1)} %add_add_fusion.4), channel_id=1, source_target_pairs={{0,8},{1,9},{2,10},{3,11},{4,12},{5,13},{6,14},{7,15},{8,0},{9,1},... | collective-permute-start | bytes 24584 | tf_op jit(solution)/shard_map/ppermute | solution.py:406
  44.9 3.7 %collective-permute-start.15 = (f32[1,2048]{1,0:T(1,128)S(1)}, f32[1,2048]{1,0:T(1,128)S(1)}, u32[]{:S(2)}, u32[]{:S(2)}) collective-permute-start(f32[1,2048]{1,0:T(1,128)S(1)} %add_add_fusion.4), channel_id=1, source_target_pairs={{0,4},{1,5},{2,6},{3,7},{4,0},{5,1},{6,2},{7,3},{8,12},{9,13},{10,... | collective-permute-start | bytes 24584 | tf_op jit(solution)/shard_map/ppermute | solution.py:406
  50.1 3.1 %collective-permute-start.20 = (f32[1,2048]{1,0:T(1,128)S(1)}, f32[1,2048]{1,0:T(1,128)S(1)}, u32[]{:S(2)}, u32[]{:S(2)}) collective-permute-start(f32[1,2048]{1,0:T(1,128)S(1)} %get-tuple-element.60), channel_id=1, source_target_pairs={{0,3},{1,2},{2,1},{3,0},{4,7},{5,6},{6,5},{7,4},{8,11},{9,10},{10,... | collective-permute-start | bytes 24584 | tf_op jit(solution)/shard_map/ppermute | solution.py:406
  50.2 3.7 %collective-permute-start.19 = (f32[1,2048]{1,0:T(1,128)S(1)}, f32[1,2048]{1,0:T(1,128)S(1)}, u32[]{:S(2)}, u32[]{:S(2)}) collective-permute-start(f32[1,2048]{1,0:T(1,128)S(1)} %get-tuple-element.60), channel_id=1, source_target_pairs={{0,2},{1,3},{2,0},{3,1},{4,6},{5,7},{6,4},{7,5},{8,10},{9,11},{10,... | collective-permute-start | bytes 24584 | tf_op jit(solution)/shard_map/ppermute | solution.py:406
  50.9 3.0 %collective-permute-start.18 = (f32[1,2048]{1,0:T(1,128)S(1)}, f32[1,2048]{1,0:T(1,128)S(1)}, u32[]{:S(2)}, u32[]{:S(2)}) collective-permute-start(f32[1,2048]{1,0:T(1,128)S(1)} %get-tuple-element.60), channel_id=1, source_target_pairs={{0,1},{1,0},{2,3},{3,2},{4,5},{5,4},{6,7},{7,6},{8,9},{9,8},{10,11... | collective-permute-start | bytes 24584 | tf_op jit(solution)/shard_map/ppermute | solution.py:406
  53.9 5.5 %collective-permute-start.23 = (f32[1,2048]{1,0:T(1,128)S(1)}, f32[1,2048]{1,0:T(1,128)S(1)}, u32[]{:S(2)}, u32[]{:S(2)}) collective-permute-start(f32[1,2048]{1,0:T(1,128)S(1)} %add_add_fusion.3), channel_id=1, source_target_pairs={{0,12},{1,13},{2,14},{3,15},{4,8},{5,9},{6,10},{7,11},{8,4},{9,5},... | collective-permute-start | bytes 24584 | tf_op jit(solution)/shard_map/ppermute | solution.py:406
  55.4 4.5 %collective-permute-start.22 = (f32[1,2048]{1,0:T(1,128)S(1)}, f32[1,2048]{1,0:T(1,128)S(1)}, u32[]{:S(2)}, u32[]{:S(2)}) collective-permute-start(f32[1,2048]{1,0:T(1,128)S(1)} %add_add_fusion.3), channel_id=1, source_target_pairs={{0,8},{1,9},{2,10},{3,11},{4,12},{5,13},{6,14},{7,15},{8,0},{9,1},... | collective-permute-start | bytes 24584 | tf_op jit(solution)/shard_map/ppermute | solution.py:406
  56.4 3.7 %collective-permute-start.21 = (f32[1,2048]{1,0:T(1,128)S(1)}, f32[1,2048]{1,0:T(1,128)S(1)}, u32[]{:S(2)}, u32[]{:S(2)}) collective-permute-start(f32[1,2048]{1,0:T(1,128)S(1)} %add_add_fusion.3), channel_id=1, source_target_pairs={{0,4},{1,5},{2,6},{3,7},{4,0},{5,1},{6,2},{7,3},{8,12},{9,13},{10,... | collective-permute-start | bytes 24584 | tf_op jit(solution)/shard_map/ppermute | solution.py:406
  61.4 3.1 %collective-permute-start.26 = (f32[1,2048]{1,0:T(1,128)S(1)}, f32[1,2048]{1,0:T(1,128)S(1)}, u32[]{:S(2)}, u32[]{:S(2)}) collective-permute-start(f32[1,2048]{1,0:T(1,128)S(1)} %get-tuple-element.65), channel_id=1, source_target_pairs={{0,3},{1,2},{2,1},{3,0},{4,7},{5,6},{6,5},{7,4},{8,11},{9,10},{10,... | collective-permute-start | bytes 24584 | tf_op jit(solution)/shard_map/ppermute | solution.py:406
  61.5 3.7 %collective-permute-start.25 = (f32[1,2048]{1,0:T(1,128)S(1)}, f32[1,2048]{1,0:T(1,128)S(1)}, u32[]{:S(2)}, u32[]{:S(2)}) collective-permute-start(f32[1,2048]{1,0:T(1,128)S(1)} %get-tuple-element.65), channel_id=1, source_target_pairs={{0,2},{1,3},{2,0},{3,1},{4,6},{5,7},{6,4},{7,5},{8,10},{9,11},{10,... | collective-permute-start | bytes 24584 | tf_op jit(solution)/shard_map/ppermute | solution.py:406
  62.2 3.0 %collective-permute-start.24 = (f32[1,2048]{1,0:T(1,128)S(1)}, f32[1,2048]{1,0:T(1,128)S(1)}, u32[]{:S(2)}, u32[]{:S(2)}) collective-permute-start(f32[1,2048]{1,0:T(1,128)S(1)} %get-tuple-element.65), channel_id=1, source_target_pairs={{0,1},{1,0},{2,3},{3,2},{4,5},{5,4},{6,7},{7,6},{8,9},{9,8},{10,11... | collective-permute-start | bytes 24584 | tf_op jit(solution)/shard_map/ppermute | solution.py:406
  65.3 5.5 %collective-permute-start.29 = (f32[1,2048]{1,0:T(1,128)S(1)}, f32[1,2048]{1,0:T(1,128)S(1)}, u32[]{:S(2)}, u32[]{:S(2)}) collective-permute-start(f32[1,2048]{1,0:T(1,128)S(1)} %add_add_fusion.2), channel_id=1, source_target_pairs={{0,12},{1,13},{2,14},{3,15},{4,8},{5,9},{6,10},{7,11},{8,4},{9,5},... | collective-permute-start | bytes 24584 | tf_op jit(solution)/shard_map/ppermute | solution.py:406
  67.8 4.5 %collective-permute-start.28 = (f32[1,2048]{1,0:T(1,128)S(1)}, f32[1,2048]{1,0:T(1,128)S(1)}, u32[]{:S(2)}, u32[]{:S(2)}) collective-permute-start(f32[1,2048]{1,0:T(1,128)S(1)} %add_add_fusion.2), channel_id=1, source_target_pairs={{0,8},{1,9},{2,10},{3,11},{4,12},{5,13},{6,14},{7,15},{8,0},{9,1},... | collective-permute-start | bytes 24584 | tf_op jit(solution)/shard_map/ppermute | solution.py:406
  68.8 3.7 %collective-permute-start.27 = (f32[1,2048]{1,0:T(1,128)S(1)}, f32[1,2048]{1,0:T(1,128)S(1)}, u32[]{:S(2)}, u32[]{:S(2)}) collective-permute-start(f32[1,2048]{1,0:T(1,128)S(1)} %add_add_fusion.2), channel_id=1, source_target_pairs={{0,4},{1,5},{2,6},{3,7},{4,0},{5,1},{6,2},{7,3},{8,12},{9,13},{10,... | collective-permute-start | bytes 24584 | tf_op jit(solution)/shard_map/ppermute | solution.py:406
  72.5 11.6 %copy-start = (bf16[1024,512]{1,0:T(8,128)(2,1)S(1)}, bf16[1024,512]{1,0:T(8,128)(2,1)}, u32[]{:S(2)}) copy-start(bf16[1024,512]{1,0:T(8,128)(2,1)} %y_ref.3) | copy-start | bytes 3145732
  74.1 3.1 %collective-permute-start.32 = (f32[1,2048]{1,0:T(1,128)S(1)}, f32[1,2048]{1,0:T(1,128)S(1)}, u32[]{:S(2)}, u32[]{:S(2)}) collective-permute-start(f32[1,2048]{1,0:T(1,128)S(1)} %get-tuple-element.67.after_ref), channel_id=1, source_target_pairs={{0,3},{1,2},{2,1},{3,0},{4,7},{5,6},{6,5},{7,4},{8,11},{9,10},{10,... | collective-permute-start | bytes 24584 | tf_op jit(solution)/shard_map/ppermute | solution.py:406
  74.2 3.7 %collective-permute-start.31 = (f32[1,2048]{1,0:T(1,128)S(1)}, f32[1,2048]{1,0:T(1,128)S(1)}, u32[]{:S(2)}, u32[]{:S(2)}) collective-permute-start(f32[1,2048]{1,0:T(1,128)S(1)} %get-tuple-element.67.after_ref), channel_id=1, source_target_pairs={{0,2},{1,3},{2,0},{3,1},{4,6},{5,7},{6,4},{7,5},{8,10},{9,11},{10,... | collective-permute-start | bytes 24584 | tf_op jit(solution)/shard_map/ppermute | solution.py:406
  74.9 3.0 %collective-permute-start.30 = (f32[1,2048]{1,0:T(1,128)S(1)}, f32[1,2048]{1,0:T(1,128)S(1)}, u32[]{:S(2)}, u32[]{:S(2)}) collective-permute-start(f32[1,2048]{1,0:T(1,128)S(1)} %get-tuple-element.67.after_ref), channel_id=1, source_target_pairs={{0,1},{1,0},{2,3},{3,2},{4,5},{5,4},{6,7},{7,6},{8,9},{9,8},{10,11... | collective-permute-start | bytes 24584 | tf_op jit(solution)/shard_map/ppermute | solution.py:406
  77.9 5.5 %collective-permute-start.35 = (f32[1,2048]{1,0:T(1,128)S(1)}, f32[1,2048]{1,0:T(1,128)S(1)}, u32[]{:S(2)}, u32[]{:S(2)}) collective-permute-start(f32[1,2048]{1,0:T(1,128)S(1)} %add_add_fusion.1), channel_id=1, source_target_pairs={{0,12},{1,13},{2,14},{3,15},{4,8},{5,9},{6,10},{7,11},{8,4},{9,5},... | collective-permute-start | bytes 24584 | tf_op jit(solution)/shard_map/ppermute | solution.py:406
  79.4 4.5 %collective-permute-start.34 = (f32[1,2048]{1,0:T(1,128)S(1)}, f32[1,2048]{1,0:T(1,128)S(1)}, u32[]{:S(2)}, u32[]{:S(2)}) collective-permute-start(f32[1,2048]{1,0:T(1,128)S(1)} %add_add_fusion.1), channel_id=1, source_target_pairs={{0,8},{1,9},{2,10},{3,11},{4,12},{5,13},{6,14},{7,15},{8,0},{9,1},... | collective-permute-start | bytes 24584 | tf_op jit(solution)/shard_map/ppermute | solution.py:406
  80.4 3.7 %collective-permute-start.33 = (f32[1,2048]{1,0:T(1,128)S(1)}, f32[1,2048]{1,0:T(1,128)S(1)}, u32[]{:S(2)}, u32[]{:S(2)}) collective-permute-start(f32[1,2048]{1,0:T(1,128)S(1)} %add_add_fusion.1), channel_id=1, source_target_pairs={{0,4},{1,5},{2,6},{3,7},{4,0},{5,1},{6,2},{7,3},{8,12},{9,13},{10,... | collective-permute-start | bytes 24584 | tf_op jit(solution)/shard_map/ppermute | solution.py:406
  89.1 7.0 %copy-start.1 = (bf16[2048,512]{1,0:T(8,128)(2,1)S(1)}, bf16[2048,512]{1,0:T(8,128)(2,1)}, u32[]{:S(2)}) copy-start(bf16[2048,512]{1,0:T(8,128)(2,1)} %x_ref.1) | copy-start | bytes 6291460
  89.1 2.4 %collective-permute-start.38 = (f32[8,48,512]{2,1,0:T(8,128)S(1)}, f32[8,48,512]{2,1,0:T(8,128)S(1)}, u32[]{:S(2)}, u32[]{:S(2)}) collective-permute-start(f32[8,48,512]{2,1,0:T(8,128)S(1)} %get-tuple-element.75), channel_id=1, source_target_pairs={{0,1},{1,0},{2,3},{3,2},{4,5},{5,4},{6,7},{7,6},{8,9},{9,8},{10,11... | collective-permute-start | bytes 2359304 | tf_op jit(solution)/shard_map/ppermute | solution.py:406
  89.2 3.4 %collective-permute-start.37 = (f32[8,48,512]{2,1,0:T(8,128)S(1)}, f32[8,48,512]{2,1,0:T(8,128)S(1)}, u32[]{:S(2)}, u32[]{:S(2)}) collective-permute-start(f32[8,48,512]{2,1,0:T(8,128)S(1)} %get-tuple-element.73), channel_id=1, source_target_pairs={{0,1},{1,0},{2,3},{3,2},{4,5},{5,4},{6,7},{7,6},{8,9},{9,8},{10,11... | collective-permute-start | bytes 2359304 | tf_op jit(solution)/shard_map/ppermute | solution.py:406
  89.7 3.6 %collective-permute-start.36 = (f32[8,32,512]{2,1,0:T(8,128)S(1)}, f32[8,32,512]{2,1,0:T(8,128)S(1)}, u32[]{:S(2)}, u32[]{:S(2)}) collective-permute-start(f32[8,32,512]{2,1,0:T(8,128)S(1)} %get-tuple-element.71), channel_id=1, source_target_pairs={{0,1},{1,0},{2,3},{3,2},{4,5},{5,4},{6,7},{7,6},{8,9},{9,8},{10,11... | collective-permute-start | bytes 1572872 | tf_op jit(solution)/shard_map/ppermute | solution.py:406
  91.6 12.0 %collective-permute-start.39 = (f32[4,48,512]{2,1,0:T(8,128)S(1)}, f32[4,48,512]{2,1,0:T(8,128)S(1)}, u32[]{:S(2)}, u32[]{:S(2)}) collective-permute-start(f32[4,48,512]{2,1,0:T(8,128)S(1)} %get-tuple-element.76.after_ref), channel_id=1, source_target_pairs={{0,2},{1,3},{2,0},{3,1},{4,6},{5,7},{6,4},{7,5},{8,10},{9,11},{10,... | collective-permute-start | bytes 1179656 | tf_op jit(solution)/shard_map/ppermute | solution.py:406
  93.4 8.7 %collective-permute-start.40 = (f32[4,32,512]{2,1,0:T(8,128)S(1)}, f32[4,32,512]{2,1,0:T(8,128)S(1)}, u32[]{:S(2)}, u32[]{:S(2)}) collective-permute-start(f32[4,32,512]{2,1,0:T(8,128)S(1)} %get-tuple-element.78.after_ref), channel_id=1, source_target_pairs={{0,4},{1,5},{2,6},{3,7},{4,0},{5,1},{6,2},{7,3},{8,12},{9,13},{10,... | collective-permute-start | bytes 786440 | tf_op jit(solution)/shard_map/ppermute | solution.py:406
  95.5 16.7 %collective-permute-start.44 = (f32[4,48,512]{2,1,0:T(8,128)S(1)}, f32[4,48,512]{2,1,0:T(8,128)S(1)}, u32[]{:S(2)}, u32[]{:S(2)}) collective-permute-start(f32[4,48,512]{2,1,0:T(8,128)S(1)} %get-tuple-element.77.after_ref), channel_id=1, source_target_pairs={{0,2},{1,3},{2,0},{3,1},{4,6},{5,7},{6,4},{7,5},{8,10},{9,11},{10,... | collective-permute-start | bytes 1179656 | tf_op jit(solution)/shard_map/ppermute | solution.py:406
  102.1 0.7 copy-start.2
  103.6 8.6 %collective-permute-start.41 = (f32[2,48,512]{2,1,0:T(8,128)S(1)}, f32[2,48,512]{2,1,0:T(8,128)S(1)}, u32[]{:S(2)}, u32[]{:S(2)}) collective-permute-start(f32[2,48,512]{2,1,0:T(8,128)S(1)} %get-tuple-element.86.after_ref), channel_id=1, source_target_pairs={{0,4},{1,5},{2,6},{3,7},{4,0},{5,1},{6,2},{7,3},{8,12},{9,13},{10,... | collective-permute-start | bytes 589832 | tf_op jit(solution)/shard_map/ppermute | solution.py:406
  105.7 6.2 %collective-permute-start.42 = (f32[2,32,512]{2,1,0:T(8,128)S(1)}, f32[2,32,512]{2,1,0:T(8,128)S(1)}, u32[]{:S(2)}, u32[]{:S(2)}) collective-permute-start(f32[2,32,512]{2,1,0:T(8,128)S(1)} %get-tuple-element.84.after_ref), channel_id=1, source_target_pairs={{0,8},{1,9},{2,10},{3,11},{4,12},{5,13},{6,14},{7,15},{8,0},{9,1},... | collective-permute-start | bytes 393224 | tf_op jit(solution)/shard_map/ppermute | solution.py:406
  112.3 8.4 %collective-permute-start.45 = (f32[2,48,512]{2,1,0:T(8,128)S(1)}, f32[2,48,512]{2,1,0:T(8,128)S(1)}, u32[]{:S(2)}, u32[]{:S(2)}) collective-permute-start(f32[2,48,512]{2,1,0:T(8,128)S(1)} %get-tuple-element.93.after_ref), channel_id=1, source_target_pairs={{0,4},{1,5},{2,6},{3,7},{4,0},{5,1},{6,2},{7,3},{8,12},{9,13},{10,... | collective-permute-start | bytes 589832 | tf_op jit(solution)/shard_map/ppermute | solution.py:406
  114.0 11.2 %collective-permute-start.43 = (f32[1,48,512]{2,1,0:T(8,128)S(1)}, f32[1,48,512]{2,1,0:T(8,128)S(1)}, u32[]{:S(2)}, u32[]{:S(2)}) collective-permute-start(f32[1,48,512]{2,1,0:T(8,128)S(1)} %get-tuple-element.90.after_ref), channel_id=1, source_target_pairs={{0,8},{1,9},{2,10},{3,11},{4,12},{5,13},{6,14},{7,15},{8,0},{9,1},... | collective-permute-start | bytes 294920 | tf_op jit(solution)/shard_map/ppermute | solution.py:406
  120.8 6.1 %collective-permute-start.46 = (f32[1,48,512]{2,1,0:T(8,128)S(1)}, f32[1,48,512]{2,1,0:T(8,128)S(1)}, u32[]{:S(2)}, u32[]{:S(2)}) collective-permute-start(f32[1,48,512]{2,1,0:T(8,128)S(1)} %get-tuple-element.95), channel_id=1, source_target_pairs={{0,8},{1,9},{2,10},{3,11},{4,12},{5,13},{6,14},{7,15},{8,0},{9,1},... | collective-permute-start | bytes 294920 | tf_op jit(solution)/shard_map/ppermute | solution.py:406
  120.8 4.3 %collective-permute-start.47 = (f32[1,32,512]{2,1,0:T(8,128)S(1)}, f32[1,32,512]{2,1,0:T(8,128)S(1)}, u32[]{:S(2)}, u32[]{:S(2)}) collective-permute-start(f32[1,32,512]{2,1,0:T(8,128)S(1)} %get-tuple-element.88.after_ref), channel_id=1, source_target_pairs={{0,2},{1,3},{2,0},{3,1},{4,6},{5,7},{6,4},{7,5},{8,10},{9,11},{10,... | collective-permute-start | bytes 196616 | tf_op jit(solution)/shard_map/ppermute | solution.py:406

commit v6 on v5

--- a/solution.py
+++ b/solution.py
@@ -264,7 +264,7 @@
 def mix_kernel(share, pieces, e_ref, y_ref, *refs):
     c_refs, r_refs = refs[:6], refs[6:11]
     half_ref, (prod_ref, left_ref, right_ref) = refs[11], refs[-3:]
-    keep_refs, send_refs = refs[12:-3:2], refs[13:-3:2]
+    send_refs = refs[12:-3]
     cols, rows = e_ref.shape
     pair = 2 * share
     me = lax.axis_index("cols")
@@ -292,15 +292,35 @@
             s = pl.ds(g * MIX, MIX)
             scale = jnp.dot(left_ref[s, :], right_ref[:, block], preferred_element_type=F32)
             half_ref[s, block] = (e_ref[s, block] * scale).astype(BF16)
-        prod_ref[p % 2] = lax.dot_general(
-            half_ref[:, block], y_ref[...], (((0,), (0,)), ((), ())),
-            preferred_element_type=F32,
-        )
-        for refs, side in ((keep_refs, core), (send_refs, 1 - core)):
-            at = side * share
-            for ref, (n, bits) in zip(refs, pieces):
-                ref[spot(p, bits)] = prod_ref[p % 2, pl.ds(pl.multiple_of(at, SUB), n), :]
-                at = at + n
+        if p % 2:
+            products(share, pieces, p - 1, 1 - core, half_ref, y_ref, prod_ref, send_refs)
+
+
+def products(share, pieces, p, side, half_ref, y_ref, prod_ref, out_refs):
+    me = lax.axis_index("cols")
+    pair = 2 * share
+    split = share % LANES == 0
+    size = share if split else pair
+    blocks = []
+    for q in range(2):
+        lo = ((me // 2) ^ (p + q)) * pair + (side * share if split else 0)
+        blocks.append(half_ref[:, pl.ds(pl.multiple_of(lo, LANES), size)])
+    slot = p // 2 % 2
+    prod_ref[slot] = lax.dot_general(
+        jnp.concatenate(blocks, axis=1), y_ref[...], (((0,), (0,)), ((), ())),
+        preferred_element_type=F32,
+    )
+    for q in range(2):
+        at = q * size + (0 if split else side * share)
+        for ref, (n, bits) in zip(out_refs, pieces):
+            ref[spot(p + q, bits)] = prod_ref[slot, pl.ds(pl.multiple_of(at, SUB), n), :]
+            at = at + n
+
+
+def keep_kernel(share, pieces, half_ref, y_ref, *refs):
+    core = lax.axis_index("cols") % 2
+    for p in range(0, half_ref.shape[1] // (2 * share), 2):
+        products(share, pieces, p, core, half_ref, y_ref, refs[-1], refs[:-1])
 
 
 LEFT = (0, 0, 1, 0, 1, 2)
@@ -323,26 +343,42 @@
     return sum(bool(2 * p & k) << i for i, k in enumerate(reversed(bits)))
 
 
+def product_shapes(share, pieces, rows, width):
+    out = [jax.ShapeDtypeStruct((rows // (2 * share), n, width), F32) for n, _ in pieces]
+    size = share if share % LANES == 0 else 2 * share
+    return out, pltpu.VMEM((2, 2 * size, width), F32)
+
+
 def mix(share, pieces, e, y, columns, weights):
     cols, rows = e.shape
-    width = y.shape[1]
-    out = [VMEM((cols, rows), BF16)]
-    for n, _ in pieces:
-        out += [jax.ShapeDtypeStruct((rows // (2 * share), n, width), F32)] * 2
-    half, *got = pl.pallas_call(
+    out, scratch = product_shapes(share, pieces, rows, y.shape[1])
+    half, *sends = pl.pallas_call(
         functools.partial(mix_kernel, share, pieces),
-        out_shape=tuple(out),
+        out_shape=(VMEM((cols, rows), BF16), *out),
         in_specs=full(13),
-        out_specs=tuple(full(len(out))),
+        out_specs=tuple(full(1 + len(out))),
         scratch_shapes=[
-            pltpu.VMEM((2, 2 * share, width), F32),
+            scratch,
             pltpu.VMEM((cols, LANES), BF16),
             pltpu.VMEM((LANES, rows), BF16),
         ],
         compiler_params=params(16),
         name="mix",
     )(e, y, *columns, *weights)
-    return half, got[0::2], got[1::2]
+    return half, sends
+
+
+def keep(share, pieces, half, y):
+    out, scratch = product_shapes(share, pieces, half.shape[1], y.shape[1])
+    return pl.pallas_call(
+        functools.partial(keep_kernel, share, pieces),
+        out_shape=tuple(out),
+        in_specs=full(2),
+        out_specs=tuple(full(len(out))),
+        scratch_shapes=[scratch],
+        compiler_params=params(16),
+        name="keep",
+    )(half, y)
 
 
 def back_kernel(total_cols, half_ref, x_ref, y_ref, e_ref, b_ref, r_ref, n_ref, sq_ref, bv2_ref,
@@ -537,9 +573,10 @@
     fbar1 = reduce_add(part)
     w1 = fbar1 / a
     pieces = routes(share, count)
-    half, keeps, sends = mix(
+    half, sends = mix(
         share, pieces, e, arch_points, (bv3, bv2, mid, br, vbr, gb1), (u3, w3, u2, w2, w1)
     )
+    keeps = keep(share, pieces, half, arch_points)
     terms, (pot, arch_grad, new_pot) = scatter_sum(
         keeps, sends, pieces, count, part,
         lambda after: back(

time: 128 us -> 127 us (level)
  waiting for transfers between devices: 46.7 us -> 45.2 us
    ppermute x48, waiting for transfers between devices: 46.7 us -> 45.2 us  [swap(): return lax.ppermute(v, 'cols', [(i, i ^ k) for i in range(count)])]
    pallas_call x1 -> x2, Pallas kernels: 5.01 us -> 4.93 us  [the longest x1 3.61 us: mix(): pl.pallas_call(functools.partial(mix_kernel, share, pieces), out_shape=(V...]
  transfers between devices with their start and end apart: 48 -> 48, of which waited for: 39 -> 39; matrix products, arithmetic and copies ran while one was open for 1% -> 1% of each run, Pallas kernels for 4% -> 6%
where the time goes in v6:
time: 127 us; the launch traced here: 126 us
  starting transfers between devices  50.3 us (40%)
  waiting for transfers between devices  45.2 us (36%)
  Pallas kernels  27.5 us (22%)
  other arithmetic  1.8 us (1%)
    ppermute x48, starting transfers between devices, swap(): return lax.ppermute(v, 'cols', [(i, i ^ k) for i in range(count)])  50.3 us
    ppermute x48, waiting for transfers between devices, swap(): return lax.ppermute(v, 'cols', [(i, i ^ k) for i in range(count)])  45.2 us
    pallas_call x4, Pallas kernels, sweep(): pl.pallas_call(functools.partial(sweep_kernel, kind), out_shape=(VMEM((co...  5.83 us
    pallas_call x1, Pallas kernels, scores(): pl.pallas_call(functools.partial(scores_kernel, total_cols, share), out_s...  5.83 us
    pallas_call x1, Pallas kernels, back(): pl.pallas_call(functools.partial(back_kernel, float(total_cols)), out_sha...  5.25 us
    pallas_call x1, Pallas kernels, plan(): pl.pallas_call(plan_kernel, out_shape=(VMEM((cols, rows), F32),) + (VMEM(...  4.33 us
    pallas_call x1, Pallas kernels, mix(): pl.pallas_call(functools.partial(mix_kernel, share, pieces), out_shape=(V...  3.61 us
  transfers between devices with their start and end apart: 48, of which 39 were waited for; matrix products, arithmetic and copies ran while one was open for 1% of the time, Pallas kernels for 6%

profile of v6, /device:TPU:0, one launch (start us, length us, event | category | flops | bytes accessed | tf_op | source)
XLA Modules:
  0.0 126.4 jit_solution(17684325059019638078)
XLA Ops:
  0.6 5.8 %scores.1 = (f32[1024,2048]{1,0:T(8,128)S(1)}, f32[1024,128]{1,0:T(8,128)S(1)}, f32[1024,128]{1,0:T(8,128)S(1)}, f32[1,2048]{1,0:T(1,128)}, f32[128,512]{1,0:T(8,128)S(1)}) custom-call(bf16[2048,512]{1,0:T(8,128)(2,1)} %x_ref.1, bf16[1024,512]{1,0:T(8,128)(2,1)} %y_ref.5, f32[1,1024]{1,0:T(1,128)} %bitcast.25), custom_call_target="tpu_custom_call" | custom-call | tf_op jit(solution)/shard_map/scores/pallas_call | solution.py:113
  6.5 2.5 %collective-permute-start.2 = (f32[1,2048]{1,0:T(1,128)}, f32[1,2048]{1,0:T(1,128)S(1)}, u32[]{:S(2)}, u32[]{:S(2)}) collective-permute-start(f32[1,2048]{1,0:T(1,128)} %get-tuple-element.54), channel_id=1, source_target_pairs={{0,3},{1,2},{2,1},{3,0},{4,7},{5,6},{6,5},{7,4},{8,11},{9,10},{10,... | collective-permute-start | bytes 24584 | tf_op jit(solution)/shard_map/ppermute | solution.py:442
  9.6 0.9 collective-permute-done.2
  10.5 2.3 %collective-permute-done.1 = f32[1,2048]{1,0:T(1,128)S(1)} collective-permute-done((f32[1,2048]{1,0:T(1,128)}, f32[1,2048]{1,0:T(1,128)S(1)}, u32[]{:S(2)}, u32[]{:S(2)}) %collective-permute-start.1) | collective-permute-done | bytes 8224 | tf_op jit(solution)/shard_map/ppermute | solution.py:442
  12.8 0.8 multiply_add_fusion.1
  13.6 3.7 %collective-permute-start.5 = (f32[1,2048]{1,0:T(1,128)S(1)}, f32[1,2048]{1,0:T(1,128)S(1)}, u32[]{:S(2)}, u32[]{:S(2)}) collective-permute-start(f32[1,2048]{1,0:T(1,128)S(1)} %multiply_add_fusion.1), channel_id=1, source_target_pairs={{0,12},{1,13},{2,14},{3,15},{4,8},{5,9},{6,10},{7,11},{8,4},{9,5},... | collective-permute-start | bytes 24584 | tf_op jit(solution)/shard_map/ppermute | solution.py:442
  17.3 0.8 collective-permute-start.3
  18.0 0.7 broadcast_multiply_fusion
  19.2 2.6 %collective-permute-done.4 = f32[1,2048]{1,0:T(1,128)S(1)} collective-permute-done((f32[1,2048]{1,0:T(1,128)S(1)}, f32[1,2048]{1,0:T(1,128)S(1)}, u32[]{:S(2)}, u32[]{:S(2)}) %collective-permute-start.4) | collective-permute-done | bytes 8224 | tf_op jit(solution)/shard_map/ppermute | solution.py:442
  21.9 4.3 %plan.1 = (f32[1024,2048]{1,0:T(8,128)S(1)}, f32[1024,128]{1,0:T(8,128)S(1)}, f32[1024,128]{1,0:T(8,128)S(1)}, f32[1024,128]{1,0:T(8,128)S(1)}, f32[1024,128]{1,0:T(8,128)S(1)}, /*index=5*/f32[1,2048]{1,0:T(1,128)S(1)}) custom-call(f32[1024,2048]{1,0:T(8,128)S(1)} %get-tuple-element.51.z_ref, ...), custom_call_target="tpu_custom_call", output_to_operand_aliasing={{0}: (0, {})} | custom-call | tf_op jit(solution)/shard_map/plan/pallas_call | solution.py:214
  26.3 0.7 collective-permute-start.7
  27.0 1.1 collective-permute-start.6
  28.1 1.2 collective-permute-done.8
  30.0 1.5 %collective-permute-start.11 = (f32[1,2048]{1,0:T(1,128)S(1)}, f32[1,2048]{1,0:T(1,128)S(1)}, u32[]{:S(2)}, u32[]{:S(2)}) collective-permute-start(f32[1,2048]{1,0:T(1,128)S(1)} %add_add_fusion.5), channel_id=1, source_target_pairs={{0,12},{1,13},{2,14},{3,15},{4,8},{5,9},{6,10},{7,11},{8,4},{9,5},... | collective-permute-start | bytes 24584 | tf_op jit(solution)/shard_map/ppermute | solution.py:442
  32.2 2.3 %collective-permute-start.9 = (f32[1,2048]{1,0:T(1,128)S(1)}, f32[1,2048]{1,0:T(1,128)S(1)}, u32[]{:S(2)}, u32[]{:S(2)}) collective-permute-start(f32[1,2048]{1,0:T(1,128)S(1)} %add_add_fusion.5), channel_id=1, source_target_pairs={{0,4},{1,5},{2,6},{3,7},{4,0},{5,1},{6,2},{7,3},{8,12},{9,13},{10,... | collective-permute-start | bytes 24584 | tf_op jit(solution)/shard_map/ppermute | solution.py:442
  34.5 1.1 collective-permute-done.11
  36.2 1.4 %sweep_fwd.2 = (f32[1024,128]{1,0:T(8,128)S(1)}, f32[1,2048]{1,0:T(1,128)S(1)}) custom-call(f32[1024,2048]{1,0:T(8,128)S(1)} %get-tuple-element.55.e_ref, f32[1024,128]{1,0:T(8,128)S(1)} %get-tuple-element.52.b_ref, f32[1,2048]{1,0:T(1,128)S(1)} %add_divide_fusion.1.refs_0_.refs_8_), custom_call_target="tpu_custom_call" | custom-call | tf_op jit(solution)/shard_map/sweep_fwd/pallas_call | solution.py:253
  37.7 0.7 collective-permute-start.13
  38.4 1.1 collective-permute-start.12
  39.6 1.2 collective-permute-done.14
  41.5 2.6 %collective-permute-start.17 = (f32[1,2048]{1,0:T(1,128)S(1)}, f32[1,2048]{1,0:T(1,128)S(1)}, u32[]{:S(2)}, u32[]{:S(2)}) collective-permute-start(f32[1,2048]{1,0:T(1,128)S(1)} %add_add_fusion.4), channel_id=1, source_target_pairs={{0,12},{1,13},{2,14},{3,15},{4,8},{5,9},{6,10},{7,11},{8,4},{9,5},... | collective-permute-start | bytes 24584 | tf_op jit(solution)/shard_map/ppermute | solution.py:442
  44.0 0.9 collective-permute-start.16
  44.9 1.0 collective-permute-start.15
  45.9 1.1 collective-permute-done.17
  47.0 1.6 %collective-permute-done.16 = f32[1,2048]{1,0:T(1,128)S(1)} collective-permute-done((f32[1,2048]{1,0:T(1,128)S(1)}, f32[1,2048]{1,0:T(1,128)S(1)}, u32[]{:S(2)}, u32[]{:S(2)}) %collective-permute-start.16) | collective-permute-done | bytes 8224 | tf_op jit(solution)/shard_map/ppermute | solution.py:442
  48.7 1.4 %sweep_fwd.3 = (f32[1024,128]{1,0:T(8,128)S(1)}, f32[1,2048]{1,0:T(1,128)S(1)}) custom-call(f32[1024,2048]{1,0:T(8,128)S(1)} %get-tuple-element.55.e_ref, f32[1024,128]{1,0:T(8,128)S(1)} %get-tuple-element.52.b_ref, f32[1,2048]{1,0:T(1,128)S(1)} %add_divide_fusion.refs_0_.refs_6_.u3_ref), custom_call_target="tpu_custom_call" | custom-call | tf_op jit(solution)/shard_map/sweep_fwd/pallas_call | solution.py:253
  50.9 1.1 collective-permute-start.18
  52.0 1.2 collective-permute-done.20
  53.9 1.4 %collective-permute-start.23 = (f32[1,2048]{1,0:T(1,128)S(1)}, f32[1,2048]{1,0:T(1,128)S(1)}, u32[]{:S(2)}, u32[]{:S(2)}) collective-permute-start(f32[1,2048]{1,0:T(1,128)S(1)} %add_add_fusion.3), channel_id=1, source_target_pairs={{0,12},{1,13},{2,14},{3,15},{4,8},{5,9},{6,10},{7,11},{8,4},{9,5},... | collective-permute-start | bytes 24584 | tf_op jit(solution)/shard_map/ppermute | solution.py:442
  55.4 1.0 collective-permute-start.22
  56.4 2.0 %collective-permute-start.21 = (f32[1,2048]{1,0:T(1,128)S(1)}, f32[1,2048]{1,0:T(1,128)S(1)}, u32[]{:S(2)}, u32[]{:S(2)}) collective-permute-start(f32[1,2048]{1,0:T(1,128)S(1)} %add_add_fusion.3), channel_id=1, source_target_pairs={{0,4},{1,5},{2,6},{3,7},{4,0},{5,1},{6,2},{7,3},{8,12},{9,13},{10,... | collective-permute-start | bytes 24584 | tf_op jit(solution)/shard_map/ppermute | solution.py:442
  58.4 1.1 collective-permute-done.23
  60.0 1.4 %sweep_mid.1 = (f32[1024,128]{1,0:T(8,128)S(1)}, f32[1,2048]{1,0:T(1,128)S(1)}) custom-call(f32[1024,2048]{1,0:T(8,128)S(1)} %get-tuple-element.55.e_ref, f32[1024,128]{1,0:T(8,128)S(1)} %get-tuple-element.52.b_ref, f32[1024,128]{1,0:T(8,128)S(1)} %get-tuple-element.59.refs_0_.refs_1_.bv2_ref, f32[1,2048]{1,0:T(1,128)S(1)} %get-tuple-element.102.refs_1_.refs_7_), custom_call_target="tpu_custom_call" | custom-call | tf_op jit(solution)/shard_map/sweep_mid/pallas_call | solution.py:253
  61.5 0.7 collective-permute-start.25
  62.2 1.1 collective-permute-start.24
  63.4 1.2 collective-permute-done.26
  65.3 2.6 %collective-permute-start.29 = (f32[1,2048]{1,0:T(1,128)S(1)}, f32[1,2048]{1,0:T(1,128)S(1)}, u32[]{:S(2)}, u32[]{:S(2)}) collective-permute-start(f32[1,2048]{1,0:T(1,128)S(1)} %add_add_fusion.2), channel_id=1, source_target_pairs={{0,12},{1,13},{2,14},{3,15},{4,8},{5,9},{6,10},{7,11},{8,4},{9,5},... | collective-permute-start | bytes 24584 | tf_op jit(solution)/shard_map/ppermute | solution.py:442
  67.9 1.0 collective-permute-start.28
  68.8 0.9 collective-permute-start.27
  69.7 1.1 collective-permute-done.29
  70.8 1.6 %collective-permute-done.28 = f32[1,2048]{1,0:T(1,128)S(1)} collective-permute-done((f32[1,2048]{1,0:T(1,128)S(1)}, f32[1,2048]{1,0:T(1,128)S(1)}, u32[]{:S(2)}, u32[]{:S(2)}) %collective-permute-start.28) | collective-permute-done | bytes 8224 | tf_op jit(solution)/shard_map/ppermute | solution.py:442
  72.5 1.6 %sweep_bwd.1 = (f32[1024,128]{1,0:T(8,128)S(1)}, f32[1,2048]{1,0:T(1,128)S(1)}) custom-call(f32[1024,2048]{1,0:T(8,128)S(1)} %get-tuple-element.55.e_ref, f32[1024,128]{1,0:T(8,128)S(1)} %get-tuple-element.62.b_ref.refs_3_, f32[1024,128]{1,0:T(8,128)S(1)} %get-tuple-element.64.refs_0_.r_ref, f32[1,2048]{1,0:T(1,128)S(1)} %get-tuple-element.100.refs_1_.refs_9_), custom_call_target="tpu_custom_call" | custom-call | tf_op jit(solution)/shard_map/sweep_bwd/pallas_call | solution.py:253
  74.9 1.1 collective-permute-start.30
  76.1 1.2 collective-permute-done.32
  78.0 1.4 %collective-permute-start.35 = (f32[1,2048]{1,0:T(1,128)S(1)}, f32[1,2048]{1,0:T(1,128)S(1)}, u32[]{:S(2)}, u32[]{:S(2)}) collective-permute-start(f32[1,2048]{1,0:T(1,128)S(1)} %add_add_fusion.1), channel_id=1, source_target_pairs={{0,12},{1,13},{2,14},{3,15},{4,8},{5,9},{6,10},{7,11},{8,4},{9,5},... | collective-permute-start | bytes 24584 | tf_op jit(solution)/shard_map/ppermute | solution.py:442
  79.4 1.0 collective-permute-start.34
  80.4 2.0 %collective-permute-start.33 = (f32[1,2048]{1,0:T(1,128)S(1)}, f32[1,2048]{1,0:T(1,128)S(1)}, u32[]{:S(2)}, u32[]{:S(2)}) collective-permute-start(f32[1,2048]{1,0:T(1,128)S(1)} %add_add_fusion.1), channel_id=1, source_target_pairs={{0,4},{1,5},{2,6},{3,7},{4,0},{5,1},{6,2},{7,3},{8,12},{9,13},{10,... | collective-permute-start | bytes 24584 | tf_op jit(solution)/shard_map/ppermute | solution.py:442
  82.4 1.1 collective-permute-done.35
  84.1 3.6 %mix.1 = (bf16[1024,2048]{1,0:T(8,128)(2,1)S(1)}, f32[8,48,512]{2,1,0:T(8,128)S(1)}, f32[8,48,512]{2,1,0:T(8,128)S(1)}, f32[8,32,512]{2,1,0:T(8,128)S(1)}) custom-call(f32[1024,2048]{1,0:T(8,128)S(1)} %get-tuple-element.55.e_ref, bf16[1024,512]{1,0:T(8,128)(2,1)S(1)} %copy-done, f32[1024,128]{1,0:T(8,128)S(1)} %get-tuple-element.58.refs_0_.bv3_ref, ...), custom_call_target="tpu_custom_call" | custom-call | tf_op jit(solution)/shard_map/mix/pallas_call | solution.py:355
  88.4 1.3 %keep.1 = (f32[8,48,512]{2,1,0:T(8,128)S(1)}, f32[8,48,512]{2,1,0:T(8,128)S(1)}, f32[8,32,512]{2,1,0:T(8,128)S(1)}) custom-call(bf16[1024,2048]{1,0:T(8,128)(2,1)S(1)} %get-tuple-element.68.half_ref, bf16[1024,512]{1,0:T(8,128)(2,1)S(1)} %copy-done), custom_call_target="tpu_custom_call" | custom-call | tf_op jit(solution)/shard_map/keep/pallas_call | solution.py:373
  90.2 0.7 collective-permute-start.39
  92.0 2.1 %collective-permute-start.40 = (f32[4,32,512]{2,1,0:T(8,128)S(1)}, f32[4,32,512]{2,1,0:T(8,128)S(1)}, u32[]{:S(2)}, u32[]{:S(2)}) collective-permute-start(f32[4,32,512]{2,1,0:T(8,128)S(1)} %get-tuple-element.78.after_ref), channel_id=1, source_target_pairs={{0,4},{1,5},{2,6},{3,7},{4,0},{5,1},{6,2},{7,3},{8,12},{9,13},{10,... | collective-permute-start | bytes 786440 | tf_op jit(solution)/shard_map/ppermute | solution.py:442
  94.8 5.2 %back.1 = (f32[1,1024]{1,0:T(1,128)}, f32[1024,512]{1,0:T(8,128)}, f32[1,2048]{1,0:T(1,128)}) custom-call(bf16[1024,2048]{1,0:T(8,128)(2,1)S(1)} %get-tuple-element.68.half_ref, bf16[2048,512]{1,0:T(8,128)(2,1)S(1)} %copy-done.1, bf16[1024,512]{1,0:T(8,128)(2,1)S(1)} %copy-done, f32[1024,2048]{1,0:T(8,128)S(1)} %get-tuple-element.55.e_ref, ...), custom_call_target="tpu_custom_call" | custom-call | flops 2147483648 | bytes 16777216 | tf_op jit(solution)/shard_map/back/pallas_call | solution.py:423
  101.4 0.8 collective-permute-done.39.got_ref
  102.3 2.1 %collective-permute-start.41 = (f32[2,48,512]{2,1,0:T(8,128)S(1)}, f32[2,48,512]{2,1,0:T(8,128)S(1)}, u32[]{:S(2)}, u32[]{:S(2)}) collective-permute-start(f32[2,48,512]{2,1,0:T(8,128)S(1)} %get-tuple-element.86.after_ref), channel_id=1, source_target_pairs={{0,4},{1,5},{2,6},{3,7},{4,0},{5,1},{6,2},{7,3},{8,12},{9,13},{10,... | collective-permute-start | bytes 589832 | tf_op jit(solution)/shard_map/ppermute | solution.py:442
  104.4 1.0 collective-permute-start.42
  105.4 5.1 %collective-permute-done.42.got_ref = f32[2,32,512]{2,1,0:T(8,128)S(1)} collective-permute-done((f32[2,32,512]{2,1,0:T(8,128)S(1)}, f32[2,32,512]{2,1,0:T(8,128)S(1)}, u32[]{:S(2)}, u32[]{:S(2)}) %collective-permute-start.42) | collective-permute-done | bytes 131104 | tf_op jit(solution)/shard_map/ppermute | solution.py:442
  110.9 1.7 %collective-permute-start.45 = (f32[2,48,512]{2,1,0:T(8,128)S(1)}, f32[2,48,512]{2,1,0:T(8,128)S(1)}, u32[]{:S(2)}, u32[]{:S(2)}) collective-permute-start(f32[2,48,512]{2,1,0:T(8,128)S(1)} %get-tuple-element.93.after_ref), channel_id=1, source_target_pairs={{0,4},{1,5},{2,6},{3,7},{4,0},{5,1},{6,2},{7,3},{8,12},{9,13},{10,... | collective-permute-start | bytes 589832 | tf_op jit(solution)/shard_map/ppermute | solution.py:442
  112.6 1.1 collective-permute-start.43
  113.7 5.7 %collective-permute-done.45.got_ref = f32[2,48,512]{2,1,0:T(8,128)S(1)} collective-permute-done((f32[2,48,512]{2,1,0:T(8,128)S(1)}, f32[2,48,512]{2,1,0:T(8,128)S(1)}, u32[]{:S(2)}, u32[]{:S(2)}) %collective-permute-start.45) | collective-permute-done | bytes 196640 | tf_op jit(solution)/shard_map/ppermute | solution.py:442
  119.5 0.7 collective-permute-start.47
  120.2 3.6 %collective-permute-done.47 = f32[1,32,512]{2,1,0:T(8,128)S(1)} collective-permute-done((f32[1,32,512]{2,1,0:T(8,128)S(1)}, f32[1,32,512]{2,1,0:T(8,128)S(1)}, u32[]{:S(2)}, u32[]{:S(2)}) %collective-permute-start.47) | collective-permute-done | bytes 65568 | tf_op jit(solution)/shard_map/ppermute | solution.py:442
  123.8 1.7 %collective-permute-done.46 = f32[1,48,512]{2,1,0:T(8,128)S(1)} collective-permute-done((f32[1,48,512]{2,1,0:T(8,128)S(1)}, f32[1,48,512]{2,1,0:T(8,128)S(1)}, u32[]{:S(2)}, u32[]{:S(2)}) %collective-permute-start.46) | collective-permute-done | bytes 98336 | tf_op jit(solution)/shard_map/ppermute | solution.py:442
  125.5 0.9 gradient.1
  (71 shorter events, 13.8 us)
Async XLA Ops:
  6.5 4.0 %collective-permute-start.2 = (f32[1,2048]{1,0:T(1,128)}, f32[1,2048]{1,0:T(1,128)S(1)}, u32[]{:S(2)}, u32[]{:S(2)}) collective-permute-start(f32[1,2048]{1,0:T(1,128)} %get-tuple-element.54), channel_id=1, source_target_pairs={{0,3},{1,2},{2,1},{3,0},{4,7},{5,6},{6,5},{7,4},{8,11},{9,10},{10,... | collective-permute-start | bytes 24584 | tf_op jit(solution)/shard_map/ppermute | solution.py:442
  8.9 3.9 %collective-permute-start.1 = (f32[1,2048]{1,0:T(1,128)}, f32[1,2048]{1,0:T(1,128)S(1)}, u32[]{:S(2)}, u32[]{:S(2)}) collective-permute-start(f32[1,2048]{1,0:T(1,128)} %get-tuple-element.54), channel_id=1, source_target_pairs={{0,2},{1,3},{2,0},{3,1},{4,6},{5,7},{6,4},{7,5},{8,10},{9,11},{10,... | collective-permute-start | bytes 24584 | tf_op jit(solution)/shard_map/ppermute | solution.py:442
  9.6 3.2 %collective-permute-start = (f32[1,2048]{1,0:T(1,128)}, f32[1,2048]{1,0:T(1,128)S(1)}, u32[]{:S(2)}, u32[]{:S(2)}) collective-permute-start(f32[1,2048]{1,0:T(1,128)} %get-tuple-element.54), channel_id=1, source_target_pairs={{0,1},{1,0},{2,3},{3,2},{4,5},{5,4},{6,7},{7,6},{8,9},{9,8},{10,11... | collective-permute-start | bytes 24584 | tf_op jit(solution)/shard_map/ppermute | solution.py:442
  13.6 5.6 %collective-permute-start.5 = (f32[1,2048]{1,0:T(1,128)S(1)}, f32[1,2048]{1,0:T(1,128)S(1)}, u32[]{:S(2)}, u32[]{:S(2)}) collective-permute-start(f32[1,2048]{1,0:T(1,128)S(1)} %multiply_add_fusion.1), channel_id=1, source_target_pairs={{0,12},{1,13},{2,14},{3,15},{4,8},{5,9},{6,10},{7,11},{8,4},{9,5},... | collective-permute-start | bytes 24584 | tf_op jit(solution)/shard_map/ppermute | solution.py:442
  17.3 4.5 %collective-permute-start.4 = (f32[1,2048]{1,0:T(1,128)S(1)}, f32[1,2048]{1,0:T(1,128)S(1)}, u32[]{:S(2)}, u32[]{:S(2)}) collective-permute-start(f32[1,2048]{1,0:T(1,128)S(1)} %multiply_add_fusion.1), channel_id=1, source_target_pairs={{0,8},{1,9},{2,10},{3,11},{4,12},{5,13},{6,14},{7,15},{8,0},{9,1},... | collective-permute-start | bytes 24584 | tf_op jit(solution)/shard_map/ppermute | solution.py:442
  17.3 4.5 %collective-permute-start.3 = (f32[1,2048]{1,0:T(1,128)S(1)}, f32[1,2048]{1,0:T(1,128)S(1)}, u32[]{:S(2)}, u32[]{:S(2)}) collective-permute-start(f32[1,2048]{1,0:T(1,128)S(1)} %multiply_add_fusion.1), channel_id=1, source_target_pairs={{0,4},{1,5},{2,6},{3,7},{4,0},{5,1},{6,2},{7,3},{8,12},{9,13},{10,... | collective-permute-start | bytes 24584 | tf_op jit(solution)/shard_map/ppermute | solution.py:442
  26.2 3.1 %collective-permute-start.8 = (f32[1,2048]{1,0:T(1,128)S(1)}, f32[1,2048]{1,0:T(1,128)S(1)}, u32[]{:S(2)}, u32[]{:S(2)}) collective-permute-start(f32[1,2048]{1,0:T(1,128)S(1)} %get-tuple-element.56), channel_id=1, source_target_pairs={{0,3},{1,2},{2,1},{3,0},{4,7},{5,6},{6,5},{7,4},{8,11},{9,10},{10,... | collective-permute-start | bytes 24584 | tf_op jit(solution)/shard_map/ppermute | solution.py:442
  26.3 3.7 %collective-permute-start.7 = (f32[1,2048]{1,0:T(1,128)S(1)}, f32[1,2048]{1,0:T(1,128)S(1)}, u32[]{:S(2)}, u32[]{:S(2)}) collective-permute-start(f32[1,2048]{1,0:T(1,128)S(1)} %get-tuple-element.56), channel_id=1, source_target_pairs={{0,2},{1,3},{2,0},{3,1},{4,6},{5,7},{6,4},{7,5},{8,10},{9,11},{10,... | collective-permute-start | bytes 24584 | tf_op jit(solution)/shard_map/ppermute | solution.py:442
  27.0 3.0 %collective-permute-start.6 = (f32[1,2048]{1,0:T(1,128)S(1)}, f32[1,2048]{1,0:T(1,128)S(1)}, u32[]{:S(2)}, u32[]{:S(2)}) collective-permute-start(f32[1,2048]{1,0:T(1,128)S(1)} %get-tuple-element.56), channel_id=1, source_target_pairs={{0,1},{1,0},{2,3},{3,2},{4,5},{5,4},{6,7},{7,6},{8,9},{9,8},{10,11... | collective-permute-start | bytes 24584 | tf_op jit(solution)/shard_map/ppermute | solution.py:442
  30.0 5.6 %collective-permute-start.11 = (f32[1,2048]{1,0:T(1,128)S(1)}, f32[1,2048]{1,0:T(1,128)S(1)}, u32[]{:S(2)}, u32[]{:S(2)}) collective-permute-start(f32[1,2048]{1,0:T(1,128)S(1)} %add_add_fusion.5), channel_id=1, source_target_pairs={{0,12},{1,13},{2,14},{3,15},{4,8},{5,9},{6,10},{7,11},{8,4},{9,5},... | collective-permute-start | bytes 24584 | tf_op jit(solution)/shard_map/ppermute | solution.py:442
  31.6 4.6 %collective-permute-start.10 = (f32[1,2048]{1,0:T(1,128)S(1)}, f32[1,2048]{1,0:T(1,128)S(1)}, u32[]{:S(2)}, u32[]{:S(2)}) collective-permute-start(f32[1,2048]{1,0:T(1,128)S(1)} %add_add_fusion.5), channel_id=1, source_target_pairs={{0,8},{1,9},{2,10},{3,11},{4,12},{5,13},{6,14},{7,15},{8,0},{9,1},... | collective-permute-start | bytes 24584 | tf_op jit(solution)/shard_map/ppermute | solution.py:442
  32.2 4.0 %collective-permute-start.9 = (f32[1,2048]{1,0:T(1,128)S(1)}, f32[1,2048]{1,0:T(1,128)S(1)}, u32[]{:S(2)}, u32[]{:S(2)}) collective-permute-start(f32[1,2048]{1,0:T(1,128)S(1)} %add_add_fusion.5), channel_id=1, source_target_pairs={{0,4},{1,5},{2,6},{3,7},{4,0},{5,1},{6,2},{7,3},{8,12},{9,13},{10,... | collective-permute-start | bytes 24584 | tf_op jit(solution)/shard_map/ppermute | solution.py:442
  37.6 3.1 %collective-permute-start.14 = (f32[1,2048]{1,0:T(1,128)S(1)}, f32[1,2048]{1,0:T(1,128)S(1)}, u32[]{:S(2)}, u32[]{:S(2)}) collective-permute-start(f32[1,2048]{1,0:T(1,128)S(1)} %get-tuple-element.57), channel_id=1, source_target_pairs={{0,3},{1,2},{2,1},{3,0},{4,7},{5,6},{6,5},{7,4},{8,11},{9,10},{10,... | collective-permute-start | bytes 24584 | tf_op jit(solution)/shard_map/ppermute | solution.py:442
  37.7 3.7 %collective-permute-start.13 = (f32[1,2048]{1,0:T(1,128)S(1)}, f32[1,2048]{1,0:T(1,128)S(1)}, u32[]{:S(2)}, u32[]{:S(2)}) collective-permute-start(f32[1,2048]{1,0:T(1,128)S(1)} %get-tuple-element.57), channel_id=1, source_target_pairs={{0,2},{1,3},{2,0},{3,1},{4,6},{5,7},{6,4},{7,5},{8,10},{9,11},{10,... | collective-permute-start | bytes 24584 | tf_op jit(solution)/shard_map/ppermute | solution.py:442
  38.4 3.0 %collective-permute-start.12 = (f32[1,2048]{1,0:T(1,128)S(1)}, f32[1,2048]{1,0:T(1,128)S(1)}, u32[]{:S(2)}, u32[]{:S(2)}) collective-permute-start(f32[1,2048]{1,0:T(1,128)S(1)} %get-tuple-element.57), channel_id=1, source_target_pairs={{0,1},{1,0},{2,3},{3,2},{4,5},{5,4},{6,7},{7,6},{8,9},{9,8},{10,11... | collective-permute-start | bytes 24584 | tf_op jit(solution)/shard_map/ppermute | solution.py:442
  41.5 5.5 %collective-permute-start.17 = (f32[1,2048]{1,0:T(1,128)S(1)}, f32[1,2048]{1,0:T(1,128)S(1)}, u32[]{:S(2)}, u32[]{:S(2)}) collective-permute-start(f32[1,2048]{1,0:T(1,128)S(1)} %add_add_fusion.4), channel_id=1, source_target_pairs={{0,12},{1,13},{2,14},{3,15},{4,8},{5,9},{6,10},{7,11},{8,4},{9,5},... | collective-permute-start | bytes 24584 | tf_op jit(solution)/shard_map/ppermute | solution.py:442
  44.0 4.6 %collective-permute-start.16 = (f32[1,2048]{1,0:T(1,128)S(1)}, f32[1,2048]{1,0:T(1,128)S(1)}, u32[]{:S(2)}, u32[]{:S(2)}) collective-permute-start(f32[1,2048]{1,0:T(1,128)S(1)} %add_add_fusion.4), channel_id=1, source_target_pairs={{0,8},{1,9},{2,10},{3,11},{4,12},{5,13},{6,14},{7,15},{8,0},{9,1},... | collective-permute-start | bytes 24584 | tf_op jit(solution)/shard_map/ppermute | solution.py:442
  44.9 3.7 %collective-permute-start.15 = (f32[1,2048]{1,0:T(1,128)S(1)}, f32[1,2048]{1,0:T(1,128)S(1)}, u32[]{:S(2)}, u32[]{:S(2)}) collective-permute-start(f32[1,2048]{1,0:T(1,128)S(1)} %add_add_fusion.4), channel_id=1, source_target_pairs={{0,4},{1,5},{2,6},{3,7},{4,0},{5,1},{6,2},{7,3},{8,12},{9,13},{10,... | collective-permute-start | bytes 24584 | tf_op jit(solution)/shard_map/ppermute | solution.py:442
  50.1 3.1 %collective-permute-start.20 = (f32[1,2048]{1,0:T(1,128)S(1)}, f32[1,2048]{1,0:T(1,128)S(1)}, u32[]{:S(2)}, u32[]{:S(2)}) collective-permute-start(f32[1,2048]{1,0:T(1,128)S(1)} %get-tuple-element.60), channel_id=1, source_target_pairs={{0,3},{1,2},{2,1},{3,0},{4,7},{5,6},{6,5},{7,4},{8,11},{9,10},{10,... | collective-permute-start | bytes 24584 | tf_op jit(solution)/shard_map/ppermute | solution.py:442
  50.2 3.7 %collective-permute-start.19 = (f32[1,2048]{1,0:T(1,128)S(1)}, f32[1,2048]{1,0:T(1,128)S(1)}, u32[]{:S(2)}, u32[]{:S(2)}) collective-permute-start(f32[1,2048]{1,0:T(1,128)S(1)} %get-tuple-element.60), channel_id=1, source_target_pairs={{0,2},{1,3},{2,0},{3,1},{4,6},{5,7},{6,4},{7,5},{8,10},{9,11},{10,... | collective-permute-start | bytes 24584 | tf_op jit(solution)/shard_map/ppermute | solution.py:442
  50.9 3.0 %collective-permute-start.18 = (f32[1,2048]{1,0:T(1,128)S(1)}, f32[1,2048]{1,0:T(1,128)S(1)}, u32[]{:S(2)}, u32[]{:S(2)}) collective-permute-start(f32[1,2048]{1,0:T(1,128)S(1)} %get-tuple-element.60), channel_id=1, source_target_pairs={{0,1},{1,0},{2,3},{3,2},{4,5},{5,4},{6,7},{7,6},{8,9},{9,8},{10,11... | collective-permute-start | bytes 24584 | tf_op jit(solution)/shard_map/ppermute | solution.py:442
  53.9 5.5 %collective-permute-start.23 = (f32[1,2048]{1,0:T(1,128)S(1)}, f32[1,2048]{1,0:T(1,128)S(1)}, u32[]{:S(2)}, u32[]{:S(2)}) collective-permute-start(f32[1,2048]{1,0:T(1,128)S(1)} %add_add_fusion.3), channel_id=1, source_target_pairs={{0,12},{1,13},{2,14},{3,15},{4,8},{5,9},{6,10},{7,11},{8,4},{9,5},... | collective-permute-start | bytes 24584 | tf_op jit(solution)/shard_map/ppermute | solution.py:442
  55.4 4.5 %collective-permute-start.22 = (f32[1,2048]{1,0:T(1,128)S(1)}, f32[1,2048]{1,0:T(1,128)S(1)}, u32[]{:S(2)}, u32[]{:S(2)}) collective-permute-start(f32[1,2048]{1,0:T(1,128)S(1)} %add_add_fusion.3), channel_id=1, source_target_pairs={{0,8},{1,9},{2,10},{3,11},{4,12},{5,13},{6,14},{7,15},{8,0},{9,1},... | collective-permute-start | bytes 24584 | tf_op jit(solution)/shard_map/ppermute | solution.py:442
  56.4 3.7 %collective-permute-start.21 = (f32[1,2048]{1,0:T(1,128)S(1)}, f32[1,2048]{1,0:T(1,128)S(1)}, u32[]{:S(2)}, u32[]{:S(2)}) collective-permute-start(f32[1,2048]{1,0:T(1,128)S(1)} %add_add_fusion.3), channel_id=1, source_target_pairs={{0,4},{1,5},{2,6},{3,7},{4,0},{5,1},{6,2},{7,3},{8,12},{9,13},{10,... | collective-permute-start | bytes 24584 | tf_op jit(solution)/shard_map/ppermute | solution.py:442
  61.5 3.1 %collective-permute-start.26 = (f32[1,2048]{1,0:T(1,128)S(1)}, f32[1,2048]{1,0:T(1,128)S(1)}, u32[]{:S(2)}, u32[]{:S(2)}) collective-permute-start(f32[1,2048]{1,0:T(1,128)S(1)} %get-tuple-element.65), channel_id=1, source_target_pairs={{0,3},{1,2},{2,1},{3,0},{4,7},{5,6},{6,5},{7,4},{8,11},{9,10},{10,... | collective-permute-start | bytes 24584 | tf_op jit(solution)/shard_map/ppermute | solution.py:442
  61.5 3.7 %collective-permute-start.25 = (f32[1,2048]{1,0:T(1,128)S(1)}, f32[1,2048]{1,0:T(1,128)S(1)}, u32[]{:S(2)}, u32[]{:S(2)}) collective-permute-start(f32[1,2048]{1,0:T(1,128)S(1)} %get-tuple-element.65), channel_id=1, source_target_pairs={{0,2},{1,3},{2,0},{3,1},{4,6},{5,7},{6,4},{7,5},{8,10},{9,11},{10,... | collective-permute-start | bytes 24584 | tf_op jit(solution)/shard_map/ppermute | solution.py:442
  62.2 3.0 %collective-permute-start.24 = (f32[1,2048]{1,0:T(1,128)S(1)}, f32[1,2048]{1,0:T(1,128)S(1)}, u32[]{:S(2)}, u32[]{:S(2)}) collective-permute-start(f32[1,2048]{1,0:T(1,128)S(1)} %get-tuple-element.65), channel_id=1, source_target_pairs={{0,1},{1,0},{2,3},{3,2},{4,5},{5,4},{6,7},{7,6},{8,9},{9,8},{10,11... | collective-permute-start | bytes 24584 | tf_op jit(solution)/shard_map/ppermute | solution.py:442
  65.3 5.5 %collective-permute-start.29 = (f32[1,2048]{1,0:T(1,128)S(1)}, f32[1,2048]{1,0:T(1,128)S(1)}, u32[]{:S(2)}, u32[]{:S(2)}) collective-permute-start(f32[1,2048]{1,0:T(1,128)S(1)} %add_add_fusion.2), channel_id=1, source_target_pairs={{0,12},{1,13},{2,14},{3,15},{4,8},{5,9},{6,10},{7,11},{8,4},{9,5},... | collective-permute-start | bytes 24584 | tf_op jit(solution)/shard_map/ppermute | solution.py:442
  67.9 4.5 %collective-permute-start.28 = (f32[1,2048]{1,0:T(1,128)S(1)}, f32[1,2048]{1,0:T(1,128)S(1)}, u32[]{:S(2)}, u32[]{:S(2)}) collective-permute-start(f32[1,2048]{1,0:T(1,128)S(1)} %add_add_fusion.2), channel_id=1, source_target_pairs={{0,8},{1,9},{2,10},{3,11},{4,12},{5,13},{6,14},{7,15},{8,0},{9,1},... | collective-permute-start | bytes 24584 | tf_op jit(solution)/shard_map/ppermute | solution.py:442
  68.8 3.7 %collective-permute-start.27 = (f32[1,2048]{1,0:T(1,128)S(1)}, f32[1,2048]{1,0:T(1,128)S(1)}, u32[]{:S(2)}, u32[]{:S(2)}) collective-permute-start(f32[1,2048]{1,0:T(1,128)S(1)} %add_add_fusion.2), channel_id=1, source_target_pairs={{0,4},{1,5},{2,6},{3,7},{4,0},{5,1},{6,2},{7,3},{8,12},{9,13},{10,... | collective-permute-start | bytes 24584 | tf_op jit(solution)/shard_map/ppermute | solution.py:442
  72.5 11.6 %copy-start = (bf16[1024,512]{1,0:T(8,128)(2,1)S(1)}, bf16[1024,512]{1,0:T(8,128)(2,1)}, u32[]{:S(2)}) copy-start(bf16[1024,512]{1,0:T(8,128)(2,1)} %y_ref.5) | copy-start | bytes 3145732
  74.1 3.1 %collective-permute-start.32 = (f32[1,2048]{1,0:T(1,128)S(1)}, f32[1,2048]{1,0:T(1,128)S(1)}, u32[]{:S(2)}, u32[]{:S(2)}) collective-permute-start(f32[1,2048]{1,0:T(1,128)S(1)} %get-tuple-element.67.after_ref), channel_id=1, source_target_pairs={{0,3},{1,2},{2,1},{3,0},{4,7},{5,6},{6,5},{7,4},{8,11},{9,10},{10,... | collective-permute-start | bytes 24584 | tf_op jit(solution)/shard_map/ppermute | solution.py:442
  74.2 3.7 %collective-permute-start.31 = (f32[1,2048]{1,0:T(1,128)S(1)}, f32[1,2048]{1,0:T(1,128)S(1)}, u32[]{:S(2)}, u32[]{:S(2)}) collective-permute-start(f32[1,2048]{1,0:T(1,128)S(1)} %get-tuple-element.67.after_ref), channel_id=1, source_target_pairs={{0,2},{1,3},{2,0},{3,1},{4,6},{5,7},{6,4},{7,5},{8,10},{9,11},{10,... | collective-permute-start | bytes 24584 | tf_op jit(solution)/shard_map/ppermute | solution.py:442
  74.9 3.0 %collective-permute-start.30 = (f32[1,2048]{1,0:T(1,128)S(1)}, f32[1,2048]{1,0:T(1,128)S(1)}, u32[]{:S(2)}, u32[]{:S(2)}) collective-permute-start(f32[1,2048]{1,0:T(1,128)S(1)} %get-tuple-element.67.after_ref), channel_id=1, source_target_pairs={{0,1},{1,0},{2,3},{3,2},{4,5},{5,4},{6,7},{7,6},{8,9},{9,8},{10,11... | collective-permute-start | bytes 24584 | tf_op jit(solution)/shard_map/ppermute | solution.py:442
  78.0 5.5 %collective-permute-start.35 = (f32[1,2048]{1,0:T(1,128)S(1)}, f32[1,2048]{1,0:T(1,128)S(1)}, u32[]{:S(2)}, u32[]{:S(2)}) collective-permute-start(f32[1,2048]{1,0:T(1,128)S(1)} %add_add_fusion.1), channel_id=1, source_target_pairs={{0,12},{1,13},{2,14},{3,15},{4,8},{5,9},{6,10},{7,11},{8,4},{9,5},... | collective-permute-start | bytes 24584 | tf_op jit(solution)/shard_map/ppermute | solution.py:442
  79.4 4.5 %collective-permute-start.34 = (f32[1,2048]{1,0:T(1,128)S(1)}, f32[1,2048]{1,0:T(1,128)S(1)}, u32[]{:S(2)}, u32[]{:S(2)}) collective-permute-start(f32[1,2048]{1,0:T(1,128)S(1)} %add_add_fusion.1), channel_id=1, source_target_pairs={{0,8},{1,9},{2,10},{3,11},{4,12},{5,13},{6,14},{7,15},{8,0},{9,1},... | collective-permute-start | bytes 24584 | tf_op jit(solution)/shard_map/ppermute | solution.py:442
  80.4 3.7 %collective-permute-start.33 = (f32[1,2048]{1,0:T(1,128)S(1)}, f32[1,2048]{1,0:T(1,128)S(1)}, u32[]{:S(2)}, u32[]{:S(2)}) collective-permute-start(f32[1,2048]{1,0:T(1,128)S(1)} %add_add_fusion.1), channel_id=1, source_target_pairs={{0,4},{1,5},{2,6},{3,7},{4,0},{5,1},{6,2},{7,3},{8,12},{9,13},{10,... | collective-permute-start | bytes 24584 | tf_op jit(solution)/shard_map/ppermute | solution.py:442
  87.7 2.4 %collective-permute-start.38 = (f32[8,48,512]{2,1,0:T(8,128)S(1)}, f32[8,48,512]{2,1,0:T(8,128)S(1)}, u32[]{:S(2)}, u32[]{:S(2)}) collective-permute-start(f32[8,48,512]{2,1,0:T(8,128)S(1)} %get-tuple-element.75), channel_id=1, source_target_pairs={{0,1},{1,0},{2,3},{3,2},{4,5},{5,4},{6,7},{7,6},{8,9},{9,8},{10,11... | collective-permute-start | bytes 2359304 | tf_op jit(solution)/shard_map/ppermute | solution.py:442
  87.8 3.4 %collective-permute-start.37 = (f32[8,48,512]{2,1,0:T(8,128)S(1)}, f32[8,48,512]{2,1,0:T(8,128)S(1)}, u32[]{:S(2)}, u32[]{:S(2)}) collective-permute-start(f32[8,48,512]{2,1,0:T(8,128)S(1)} %get-tuple-element.73), channel_id=1, source_target_pairs={{0,1},{1,0},{2,3},{3,2},{4,5},{5,4},{6,7},{7,6},{8,9},{9,8},{10,11... | collective-permute-start | bytes 2359304 | tf_op jit(solution)/shard_map/ppermute | solution.py:442
  88.3 3.6 %collective-permute-start.36 = (f32[8,32,512]{2,1,0:T(8,128)S(1)}, f32[8,32,512]{2,1,0:T(8,128)S(1)}, u32[]{:S(2)}, u32[]{:S(2)}) collective-permute-start(f32[8,32,512]{2,1,0:T(8,128)S(1)} %get-tuple-element.71), channel_id=1, source_target_pairs={{0,1},{1,0},{2,3},{3,2},{4,5},{5,4},{6,7},{7,6},{8,9},{9,8},{10,11... | collective-permute-start | bytes 1572872 | tf_op jit(solution)/shard_map/ppermute | solution.py:442
  88.4 6.4 %copy-start.1 = (bf16[2048,512]{1,0:T(8,128)(2,1)S(1)}, bf16[2048,512]{1,0:T(8,128)(2,1)}, u32[]{:S(2)}) copy-start(bf16[2048,512]{1,0:T(8,128)(2,1)} %x_ref.1) | copy-start | bytes 6291460
  90.2 12.0 %collective-permute-start.39 = (f32[4,48,512]{2,1,0:T(8,128)S(1)}, f32[4,48,512]{2,1,0:T(8,128)S(1)}, u32[]{:S(2)}, u32[]{:S(2)}) collective-permute-start(f32[4,48,512]{2,1,0:T(8,128)S(1)} %get-tuple-element.76.after_ref), channel_id=1, source_target_pairs={{0,2},{1,3},{2,0},{3,1},{4,6},{5,7},{6,4},{7,5},{8,10},{9,11},{10,... | collective-permute-start | bytes 1179656 | tf_op jit(solution)/shard_map/ppermute | solution.py:442
  92.0 8.7 %collective-permute-start.40 = (f32[4,32,512]{2,1,0:T(8,128)S(1)}, f32[4,32,512]{2,1,0:T(8,128)S(1)}, u32[]{:S(2)}, u32[]{:S(2)}) collective-permute-start(f32[4,32,512]{2,1,0:T(8,128)S(1)} %get-tuple-element.78.after_ref), channel_id=1, source_target_pairs={{0,4},{1,5},{2,6},{3,7},{4,0},{5,1},{6,2},{7,3},{8,12},{9,13},{10,... | collective-permute-start | bytes 786440 | tf_op jit(solution)/shard_map/ppermute | solution.py:442
  94.1 16.7 %collective-permute-start.44 = (f32[4,48,512]{2,1,0:T(8,128)S(1)}, f32[4,48,512]{2,1,0:T(8,128)S(1)}, u32[]{:S(2)}, u32[]{:S(2)}) collective-permute-start(f32[4,48,512]{2,1,0:T(8,128)S(1)} %get-tuple-element.77.after_ref), channel_id=1, source_target_pairs={{0,2},{1,3},{2,0},{3,1},{4,6},{5,7},{6,4},{7,5},{8,10},{9,11},{10,... | collective-permute-start | bytes 1179656 | tf_op jit(solution)/shard_map/ppermute | solution.py:442
  100.7 0.7 copy-start.2
  102.3 8.5 %collective-permute-start.41 = (f32[2,48,512]{2,1,0:T(8,128)S(1)}, f32[2,48,512]{2,1,0:T(8,128)S(1)}, u32[]{:S(2)}, u32[]{:S(2)}) collective-permute-start(f32[2,48,512]{2,1,0:T(8,128)S(1)} %get-tuple-element.86.after_ref), channel_id=1, source_target_pairs={{0,4},{1,5},{2,6},{3,7},{4,0},{5,1},{6,2},{7,3},{8,12},{9,13},{10,... | collective-permute-start | bytes 589832 | tf_op jit(solution)/shard_map/ppermute | solution.py:442
  104.4 6.2 %collective-permute-start.42 = (f32[2,32,512]{2,1,0:T(8,128)S(1)}, f32[2,32,512]{2,1,0:T(8,128)S(1)}, u32[]{:S(2)}, u32[]{:S(2)}) collective-permute-start(f32[2,32,512]{2,1,0:T(8,128)S(1)} %get-tuple-element.84.after_ref), channel_id=1, source_target_pairs={{0,8},{1,9},{2,10},{3,11},{4,12},{5,13},{6,14},{7,15},{8,0},{9,1},... | collective-permute-start | bytes 393224 | tf_op jit(solution)/shard_map/ppermute | solution.py:442
  110.9 8.4 %collective-permute-start.45 = (f32[2,48,512]{2,1,0:T(8,128)S(1)}, f32[2,48,512]{2,1,0:T(8,128)S(1)}, u32[]{:S(2)}, u32[]{:S(2)}) collective-permute-start(f32[2,48,512]{2,1,0:T(8,128)S(1)} %get-tuple-element.93.after_ref), channel_id=1, source_target_pairs={{0,4},{1,5},{2,6},{3,7},{4,0},{5,1},{6,2},{7,3},{8,12},{9,13},{10,... | collective-permute-start | bytes 589832 | tf_op jit(solution)/shard_map/ppermute | solution.py:442
  112.6 11.2 %collective-permute-start.43 = (f32[1,48,512]{2,1,0:T(8,128)S(1)}, f32[1,48,512]{2,1,0:T(8,128)S(1)}, u32[]{:S(2)}, u32[]{:S(2)}) collective-permute-start(f32[1,48,512]{2,1,0:T(8,128)S(1)} %get-tuple-element.90.after_ref), channel_id=1, source_target_pairs={{0,8},{1,9},{2,10},{3,11},{4,12},{5,13},{6,14},{7,15},{8,0},{9,1},... | collective-permute-start | bytes 294920 | tf_op jit(solution)/shard_map/ppermute | solution.py:442
  119.4 6.1 %collective-permute-start.46 = (f32[1,48,512]{2,1,0:T(8,128)S(1)}, f32[1,48,512]{2,1,0:T(8,128)S(1)}, u32[]{:S(2)}, u32[]{:S(2)}) collective-permute-start(f32[1,48,512]{2,1,0:T(8,128)S(1)} %get-tuple-element.95), channel_id=1, source_target_pairs={{0,8},{1,9},{2,10},{3,11},{4,12},{5,13},{6,14},{7,15},{8,0},{9,1},... | collective-permute-start | bytes 294920 | tf_op jit(solution)/shard_map/ppermute | solution.py:442
  119.5 4.3 %collective-permute-start.47 = (f32[1,32,512]{2,1,0:T(8,128)S(1)}, f32[1,32,512]{2,1,0:T(8,128)S(1)}, u32[]{:S(2)}, u32[]{:S(2)}) collective-permute-start(f32[1,32,512]{2,1,0:T(8,128)S(1)} %get-tuple-element.88.after_ref), channel_id=1, source_target_pairs={{0,2},{1,3},{2,0},{3,1},{4,6},{5,7},{6,4},{7,5},{8,10},{9,11},{10,... | collective-permute-start | bytes 196616 | tf_op jit(solution)/shard_map/ppermute | solution.py:442

commit v7 on v6

--- a/solution.py
+++ b/solution.py
@@ -116,7 +116,7 @@
             VMEM((cols, rows), F32),
             VMEM((cols, LANES), F32),
             VMEM((cols, LANES), F32),
-            jax.ShapeDtypeStruct((1, rows), F32),
+            VMEM((1, rows), F32),
             VMEM((share, new_points.shape[1]), F32),
         ),
         in_specs=[pl.BlockSpec(memory_space=pltpu.HBM)] * 3,
@@ -382,9 +382,20 @@
 
 
 def back_kernel(total_cols, half_ref, x_ref, y_ref, e_ref, b_ref, r_ref, n_ref, sq_ref, bv2_ref,
-                bv3_ref, mid_ref, gb1_ref, vbr_ref, w_ref, alpha_ref, u3_ref, after_ref, pot_ref, arch_ref,
-                new_ref, tmp_ref):
+                bv3_ref, mid_ref, gb1_ref, vbr_ref, w_ref, alpha_ref, u3_ref, weight_ref, mine_ref, after_ref,
+                pot_ref, arch_ref, new_ref, base_ref, tmp_ref, col_ref):
     del after_ref
+    share = mine_ref.shape[0]
+    pair = 2 * share
+    me = lax.axis_index("cols")
+    lo = pl.multiple_of((me // 2) * pair, pair)
+    for l in range(pair // LANES):
+        at = pl.multiple_of(lo + l * LANES, LANES)
+        col_ref[pl.ds(l * LANES, LANES), :] = column(weight_ref[:, pl.ds(at, LANES)])
+    col = col_ref[pl.ds(pl.multiple_of((me % 2) * share, share), share), :]
+    for l in range(mine_ref.shape[1] // LANES):
+        ls = pl.ds(l * LANES, LANES)
+        base_ref[:, ls] = col * mine_ref[:, ls]
     cols, rows = e_ref.shape
     width = y_ref.shape[1]
     column_dots(e_ref, [wide(a) for a in lanes(w_ref[...])], tmp_ref)
@@ -417,7 +428,7 @@
         new_ref[:, s] = (alpha_ref[:, s] + jnp.log2(u3_ref[:, s]) + sq) * (1.0 / LOGK)
 
 
-def back(total_cols, half, x, y, *rest):
+def back(total_cols, half, x, y, *rest, mine, after):
     cols, rows = half.shape
     width = y.shape[1]
     return pl.pallas_call(
@@ -426,16 +437,19 @@
             jax.ShapeDtypeStruct((1, cols), F32),
             jax.ShapeDtypeStruct((cols, width), F32),
             jax.ShapeDtypeStruct((1, rows), F32),
+            VMEM(mine.shape, F32),
         ),
-        in_specs=full(2 + len(rest)) + [pl.BlockSpec(memory_space=pl.ANY)],
-        out_specs=tuple(full(3)),
-        scratch_shapes=[pltpu.VMEM((cols, LANES), F32)],
+        in_specs=full(4 + len(rest)) + [pl.BlockSpec(memory_space=pl.ANY)],
+        out_specs=tuple(full(4)),
+        scratch_shapes=[
+            pltpu.VMEM((cols, LANES), F32), pltpu.VMEM((2 * mine.shape[0], LANES), F32)
+        ],
         compiler_params=params(16),
         cost_estimate=pl.CostEstimate(
             flops=2 * cols * rows * width, bytes_accessed=16 * 1024 * 1024, transcendentals=0
         ),
         name="back",
-    )(half, x, y, *rest)
+    )(half, x, y, *rest, mine, after)
 
 
 def swap(v, k, count):
@@ -480,42 +494,28 @@
                 after = advance(i, step, after)
         if t == 0:
             other = meanwhile(after)
-            after = other[0]
+            after = other[-1]
     return [x[0] for pair in zip(keeps, gots) for x in pair], other
 
 
-def gradient_kernel(pieces, scale, *refs):
-    weight_ref, mine_ref = refs[:2]
-    terms, (out_ref, col_ref) = refs[2:-2], refs[-2:]
-    share, width = mine_ref.shape
-    pair = 2 * share
-    me = lax.axis_index("cols")
-    lo = pl.multiple_of((me // 2) * pair, pair)
-    for l in range(pair // LANES):
-        at = pl.multiple_of(lo + l * LANES, LANES)
-        col_ref[pl.ds(l * LANES, LANES), :] = column(weight_ref[:, pl.ds(at, LANES)])
+def gradient_kernel(pieces, scale, base_ref, *refs):
+    terms, out_ref = refs[:-1], refs[-1]
     at = 0
     for i, (n, _) in enumerate(pieces):
-        col = col_ref[pl.ds(pl.multiple_of((me % 2) * share + at, 8), n), :]
-        for l in range(width // LANES):
-            ls = pl.ds(l * LANES, LANES)
-            out_ref[pl.ds(at, n), ls] = scale * (
-                col * mine_ref[pl.ds(at, n), ls] - (terms[2 * i][:, ls] + terms[2 * i + 1][:, ls])
-            )
+        s = pl.ds(at, n)
+        out_ref[s, :] = scale * (base_ref[s, :] - (terms[2 * i][...] + terms[2 * i + 1][...]))
         at += n
 
 
-def gradient(pieces, scale, weight, mine, terms):
-    share, width = mine.shape
+def gradient(pieces, scale, base, terms):
     return pl.pallas_call(
         functools.partial(gradient_kernel, pieces, float(scale)),
-        out_shape=jax.ShapeDtypeStruct((share, width), F32),
-        in_specs=full(2 + len(terms)),
+        out_shape=jax.ShapeDtypeStruct(base.shape, F32),
+        in_specs=full(1 + len(terms)),
         out_specs=full(1)[0],
-        scratch_shapes=[pltpu.VMEM((2 * share, LANES), F32)],
         compiler_params=params(8),
         name="gradient",
-    )(weight, mine, *terms)
+    )(base, *terms)
 
 
 def combine(x, count, join):
@@ -534,9 +534,23 @@
     return tree(jnp.add, xs)
 
 
+def lse_kernel(*refs):
+    for l in range(refs[0].shape[1] // LANES):
+        ls = pl.ds(l * LANES, LANES)
+        xs = [ref[:, ls] for ref in refs[:-1]]
+        m = tree(jnp.maximum, xs)
+        refs[-1][:, ls] = m + jnp.log2(tree(jnp.add, [jnp.exp2(x - m) for x in xs]))
+
+
 def lse_join(xs):
-    m = tree(jnp.maximum, xs)
-    return m + jnp.log2(tree(jnp.add, [jnp.exp2(x - m) for x in xs]))
+    return pl.pallas_call(
+        lse_kernel,
+        out_shape=jax.ShapeDtypeStruct(xs[0].shape, F32),
+        in_specs=full(len(xs)),
+        out_specs=full(1)[0],
+        compiler_params=params(8),
+        name="lse_join",
+    )(*xs)
 
 
 def routes(share, count):
@@ -577,15 +591,15 @@
         share, pieces, e, arch_points, (bv3, bv2, mid, br, vbr, gb1), (u3, w3, u2, w2, w1)
     )
     keeps = keep(share, pieces, half, arch_points)
-    terms, (pot, arch_grad, new_pot) = scatter_sum(
+    row_weight = 2.0 * (fbar3 + fbar2 + fbar1) - a
+    terms, (pot, arch_grad, new_pot, base) = scatter_sum(
         keeps, sends, pieces, count, part,
         lambda after: back(
             total_cols, half, new_points, arch_points, e, b, r, n, sq, bv2, bv3, mid, gb1, vbr, w1,
-            alpha, u3, after
+            alpha, u3, row_weight, mine=mine, after=after
         ),
     )
-    row_weight = 2.0 * (fbar3 + fbar2 + fbar1) - a
-    new_grad = gradient(pieces, rows, row_weight, mine, terms)
+    new_grad = gradient(pieces, rows, base, terms)
     return (new_pot.reshape(-1), pot.reshape(-1), new_grad, arch_grad)
 
 

time: 127 us -> 125 us (0.984)
  no operation moved by 1% of the time
where the time goes in v7:
time: 125 us
  starting transfers between devices  50.3 us (40%)
  waiting for transfers between devices  45.5 us (36%)
  Pallas kernels  27.3 us (22%)
    ppermute x48, starting transfers between devices, swap(): return lax.ppermute(v, 'cols', [(i, i ^ k) for i in range(count)])  50.3 us
    ppermute x48, waiting for transfers between devices, swap(): return lax.ppermute(v, 'cols', [(i, i ^ k) for i in range(count)])  45.5 us
    pallas_call x4, Pallas kernels, sweep(): pl.pallas_call(functools.partial(sweep_kernel, kind), out_shape=(VMEM((co...  5.87 us
    pallas_call x1, Pallas kernels, scores(): pl.pallas_call(functools.partial(scores_kernel, total_cols, share), out_s...  5.5 us
    pallas_call x1, Pallas kernels, back(): pl.pallas_call(functools.partial(back_kernel, float(total_cols)), out_sha...  5.41 us
    pallas_call x1, Pallas kernels, plan(): pl.pallas_call(plan_kernel, out_shape=(VMEM((cols, rows), F32),) + (VMEM(...  4.33 us
    pallas_call x1, Pallas kernels, mix(): pl.pallas_call(functools.partial(mix_kernel, share, pieces), out_shape=(V...  3.62 us
  transfers between devices with their start and end apart: 48, of which 39 were waited for; matrix products, arithmetic and copies ran while one was open for 1% of the time, Pallas kernels for 6%

profile of v7, /device:TPU:0, one launch (start us, length us, event | category | flops | bytes accessed | tf_op | source)
XLA Modules:
  0.0 125.0 jit_solution(11452212756709016465)
XLA Ops:
  0.6 5.5 %scores.1 = (f32[1024,2048]{1,0:T(8,128)S(1)}, f32[1024,128]{1,0:T(8,128)S(1)}, f32[1024,128]{1,0:T(8,128)S(1)}, f32[1,2048]{1,0:T(1,128)S(1)}, f32[128,512]{1,0:T(8,128)S(1)}) custom-call(bf16[2048,512]{1,0:T(8,128)(2,1)} %x_ref.1, bf16[1024,512]{1,0:T(8,128)(2,1)} %y_ref.5, f32[1,1024]{1,0:T(1,128)} %bitcast.24), custom_call_target="tpu_custom_call" | custom-call | tf_op jit(solution)/shard_map/scores/pallas_call | solution.py:113
  6.1 2.5 %collective-permute-start.2 = (f32[1,2048]{1,0:T(1,128)S(1)}, f32[1,2048]{1,0:T(1,128)S(1)}, u32[]{:S(2)}, u32[]{:S(2)}) collective-permute-start(f32[1,2048]{1,0:T(1,128)S(1)} %get-tuple-element.55.refs_0_), channel_id=1, source_target_pairs={{0,3},{1,2},{2,1},{3,0},{4,7},{5,6},{6,5},{7,4},{8,11},{9,10},{10,... | collective-permute-start | bytes 24584 | tf_op jit(solution)/shard_map/ppermute | solution.py:456
  10.0 2.3 %collective-permute-done.1.refs_2_ = f32[1,2048]{1,0:T(1,128)S(1)} collective-permute-done((f32[1,2048]{1,0:T(1,128)S(1)}, f32[1,2048]{1,0:T(1,128)S(1)}, u32[]{:S(2)}, u32[]{:S(2)}) %collective-permute-start.1) | collective-permute-done | bytes 8224 | tf_op jit(solution)/shard_map/ppermute | solution.py:456
  12.3 3.7 %collective-permute-start.5 = (f32[1,2048]{1,0:T(1,128)S(1)}, f32[1,2048]{1,0:T(1,128)S(1)}, u32[]{:S(2)}, u32[]{:S(2)}) collective-permute-start(f32[1,2048]{1,0:T(1,128)S(1)} %lse_join.2.refs_0_), channel_id=1, source_target_pairs={{0,12},{1,13},{2,14},{3,15},{4,8},{5,9},{6,10},{7,11},{8,4},{9,5},... | collective-permute-start | bytes 24584 | tf_op jit(solution)/shard_map/ppermute | solution.py:456
  16.0 0.8 collective-permute-start.3
  16.8 0.7 broadcast_multiply_fusion
  18.0 2.6 %collective-permute-done.4.refs_2_ = f32[1,2048]{1,0:T(1,128)S(1)} collective-permute-done((f32[1,2048]{1,0:T(1,128)S(1)}, f32[1,2048]{1,0:T(1,128)S(1)}, u32[]{:S(2)}, u32[]{:S(2)}) %collective-permute-start.4) | collective-permute-done | bytes 8224 | tf_op jit(solution)/shard_map/ppermute | solution.py:456
  20.6 4.3 %plan.1 = (f32[1024,2048]{1,0:T(8,128)S(1)}, f32[1024,128]{1,0:T(8,128)S(1)}, f32[1024,128]{1,0:T(8,128)S(1)}, f32[1024,128]{1,0:T(8,128)S(1)}, f32[1024,128]{1,0:T(8,128)S(1)}, /*index=5*/f32[1,2048]{1,0:T(1,128)S(1)}) custom-call(f32[1024,2048]{1,0:T(8,128)S(1)} %get-tuple-element.52.z_ref, ...), custom_call_target="tpu_custom_call", output_to_operand_aliasing={{0}: (0, {})} | custom-call | tf_op jit(solution)/shard_map/plan/pallas_call | solution.py:214
  25.1 0.7 collective-permute-start.7
  25.8 1.1 collective-permute-start.6
  26.9 1.2 collective-permute-done.8
  28.8 1.5 %collective-permute-start.11 = (f32[1,2048]{1,0:T(1,128)S(1)}, f32[1,2048]{1,0:T(1,128)S(1)}, u32[]{:S(2)}, u32[]{:S(2)}) collective-permute-start(f32[1,2048]{1,0:T(1,128)S(1)} %add_add_fusion.5), channel_id=1, source_target_pairs={{0,12},{1,13},{2,14},{3,15},{4,8},{5,9},{6,10},{7,11},{8,4},{9,5},... | collective-permute-start | bytes 24584 | tf_op jit(solution)/shard_map/ppermute | solution.py:456
  31.0 2.3 %collective-permute-start.9 = (f32[1,2048]{1,0:T(1,128)S(1)}, f32[1,2048]{1,0:T(1,128)S(1)}, u32[]{:S(2)}, u32[]{:S(2)}) collective-permute-start(f32[1,2048]{1,0:T(1,128)S(1)} %add_add_fusion.5), channel_id=1, source_target_pairs={{0,4},{1,5},{2,6},{3,7},{4,0},{5,1},{6,2},{7,3},{8,12},{9,13},{10,... | collective-permute-start | bytes 24584 | tf_op jit(solution)/shard_map/ppermute | solution.py:456
  33.3 1.1 collective-permute-done.11
  35.0 1.4 %sweep_fwd.2 = (f32[1024,128]{1,0:T(8,128)S(1)}, f32[1,2048]{1,0:T(1,128)S(1)}) custom-call(f32[1024,2048]{1,0:T(8,128)S(1)} %get-tuple-element.56.e_ref, f32[1024,128]{1,0:T(8,128)S(1)} %get-tuple-element.53.b_ref, f32[1,2048]{1,0:T(1,128)S(1)} %add_divide_fusion.1.refs_0_.refs_8_), custom_call_target="tpu_custom_call" | custom-call | tf_op jit(solution)/shard_map/sweep_fwd/pallas_call | solution.py:253
  36.5 0.7 collective-permute-start.13
  37.2 1.1 collective-permute-start.12
  38.4 1.2 collective-permute-done.14
  40.2 2.6 %collective-permute-start.17 = (f32[1,2048]{1,0:T(1,128)S(1)}, f32[1,2048]{1,0:T(1,128)S(1)}, u32[]{:S(2)}, u32[]{:S(2)}) collective-permute-start(f32[1,2048]{1,0:T(1,128)S(1)} %add_add_fusion.4), channel_id=1, source_target_pairs={{0,12},{1,13},{2,14},{3,15},{4,8},{5,9},{6,10},{7,11},{8,4},{9,5},... | collective-permute-start | bytes 24584 | tf_op jit(solution)/shard_map/ppermute | solution.py:456
  42.8 0.9 collective-permute-start.16
  43.7 1.0 collective-permute-start.15
  44.7 1.1 collective-permute-done.17
  45.8 1.6 %collective-permute-done.16 = f32[1,2048]{1,0:T(1,128)S(1)} collective-permute-done((f32[1,2048]{1,0:T(1,128)S(1)}, f32[1,2048]{1,0:T(1,128)S(1)}, u32[]{:S(2)}, u32[]{:S(2)}) %collective-permute-start.16) | collective-permute-done | bytes 8224 | tf_op jit(solution)/shard_map/ppermute | solution.py:456
  47.5 1.4 %sweep_fwd.3 = (f32[1024,128]{1,0:T(8,128)S(1)}, f32[1,2048]{1,0:T(1,128)S(1)}) custom-call(f32[1024,2048]{1,0:T(8,128)S(1)} %get-tuple-element.56.e_ref, f32[1024,128]{1,0:T(8,128)S(1)} %get-tuple-element.53.b_ref, f32[1,2048]{1,0:T(1,128)S(1)} %add_divide_fusion.refs_0_.refs_6_.u3_ref), custom_call_target="tpu_custom_call" | custom-call | tf_op jit(solution)/shard_map/sweep_fwd/pallas_call | solution.py:253
  49.0 0.7 collective-permute-start.19
  49.7 1.1 collective-permute-start.18
  50.8 1.2 collective-permute-done.20
  52.7 1.4 %collective-permute-start.23 = (f32[1,2048]{1,0:T(1,128)S(1)}, f32[1,2048]{1,0:T(1,128)S(1)}, u32[]{:S(2)}, u32[]{:S(2)}) collective-permute-start(f32[1,2048]{1,0:T(1,128)S(1)} %add_add_fusion.3), channel_id=1, source_target_pairs={{0,12},{1,13},{2,14},{3,15},{4,8},{5,9},{6,10},{7,11},{8,4},{9,5},... | collective-permute-start | bytes 24584 | tf_op jit(solution)/shard_map/ppermute | solution.py:456
  54.2 1.0 collective-permute-start.22
  55.1 2.0 %collective-permute-start.21 = (f32[1,2048]{1,0:T(1,128)S(1)}, f32[1,2048]{1,0:T(1,128)S(1)}, u32[]{:S(2)}, u32[]{:S(2)}) collective-permute-start(f32[1,2048]{1,0:T(1,128)S(1)} %add_add_fusion.3), channel_id=1, source_target_pairs={{0,4},{1,5},{2,6},{3,7},{4,0},{5,1},{6,2},{7,3},{8,12},{9,13},{10,... | collective-permute-start | bytes 24584 | tf_op jit(solution)/shard_map/ppermute | solution.py:456
  57.2 1.1 collective-permute-done.23
  58.8 1.4 %sweep_mid.1 = (f32[1024,128]{1,0:T(8,128)S(1)}, f32[1,2048]{1,0:T(1,128)S(1)}) custom-call(f32[1024,2048]{1,0:T(8,128)S(1)} %get-tuple-element.56.e_ref, f32[1024,128]{1,0:T(8,128)S(1)} %get-tuple-element.53.b_ref, f32[1024,128]{1,0:T(8,128)S(1)} %get-tuple-element.60.refs_0_.refs_1_.bv2_ref, f32[1,2048]{1,0:T(1,128)S(1)} %get-tuple-element.104.refs_1_.refs_7_), custom_call_target="tpu_custom_call" | custom-call | tf_op jit(solution)/shard_map/sweep_mid/pallas_call | solution.py:253
  60.3 0.7 collective-permute-start.25
  61.0 1.1 collective-permute-start.24
  62.2 1.2 collective-permute-done.26
  64.1 2.6 %collective-permute-start.29 = (f32[1,2048]{1,0:T(1,128)S(1)}, f32[1,2048]{1,0:T(1,128)S(1)}, u32[]{:S(2)}, u32[]{:S(2)}) collective-permute-start(f32[1,2048]{1,0:T(1,128)S(1)} %add_add_fusion.2), channel_id=1, source_target_pairs={{0,12},{1,13},{2,14},{3,15},{4,8},{5,9},{6,10},{7,11},{8,4},{9,5},... | collective-permute-start | bytes 24584 | tf_op jit(solution)/shard_map/ppermute | solution.py:456
  66.6 1.0 collective-permute-start.28
  67.6 0.9 collective-permute-start.27
  68.5 1.1 collective-permute-done.29
  69.6 1.6 %collective-permute-done.28 = f32[1,2048]{1,0:T(1,128)S(1)} collective-permute-done((f32[1,2048]{1,0:T(1,128)S(1)}, f32[1,2048]{1,0:T(1,128)S(1)}, u32[]{:S(2)}, u32[]{:S(2)}) %collective-permute-start.28) | collective-permute-done | bytes 8224 | tf_op jit(solution)/shard_map/ppermute | solution.py:456
  71.3 1.6 %sweep_bwd.1 = (f32[1024,128]{1,0:T(8,128)S(1)}, f32[1,2048]{1,0:T(1,128)S(1)}) custom-call(f32[1024,2048]{1,0:T(8,128)S(1)} %get-tuple-element.56.e_ref, f32[1024,128]{1,0:T(8,128)S(1)} %get-tuple-element.63.b_ref.refs_3_, f32[1024,128]{1,0:T(8,128)S(1)} %get-tuple-element.65.refs_0_.r_ref, f32[1,2048]{1,0:T(1,128)S(1)} %get-tuple-element.102.refs_1_.refs_9_), custom_call_target="tpu_custom_call" | custom-call | tf_op jit(solution)/shard_map/sweep_bwd/pallas_call | solution.py:253
  73.0 0.7 collective-permute-start.31
  73.7 1.1 collective-permute-start.30
  74.9 1.2 collective-permute-done.32
  76.8 1.4 %collective-permute-start.35 = (f32[1,2048]{1,0:T(1,128)S(1)}, f32[1,2048]{1,0:T(1,128)S(1)}, u32[]{:S(2)}, u32[]{:S(2)}) collective-permute-start(f32[1,2048]{1,0:T(1,128)S(1)} %add_add_fusion.1), channel_id=1, source_target_pairs={{0,12},{1,13},{2,14},{3,15},{4,8},{5,9},{6,10},{7,11},{8,4},{9,5},... | collective-permute-start | bytes 24584 | tf_op jit(solution)/shard_map/ppermute | solution.py:456
  78.2 1.0 collective-permute-start.34
  79.2 2.0 %collective-permute-start.33 = (f32[1,2048]{1,0:T(1,128)S(1)}, f32[1,2048]{1,0:T(1,128)S(1)}, u32[]{:S(2)}, u32[]{:S(2)}) collective-permute-start(f32[1,2048]{1,0:T(1,128)S(1)} %add_add_fusion.1), channel_id=1, source_target_pairs={{0,4},{1,5},{2,6},{3,7},{4,0},{5,1},{6,2},{7,3},{8,12},{9,13},{10,... | collective-permute-start | bytes 24584 | tf_op jit(solution)/shard_map/ppermute | solution.py:456
  81.2 1.1 collective-permute-done.35
  82.9 3.6 %mix.1 = (bf16[1024,2048]{1,0:T(8,128)(2,1)S(1)}, f32[8,48,512]{2,1,0:T(8,128)S(1)}, f32[8,48,512]{2,1,0:T(8,128)S(1)}, f32[8,32,512]{2,1,0:T(8,128)S(1)}) custom-call(f32[1024,2048]{1,0:T(8,128)S(1)} %get-tuple-element.56.e_ref, bf16[1024,512]{1,0:T(8,128)(2,1)S(1)} %copy-done, f32[1024,128]{1,0:T(8,128)S(1)} %get-tuple-element.59.refs_0_.bv3_ref, ...), custom_call_target="tpu_custom_call" | custom-call | tf_op jit(solution)/shard_map/mix/pallas_call | solution.py:355
  87.2 1.3 %keep.1 = (f32[8,48,512]{2,1,0:T(8,128)S(1)}, f32[8,48,512]{2,1,0:T(8,128)S(1)}, f32[8,32,512]{2,1,0:T(8,128)S(1)}) custom-call(bf16[1024,2048]{1,0:T(8,128)(2,1)S(1)} %get-tuple-element.69.half_ref, bf16[1024,512]{1,0:T(8,128)(2,1)S(1)} %copy-done), custom_call_target="tpu_custom_call" | custom-call | tf_op jit(solution)/shard_map/keep/pallas_call | solution.py:373
  89.0 0.7 collective-permute-start.39
  90.8 2.1 %collective-permute-start.40 = (f32[4,32,512]{2,1,0:T(8,128)S(1)}, f32[4,32,512]{2,1,0:T(8,128)S(1)}, u32[]{:S(2)}, u32[]{:S(2)}) collective-permute-start(f32[4,32,512]{2,1,0:T(8,128)S(1)} %get-tuple-element.80.after_ref), channel_id=1, source_target_pairs={{0,4},{1,5},{2,6},{3,7},{4,0},{5,1},{6,2},{7,3},{8,12},{9,13},{10,... | collective-permute-start | bytes 786440 | tf_op jit(solution)/shard_map/ppermute | solution.py:456
  93.6 5.4 %back.1 = (f32[1,1024]{1,0:T(1,128)}, f32[1024,512]{1,0:T(8,128)}, f32[1,2048]{1,0:T(1,128)}, f32[128,512]{1,0:T(8,128)S(1)}) custom-call(bf16[1024,2048]{1,0:T(8,128)(2,1)S(1)} %get-tuple-element.69.half_ref, bf16[2048,512]{1,0:T(8,128)(2,1)S(1)} %copy-done.1, bf16[1024,512]{1,0:T(8,128)(2,1)S(1)} %copy-done, f32[1024,2048]{1,0:T(8,128)S(1)} %get-tuple-element.56.e_ref, ...), custom_call_target="tpu_custom_call" | custom-call | flops 2147483648 | bytes 16777216 | tf_op jit(solution)/shard_map/back/pallas_call | solution.py:434
  99.6 1.5 %collective-permute-done.39.got_ref = f32[4,48,512]{2,1,0:T(8,128)S(1)} collective-permute-done((f32[4,48,512]{2,1,0:T(8,128)S(1)}, f32[4,48,512]{2,1,0:T(8,128)S(1)}, u32[]{:S(2)}, u32[]{:S(2)}) %collective-permute-start.39) | collective-permute-done | bytes 393248 | tf_op jit(solution)/shard_map/ppermute | solution.py:456
  101.1 2.1 %collective-permute-start.41 = (f32[2,48,512]{2,1,0:T(8,128)S(1)}, f32[2,48,512]{2,1,0:T(8,128)S(1)}, u32[]{:S(2)}, u32[]{:S(2)}) collective-permute-start(f32[2,48,512]{2,1,0:T(8,128)S(1)} %get-tuple-element.88.after_ref), channel_id=1, source_target_pairs={{0,4},{1,5},{2,6},{3,7},{4,0},{5,1},{6,2},{7,3},{8,12},{9,13},{10,... | collective-permute-start | bytes 589832 | tf_op jit(solution)/shard_map/ppermute | solution.py:456
  103.1 1.0 collective-permute-start.42
  104.2 5.1 %collective-permute-done.42.got_ref = f32[2,32,512]{2,1,0:T(8,128)S(1)} collective-permute-done((f32[2,32,512]{2,1,0:T(8,128)S(1)}, f32[2,32,512]{2,1,0:T(8,128)S(1)}, u32[]{:S(2)}, u32[]{:S(2)}) %collective-permute-start.42) | collective-permute-done | bytes 131104 | tf_op jit(solution)/shard_map/ppermute | solution.py:456
  109.7 1.7 %collective-permute-start.45 = (f32[2,48,512]{2,1,0:T(8,128)S(1)}, f32[2,48,512]{2,1,0:T(8,128)S(1)}, u32[]{:S(2)}, u32[]{:S(2)}) collective-permute-start(f32[2,48,512]{2,1,0:T(8,128)S(1)} %get-tuple-element.95.after_ref), channel_id=1, source_target_pairs={{0,4},{1,5},{2,6},{3,7},{4,0},{5,1},{6,2},{7,3},{8,12},{9,13},{10,... | collective-permute-start | bytes 589832 | tf_op jit(solution)/shard_map/ppermute | solution.py:456
  111.4 1.0 collective-permute-start.43
  112.5 5.7 %collective-permute-done.45.got_ref = f32[2,48,512]{2,1,0:T(8,128)S(1)} collective-permute-done((f32[2,48,512]{2,1,0:T(8,128)S(1)}, f32[2,48,512]{2,1,0:T(8,128)S(1)}, u32[]{:S(2)}, u32[]{:S(2)}) %collective-permute-start.45) | collective-permute-done | bytes 196640 | tf_op jit(solution)/shard_map/ppermute | solution.py:456
  118.2 0.7 collective-permute-start.47
  119.0 3.6 %collective-permute-done.47 = f32[1,32,512]{2,1,0:T(8,128)S(1)} collective-permute-done((f32[1,32,512]{2,1,0:T(8,128)S(1)}, f32[1,32,512]{2,1,0:T(8,128)S(1)}, u32[]{:S(2)}, u32[]{:S(2)}) %collective-permute-start.47) | collective-permute-done | bytes 65568 | tf_op jit(solution)/shard_map/ppermute | solution.py:456
  122.6 1.7 %collective-permute-done.46 = f32[1,48,512]{2,1,0:T(8,128)S(1)} collective-permute-done((f32[1,48,512]{2,1,0:T(8,128)S(1)}, f32[1,48,512]{2,1,0:T(8,128)S(1)}, u32[]{:S(2)}, u32[]{:S(2)}) %collective-permute-start.46) | collective-permute-done | bytes 98336 | tf_op jit(solution)/shard_map/ppermute | solution.py:456
  124.3 0.7 gradient.1
  (70 shorter events, 12.3 us)
Async XLA Ops:
  6.1 3.8 %collective-permute-start.2 = (f32[1,2048]{1,0:T(1,128)S(1)}, f32[1,2048]{1,0:T(1,128)S(1)}, u32[]{:S(2)}, u32[]{:S(2)}) collective-permute-start(f32[1,2048]{1,0:T(1,128)S(1)} %get-tuple-element.55.refs_0_), channel_id=1, source_target_pairs={{0,3},{1,2},{2,1},{3,0},{4,7},{5,6},{6,5},{7,4},{8,11},{9,10},{10,... | collective-permute-start | bytes 24584 | tf_op jit(solution)/shard_map/ppermute | solution.py:456
  8.6 3.7 %collective-permute-start.1 = (f32[1,2048]{1,0:T(1,128)S(1)}, f32[1,2048]{1,0:T(1,128)S(1)}, u32[]{:S(2)}, u32[]{:S(2)}) collective-permute-start(f32[1,2048]{1,0:T(1,128)S(1)} %get-tuple-element.55.refs_0_), channel_id=1, source_target_pairs={{0,2},{1,3},{2,0},{3,1},{4,6},{5,7},{6,4},{7,5},{8,10},{9,11},{10,... | collective-permute-start | bytes 24584 | tf_op jit(solution)/shard_map/ppermute | solution.py:456
  9.2 3.0 %collective-permute-start = (f32[1,2048]{1,0:T(1,128)S(1)}, f32[1,2048]{1,0:T(1,128)S(1)}, u32[]{:S(2)}, u32[]{:S(2)}) collective-permute-start(f32[1,2048]{1,0:T(1,128)S(1)} %get-tuple-element.55.refs_0_), channel_id=1, source_target_pairs={{0,1},{1,0},{2,3},{3,2},{4,5},{5,4},{6,7},{7,6},{8,9},{9,8},{10,11... | collective-permute-start | bytes 24584 | tf_op jit(solution)/shard_map/ppermute | solution.py:456
  12.3 5.6 %collective-permute-start.5 = (f32[1,2048]{1,0:T(1,128)S(1)}, f32[1,2048]{1,0:T(1,128)S(1)}, u32[]{:S(2)}, u32[]{:S(2)}) collective-permute-start(f32[1,2048]{1,0:T(1,128)S(1)} %lse_join.2.refs_0_), channel_id=1, source_target_pairs={{0,12},{1,13},{2,14},{3,15},{4,8},{5,9},{6,10},{7,11},{8,4},{9,5},... | collective-permute-start | bytes 24584 | tf_op jit(solution)/shard_map/ppermute | solution.py:456
  16.0 4.5 %collective-permute-start.4 = (f32[1,2048]{1,0:T(1,128)S(1)}, f32[1,2048]{1,0:T(1,128)S(1)}, u32[]{:S(2)}, u32[]{:S(2)}) collective-permute-start(f32[1,2048]{1,0:T(1,128)S(1)} %lse_join.2.refs_0_), channel_id=1, source_target_pairs={{0,8},{1,9},{2,10},{3,11},{4,12},{5,13},{6,14},{7,15},{8,0},{9,1},... | collective-permute-start | bytes 24584 | tf_op jit(solution)/shard_map/ppermute | solution.py:456
  16.0 4.5 %collective-permute-start.3 = (f32[1,2048]{1,0:T(1,128)S(1)}, f32[1,2048]{1,0:T(1,128)S(1)}, u32[]{:S(2)}, u32[]{:S(2)}) collective-permute-start(f32[1,2048]{1,0:T(1,128)S(1)} %lse_join.2.refs_0_), channel_id=1, source_target_pairs={{0,4},{1,5},{2,6},{3,7},{4,0},{5,1},{6,2},{7,3},{8,12},{9,13},{10,... | collective-permute-start | bytes 24584 | tf_op jit(solution)/shard_map/ppermute | solution.py:456
  25.0 3.1 %collective-permute-start.8 = (f32[1,2048]{1,0:T(1,128)S(1)}, f32[1,2048]{1,0:T(1,128)S(1)}, u32[]{:S(2)}, u32[]{:S(2)}) collective-permute-start(f32[1,2048]{1,0:T(1,128)S(1)} %get-tuple-element.57), channel_id=1, source_target_pairs={{0,3},{1,2},{2,1},{3,0},{4,7},{5,6},{6,5},{7,4},{8,11},{9,10},{10,... | collective-permute-start | bytes 24584 | tf_op jit(solution)/shard_map/ppermute | solution.py:456
  25.1 3.7 %collective-permute-start.7 = (f32[1,2048]{1,0:T(1,128)S(1)}, f32[1,2048]{1,0:T(1,128)S(1)}, u32[]{:S(2)}, u32[]{:S(2)}) collective-permute-start(f32[1,2048]{1,0:T(1,128)S(1)} %get-tuple-element.57), channel_id=1, source_target_pairs={{0,2},{1,3},{2,0},{3,1},{4,6},{5,7},{6,4},{7,5},{8,10},{9,11},{10,... | collective-permute-start | bytes 24584 | tf_op jit(solution)/shard_map/ppermute | solution.py:456
  25.8 3.0 %collective-permute-start.6 = (f32[1,2048]{1,0:T(1,128)S(1)}, f32[1,2048]{1,0:T(1,128)S(1)}, u32[]{:S(2)}, u32[]{:S(2)}) collective-permute-start(f32[1,2048]{1,0:T(1,128)S(1)} %get-tuple-element.57), channel_id=1, source_target_pairs={{0,1},{1,0},{2,3},{3,2},{4,5},{5,4},{6,7},{7,6},{8,9},{9,8},{10,11... | collective-permute-start | bytes 24584 | tf_op jit(solution)/shard_map/ppermute | solution.py:456
  28.8 5.6 %collective-permute-start.11 = (f32[1,2048]{1,0:T(1,128)S(1)}, f32[1,2048]{1,0:T(1,128)S(1)}, u32[]{:S(2)}, u32[]{:S(2)}) collective-permute-start(f32[1,2048]{1,0:T(1,128)S(1)} %add_add_fusion.5), channel_id=1, source_target_pairs={{0,12},{1,13},{2,14},{3,15},{4,8},{5,9},{6,10},{7,11},{8,4},{9,5},... | collective-permute-start | bytes 24584 | tf_op jit(solution)/shard_map/ppermute | solution.py:456
  30.3 4.6 %collective-permute-start.10 = (f32[1,2048]{1,0:T(1,128)S(1)}, f32[1,2048]{1,0:T(1,128)S(1)}, u32[]{:S(2)}, u32[]{:S(2)}) collective-permute-start(f32[1,2048]{1,0:T(1,128)S(1)} %add_add_fusion.5), channel_id=1, source_target_pairs={{0,8},{1,9},{2,10},{3,11},{4,12},{5,13},{6,14},{7,15},{8,0},{9,1},... | collective-permute-start | bytes 24584 | tf_op jit(solution)/shard_map/ppermute | solution.py:456
  31.0 4.0 %collective-permute-start.9 = (f32[1,2048]{1,0:T(1,128)S(1)}, f32[1,2048]{1,0:T(1,128)S(1)}, u32[]{:S(2)}, u32[]{:S(2)}) collective-permute-start(f32[1,2048]{1,0:T(1,128)S(1)} %add_add_fusion.5), channel_id=1, source_target_pairs={{0,4},{1,5},{2,6},{3,7},{4,0},{5,1},{6,2},{7,3},{8,12},{9,13},{10,... | collective-permute-start | bytes 24584 | tf_op jit(solution)/shard_map/ppermute | solution.py:456
  36.4 3.1 %collective-permute-start.14 = (f32[1,2048]{1,0:T(1,128)S(1)}, f32[1,2048]{1,0:T(1,128)S(1)}, u32[]{:S(2)}, u32[]{:S(2)}) collective-permute-start(f32[1,2048]{1,0:T(1,128)S(1)} %get-tuple-element.58), channel_id=1, source_target_pairs={{0,3},{1,2},{2,1},{3,0},{4,7},{5,6},{6,5},{7,4},{8,11},{9,10},{10,... | collective-permute-start | bytes 24584 | tf_op jit(solution)/shard_map/ppermute | solution.py:456
  36.5 3.7 %collective-permute-start.13 = (f32[1,2048]{1,0:T(1,128)S(1)}, f32[1,2048]{1,0:T(1,128)S(1)}, u32[]{:S(2)}, u32[]{:S(2)}) collective-permute-start(f32[1,2048]{1,0:T(1,128)S(1)} %get-tuple-element.58), channel_id=1, source_target_pairs={{0,2},{1,3},{2,0},{3,1},{4,6},{5,7},{6,4},{7,5},{8,10},{9,11},{10,... | collective-permute-start | bytes 24584 | tf_op jit(solution)/shard_map/ppermute | solution.py:456
  37.2 3.0 %collective-permute-start.12 = (f32[1,2048]{1,0:T(1,128)S(1)}, f32[1,2048]{1,0:T(1,128)S(1)}, u32[]{:S(2)}, u32[]{:S(2)}) collective-permute-start(f32[1,2048]{1,0:T(1,128)S(1)} %get-tuple-element.58), channel_id=1, source_target_pairs={{0,1},{1,0},{2,3},{3,2},{4,5},{5,4},{6,7},{7,6},{8,9},{9,8},{10,11... | collective-permute-start | bytes 24584 | tf_op jit(solution)/shard_map/ppermute | solution.py:456
  40.2 5.5 %collective-permute-start.17 = (f32[1,2048]{1,0:T(1,128)S(1)}, f32[1,2048]{1,0:T(1,128)S(1)}, u32[]{:S(2)}, u32[]{:S(2)}) collective-permute-start(f32[1,2048]{1,0:T(1,128)S(1)} %add_add_fusion.4), channel_id=1, source_target_pairs={{0,12},{1,13},{2,14},{3,15},{4,8},{5,9},{6,10},{7,11},{8,4},{9,5},... | collective-permute-start | bytes 24584 | tf_op jit(solution)/shard_map/ppermute | solution.py:456
  42.8 4.6 %collective-permute-start.16 = (f32[1,2048]{1,0:T(1,128)S(1)}, f32[1,2048]{1,0:T(1,128)S(1)}, u32[]{:S(2)}, u32[]{:S(2)}) collective-permute-start(f32[1,2048]{1,0:T(1,128)S(1)} %add_add_fusion.4), channel_id=1, source_target_pairs={{0,8},{1,9},{2,10},{3,11},{4,12},{5,13},{6,14},{7,15},{8,0},{9,1},... | collective-permute-start | bytes 24584 | tf_op jit(solution)/shard_map/ppermute | solution.py:456
  43.7 3.7 %collective-permute-start.15 = (f32[1,2048]{1,0:T(1,128)S(1)}, f32[1,2048]{1,0:T(1,128)S(1)}, u32[]{:S(2)}, u32[]{:S(2)}) collective-permute-start(f32[1,2048]{1,0:T(1,128)S(1)} %add_add_fusion.4), channel_id=1, source_target_pairs={{0,4},{1,5},{2,6},{3,7},{4,0},{5,1},{6,2},{7,3},{8,12},{9,13},{10,... | collective-permute-start | bytes 24584 | tf_op jit(solution)/shard_map/ppermute | solution.py:456
  48.9 3.1 %collective-permute-start.20 = (f32[1,2048]{1,0:T(1,128)S(1)}, f32[1,2048]{1,0:T(1,128)S(1)}, u32[]{:S(2)}, u32[]{:S(2)}) collective-permute-start(f32[1,2048]{1,0:T(1,128)S(1)} %get-tuple-element.61), channel_id=1, source_target_pairs={{0,3},{1,2},{2,1},{3,0},{4,7},{5,6},{6,5},{7,4},{8,11},{9,10},{10,... | collective-permute-start | bytes 24584 | tf_op jit(solution)/shard_map/ppermute | solution.py:456
  49.0 3.7 %collective-permute-start.19 = (f32[1,2048]{1,0:T(1,128)S(1)}, f32[1,2048]{1,0:T(1,128)S(1)}, u32[]{:S(2)}, u32[]{:S(2)}) collective-permute-start(f32[1,2048]{1,0:T(1,128)S(1)} %get-tuple-element.61), channel_id=1, source_target_pairs={{0,2},{1,3},{2,0},{3,1},{4,6},{5,7},{6,4},{7,5},{8,10},{9,11},{10,... | collective-permute-start | bytes 24584 | tf_op jit(solution)/shard_map/ppermute | solution.py:456
  49.7 3.0 %collective-permute-start.18 = (f32[1,2048]{1,0:T(1,128)S(1)}, f32[1,2048]{1,0:T(1,128)S(1)}, u32[]{:S(2)}, u32[]{:S(2)}) collective-permute-start(f32[1,2048]{1,0:T(1,128)S(1)} %get-tuple-element.61), channel_id=1, source_target_pairs={{0,1},{1,0},{2,3},{3,2},{4,5},{5,4},{6,7},{7,6},{8,9},{9,8},{10,11... | collective-permute-start | bytes 24584 | tf_op jit(solution)/shard_map/ppermute | solution.py:456
  52.7 5.5 %collective-permute-start.23 = (f32[1,2048]{1,0:T(1,128)S(1)}, f32[1,2048]{1,0:T(1,128)S(1)}, u32[]{:S(2)}, u32[]{:S(2)}) collective-permute-start(f32[1,2048]{1,0:T(1,128)S(1)} %add_add_fusion.3), channel_id=1, source_target_pairs={{0,12},{1,13},{2,14},{3,15},{4,8},{5,9},{6,10},{7,11},{8,4},{9,5},... | collective-permute-start | bytes 24584 | tf_op jit(solution)/shard_map/ppermute | solution.py:456
  54.2 4.5 %collective-permute-start.22 = (f32[1,2048]{1,0:T(1,128)S(1)}, f32[1,2048]{1,0:T(1,128)S(1)}, u32[]{:S(2)}, u32[]{:S(2)}) collective-permute-start(f32[1,2048]{1,0:T(1,128)S(1)} %add_add_fusion.3), channel_id=1, source_target_pairs={{0,8},{1,9},{2,10},{3,11},{4,12},{5,13},{6,14},{7,15},{8,0},{9,1},... | collective-permute-start | bytes 24584 | tf_op jit(solution)/shard_map/ppermute | solution.py:456
  55.1 3.7 %collective-permute-start.21 = (f32[1,2048]{1,0:T(1,128)S(1)}, f32[1,2048]{1,0:T(1,128)S(1)}, u32[]{:S(2)}, u32[]{:S(2)}) collective-permute-start(f32[1,2048]{1,0:T(1,128)S(1)} %add_add_fusion.3), channel_id=1, source_target_pairs={{0,4},{1,5},{2,6},{3,7},{4,0},{5,1},{6,2},{7,3},{8,12},{9,13},{10,... | collective-permute-start | bytes 24584 | tf_op jit(solution)/shard_map/ppermute | solution.py:456
  60.3 3.1 %collective-permute-start.26 = (f32[1,2048]{1,0:T(1,128)S(1)}, f32[1,2048]{1,0:T(1,128)S(1)}, u32[]{:S(2)}, u32[]{:S(2)}) collective-permute-start(f32[1,2048]{1,0:T(1,128)S(1)} %get-tuple-element.66), channel_id=1, source_target_pairs={{0,3},{1,2},{2,1},{3,0},{4,7},{5,6},{6,5},{7,4},{8,11},{9,10},{10,... | collective-permute-start | bytes 24584 | tf_op jit(solution)/shard_map/ppermute | solution.py:456
  60.3 3.7 %collective-permute-start.25 = (f32[1,2048]{1,0:T(1,128)S(1)}, f32[1,2048]{1,0:T(1,128)S(1)}, u32[]{:S(2)}, u32[]{:S(2)}) collective-permute-start(f32[1,2048]{1,0:T(1,128)S(1)} %get-tuple-element.66), channel_id=1, source_target_pairs={{0,2},{1,3},{2,0},{3,1},{4,6},{5,7},{6,4},{7,5},{8,10},{9,11},{10,... | collective-permute-start | bytes 24584 | tf_op jit(solution)/shard_map/ppermute | solution.py:456
  61.0 3.0 %collective-permute-start.24 = (f32[1,2048]{1,0:T(1,128)S(1)}, f32[1,2048]{1,0:T(1,128)S(1)}, u32[]{:S(2)}, u32[]{:S(2)}) collective-permute-start(f32[1,2048]{1,0:T(1,128)S(1)} %get-tuple-element.66), channel_id=1, source_target_pairs={{0,1},{1,0},{2,3},{3,2},{4,5},{5,4},{6,7},{7,6},{8,9},{9,8},{10,11... | collective-permute-start | bytes 24584 | tf_op jit(solution)/shard_map/ppermute | solution.py:456
  64.1 5.5 %collective-permute-start.29 = (f32[1,2048]{1,0:T(1,128)S(1)}, f32[1,2048]{1,0:T(1,128)S(1)}, u32[]{:S(2)}, u32[]{:S(2)}) collective-permute-start(f32[1,2048]{1,0:T(1,128)S(1)} %add_add_fusion.2), channel_id=1, source_target_pairs={{0,12},{1,13},{2,14},{3,15},{4,8},{5,9},{6,10},{7,11},{8,4},{9,5},... | collective-permute-start | bytes 24584 | tf_op jit(solution)/shard_map/ppermute | solution.py:456
  66.6 4.5 %collective-permute-start.28 = (f32[1,2048]{1,0:T(1,128)S(1)}, f32[1,2048]{1,0:T(1,128)S(1)}, u32[]{:S(2)}, u32[]{:S(2)}) collective-permute-start(f32[1,2048]{1,0:T(1,128)S(1)} %add_add_fusion.2), channel_id=1, source_target_pairs={{0,8},{1,9},{2,10},{3,11},{4,12},{5,13},{6,14},{7,15},{8,0},{9,1},... | collective-permute-start | bytes 24584 | tf_op jit(solution)/shard_map/ppermute | solution.py:456
  67.6 3.7 %collective-permute-start.27 = (f32[1,2048]{1,0:T(1,128)S(1)}, f32[1,2048]{1,0:T(1,128)S(1)}, u32[]{:S(2)}, u32[]{:S(2)}) collective-permute-start(f32[1,2048]{1,0:T(1,128)S(1)} %add_add_fusion.2), channel_id=1, source_target_pairs={{0,4},{1,5},{2,6},{3,7},{4,0},{5,1},{6,2},{7,3},{8,12},{9,13},{10,... | collective-permute-start | bytes 24584 | tf_op jit(solution)/shard_map/ppermute | solution.py:456
  71.3 11.6 %copy-start = (bf16[1024,512]{1,0:T(8,128)(2,1)S(1)}, bf16[1024,512]{1,0:T(8,128)(2,1)}, u32[]{:S(2)}) copy-start(bf16[1024,512]{1,0:T(8,128)(2,1)} %y_ref.5) | copy-start | bytes 3145732
  72.9 3.1 %collective-permute-start.32 = (f32[1,2048]{1,0:T(1,128)S(1)}, f32[1,2048]{1,0:T(1,128)S(1)}, u32[]{:S(2)}, u32[]{:S(2)}) collective-permute-start(f32[1,2048]{1,0:T(1,128)S(1)} %get-tuple-element.68.after_ref), channel_id=1, source_target_pairs={{0,3},{1,2},{2,1},{3,0},{4,7},{5,6},{6,5},{7,4},{8,11},{9,10},{10,... | collective-permute-start | bytes 24584 | tf_op jit(solution)/shard_map/ppermute | solution.py:456
  73.0 3.7 %collective-permute-start.31 = (f32[1,2048]{1,0:T(1,128)S(1)}, f32[1,2048]{1,0:T(1,128)S(1)}, u32[]{:S(2)}, u32[]{:S(2)}) collective-permute-start(f32[1,2048]{1,0:T(1,128)S(1)} %get-tuple-element.68.after_ref), channel_id=1, source_target_pairs={{0,2},{1,3},{2,0},{3,1},{4,6},{5,7},{6,4},{7,5},{8,10},{9,11},{10,... | collective-permute-start | bytes 24584 | tf_op jit(solution)/shard_map/ppermute | solution.py:456
  73.7 3.0 %collective-permute-start.30 = (f32[1,2048]{1,0:T(1,128)S(1)}, f32[1,2048]{1,0:T(1,128)S(1)}, u32[]{:S(2)}, u32[]{:S(2)}) collective-permute-start(f32[1,2048]{1,0:T(1,128)S(1)} %get-tuple-element.68.after_ref), channel_id=1, source_target_pairs={{0,1},{1,0},{2,3},{3,2},{4,5},{5,4},{6,7},{7,6},{8,9},{9,8},{10,11... | collective-permute-start | bytes 24584 | tf_op jit(solution)/shard_map/ppermute | solution.py:456
  76.8 5.5 %collective-permute-start.35 = (f32[1,2048]{1,0:T(1,128)S(1)}, f32[1,2048]{1,0:T(1,128)S(1)}, u32[]{:S(2)}, u32[]{:S(2)}) collective-permute-start(f32[1,2048]{1,0:T(1,128)S(1)} %add_add_fusion.1), channel_id=1, source_target_pairs={{0,12},{1,13},{2,14},{3,15},{4,8},{5,9},{6,10},{7,11},{8,4},{9,5},... | collective-permute-start | bytes 24584 | tf_op jit(solution)/shard_map/ppermute | solution.py:456
  78.2 4.5 %collective-permute-start.34 = (f32[1,2048]{1,0:T(1,128)S(1)}, f32[1,2048]{1,0:T(1,128)S(1)}, u32[]{:S(2)}, u32[]{:S(2)}) collective-permute-start(f32[1,2048]{1,0:T(1,128)S(1)} %add_add_fusion.1), channel_id=1, source_target_pairs={{0,8},{1,9},{2,10},{3,11},{4,12},{5,13},{6,14},{7,15},{8,0},{9,1},... | collective-permute-start | bytes 24584 | tf_op jit(solution)/shard_map/ppermute | solution.py:456
  79.2 3.7 %collective-permute-start.33 = (f32[1,2048]{1,0:T(1,128)S(1)}, f32[1,2048]{1,0:T(1,128)S(1)}, u32[]{:S(2)}, u32[]{:S(2)}) collective-permute-start(f32[1,2048]{1,0:T(1,128)S(1)} %add_add_fusion.1), channel_id=1, source_target_pairs={{0,4},{1,5},{2,6},{3,7},{4,0},{5,1},{6,2},{7,3},{8,12},{9,13},{10,... | collective-permute-start | bytes 24584 | tf_op jit(solution)/shard_map/ppermute | solution.py:456
  86.5 2.4 %collective-permute-start.38 = (f32[8,48,512]{2,1,0:T(8,128)S(1)}, f32[8,48,512]{2,1,0:T(8,128)S(1)}, u32[]{:S(2)}, u32[]{:S(2)}) collective-permute-start(f32[8,48,512]{2,1,0:T(8,128)S(1)} %get-tuple-element.77), channel_id=1, source_target_pairs={{0,1},{1,0},{2,3},{3,2},{4,5},{5,4},{6,7},{7,6},{8,9},{9,8},{10,11... | collective-permute-start | bytes 2359304 | tf_op jit(solution)/shard_map/ppermute | solution.py:456
  86.6 3.4 %collective-permute-start.37 = (f32[8,48,512]{2,1,0:T(8,128)S(1)}, f32[8,48,512]{2,1,0:T(8,128)S(1)}, u32[]{:S(2)}, u32[]{:S(2)}) collective-permute-start(f32[8,48,512]{2,1,0:T(8,128)S(1)} %get-tuple-element.75), channel_id=1, source_target_pairs={{0,1},{1,0},{2,3},{3,2},{4,5},{5,4},{6,7},{7,6},{8,9},{9,8},{10,11... | collective-permute-start | bytes 2359304 | tf_op jit(solution)/shard_map/ppermute | solution.py:456
  87.1 3.6 %collective-permute-start.36 = (f32[8,32,512]{2,1,0:T(8,128)S(1)}, f32[8,32,512]{2,1,0:T(8,128)S(1)}, u32[]{:S(2)}, u32[]{:S(2)}) collective-permute-start(f32[8,32,512]{2,1,0:T(8,128)S(1)} %get-tuple-element.73), channel_id=1, source_target_pairs={{0,1},{1,0},{2,3},{3,2},{4,5},{5,4},{6,7},{7,6},{8,9},{9,8},{10,11... | collective-permute-start | bytes 1572872 | tf_op jit(solution)/shard_map/ppermute | solution.py:456
  87.2 6.4 %copy-start.1 = (bf16[2048,512]{1,0:T(8,128)(2,1)S(1)}, bf16[2048,512]{1,0:T(8,128)(2,1)}, u32[]{:S(2)}) copy-start(bf16[2048,512]{1,0:T(8,128)(2,1)} %x_ref.1) | copy-start | bytes 6291460
  89.0 12.0 %collective-permute-start.39 = (f32[4,48,512]{2,1,0:T(8,128)S(1)}, f32[4,48,512]{2,1,0:T(8,128)S(1)}, u32[]{:S(2)}, u32[]{:S(2)}) collective-permute-start(f32[4,48,512]{2,1,0:T(8,128)S(1)} %get-tuple-element.78.after_ref), channel_id=1, source_target_pairs={{0,2},{1,3},{2,0},{3,1},{4,6},{5,7},{6,4},{7,5},{8,10},{9,11},{10,... | collective-permute-start | bytes 1179656 | tf_op jit(solution)/shard_map/ppermute | solution.py:456
  90.8 8.7 %collective-permute-start.40 = (f32[4,32,512]{2,1,0:T(8,128)S(1)}, f32[4,32,512]{2,1,0:T(8,128)S(1)}, u32[]{:S(2)}, u32[]{:S(2)}) collective-permute-start(f32[4,32,512]{2,1,0:T(8,128)S(1)} %get-tuple-element.80.after_ref), channel_id=1, source_target_pairs={{0,4},{1,5},{2,6},{3,7},{4,0},{5,1},{6,2},{7,3},{8,12},{9,13},{10,... | collective-permute-start | bytes 786440 | tf_op jit(solution)/shard_map/ppermute | solution.py:456
  92.9 16.7 %collective-permute-start.44 = (f32[4,48,512]{2,1,0:T(8,128)S(1)}, f32[4,48,512]{2,1,0:T(8,128)S(1)}, u32[]{:S(2)}, u32[]{:S(2)}) collective-permute-start(f32[4,48,512]{2,1,0:T(8,128)S(1)} %get-tuple-element.79.after_ref), channel_id=1, source_target_pairs={{0,2},{1,3},{2,0},{3,1},{4,6},{5,7},{6,4},{7,5},{8,10},{9,11},{10,... | collective-permute-start | bytes 1179656 | tf_op jit(solution)/shard_map/ppermute | solution.py:456
  101.1 8.5 %collective-permute-start.41 = (f32[2,48,512]{2,1,0:T(8,128)S(1)}, f32[2,48,512]{2,1,0:T(8,128)S(1)}, u32[]{:S(2)}, u32[]{:S(2)}) collective-permute-start(f32[2,48,512]{2,1,0:T(8,128)S(1)} %get-tuple-element.88.after_ref), channel_id=1, source_target_pairs={{0,4},{1,5},{2,6},{3,7},{4,0},{5,1},{6,2},{7,3},{8,12},{9,13},{10,... | collective-permute-start | bytes 589832 | tf_op jit(solution)/shard_map/ppermute | solution.py:456
  103.1 6.2 %collective-permute-start.42 = (f32[2,32,512]{2,1,0:T(8,128)S(1)}, f32[2,32,512]{2,1,0:T(8,128)S(1)}, u32[]{:S(2)}, u32[]{:S(2)}) collective-permute-start(f32[2,32,512]{2,1,0:T(8,128)S(1)} %get-tuple-element.86.after_ref), channel_id=1, source_target_pairs={{0,8},{1,9},{2,10},{3,11},{4,12},{5,13},{6,14},{7,15},{8,0},{9,1},... | collective-permute-start | bytes 393224 | tf_op jit(solution)/shard_map/ppermute | solution.py:456
  109.7 8.4 %collective-permute-start.45 = (f32[2,48,512]{2,1,0:T(8,128)S(1)}, f32[2,48,512]{2,1,0:T(8,128)S(1)}, u32[]{:S(2)}, u32[]{:S(2)}) collective-permute-start(f32[2,48,512]{2,1,0:T(8,128)S(1)} %get-tuple-element.95.after_ref), channel_id=1, source_target_pairs={{0,4},{1,5},{2,6},{3,7},{4,0},{5,1},{6,2},{7,3},{8,12},{9,13},{10,... | collective-permute-start | bytes 589832 | tf_op jit(solution)/shard_map/ppermute | solution.py:456
  111.4 11.2 %collective-permute-start.43 = (f32[1,48,512]{2,1,0:T(8,128)S(1)}, f32[1,48,512]{2,1,0:T(8,128)S(1)}, u32[]{:S(2)}, u32[]{:S(2)}) collective-permute-start(f32[1,48,512]{2,1,0:T(8,128)S(1)} %get-tuple-element.92.after_ref), channel_id=1, source_target_pairs={{0,8},{1,9},{2,10},{3,11},{4,12},{5,13},{6,14},{7,15},{8,0},{9,1},... | collective-permute-start | bytes 294920 | tf_op jit(solution)/shard_map/ppermute | solution.py:456
  118.2 6.1 %collective-permute-start.46 = (f32[1,48,512]{2,1,0:T(8,128)S(1)}, f32[1,48,512]{2,1,0:T(8,128)S(1)}, u32[]{:S(2)}, u32[]{:S(2)}) collective-permute-start(f32[1,48,512]{2,1,0:T(8,128)S(1)} %get-tuple-element.97), channel_id=1, source_target_pairs={{0,8},{1,9},{2,10},{3,11},{4,12},{5,13},{6,14},{7,15},{8,0},{9,1},... | collective-permute-start | bytes 294920 | tf_op jit(solution)/shard_map/ppermute | solution.py:456
  118.2 4.3 %collective-permute-start.47 = (f32[1,32,512]{2,1,0:T(8,128)S(1)}, f32[1,32,512]{2,1,0:T(8,128)S(1)}, u32[]{:S(2)}, u32[]{:S(2)}) collective-permute-start(f32[1,32,512]{2,1,0:T(8,128)S(1)} %get-tuple-element.90.after_ref), channel_id=1, source_target_pairs={{0,2},{1,3},{2,0},{3,1},{4,6},{5,7},{6,4},{7,5},{8,10},{9,11},{10,... | collective-permute-start | bytes 196616 | tf_op jit(solution)/shard_map/ppermute | solution.py:456

commit v8 on v7

--- a/solution.py
+++ b/solution.py
@@ -62,12 +62,12 @@
     step = 2 * LANES
     copies = [
         pltpu.make_async_copy(hbm, ref, sems.at[i])
-        for i, (hbm, ref) in enumerate(((x_hbm, x_ref), (y_hbm, y_ref), (mass_hbm, mass_ref)))
+        for i, (hbm, ref) in enumerate(((mass_hbm, mass_ref), (y_hbm, y_ref), (x_hbm, x_ref)))
     ]
     for copy in copies:
         copy.start()
-    for copy in copies:
-        copy.wait()
+    copies[0].wait()
+    copies[1].wait()
     for c in range(cols // LANES):
         s = pl.ds(c * LANES, LANES)
         b = column(mass_ref[:, s] * (1.0 / total_cols))
@@ -77,6 +77,7 @@
         sq = jnp.broadcast_to(sq, (LANES, LANES))
         sq_ref[s, :] = sq
         cb_ref[s, :] = jnp.log2(b) - sq
+    copies[2].wait()
     many = 4
 
     def reduce_block(r):

time: 125 us -> 125 us (level)
  no operation moved by 1% of the time
where the time goes in v8:
time: 125 us
  starting transfers between devices  50.2 us (40%)
  waiting for transfers between devices  45.6 us (36%)
  Pallas kernels  27.4 us (22%)
    ppermute x48, starting transfers between devices, swap(): return lax.ppermute(v, 'cols', [(i, i ^ k) for i in range(count)])  50.2 us
    ppermute x48, waiting for transfers between devices, swap(): return lax.ppermute(v, 'cols', [(i, i ^ k) for i in range(count)])  45.6 us
    pallas_call x4, Pallas kernels, sweep(): pl.pallas_call(functools.partial(sweep_kernel, kind), out_shape=(VMEM((co...  5.87 us
    pallas_call x1, Pallas kernels, scores(): pl.pallas_call(functools.partial(scores_kernel, total_cols, share), out_s...  5.51 us
    pallas_call x1, Pallas kernels, back(): pl.pallas_call(functools.partial(back_kernel, float(total_cols)), out_sha...  5.41 us
    pallas_call x1, Pallas kernels, plan(): pl.pallas_call(plan_kernel, out_shape=(VMEM((cols, rows), F32),) + (VMEM(...  4.33 us
    pallas_call x1, Pallas kernels, mix(): pl.pallas_call(functools.partial(mix_kernel, share, pieces), out_shape=(V...  3.62 us
  transfers between devices with their start and end apart: 48, of which 39 were waited for; matrix products, arithmetic and copies ran while one was open for 1% of the time, Pallas kernels for 6%

profile of v8, /device:TPU:0, one launch (start us, length us, event | category | flops | bytes accessed | tf_op | source)
XLA Modules:
  0.0 125.1 jit_solution(6186900735342791853)
XLA Ops:
  0.6 5.5 %scores.1 = (f32[1024,2048]{1,0:T(8,128)S(1)}, f32[1024,128]{1,0:T(8,128)S(1)}, f32[1024,128]{1,0:T(8,128)S(1)}, f32[1,2048]{1,0:T(1,128)S(1)}, f32[128,512]{1,0:T(8,128)S(1)}) custom-call(bf16[2048,512]{1,0:T(8,128)(2,1)} %x_ref.1, bf16[1024,512]{1,0:T(8,128)(2,1)} %y_ref.5, f32[1,1024]{1,0:T(1,128)} %bitcast.24), custom_call_target="tpu_custom_call" | custom-call | tf_op jit(solution)/shard_map/scores/pallas_call | solution.py:114
  6.1 2.5 %collective-permute-start.2 = (f32[1,2048]{1,0:T(1,128)S(1)}, f32[1,2048]{1,0:T(1,128)S(1)}, u32[]{:S(2)}, u32[]{:S(2)}) collective-permute-start(f32[1,2048]{1,0:T(1,128)S(1)} %get-tuple-element.55.refs_0_), channel_id=1, source_target_pairs={{0,3},{1,2},{2,1},{3,0},{4,7},{5,6},{6,5},{7,4},{8,11},{9,10},{10,... | collective-permute-start | bytes 24584 | tf_op jit(solution)/shard_map/ppermute | solution.py:457
  10.0 2.3 %collective-permute-done.1.refs_2_ = f32[1,2048]{1,0:T(1,128)S(1)} collective-permute-done((f32[1,2048]{1,0:T(1,128)S(1)}, f32[1,2048]{1,0:T(1,128)S(1)}, u32[]{:S(2)}, u32[]{:S(2)}) %collective-permute-start.1) | collective-permute-done | bytes 8224 | tf_op jit(solution)/shard_map/ppermute | solution.py:457
  12.3 3.7 %collective-permute-start.5 = (f32[1,2048]{1,0:T(1,128)S(1)}, f32[1,2048]{1,0:T(1,128)S(1)}, u32[]{:S(2)}, u32[]{:S(2)}) collective-permute-start(f32[1,2048]{1,0:T(1,128)S(1)} %lse_join.2.refs_0_), channel_id=1, source_target_pairs={{0,12},{1,13},{2,14},{3,15},{4,8},{5,9},{6,10},{7,11},{8,4},{9,5},... | collective-permute-start | bytes 24584 | tf_op jit(solution)/shard_map/ppermute | solution.py:457
  16.0 0.8 collective-permute-start.3
  16.8 0.7 broadcast_multiply_fusion
  18.0 2.6 %collective-permute-done.4.refs_2_ = f32[1,2048]{1,0:T(1,128)S(1)} collective-permute-done((f32[1,2048]{1,0:T(1,128)S(1)}, f32[1,2048]{1,0:T(1,128)S(1)}, u32[]{:S(2)}, u32[]{:S(2)}) %collective-permute-start.4) | collective-permute-done | bytes 8224 | tf_op jit(solution)/shard_map/ppermute | solution.py:457
  20.6 4.3 %plan.1 = (f32[1024,2048]{1,0:T(8,128)S(1)}, f32[1024,128]{1,0:T(8,128)S(1)}, f32[1024,128]{1,0:T(8,128)S(1)}, f32[1024,128]{1,0:T(8,128)S(1)}, f32[1024,128]{1,0:T(8,128)S(1)}, /*index=5*/f32[1,2048]{1,0:T(1,128)S(1)}) custom-call(f32[1024,2048]{1,0:T(8,128)S(1)} %get-tuple-element.52.z_ref, ...), custom_call_target="tpu_custom_call", output_to_operand_aliasing={{0}: (0, {})} | custom-call | tf_op jit(solution)/shard_map/plan/pallas_call | solution.py:215
  25.1 0.7 collective-permute-start.7
  25.8 1.1 collective-permute-start.6
  26.9 1.2 collective-permute-done.8
  28.8 1.5 %collective-permute-start.11 = (f32[1,2048]{1,0:T(1,128)S(1)}, f32[1,2048]{1,0:T(1,128)S(1)}, u32[]{:S(2)}, u32[]{:S(2)}) collective-permute-start(f32[1,2048]{1,0:T(1,128)S(1)} %add_add_fusion.5), channel_id=1, source_target_pairs={{0,12},{1,13},{2,14},{3,15},{4,8},{5,9},{6,10},{7,11},{8,4},{9,5},... | collective-permute-start | bytes 24584 | tf_op jit(solution)/shard_map/ppermute | solution.py:457
  31.0 2.3 %collective-permute-start.9 = (f32[1,2048]{1,0:T(1,128)S(1)}, f32[1,2048]{1,0:T(1,128)S(1)}, u32[]{:S(2)}, u32[]{:S(2)}) collective-permute-start(f32[1,2048]{1,0:T(1,128)S(1)} %add_add_fusion.5), channel_id=1, source_target_pairs={{0,4},{1,5},{2,6},{3,7},{4,0},{5,1},{6,2},{7,3},{8,12},{9,13},{10,... | collective-permute-start | bytes 24584 | tf_op jit(solution)/shard_map/ppermute | solution.py:457
  33.3 1.1 collective-permute-done.11
  35.0 1.4 %sweep_fwd.2 = (f32[1024,128]{1,0:T(8,128)S(1)}, f32[1,2048]{1,0:T(1,128)S(1)}) custom-call(f32[1024,2048]{1,0:T(8,128)S(1)} %get-tuple-element.56.e_ref, f32[1024,128]{1,0:T(8,128)S(1)} %get-tuple-element.53.b_ref, f32[1,2048]{1,0:T(1,128)S(1)} %add_divide_fusion.1.refs_0_.refs_8_), custom_call_target="tpu_custom_call" | custom-call | tf_op jit(solution)/shard_map/sweep_fwd/pallas_call | solution.py:254
  36.5 0.7 collective-permute-start.13
  37.2 1.1 collective-permute-start.12
  38.4 1.2 collective-permute-done.14
  40.3 2.6 %collective-permute-start.17 = (f32[1,2048]{1,0:T(1,128)S(1)}, f32[1,2048]{1,0:T(1,128)S(1)}, u32[]{:S(2)}, u32[]{:S(2)}) collective-permute-start(f32[1,2048]{1,0:T(1,128)S(1)} %add_add_fusion.4), channel_id=1, source_target_pairs={{0,12},{1,13},{2,14},{3,15},{4,8},{5,9},{6,10},{7,11},{8,4},{9,5},... | collective-permute-start | bytes 24584 | tf_op jit(solution)/shard_map/ppermute | solution.py:457
  42.8 0.9 collective-permute-start.16
  43.7 1.0 collective-permute-start.15
  44.7 1.1 collective-permute-done.17
  45.8 1.6 %collective-permute-done.16 = f32[1,2048]{1,0:T(1,128)S(1)} collective-permute-done((f32[1,2048]{1,0:T(1,128)S(1)}, f32[1,2048]{1,0:T(1,128)S(1)}, u32[]{:S(2)}, u32[]{:S(2)}) %collective-permute-start.16) | collective-permute-done | bytes 8224 | tf_op jit(solution)/shard_map/ppermute | solution.py:457
  47.5 1.4 %sweep_fwd.3 = (f32[1024,128]{1,0:T(8,128)S(1)}, f32[1,2048]{1,0:T(1,128)S(1)}) custom-call(f32[1024,2048]{1,0:T(8,128)S(1)} %get-tuple-element.56.e_ref, f32[1024,128]{1,0:T(8,128)S(1)} %get-tuple-element.53.b_ref, f32[1,2048]{1,0:T(1,128)S(1)} %add_divide_fusion.refs_0_.refs_6_.u3_ref), custom_call_target="tpu_custom_call" | custom-call | tf_op jit(solution)/shard_map/sweep_fwd/pallas_call | solution.py:254
  49.0 0.7 collective-permute-start.19
  49.7 1.1 collective-permute-start.18
  50.8 1.2 collective-permute-done.20
  52.7 1.4 %collective-permute-start.23 = (f32[1,2048]{1,0:T(1,128)S(1)}, f32[1,2048]{1,0:T(1,128)S(1)}, u32[]{:S(2)}, u32[]{:S(2)}) collective-permute-start(f32[1,2048]{1,0:T(1,128)S(1)} %add_add_fusion.3), channel_id=1, source_target_pairs={{0,12},{1,13},{2,14},{3,15},{4,8},{5,9},{6,10},{7,11},{8,4},{9,5},... | collective-permute-start | bytes 24584 | tf_op jit(solution)/shard_map/ppermute | solution.py:457
  54.2 1.0 collective-permute-start.22
  55.2 2.0 %collective-permute-start.21 = (f32[1,2048]{1,0:T(1,128)S(1)}, f32[1,2048]{1,0:T(1,128)S(1)}, u32[]{:S(2)}, u32[]{:S(2)}) collective-permute-start(f32[1,2048]{1,0:T(1,128)S(1)} %add_add_fusion.3), channel_id=1, source_target_pairs={{0,4},{1,5},{2,6},{3,7},{4,0},{5,1},{6,2},{7,3},{8,12},{9,13},{10,... | collective-permute-start | bytes 24584 | tf_op jit(solution)/shard_map/ppermute | solution.py:457
  57.2 1.1 collective-permute-done.23
  58.8 1.4 %sweep_mid.1 = (f32[1024,128]{1,0:T(8,128)S(1)}, f32[1,2048]{1,0:T(1,128)S(1)}) custom-call(f32[1024,2048]{1,0:T(8,128)S(1)} %get-tuple-element.56.e_ref, f32[1024,128]{1,0:T(8,128)S(1)} %get-tuple-element.53.b_ref, f32[1024,128]{1,0:T(8,128)S(1)} %get-tuple-element.60.refs_0_.refs_1_.bv2_ref, f32[1,2048]{1,0:T(1,128)S(1)} %get-tuple-element.104.refs_1_.refs_7_), custom_call_target="tpu_custom_call" | custom-call | tf_op jit(solution)/shard_map/sweep_mid/pallas_call | solution.py:254
  60.3 0.7 collective-permute-start.25
  61.0 1.1 collective-permute-start.24
  62.2 1.2 collective-permute-done.26
  64.1 2.6 %collective-permute-start.29 = (f32[1,2048]{1,0:T(1,128)S(1)}, f32[1,2048]{1,0:T(1,128)S(1)}, u32[]{:S(2)}, u32[]{:S(2)}) collective-permute-start(f32[1,2048]{1,0:T(1,128)S(1)} %add_add_fusion.2), channel_id=1, source_target_pairs={{0,12},{1,13},{2,14},{3,15},{4,8},{5,9},{6,10},{7,11},{8,4},{9,5},... | collective-permute-start | bytes 24584 | tf_op jit(solution)/shard_map/ppermute | solution.py:457
  66.7 1.0 collective-permute-start.28
  67.6 0.9 collective-permute-start.27
  68.5 1.1 collective-permute-done.29
  69.6 1.6 %collective-permute-done.28 = f32[1,2048]{1,0:T(1,128)S(1)} collective-permute-done((f32[1,2048]{1,0:T(1,128)S(1)}, f32[1,2048]{1,0:T(1,128)S(1)}, u32[]{:S(2)}, u32[]{:S(2)}) %collective-permute-start.28) | collective-permute-done | bytes 8224 | tf_op jit(solution)/shard_map/ppermute | solution.py:457
  71.3 1.6 %sweep_bwd.1 = (f32[1024,128]{1,0:T(8,128)S(1)}, f32[1,2048]{1,0:T(1,128)S(1)}) custom-call(f32[1024,2048]{1,0:T(8,128)S(1)} %get-tuple-element.56.e_ref, f32[1024,128]{1,0:T(8,128)S(1)} %get-tuple-element.63.b_ref.refs_3_, f32[1024,128]{1,0:T(8,128)S(1)} %get-tuple-element.65.refs_0_.r_ref, f32[1,2048]{1,0:T(1,128)S(1)} %get-tuple-element.102.refs_1_.refs_9_), custom_call_target="tpu_custom_call" | custom-call | tf_op jit(solution)/shard_map/sweep_bwd/pallas_call | solution.py:254
  73.0 0.7 collective-permute-start.31
  73.7 1.1 collective-permute-start.30
  74.9 1.2 collective-permute-done.32
  76.8 1.4 %collective-permute-start.35 = (f32[1,2048]{1,0:T(1,128)S(1)}, f32[1,2048]{1,0:T(1,128)S(1)}, u32[]{:S(2)}, u32[]{:S(2)}) collective-permute-start(f32[1,2048]{1,0:T(1,128)S(1)} %add_add_fusion.1), channel_id=1, source_target_pairs={{0,12},{1,13},{2,14},{3,15},{4,8},{5,9},{6,10},{7,11},{8,4},{9,5},... | collective-permute-start | bytes 24584 | tf_op jit(solution)/shard_map/ppermute | solution.py:457
  78.2 1.0 collective-permute-start.34
  79.2 2.0 %collective-permute-start.33 = (f32[1,2048]{1,0:T(1,128)S(1)}, f32[1,2048]{1,0:T(1,128)S(1)}, u32[]{:S(2)}, u32[]{:S(2)}) collective-permute-start(f32[1,2048]{1,0:T(1,128)S(1)} %add_add_fusion.1), channel_id=1, source_target_pairs={{0,4},{1,5},{2,6},{3,7},{4,0},{5,1},{6,2},{7,3},{8,12},{9,13},{10,... | collective-permute-start | bytes 24584 | tf_op jit(solution)/shard_map/ppermute | solution.py:457
  81.2 1.1 collective-permute-done.35
  82.9 3.6 %mix.1 = (bf16[1024,2048]{1,0:T(8,128)(2,1)S(1)}, f32[8,48,512]{2,1,0:T(8,128)S(1)}, f32[8,48,512]{2,1,0:T(8,128)S(1)}, f32[8,32,512]{2,1,0:T(8,128)S(1)}) custom-call(f32[1024,2048]{1,0:T(8,128)S(1)} %get-tuple-element.56.e_ref, bf16[1024,512]{1,0:T(8,128)(2,1)S(1)} %copy-done, f32[1024,128]{1,0:T(8,128)S(1)} %get-tuple-element.59.refs_0_.bv3_ref, ...), custom_call_target="tpu_custom_call" | custom-call | tf_op jit(solution)/shard_map/mix/pallas_call | solution.py:356
  87.2 1.3 %keep.1 = (f32[8,48,512]{2,1,0:T(8,128)S(1)}, f32[8,48,512]{2,1,0:T(8,128)S(1)}, f32[8,32,512]{2,1,0:T(8,128)S(1)}) custom-call(bf16[1024,2048]{1,0:T(8,128)(2,1)S(1)} %get-tuple-element.69.half_ref, bf16[1024,512]{1,0:T(8,128)(2,1)S(1)} %copy-done), custom_call_target="tpu_custom_call" | custom-call | tf_op jit(solution)/shard_map/keep/pallas_call | solution.py:374
  89.0 0.7 collective-permute-start.39
  90.8 2.1 %collective-permute-start.40 = (f32[4,32,512]{2,1,0:T(8,128)S(1)}, f32[4,32,512]{2,1,0:T(8,128)S(1)}, u32[]{:S(2)}, u32[]{:S(2)}) collective-permute-start(f32[4,32,512]{2,1,0:T(8,128)S(1)} %get-tuple-element.80.after_ref), channel_id=1, source_target_pairs={{0,4},{1,5},{2,6},{3,7},{4,0},{5,1},{6,2},{7,3},{8,12},{9,13},{10,... | collective-permute-start | bytes 786440 | tf_op jit(solution)/shard_map/ppermute | solution.py:457
  93.6 5.4 %back.1 = (f32[1,1024]{1,0:T(1,128)}, f32[1024,512]{1,0:T(8,128)}, f32[1,2048]{1,0:T(1,128)}, f32[128,512]{1,0:T(8,128)S(1)}) custom-call(bf16[1024,2048]{1,0:T(8,128)(2,1)S(1)} %get-tuple-element.69.half_ref, bf16[2048,512]{1,0:T(8,128)(2,1)S(1)} %copy-done.1, bf16[1024,512]{1,0:T(8,128)(2,1)S(1)} %copy-done, f32[1024,2048]{1,0:T(8,128)S(1)} %get-tuple-element.56.e_ref, ...), custom_call_target="tpu_custom_call" | custom-call | flops 2147483648 | bytes 16777216 | tf_op jit(solution)/shard_map/back/pallas_call | solution.py:435
  99.6 1.5 %collective-permute-done.39.got_ref = f32[4,48,512]{2,1,0:T(8,128)S(1)} collective-permute-done((f32[4,48,512]{2,1,0:T(8,128)S(1)}, f32[4,48,512]{2,1,0:T(8,128)S(1)}, u32[]{:S(2)}, u32[]{:S(2)}) %collective-permute-start.39) | collective-permute-done | bytes 393248 | tf_op jit(solution)/shard_map/ppermute | solution.py:457
  101.1 2.1 %collective-permute-start.41 = (f32[2,48,512]{2,1,0:T(8,128)S(1)}, f32[2,48,512]{2,1,0:T(8,128)S(1)}, u32[]{:S(2)}, u32[]{:S(2)}) collective-permute-start(f32[2,48,512]{2,1,0:T(8,128)S(1)} %get-tuple-element.88.after_ref), channel_id=1, source_target_pairs={{0,4},{1,5},{2,6},{3,7},{4,0},{5,1},{6,2},{7,3},{8,12},{9,13},{10,... | collective-permute-start | bytes 589832 | tf_op jit(solution)/shard_map/ppermute | solution.py:457
  103.2 1.0 collective-permute-start.42
  104.2 5.1 %collective-permute-done.42.got_ref = f32[2,32,512]{2,1,0:T(8,128)S(1)} collective-permute-done((f32[2,32,512]{2,1,0:T(8,128)S(1)}, f32[2,32,512]{2,1,0:T(8,128)S(1)}, u32[]{:S(2)}, u32[]{:S(2)}) %collective-permute-start.42) | collective-permute-done | bytes 131104 | tf_op jit(solution)/shard_map/ppermute | solution.py:457
  109.7 1.7 %collective-permute-start.45 = (f32[2,48,512]{2,1,0:T(8,128)S(1)}, f32[2,48,512]{2,1,0:T(8,128)S(1)}, u32[]{:S(2)}, u32[]{:S(2)}) collective-permute-start(f32[2,48,512]{2,1,0:T(8,128)S(1)} %get-tuple-element.95.after_ref), channel_id=1, source_target_pairs={{0,4},{1,5},{2,6},{3,7},{4,0},{5,1},{6,2},{7,3},{8,12},{9,13},{10,... | collective-permute-start | bytes 589832 | tf_op jit(solution)/shard_map/ppermute | solution.py:457
  111.4 1.0 collective-permute-start.43
  112.5 5.7 %collective-permute-done.45.got_ref = f32[2,48,512]{2,1,0:T(8,128)S(1)} collective-permute-done((f32[2,48,512]{2,1,0:T(8,128)S(1)}, f32[2,48,512]{2,1,0:T(8,128)S(1)}, u32[]{:S(2)}, u32[]{:S(2)}) %collective-permute-start.45) | collective-permute-done | bytes 196640 | tf_op jit(solution)/shard_map/ppermute | solution.py:457
  118.3 0.7 collective-permute-start.47
  119.0 3.6 %collective-permute-done.47 = f32[1,32,512]{2,1,0:T(8,128)S(1)} collective-permute-done((f32[1,32,512]{2,1,0:T(8,128)S(1)}, f32[1,32,512]{2,1,0:T(8,128)S(1)}, u32[]{:S(2)}, u32[]{:S(2)}) %collective-permute-start.47) | collective-permute-done | bytes 65568 | tf_op jit(solution)/shard_map/ppermute | solution.py:457
  122.6 1.7 %collective-permute-done.46 = f32[1,48,512]{2,1,0:T(8,128)S(1)} collective-permute-done((f32[1,48,512]{2,1,0:T(8,128)S(1)}, f32[1,48,512]{2,1,0:T(8,128)S(1)}, u32[]{:S(2)}, u32[]{:S(2)}) %collective-permute-start.46) | collective-permute-done | bytes 98336 | tf_op jit(solution)/shard_map/ppermute | solution.py:457
  124.3 0.7 gradient.1
  (70 shorter events, 12.3 us)
Async XLA Ops:
  6.1 3.8 %collective-permute-start.2 = (f32[1,2048]{1,0:T(1,128)S(1)}, f32[1,2048]{1,0:T(1,128)S(1)}, u32[]{:S(2)}, u32[]{:S(2)}) collective-permute-start(f32[1,2048]{1,0:T(1,128)S(1)} %get-tuple-element.55.refs_0_), channel_id=1, source_target_pairs={{0,3},{1,2},{2,1},{3,0},{4,7},{5,6},{6,5},{7,4},{8,11},{9,10},{10,... | collective-permute-start | bytes 24584 | tf_op jit(solution)/shard_map/ppermute | solution.py:457
  8.6 3.7 %collective-permute-start.1 = (f32[1,2048]{1,0:T(1,128)S(1)}, f32[1,2048]{1,0:T(1,128)S(1)}, u32[]{:S(2)}, u32[]{:S(2)}) collective-permute-start(f32[1,2048]{1,0:T(1,128)S(1)} %get-tuple-element.55.refs_0_), channel_id=1, source_target_pairs={{0,2},{1,3},{2,0},{3,1},{4,6},{5,7},{6,4},{7,5},{8,10},{9,11},{10,... | collective-permute-start | bytes 24584 | tf_op jit(solution)/shard_map/ppermute | solution.py:457
  9.3 3.0 %collective-permute-start = (f32[1,2048]{1,0:T(1,128)S(1)}, f32[1,2048]{1,0:T(1,128)S(1)}, u32[]{:S(2)}, u32[]{:S(2)}) collective-permute-start(f32[1,2048]{1,0:T(1,128)S(1)} %get-tuple-element.55.refs_0_), channel_id=1, source_target_pairs={{0,1},{1,0},{2,3},{3,2},{4,5},{5,4},{6,7},{7,6},{8,9},{9,8},{10,11... | collective-permute-start | bytes 24584 | tf_op jit(solution)/shard_map/ppermute | solution.py:457
  12.3 5.6 %collective-permute-start.5 = (f32[1,2048]{1,0:T(1,128)S(1)}, f32[1,2048]{1,0:T(1,128)S(1)}, u32[]{:S(2)}, u32[]{:S(2)}) collective-permute-start(f32[1,2048]{1,0:T(1,128)S(1)} %lse_join.2.refs_0_), channel_id=1, source_target_pairs={{0,12},{1,13},{2,14},{3,15},{4,8},{5,9},{6,10},{7,11},{8,4},{9,5},... | collective-permute-start | bytes 24584 | tf_op jit(solution)/shard_map/ppermute | solution.py:457
  16.0 4.5 %collective-permute-start.4 = (f32[1,2048]{1,0:T(1,128)S(1)}, f32[1,2048]{1,0:T(1,128)S(1)}, u32[]{:S(2)}, u32[]{:S(2)}) collective-permute-start(f32[1,2048]{1,0:T(1,128)S(1)} %lse_join.2.refs_0_), channel_id=1, source_target_pairs={{0,8},{1,9},{2,10},{3,11},{4,12},{5,13},{6,14},{7,15},{8,0},{9,1},... | collective-permute-start | bytes 24584 | tf_op jit(solution)/shard_map/ppermute | solution.py:457
  16.0 4.5 %collective-permute-start.3 = (f32[1,2048]{1,0:T(1,128)S(1)}, f32[1,2048]{1,0:T(1,128)S(1)}, u32[]{:S(2)}, u32[]{:S(2)}) collective-permute-start(f32[1,2048]{1,0:T(1,128)S(1)} %lse_join.2.refs_0_), channel_id=1, source_target_pairs={{0,4},{1,5},{2,6},{3,7},{4,0},{5,1},{6,2},{7,3},{8,12},{9,13},{10,... | collective-permute-start | bytes 24584 | tf_op jit(solution)/shard_map/ppermute | solution.py:457
  25.0 3.1 %collective-permute-start.8 = (f32[1,2048]{1,0:T(1,128)S(1)}, f32[1,2048]{1,0:T(1,128)S(1)}, u32[]{:S(2)}, u32[]{:S(2)}) collective-permute-start(f32[1,2048]{1,0:T(1,128)S(1)} %get-tuple-element.57), channel_id=1, source_target_pairs={{0,3},{1,2},{2,1},{3,0},{4,7},{5,6},{6,5},{7,4},{8,11},{9,10},{10,... | collective-permute-start | bytes 24584 | tf_op jit(solution)/shard_map/ppermute | solution.py:457
  25.1 3.7 %collective-permute-start.7 = (f32[1,2048]{1,0:T(1,128)S(1)}, f32[1,2048]{1,0:T(1,128)S(1)}, u32[]{:S(2)}, u32[]{:S(2)}) collective-permute-start(f32[1,2048]{1,0:T(1,128)S(1)} %get-tuple-element.57), channel_id=1, source_target_pairs={{0,2},{1,3},{2,0},{3,1},{4,6},{5,7},{6,4},{7,5},{8,10},{9,11},{10,... | collective-permute-start | bytes 24584 | tf_op jit(solution)/shard_map/ppermute | solution.py:457
  25.8 3.0 %collective-permute-start.6 = (f32[1,2048]{1,0:T(1,128)S(1)}, f32[1,2048]{1,0:T(1,128)S(1)}, u32[]{:S(2)}, u32[]{:S(2)}) collective-permute-start(f32[1,2048]{1,0:T(1,128)S(1)} %get-tuple-element.57), channel_id=1, source_target_pairs={{0,1},{1,0},{2,3},{3,2},{4,5},{5,4},{6,7},{7,6},{8,9},{9,8},{10,11... | collective-permute-start | bytes 24584 | tf_op jit(solution)/shard_map/ppermute | solution.py:457
  28.8 5.6 %collective-permute-start.11 = (f32[1,2048]{1,0:T(1,128)S(1)}, f32[1,2048]{1,0:T(1,128)S(1)}, u32[]{:S(2)}, u32[]{:S(2)}) collective-permute-start(f32[1,2048]{1,0:T(1,128)S(1)} %add_add_fusion.5), channel_id=1, source_target_pairs={{0,12},{1,13},{2,14},{3,15},{4,8},{5,9},{6,10},{7,11},{8,4},{9,5},... | collective-permute-start | bytes 24584 | tf_op jit(solution)/shard_map/ppermute | solution.py:457
  30.3 4.6 %collective-permute-start.10 = (f32[1,2048]{1,0:T(1,128)S(1)}, f32[1,2048]{1,0:T(1,128)S(1)}, u32[]{:S(2)}, u32[]{:S(2)}) collective-permute-start(f32[1,2048]{1,0:T(1,128)S(1)} %add_add_fusion.5), channel_id=1, source_target_pairs={{0,8},{1,9},{2,10},{3,11},{4,12},{5,13},{6,14},{7,15},{8,0},{9,1},... | collective-permute-start | bytes 24584 | tf_op jit(solution)/shard_map/ppermute | solution.py:457
  31.0 4.0 %collective-permute-start.9 = (f32[1,2048]{1,0:T(1,128)S(1)}, f32[1,2048]{1,0:T(1,128)S(1)}, u32[]{:S(2)}, u32[]{:S(2)}) collective-permute-start(f32[1,2048]{1,0:T(1,128)S(1)} %add_add_fusion.5), channel_id=1, source_target_pairs={{0,4},{1,5},{2,6},{3,7},{4,0},{5,1},{6,2},{7,3},{8,12},{9,13},{10,... | collective-permute-start | bytes 24584 | tf_op jit(solution)/shard_map/ppermute | solution.py:457
  36.4 3.1 %collective-permute-start.14 = (f32[1,2048]{1,0:T(1,128)S(1)}, f32[1,2048]{1,0:T(1,128)S(1)}, u32[]{:S(2)}, u32[]{:S(2)}) collective-permute-start(f32[1,2048]{1,0:T(1,128)S(1)} %get-tuple-element.58), channel_id=1, source_target_pairs={{0,3},{1,2},{2,1},{3,0},{4,7},{5,6},{6,5},{7,4},{8,11},{9,10},{10,... | collective-permute-start | bytes 24584 | tf_op jit(solution)/shard_map/ppermute | solution.py:457
  36.5 3.7 %collective-permute-start.13 = (f32[1,2048]{1,0:T(1,128)S(1)}, f32[1,2048]{1,0:T(1,128)S(1)}, u32[]{:S(2)}, u32[]{:S(2)}) collective-permute-start(f32[1,2048]{1,0:T(1,128)S(1)} %get-tuple-element.58), channel_id=1, source_target_pairs={{0,2},{1,3},{2,0},{3,1},{4,6},{5,7},{6,4},{7,5},{8,10},{9,11},{10,... | collective-permute-start | bytes 24584 | tf_op jit(solution)/shard_map/ppermute | solution.py:457
  37.2 3.0 %collective-permute-start.12 = (f32[1,2048]{1,0:T(1,128)S(1)}, f32[1,2048]{1,0:T(1,128)S(1)}, u32[]{:S(2)}, u32[]{:S(2)}) collective-permute-start(f32[1,2048]{1,0:T(1,128)S(1)} %get-tuple-element.58), channel_id=1, source_target_pairs={{0,1},{1,0},{2,3},{3,2},{4,5},{5,4},{6,7},{7,6},{8,9},{9,8},{10,11... | collective-permute-start | bytes 24584 | tf_op jit(solution)/shard_map/ppermute | solution.py:457
  40.3 5.5 %collective-permute-start.17 = (f32[1,2048]{1,0:T(1,128)S(1)}, f32[1,2048]{1,0:T(1,128)S(1)}, u32[]{:S(2)}, u32[]{:S(2)}) collective-permute-start(f32[1,2048]{1,0:T(1,128)S(1)} %add_add_fusion.4), channel_id=1, source_target_pairs={{0,12},{1,13},{2,14},{3,15},{4,8},{5,9},{6,10},{7,11},{8,4},{9,5},... | collective-permute-start | bytes 24584 | tf_op jit(solution)/shard_map/ppermute | solution.py:457
  42.8 4.6 %collective-permute-start.16 = (f32[1,2048]{1,0:T(1,128)S(1)}, f32[1,2048]{1,0:T(1,128)S(1)}, u32[]{:S(2)}, u32[]{:S(2)}) collective-permute-start(f32[1,2048]{1,0:T(1,128)S(1)} %add_add_fusion.4), channel_id=1, source_target_pairs={{0,8},{1,9},{2,10},{3,11},{4,12},{5,13},{6,14},{7,15},{8,0},{9,1},... | collective-permute-start | bytes 24584 | tf_op jit(solution)/shard_map/ppermute | solution.py:457
  43.7 3.7 %collective-permute-start.15 = (f32[1,2048]{1,0:T(1,128)S(1)}, f32[1,2048]{1,0:T(1,128)S(1)}, u32[]{:S(2)}, u32[]{:S(2)}) collective-permute-start(f32[1,2048]{1,0:T(1,128)S(1)} %add_add_fusion.4), channel_id=1, source_target_pairs={{0,4},{1,5},{2,6},{3,7},{4,0},{5,1},{6,2},{7,3},{8,12},{9,13},{10,... | collective-permute-start | bytes 24584 | tf_op jit(solution)/shard_map/ppermute | solution.py:457
  48.9 3.1 %collective-permute-start.20 = (f32[1,2048]{1,0:T(1,128)S(1)}, f32[1,2048]{1,0:T(1,128)S(1)}, u32[]{:S(2)}, u32[]{:S(2)}) collective-permute-start(f32[1,2048]{1,0:T(1,128)S(1)} %get-tuple-element.61), channel_id=1, source_target_pairs={{0,3},{1,2},{2,1},{3,0},{4,7},{5,6},{6,5},{7,4},{8,11},{9,10},{10,... | collective-permute-start | bytes 24584 | tf_op jit(solution)/shard_map/ppermute | solution.py:457
  49.0 3.7 %collective-permute-start.19 = (f32[1,2048]{1,0:T(1,128)S(1)}, f32[1,2048]{1,0:T(1,128)S(1)}, u32[]{:S(2)}, u32[]{:S(2)}) collective-permute-start(f32[1,2048]{1,0:T(1,128)S(1)} %get-tuple-element.61), channel_id=1, source_target_pairs={{0,2},{1,3},{2,0},{3,1},{4,6},{5,7},{6,4},{7,5},{8,10},{9,11},{10,... | collective-permute-start | bytes 24584 | tf_op jit(solution)/shard_map/ppermute | solution.py:457
  49.7 3.0 %collective-permute-start.18 = (f32[1,2048]{1,0:T(1,128)S(1)}, f32[1,2048]{1,0:T(1,128)S(1)}, u32[]{:S(2)}, u32[]{:S(2)}) collective-permute-start(f32[1,2048]{1,0:T(1,128)S(1)} %get-tuple-element.61), channel_id=1, source_target_pairs={{0,1},{1,0},{2,3},{3,2},{4,5},{5,4},{6,7},{7,6},{8,9},{9,8},{10,11... | collective-permute-start | bytes 24584 | tf_op jit(solution)/shard_map/ppermute | solution.py:457
  52.7 5.5 %collective-permute-start.23 = (f32[1,2048]{1,0:T(1,128)S(1)}, f32[1,2048]{1,0:T(1,128)S(1)}, u32[]{:S(2)}, u32[]{:S(2)}) collective-permute-start(f32[1,2048]{1,0:T(1,128)S(1)} %add_add_fusion.3), channel_id=1, source_target_pairs={{0,12},{1,13},{2,14},{3,15},{4,8},{5,9},{6,10},{7,11},{8,4},{9,5},... | collective-permute-start | bytes 24584 | tf_op jit(solution)/shard_map/ppermute | solution.py:457
  54.2 4.5 %collective-permute-start.22 = (f32[1,2048]{1,0:T(1,128)S(1)}, f32[1,2048]{1,0:T(1,128)S(1)}, u32[]{:S(2)}, u32[]{:S(2)}) collective-permute-start(f32[1,2048]{1,0:T(1,128)S(1)} %add_add_fusion.3), channel_id=1, source_target_pairs={{0,8},{1,9},{2,10},{3,11},{4,12},{5,13},{6,14},{7,15},{8,0},{9,1},... | collective-permute-start | bytes 24584 | tf_op jit(solution)/shard_map/ppermute | solution.py:457
  55.2 3.7 %collective-permute-start.21 = (f32[1,2048]{1,0:T(1,128)S(1)}, f32[1,2048]{1,0:T(1,128)S(1)}, u32[]{:S(2)}, u32[]{:S(2)}) collective-permute-start(f32[1,2048]{1,0:T(1,128)S(1)} %add_add_fusion.3), channel_id=1, source_target_pairs={{0,4},{1,5},{2,6},{3,7},{4,0},{5,1},{6,2},{7,3},{8,12},{9,13},{10,... | collective-permute-start | bytes 24584 | tf_op jit(solution)/shard_map/ppermute | solution.py:457
  60.3 3.1 %collective-permute-start.26 = (f32[1,2048]{1,0:T(1,128)S(1)}, f32[1,2048]{1,0:T(1,128)S(1)}, u32[]{:S(2)}, u32[]{:S(2)}) collective-permute-start(f32[1,2048]{1,0:T(1,128)S(1)} %get-tuple-element.66), channel_id=1, source_target_pairs={{0,3},{1,2},{2,1},{3,0},{4,7},{5,6},{6,5},{7,4},{8,11},{9,10},{10,... | collective-permute-start | bytes 24584 | tf_op jit(solution)/shard_map/ppermute | solution.py:457
  60.3 3.7 %collective-permute-start.25 = (f32[1,2048]{1,0:T(1,128)S(1)}, f32[1,2048]{1,0:T(1,128)S(1)}, u32[]{:S(2)}, u32[]{:S(2)}) collective-permute-start(f32[1,2048]{1,0:T(1,128)S(1)} %get-tuple-element.66), channel_id=1, source_target_pairs={{0,2},{1,3},{2,0},{3,1},{4,6},{5,7},{6,4},{7,5},{8,10},{9,11},{10,... | collective-permute-start | bytes 24584 | tf_op jit(solution)/shard_map/ppermute | solution.py:457
  61.0 3.0 %collective-permute-start.24 = (f32[1,2048]{1,0:T(1,128)S(1)}, f32[1,2048]{1,0:T(1,128)S(1)}, u32[]{:S(2)}, u32[]{:S(2)}) collective-permute-start(f32[1,2048]{1,0:T(1,128)S(1)} %get-tuple-element.66), channel_id=1, source_target_pairs={{0,1},{1,0},{2,3},{3,2},{4,5},{5,4},{6,7},{7,6},{8,9},{9,8},{10,11... | collective-permute-start | bytes 24584 | tf_op jit(solution)/shard_map/ppermute | solution.py:457
  64.1 5.5 %collective-permute-start.29 = (f32[1,2048]{1,0:T(1,128)S(1)}, f32[1,2048]{1,0:T(1,128)S(1)}, u32[]{:S(2)}, u32[]{:S(2)}) collective-permute-start(f32[1,2048]{1,0:T(1,128)S(1)} %add_add_fusion.2), channel_id=1, source_target_pairs={{0,12},{1,13},{2,14},{3,15},{4,8},{5,9},{6,10},{7,11},{8,4},{9,5},... | collective-permute-start | bytes 24584 | tf_op jit(solution)/shard_map/ppermute | solution.py:457
  66.7 4.5 %collective-permute-start.28 = (f32[1,2048]{1,0:T(1,128)S(1)}, f32[1,2048]{1,0:T(1,128)S(1)}, u32[]{:S(2)}, u32[]{:S(2)}) collective-permute-start(f32[1,2048]{1,0:T(1,128)S(1)} %add_add_fusion.2), channel_id=1, source_target_pairs={{0,8},{1,9},{2,10},{3,11},{4,12},{5,13},{6,14},{7,15},{8,0},{9,1},... | collective-permute-start | bytes 24584 | tf_op jit(solution)/shard_map/ppermute | solution.py:457
  67.6 3.7 %collective-permute-start.27 = (f32[1,2048]{1,0:T(1,128)S(1)}, f32[1,2048]{1,0:T(1,128)S(1)}, u32[]{:S(2)}, u32[]{:S(2)}) collective-permute-start(f32[1,2048]{1,0:T(1,128)S(1)} %add_add_fusion.2), channel_id=1, source_target_pairs={{0,4},{1,5},{2,6},{3,7},{4,0},{5,1},{6,2},{7,3},{8,12},{9,13},{10,... | collective-permute-start | bytes 24584 | tf_op jit(solution)/shard_map/ppermute | solution.py:457
  71.3 11.6 %copy-start = (bf16[1024,512]{1,0:T(8,128)(2,1)S(1)}, bf16[1024,512]{1,0:T(8,128)(2,1)}, u32[]{:S(2)}) copy-start(bf16[1024,512]{1,0:T(8,128)(2,1)} %y_ref.5) | copy-start | bytes 3145732
  72.9 3.1 %collective-permute-start.32 = (f32[1,2048]{1,0:T(1,128)S(1)}, f32[1,2048]{1,0:T(1,128)S(1)}, u32[]{:S(2)}, u32[]{:S(2)}) collective-permute-start(f32[1,2048]{1,0:T(1,128)S(1)} %get-tuple-element.68.after_ref), channel_id=1, source_target_pairs={{0,3},{1,2},{2,1},{3,0},{4,7},{5,6},{6,5},{7,4},{8,11},{9,10},{10,... | collective-permute-start | bytes 24584 | tf_op jit(solution)/shard_map/ppermute | solution.py:457
  73.0 3.7 %collective-permute-start.31 = (f32[1,2048]{1,0:T(1,128)S(1)}, f32[1,2048]{1,0:T(1,128)S(1)}, u32[]{:S(2)}, u32[]{:S(2)}) collective-permute-start(f32[1,2048]{1,0:T(1,128)S(1)} %get-tuple-element.68.after_ref), channel_id=1, source_target_pairs={{0,2},{1,3},{2,0},{3,1},{4,6},{5,7},{6,4},{7,5},{8,10},{9,11},{10,... | collective-permute-start | bytes 24584 | tf_op jit(solution)/shard_map/ppermute | solution.py:457
  73.7 3.0 %collective-permute-start.30 = (f32[1,2048]{1,0:T(1,128)S(1)}, f32[1,2048]{1,0:T(1,128)S(1)}, u32[]{:S(2)}, u32[]{:S(2)}) collective-permute-start(f32[1,2048]{1,0:T(1,128)S(1)} %get-tuple-element.68.after_ref), channel_id=1, source_target_pairs={{0,1},{1,0},{2,3},{3,2},{4,5},{5,4},{6,7},{7,6},{8,9},{9,8},{10,11... | collective-permute-start | bytes 24584 | tf_op jit(solution)/shard_map/ppermute | solution.py:457
  76.8 5.5 %collective-permute-start.35 = (f32[1,2048]{1,0:T(1,128)S(1)}, f32[1,2048]{1,0:T(1,128)S(1)}, u32[]{:S(2)}, u32[]{:S(2)}) collective-permute-start(f32[1,2048]{1,0:T(1,128)S(1)} %add_add_fusion.1), channel_id=1, source_target_pairs={{0,12},{1,13},{2,14},{3,15},{4,8},{5,9},{6,10},{7,11},{8,4},{9,5},... | collective-permute-start | bytes 24584 | tf_op jit(solution)/shard_map/ppermute | solution.py:457
  78.2 4.5 %collective-permute-start.34 = (f32[1,2048]{1,0:T(1,128)S(1)}, f32[1,2048]{1,0:T(1,128)S(1)}, u32[]{:S(2)}, u32[]{:S(2)}) collective-permute-start(f32[1,2048]{1,0:T(1,128)S(1)} %add_add_fusion.1), channel_id=1, source_target_pairs={{0,8},{1,9},{2,10},{3,11},{4,12},{5,13},{6,14},{7,15},{8,0},{9,1},... | collective-permute-start | bytes 24584 | tf_op jit(solution)/shard_map/ppermute | solution.py:457
  79.2 3.7 %collective-permute-start.33 = (f32[1,2048]{1,0:T(1,128)S(1)}, f32[1,2048]{1,0:T(1,128)S(1)}, u32[]{:S(2)}, u32[]{:S(2)}) collective-permute-start(f32[1,2048]{1,0:T(1,128)S(1)} %add_add_fusion.1), channel_id=1, source_target_pairs={{0,4},{1,5},{2,6},{3,7},{4,0},{5,1},{6,2},{7,3},{8,12},{9,13},{10,... | collective-permute-start | bytes 24584 | tf_op jit(solution)/shard_map/ppermute | solution.py:457
  86.5 2.4 %collective-permute-start.38 = (f32[8,48,512]{2,1,0:T(8,128)S(1)}, f32[8,48,512]{2,1,0:T(8,128)S(1)}, u32[]{:S(2)}, u32[]{:S(2)}) collective-permute-start(f32[8,48,512]{2,1,0:T(8,128)S(1)} %get-tuple-element.77), channel_id=1, source_target_pairs={{0,1},{1,0},{2,3},{3,2},{4,5},{5,4},{6,7},{7,6},{8,9},{9,8},{10,11... | collective-permute-start | bytes 2359304 | tf_op jit(solution)/shard_map/ppermute | solution.py:457
  86.6 3.4 %collective-permute-start.37 = (f32[8,48,512]{2,1,0:T(8,128)S(1)}, f32[8,48,512]{2,1,0:T(8,128)S(1)}, u32[]{:S(2)}, u32[]{:S(2)}) collective-permute-start(f32[8,48,512]{2,1,0:T(8,128)S(1)} %get-tuple-element.75), channel_id=1, source_target_pairs={{0,1},{1,0},{2,3},{3,2},{4,5},{5,4},{6,7},{7,6},{8,9},{9,8},{10,11... | collective-permute-start | bytes 2359304 | tf_op jit(solution)/shard_map/ppermute | solution.py:457
  87.1 3.6 %collective-permute-start.36 = (f32[8,32,512]{2,1,0:T(8,128)S(1)}, f32[8,32,512]{2,1,0:T(8,128)S(1)}, u32[]{:S(2)}, u32[]{:S(2)}) collective-permute-start(f32[8,32,512]{2,1,0:T(8,128)S(1)} %get-tuple-element.73), channel_id=1, source_target_pairs={{0,1},{1,0},{2,3},{3,2},{4,5},{5,4},{6,7},{7,6},{8,9},{9,8},{10,11... | collective-permute-start | bytes 1572872 | tf_op jit(solution)/shard_map/ppermute | solution.py:457
  87.2 6.4 %copy-start.1 = (bf16[2048,512]{1,0:T(8,128)(2,1)S(1)}, bf16[2048,512]{1,0:T(8,128)(2,1)}, u32[]{:S(2)}) copy-start(bf16[2048,512]{1,0:T(8,128)(2,1)} %x_ref.1) | copy-start | bytes 6291460
  89.0 12.0 %collective-permute-start.39 = (f32[4,48,512]{2,1,0:T(8,128)S(1)}, f32[4,48,512]{2,1,0:T(8,128)S(1)}, u32[]{:S(2)}, u32[]{:S(2)}) collective-permute-start(f32[4,48,512]{2,1,0:T(8,128)S(1)} %get-tuple-element.78.after_ref), channel_id=1, source_target_pairs={{0,2},{1,3},{2,0},{3,1},{4,6},{5,7},{6,4},{7,5},{8,10},{9,11},{10,... | collective-permute-start | bytes 1179656 | tf_op jit(solution)/shard_map/ppermute | solution.py:457
  90.8 8.7 %collective-permute-start.40 = (f32[4,32,512]{2,1,0:T(8,128)S(1)}, f32[4,32,512]{2,1,0:T(8,128)S(1)}, u32[]{:S(2)}, u32[]{:S(2)}) collective-permute-start(f32[4,32,512]{2,1,0:T(8,128)S(1)} %get-tuple-element.80.after_ref), channel_id=1, source_target_pairs={{0,4},{1,5},{2,6},{3,7},{4,0},{5,1},{6,2},{7,3},{8,12},{9,13},{10,... | collective-permute-start | bytes 786440 | tf_op jit(solution)/shard_map/ppermute | solution.py:457
  92.9 16.7 %collective-permute-start.44 = (f32[4,48,512]{2,1,0:T(8,128)S(1)}, f32[4,48,512]{2,1,0:T(8,128)S(1)}, u32[]{:S(2)}, u32[]{:S(2)}) collective-permute-start(f32[4,48,512]{2,1,0:T(8,128)S(1)} %get-tuple-element.79.after_ref), channel_id=1, source_target_pairs={{0,2},{1,3},{2,0},{3,1},{4,6},{5,7},{6,4},{7,5},{8,10},{9,11},{10,... | collective-permute-start | bytes 1179656 | tf_op jit(solution)/shard_map/ppermute | solution.py:457
  101.1 8.5 %collective-permute-start.41 = (f32[2,48,512]{2,1,0:T(8,128)S(1)}, f32[2,48,512]{2,1,0:T(8,128)S(1)}, u32[]{:S(2)}, u32[]{:S(2)}) collective-permute-start(f32[2,48,512]{2,1,0:T(8,128)S(1)} %get-tuple-element.88.after_ref), channel_id=1, source_target_pairs={{0,4},{1,5},{2,6},{3,7},{4,0},{5,1},{6,2},{7,3},{8,12},{9,13},{10,... | collective-permute-start | bytes 589832 | tf_op jit(solution)/shard_map/ppermute | solution.py:457
  103.2 6.2 %collective-permute-start.42 = (f32[2,32,512]{2,1,0:T(8,128)S(1)}, f32[2,32,512]{2,1,0:T(8,128)S(1)}, u32[]{:S(2)}, u32[]{:S(2)}) collective-permute-start(f32[2,32,512]{2,1,0:T(8,128)S(1)} %get-tuple-element.86.after_ref), channel_id=1, source_target_pairs={{0,8},{1,9},{2,10},{3,11},{4,12},{5,13},{6,14},{7,15},{8,0},{9,1},... | collective-permute-start | bytes 393224 | tf_op jit(solution)/shard_map/ppermute | solution.py:457
  109.7 8.5 %collective-permute-start.45 = (f32[2,48,512]{2,1,0:T(8,128)S(1)}, f32[2,48,512]{2,1,0:T(8,128)S(1)}, u32[]{:S(2)}, u32[]{:S(2)}) collective-permute-start(f32[2,48,512]{2,1,0:T(8,128)S(1)} %get-tuple-element.95.after_ref), channel_id=1, source_target_pairs={{0,4},{1,5},{2,6},{3,7},{4,0},{5,1},{6,2},{7,3},{8,12},{9,13},{10,... | collective-permute-start | bytes 589832 | tf_op jit(solution)/shard_map/ppermute | solution.py:457
  111.4 11.2 %collective-permute-start.43 = (f32[1,48,512]{2,1,0:T(8,128)S(1)}, f32[1,48,512]{2,1,0:T(8,128)S(1)}, u32[]{:S(2)}, u32[]{:S(2)}) collective-permute-start(f32[1,48,512]{2,1,0:T(8,128)S(1)} %get-tuple-element.92.after_ref), channel_id=1, source_target_pairs={{0,8},{1,9},{2,10},{3,11},{4,12},{5,13},{6,14},{7,15},{8,0},{9,1},... | collective-permute-start | bytes 294920 | tf_op jit(solution)/shard_map/ppermute | solution.py:457
  118.2 6.1 %collective-permute-start.46 = (f32[1,48,512]{2,1,0:T(8,128)S(1)}, f32[1,48,512]{2,1,0:T(8,128)S(1)}, u32[]{:S(2)}, u32[]{:S(2)}) collective-permute-start(f32[1,48,512]{2,1,0:T(8,128)S(1)} %get-tuple-element.97), channel_id=1, source_target_pairs={{0,8},{1,9},{2,10},{3,11},{4,12},{5,13},{6,14},{7,15},{8,0},{9,1},... | collective-permute-start | bytes 294920 | tf_op jit(solution)/shard_map/ppermute | solution.py:457
  118.3 4.3 %collective-permute-start.47 = (f32[1,32,512]{2,1,0:T(8,128)S(1)}, f32[1,32,512]{2,1,0:T(8,128)S(1)}, u32[]{:S(2)}, u32[]{:S(2)}) collective-permute-start(f32[1,32,512]{2,1,0:T(8,128)S(1)} %get-tuple-element.90.after_ref), channel_id=1, source_target_pairs={{0,2},{1,3},{2,0},{3,1},{4,6},{5,7},{6,4},{7,5},{8,10},{9,11},{10,... | collective-permute-start | bytes 196616 | tf_op jit(solution)/shard_map/ppermute | solution.py:457
